TPU v7x, 32 devices: a whole 2x2x4 slice. The times are simulated.
32 devices in a mesh: rep: 4 (over x, core), fsdp: 8 (over z, y).
Axes of the slice: x: 2, y: 2, z: 4, core: 2. Of those that a mesh axis runs over, the one named last changes fastest.
Arguments:
- tokens: bfloat16 [256, 196, 768], P(('rep', 'fsdp')), may hold values from -6 to 6
- teacher: bfloat16 [256, 196, 768], P(('rep', 'fsdp')), may hold values from -6 to 6
- valid_mask: int32 [256, 196], P(('rep', 'fsdp')), may hold values from 0 to 1, as said below
- attn_gain: bfloat16 [768], P('fsdp'), may hold values from 0.099609375 to 1.8984375
- attn_shift: bfloat16 [768], P('fsdp'), may hold values from -1.75 to 1.75
- qkv_weight: bfloat16 [768, 2304], P('fsdp'), may hold values from -0.21875 to 0.21875
- query_bias: bfloat16 [768], P('fsdp'), may hold values from -3 to 3
- value_bias: bfloat16 [768], P('fsdp'), may hold values from -3 to 3
- rel_pos_h: bfloat16 [27, 64], P(None, 'fsdp'), may hold values from -0.375 to 0.375
- rel_pos_w: bfloat16 [27, 64], P(None, 'fsdp'), may hold values from -0.375 to 0.375
- proj_weight: bfloat16 [768, 768], P('fsdp'), may hold values from -0.625 to 0.625
- proj_bias: bfloat16 [768], P('fsdp'), may hold values from -1.75 to 1.75
- mlp_gain: bfloat16 [768], P('fsdp'), may hold values from 0.099609375 to 1.8984375
- mlp_shift: bfloat16 [768], P('fsdp'), may hold values from -1.75 to 1.75
- up_weight: bfloat16 [768, 3072], P('fsdp'), may hold values from -0.21875 to 0.21875
- up_bias: bfloat16 [3072], P('fsdp'), may hold values from -1.75 to 1.75
- down_weight: bfloat16 [3072, 768], P('fsdp'), may hold values from -0.15625 to 0.15625
- down_bias: bfloat16 [768], P('fsdp'), may hold values from -1.75 to 1.75
Outputs:
- block_output: bfloat16 [256, 196, 768], P(('rep', 'fsdp'))
- loss: float32 [], replicated
- input_grad: float32 [256, 196, 768], P(('rep', 'fsdp'))
- attn_gain_grad: float32 [768], P('fsdp')
- attn_shift_grad: float32 [768], P('fsdp')
- qkv_weight_grad: float32 [768, 2304], P('fsdp')
- query_bias_grad: float32 [768], P('fsdp')
- value_bias_grad: float32 [768], P('fsdp')
- rel_pos_h_grad: float32 [27, 64], P(None, 'fsdp')
- rel_pos_w_grad: float32 [27, 64], P(None, 'fsdp')
- proj_weight_grad: float32 [768, 768], P('fsdp')
- proj_bias_grad: float32 [768], P('fsdp')
- mlp_gain_grad: float32 [768], P('fsdp')
- mlp_shift_grad: float32 [768], P('fsdp')
- up_weight_grad: float32 [768, 3072], P('fsdp')
- up_bias_grad: float32 [3072], P('fsdp')
- down_weight_grad: float32 [3072, 768], P('fsdp')
- down_bias_grad: float32 [768], P('fsdp')
Inputs may be any that keep to these rules, and one draw needn't show every extreme that they name: `valid_mask`: the first slot of every window is 1.
All inputs are finite; a program needn't handle non-finite values.
Results may differ from a plain program's by a relative error of at most 0.01.
Values may be sent and summed in bfloat16 or wider, within the bound.
No kernel may reach another device: no remote copies, remote signals or barrier semaphores. Data moves between devices by JAX's collectives and lax.ppermute only.
A program may use at most 384 MiB of HBM per device.

v0:
```python
import math

import jax
import jax.numpy as jnp
from jax import lax
from jax.sharding import PartitionSpec as P

D = 768
HEADS = 12
HEAD_DIM = 64
WIN = 14
MAP = 64


LN_EPS = 1e-06
SQRT_HALF = 0.7071067811865476
INV_ROOT_TAU = 0.3989422804014327
HIGH = lax.Precision.HIGHEST


def layer_norm(values, gain, shift):
    row_mean = jnp.mean(values, axis=-1, keepdims=True)
    centred = values - row_mean
    inv_std = lax.rsqrt(jnp.mean(centred * centred, axis=-1, keepdims=True) + LN_EPS)
    scaled = centred * inv_std
    return (scaled * gain + shift, scaled, inv_std)


def norm_back(grad_norm, scaled, inv_std, gain):
    grad_scaled = grad_norm * gain
    first_mean = jnp.mean(grad_scaled, axis=-1, keepdims=True)
    second_mean = jnp.mean(grad_scaled * scaled, axis=-1, keepdims=True)
    grad_input = inv_std * (grad_scaled - first_mean - scaled * second_mean)
    return (grad_input, jnp.sum(grad_norm * scaled, axis=0), jnp.sum(grad_norm, axis=0))


def gelu_slope(values):
    return (
        0.5 * (1.0 + lax.erf(values * SQRT_HALF))
        + values * jnp.exp(-0.5 * values * values) * INV_ROOT_TAU
    )


def inner_rows(left, right):
    return lax.dot_general(
        left, right, (((0,), (0,)), ((), ())), preferred_element_type=jnp.float32
    )


def times_trans(left, right):
    return lax.dot_general(
        left, right, (((1,), (1,)), ((), ())), preferred_element_type=jnp.float32
    )


def offset_onehot():
    positions = jnp.arange(WIN, dtype=jnp.int32)
    target = positions[:, None] - positions[None, :] + WIN - 1
    return (target[:, :, None] == jnp.arange(2 * WIN - 1, dtype=jnp.int32)[None, None, :]).astype(
        jnp.float32
    )


def window_scores(query, keys, table_h, table_w):
    group_size = query.shape[0]
    slot_count = WIN * WIN
    plain = jnp.einsum(
        "aihd,ajhd->ahij", query, keys, preferred_element_type=jnp.float32
    ) * HEAD_DIM ** (-0.5)
    grid_query = query.reshape(group_size, WIN, WIN, HEADS, HEAD_DIM)
    along_h = jnp.einsum(
        "archd,rkd->ahrck", grid_query, table_h, preferred_element_type=jnp.float32
    )
    along_w = jnp.einsum(
        "archd,ckd->ahrck", grid_query, table_w, preferred_element_type=jnp.float32
    )
    scores = (
        plain.reshape(group_size, HEADS, WIN, WIN, WIN, WIN)
        + along_h[..., :, None]
        + along_w[..., None, :]
    )
    return scores.reshape(group_size, HEADS, slot_count, slot_count)


def body(
    tokens,
    teacher,
    valid_mask,
    attn_gain,
    attn_shift,
    qkv_weight,
    query_bias,
    value_bias,
    rel_pos_h,
    rel_pos_w,
    proj_weight,
    proj_bias,
    mlp_gain,
    mlp_shift,
    up_weight,
    up_bias,
    down_weight,
    down_bias,
):
    win_local = tokens.shape[0]
    slot_count = WIN * WIN
    row_count = win_local * slot_count
    grid_side = (MAP + WIN - 1) // WIN
    device = lax.axis_index("rep") * lax.axis_size("fsdp") + lax.axis_index("fsdp")
    window_ids = device * win_local + jnp.arange(win_local, dtype=jnp.int32)
    map_place = window_ids % (grid_side * grid_side)
    cell_ids = jnp.arange(slot_count, dtype=jnp.int32)
    inside = ((map_place // grid_side)[:, None] * WIN + (cell_ids // WIN)[None, :] < MAP) & (
        (map_place % grid_side)[:, None] * WIN + (cell_ids % WIN)[None, :] < MAP
    )
    keep_rows = inside.astype(jnp.float32).reshape(row_count, 1)
    valid_rows = valid_mask.reshape(row_count, 1).astype(jnp.float32) * keep_rows
    count_part = jnp.sum(valid_rows)
    attn_set = (
        lax.all_gather(qkv_weight, "fsdp", axis=0, tiled=True),
        lax.all_gather(proj_weight, "fsdp", axis=0, tiled=True),
        lax.all_gather(attn_gain, "fsdp", axis=0, tiled=True),
        lax.all_gather(attn_shift, "fsdp", axis=0, tiled=True),
        lax.all_gather(query_bias, "fsdp", axis=0, tiled=True),
        lax.all_gather(value_bias, "fsdp", axis=0, tiled=True),
        lax.all_gather(proj_bias, "fsdp", axis=0, tiled=True),
        lax.all_gather(rel_pos_h, "fsdp", axis=1, tiled=True),
        lax.all_gather(rel_pos_w, "fsdp", axis=1, tiled=True),
    )
    mlp_set = (
        lax.all_gather(up_weight, "fsdp", axis=0, tiled=True),
        lax.all_gather(down_weight, "fsdp", axis=0, tiled=True),
        lax.all_gather(mlp_gain, "fsdp", axis=0, tiled=True),
        lax.all_gather(mlp_shift, "fsdp", axis=0, tiled=True),
        lax.all_gather(up_bias, "fsdp", axis=0, tiled=True),
        lax.all_gather(down_bias, "fsdp", axis=0, tiled=True),
    )
    onehot = offset_onehot()
    score_scale = HEAD_DIM ** (-0.5)
    inputs = tokens.reshape(row_count, D).astype(jnp.float32)
    normed, scaled_first, inv_first = layer_norm(
        inputs, attn_set[2].astype(jnp.float32), attn_set[3].astype(jnp.float32)
    )
    first_in = (normed * keep_rows).astype(jnp.bfloat16)
    bias_row = jnp.concatenate(
        [
            attn_set[4].astype(jnp.float32),
            jnp.zeros((D,), jnp.float32),
            attn_set[5].astype(jnp.float32),
        ]
    )
    qkv_low = (
        jnp.dot(first_in, attn_set[0], preferred_element_type=jnp.float32) + bias_row
    ).astype(jnp.bfloat16)
    table_h = jnp.einsum("rkm,md->rkd", onehot, attn_set[7].astype(jnp.float32)).astype(
        jnp.bfloat16
    )
    table_w = jnp.einsum("rkm,md->rkd", onehot, attn_set[8].astype(jnp.float32)).astype(
        jnp.bfloat16
    )
    group_size = math.gcd(win_local, 4)
    block_count = win_local // group_size
    heads_shape = (block_count, group_size, slot_count, HEADS, HEAD_DIM)
    query = qkv_low[:, :D].reshape(heads_shape)
    keys = qkv_low[:, D : 2 * D].reshape(heads_shape)
    values = qkv_low[:, 2 * D :].reshape(heads_shape)

    def attend_forward(pieces):
        block_query, block_keys, block_values = pieces
        scores = window_scores(block_query, block_keys, table_h, table_w)
        row_peak = jnp.max(scores, axis=-1, keepdims=True)
        exponent = jnp.exp(scores - row_peak)
        row_total = jnp.sum(exponent, axis=-1, keepdims=True)
        attn_prob = (exponent / row_total).astype(jnp.bfloat16)
        mixed_heads = jnp.einsum(
            "ahij,ajhd->aihd", attn_prob, block_values, preferred_element_type=jnp.float32
        )
        return (mixed_heads.astype(jnp.bfloat16), row_peak + jnp.log(row_total))

    mixed_heads, log_total = lax.map(attend_forward, (query, keys, values))
    mixed_rows = mixed_heads.reshape(row_count, D)
    attn_out = jnp.dot(mixed_rows, attn_set[1], preferred_element_type=jnp.float32) + attn_set[
        6
    ].astype(jnp.float32)
    hidden = keep_rows * (inputs + attn_out)
    normed_second, scaled_second, inv_second = layer_norm(
        hidden, mlp_set[2].astype(jnp.float32), mlp_set[3].astype(jnp.float32)
    )
    second_in = normed_second.astype(jnp.bfloat16)
    up_pre = jnp.dot(second_in, mlp_set[0], preferred_element_type=jnp.float32) + mlp_set[4].astype(
        jnp.float32
    )
    up_low = jax.nn.gelu(up_pre, approximate=False).astype(jnp.bfloat16)
    down_out = jnp.dot(up_low, mlp_set[1], preferred_element_type=jnp.float32) + mlp_set[5].astype(
        jnp.float32
    )
    final = keep_rows * (hidden + down_out)
    error_term = final - teacher.reshape(row_count, D).astype(jnp.float32)
    loss_part = jnp.sum(valid_rows * error_term * error_term)
    valid_total, loss_total = lax.psum((count_part, loss_part), ("rep", "fsdp"))
    attn_back = (
        lax.all_gather(qkv_weight, "fsdp", axis=0, tiled=True),
        lax.all_gather(proj_weight, "fsdp", axis=0, tiled=True),
        lax.all_gather(attn_gain, "fsdp", axis=0, tiled=True),
        lax.all_gather(attn_shift, "fsdp", axis=0, tiled=True),
        lax.all_gather(query_bias, "fsdp", axis=0, tiled=True),
        lax.all_gather(value_bias, "fsdp", axis=0, tiled=True),
        lax.all_gather(proj_bias, "fsdp", axis=0, tiled=True),
        lax.all_gather(rel_pos_h, "fsdp", axis=1, tiled=True),
        lax.all_gather(rel_pos_w, "fsdp", axis=1, tiled=True),
    )
    mlp_back = (
        lax.all_gather(up_weight, "fsdp", axis=0, tiled=True),
        lax.all_gather(down_weight, "fsdp", axis=0, tiled=True),
        lax.all_gather(mlp_gain, "fsdp", axis=0, tiled=True),
        lax.all_gather(mlp_shift, "fsdp", axis=0, tiled=True),
        lax.all_gather(up_bias, "fsdp", axis=0, tiled=True),
        lax.all_gather(down_bias, "fsdp", axis=0, tiled=True),
    )
    loss_scale = 64.0 * D * win_local * lax.axis_size("rep") * lax.axis_size("fsdp")
    grad_final = loss_scale * 2.0 / (valid_total * D) * valid_rows * error_term
    grad_down = grad_final.astype(jnp.bfloat16)
    down_bias_grad = jnp.sum(grad_down, axis=0, dtype=jnp.float32)
    down_weight_grad = inner_rows(up_low, grad_down)
    grad_up = (times_trans(grad_down, mlp_back[1]) * gelu_slope(up_pre)).astype(jnp.bfloat16)
    up_bias_grad = jnp.sum(grad_up, axis=0, dtype=jnp.float32)
    up_weight_grad = inner_rows(second_in, grad_up)
    grad_second = times_trans(grad_up, mlp_back[0])
    grad_norm_two, mlp_gain_grad, mlp_shift_grad = norm_back(
        grad_second, scaled_second, inv_second, mlp_back[2].astype(jnp.float32)
    )
    grad_hidden = grad_final + grad_norm_two
    mlp_parts = (
        lax.psum_scatter(
            up_weight_grad.astype(jnp.bfloat16), "fsdp", scatter_dimension=0, tiled=True
        ).astype(jnp.float32),
        lax.psum_scatter(
            down_weight_grad.astype(jnp.bfloat16), "fsdp", scatter_dimension=0, tiled=True
        ).astype(jnp.float32),
        lax.psum_scatter(
            mlp_gain_grad.astype(jnp.bfloat16), "fsdp", scatter_dimension=0, tiled=True
        ).astype(jnp.float32),
        lax.psum_scatter(
            mlp_shift_grad.astype(jnp.bfloat16), "fsdp", scatter_dimension=0, tiled=True
        ).astype(jnp.float32),
        lax.psum_scatter(
            up_bias_grad.astype(jnp.bfloat16), "fsdp", scatter_dimension=0, tiled=True
        ).astype(jnp.float32),
        lax.psum_scatter(
            down_bias_grad.astype(jnp.bfloat16), "fsdp", scatter_dimension=0, tiled=True
        ).astype(jnp.float32),
    )
    grad_attn = (keep_rows * grad_hidden).astype(jnp.bfloat16)
    proj_bias_grad = jnp.sum(grad_attn, axis=0, dtype=jnp.float32)
    proj_weight_grad = inner_rows(mixed_rows, grad_attn)
    grad_mixed = times_trans(grad_attn, attn_back[1]).astype(jnp.bfloat16).reshape(heads_shape)
    back_table_h = jnp.einsum("rkm,md->rkd", onehot, attn_back[7].astype(jnp.float32))
    back_table_w = jnp.einsum("rkm,md->rkd", onehot, attn_back[8].astype(jnp.float32))
    low_table_h = back_table_h.astype(jnp.bfloat16)
    low_table_w = back_table_w.astype(jnp.bfloat16)

    def attend_back(pieces):
        block_query, block_keys, block_values, block_log, block_grad = pieces
        scores = window_scores(block_query, block_keys, low_table_h, low_table_w)
        attn_prob = jnp.exp(scores - block_log)
        grad_prob = jnp.einsum(
            "aihd,ajhd->ahij", block_grad, block_values, preferred_element_type=jnp.float32
        )
        row_dot = jnp.sum(attn_prob * grad_prob, axis=-1, keepdims=True)
        grad_score = (attn_prob * (grad_prob - row_dot)).astype(jnp.bfloat16)
        grad_value = jnp.einsum(
            "ahij,aihd->ajhd",
            attn_prob.astype(jnp.bfloat16),
            block_grad,
            preferred_element_type=jnp.float32,
        )
        grad_key = (
            jnp.einsum(
                "ahij,aihd->ajhd", grad_score, block_query, preferred_element_type=jnp.float32
            )
            * score_scale
        )
        grid_score = grad_score.reshape(group_size, HEADS, WIN, WIN, WIN, WIN)
        sum_rows = jnp.sum(grid_score, axis=-1, dtype=jnp.float32)
        sum_cols = jnp.sum(grid_score, axis=-2, dtype=jnp.float32)
        grad_query = (
            jnp.einsum(
                "ahij,ajhd->aihd", grad_score, block_keys, preferred_element_type=jnp.float32
            )
            * score_scale
        )
        position_part = jnp.einsum(
            "ahrck,rkd->archd", sum_rows, back_table_h, precision=HIGH
        ) + jnp.einsum("ahrck,ckd->archd", sum_cols, back_table_w, precision=HIGH)
        grad_query = grad_query + position_part.reshape(group_size, slot_count, HEADS, HEAD_DIM)
        grid_query = block_query.astype(jnp.float32).reshape(group_size, WIN, WIN, HEADS, HEAD_DIM)
        grad_table_h = jnp.einsum("ahrck,archd->rkd", sum_rows, grid_query, precision=HIGH)
        grad_table_w = jnp.einsum("ahrck,archd->ckd", sum_cols, grid_query, precision=HIGH)
        return (
            grad_query.astype(jnp.bfloat16),
            grad_key.astype(jnp.bfloat16),
            grad_value.astype(jnp.bfloat16),
            grad_table_h,
            grad_table_w,
        )

    grad_query, grad_keys, grad_values, table_h_grad, table_w_grad = lax.map(
        attend_back, (query, keys, values, log_total, grad_mixed)
    )
    rel_pos_h_grad = jnp.einsum(
        "rkm,rkd->md", onehot, jnp.sum(table_h_grad, axis=0), precision=HIGH
    )
    rel_pos_w_grad = jnp.einsum(
        "rkm,rkd->md", onehot, jnp.sum(table_w_grad, axis=0), precision=HIGH
    )
    query_rows = grad_query.reshape(row_count, D)
    value_rows = grad_values.reshape(row_count, D)
    qkv_grad_low = jnp.concatenate(
        [query_rows, grad_keys.reshape(row_count, D), value_rows], axis=1
    )
    query_bias_grad = jnp.sum(query_rows, axis=0, dtype=jnp.float32)
    value_bias_grad = jnp.sum(value_rows, axis=0, dtype=jnp.float32)
    qkv_weight_grad = inner_rows(first_in, qkv_grad_low)
    grad_first = times_trans(qkv_grad_low, attn_back[0]) * keep_rows
    grad_norm_one, attn_gain_grad, attn_shift_grad = norm_back(
        grad_first, scaled_first, inv_first, attn_back[2].astype(jnp.float32)
    )
    input_grad = keep_rows * grad_hidden + grad_norm_one
    attn_parts = (
        lax.psum_scatter(
            qkv_weight_grad.astype(jnp.bfloat16), "fsdp", scatter_dimension=0, tiled=True
        ).astype(jnp.float32),
        lax.psum_scatter(
            proj_weight_grad.astype(jnp.bfloat16), "fsdp", scatter_dimension=0, tiled=True
        ).astype(jnp.float32),
        lax.psum_scatter(
            attn_gain_grad.astype(jnp.bfloat16), "fsdp", scatter_dimension=0, tiled=True
        ).astype(jnp.float32),
        lax.psum_scatter(
            attn_shift_grad.astype(jnp.bfloat16), "fsdp", scatter_dimension=0, tiled=True
        ).astype(jnp.float32),
        lax.psum_scatter(
            query_bias_grad.astype(jnp.bfloat16), "fsdp", scatter_dimension=0, tiled=True
        ).astype(jnp.float32),
        lax.psum_scatter(
            value_bias_grad.astype(jnp.bfloat16), "fsdp", scatter_dimension=0, tiled=True
        ).astype(jnp.float32),
        lax.psum_scatter(
            proj_bias_grad.astype(jnp.bfloat16), "fsdp", scatter_dimension=0, tiled=True
        ).astype(jnp.float32),
        lax.psum_scatter(
            rel_pos_h_grad.astype(jnp.bfloat16), "fsdp", scatter_dimension=1, tiled=True
        ).astype(jnp.float32),
        lax.psum_scatter(
            rel_pos_w_grad.astype(jnp.bfloat16), "fsdp", scatter_dimension=1, tiled=True
        ).astype(jnp.float32),
    )
    summed = (
        lax.psum(attn_parts[2].astype(jnp.bfloat16), "rep").astype(jnp.float32),
        lax.psum(attn_parts[3].astype(jnp.bfloat16), "rep").astype(jnp.float32),
        lax.psum(attn_parts[0].astype(jnp.bfloat16), "rep").astype(jnp.float32),
        lax.psum(attn_parts[4].astype(jnp.bfloat16), "rep").astype(jnp.float32),
        lax.psum(attn_parts[5].astype(jnp.bfloat16), "rep").astype(jnp.float32),
        lax.psum(attn_parts[7].astype(jnp.bfloat16), "rep").astype(jnp.float32),
        lax.psum(attn_parts[8].astype(jnp.bfloat16), "rep").astype(jnp.float32),
        lax.psum(attn_parts[1].astype(jnp.bfloat16), "rep").astype(jnp.float32),
        lax.psum(attn_parts[6].astype(jnp.bfloat16), "rep").astype(jnp.float32),
        lax.psum(mlp_parts[2].astype(jnp.bfloat16), "rep").astype(jnp.float32),
        lax.psum(mlp_parts[3].astype(jnp.bfloat16), "rep").astype(jnp.float32),
        lax.psum(mlp_parts[0].astype(jnp.bfloat16), "rep").astype(jnp.float32),
        lax.psum(mlp_parts[4].astype(jnp.bfloat16), "rep").astype(jnp.float32),
        lax.psum(mlp_parts[1].astype(jnp.bfloat16), "rep").astype(jnp.float32),
        lax.psum(mlp_parts[5].astype(jnp.bfloat16), "rep").astype(jnp.float32),
    )
    loss = loss_total / (valid_total * D)
    return (
        final.astype(jnp.bfloat16).reshape(tokens.shape),
        loss,
        input_grad.reshape(tokens.shape),
        summed[0],
        summed[1],
        summed[2],
        summed[3],
        summed[4],
        summed[5],
        summed[6],
        summed[7],
        summed[8],
        summed[9],
        summed[10],
        summed[11],
        summed[12],
        summed[13],
        summed[14],
    )


def solution(mesh):
    in_specs = (
        P(("rep", "fsdp"), None, None),
        P(("rep", "fsdp"), None, None),
        P(("rep", "fsdp"), None),
        P("fsdp"),
        P("fsdp"),
        P("fsdp", None),
        P("fsdp"),
        P("fsdp"),
        P(None, "fsdp"),
        P(None, "fsdp"),
        P("fsdp", None),
        P("fsdp"),
        P("fsdp"),
        P("fsdp"),
        P("fsdp", None),
        P("fsdp"),
        P("fsdp", None),
        P("fsdp"),
    )
    out_specs = (
        P(("rep", "fsdp"), None, None),
        P(),
        P(("rep", "fsdp"), None, None),
        P("fsdp"),
        P("fsdp"),
        P("fsdp", None),
        P("fsdp"),
        P("fsdp"),
        P(None, "fsdp"),
        P(None, "fsdp"),
        P("fsdp", None),
        P("fsdp"),
        P("fsdp"),
        P("fsdp"),
        P("fsdp", None),
        P("fsdp"),
        P("fsdp", None),
        P("fsdp"),
    )
    return jax.shard_map(body, mesh=mesh, in_specs=in_specs, out_specs=out_specs, check_vma=False)
```

profile of v0, /device:TPU:0, one launch (start us, length us, event | category | flops | bytes accessed | tf_op | source)
XLA Modules:
  0.0 1987.8 jit_solution(13095303623097500694)
XLA Ops:
  18.5 39.5 %all-reduce.21 = (bf16[768]{0:T(1024)(128)(2,1)S(1)}, bf16[768]{0:T(1024)(128)(2,1)S(1)}, bf16[768]{0:T(1024)(128)(2,1)S(1)}, bf16[768]{0:T(1024)(128)(2,1)S(1)}...) all-reduce(bf16[768]{0:T(1024)(128)(2,1)S(1)} %dynamic-update-slice, ...), channel_id=1, replica_groups=mesh['rep'=4,'fsdp'=8] {'fsdp'}, use_global_device_ids=true, to_apply=%add.3 | all-reduce | flops 6144 | bytes 24576
  64.7 26.0 %all_gather.58 = bf16[27,64]{0,1:T(8,128)(2,1)S(1)} all-gather(bf16[27,8]{0,1:T(8,128)(2,1)S(1)} %copy-done.58), channel_id=1, replica_groups=mesh['rep'=4,'fsdp'=8] {'fsdp'}, dimensions={1}, use_global_device_ids=true | all-gather | bytes 3888 | tf_op jit(solution)/shard_map/all_gather | solution.py:127
  90.7 26.1 %all_gather.59 = bf16[27,64]{0,1:T(8,128)(2,1)S(1)} all-gather(bf16[27,8]{0,1:T(8,128)(2,1)S(1)} %copy-done.59), channel_id=1, replica_groups=mesh['rep'=4,'fsdp'=8] {'fsdp'}, dimensions={1}, use_global_device_ids=true | all-gather | bytes 3888 | tf_op jit(solution)/shard_map/all_gather | solution.py:128
  120.3 26.2 %all-gather = bf16[8,1,384]{2,1,0:T(2,128)(2,1)S(1)} all-gather(bf16[1,1,384]{2,1,0:T(2,128)(2,1)S(1)} %reshape.378), channel_id=1, replica_groups=mesh['rep'=4,'fsdp'=8] {'fsdp'}, dimensions={0}, use_global_device_ids=true | all-gather | bytes 6912 | tf_op jit(solution)/shard_map/all_gather | solution.py:135
  224.6 391.0 %while.30 = (s32[]{:T(128)}, bf16[2,4,196,12,64]{2,1,0,4,3:T(4,128)(2,1)}, f32[2,4,12,196,1]{3,2,1,4,0:T(8,128)S(1)}, bf16[2,4,196,12,64]{2,4,3,1,0:T(8,128)(2,1...) while((s32[]{:T(128)}, ...), condition=%wide.region_5.6_spmd, body=%wide.region_2.5_spmd.sunk | while | flops 522962496 | bytes 148267408 | solution.py:180
  234.7 26.3 %add.539 = f32[4,12,14,14,14,14]{5,4,3,2,1,0:T(8,128)} broadcast(f32[4,12,14,14,14]{4,3,2,1,0:T(8,128)} %copy.323), dimensions={0,1,2,3,5} | broadcast | bytes 7902720 | tf_op jit(solution)/shard_map/while/body/eval_jaxpr/add | solution.py:78
  261.0 44.7 %add.540 = f32[4,12,196,196]{3,2,1,0:T(8,128)} reshape(f32[4,12,14,14,14,14]{5,4,3,2,1,0:T(8,128)} %add.539) | data formatting | bytes 14751744 | tf_op jit(solution)/shard_map/while/body/eval_jaxpr/add | solution.py:78
  319.2 25.3 %add.541 = f32[4,12,14,14,14,14]{5,4,3,2,1,0:T(8,128)} broadcast(f32[4,12,14,14,14]{4,3,2,1,0:T(8,128)S(1)} %copy.325), dimensions={0,1,2,3,4} | broadcast | bytes 7902720 | tf_op jit(solution)/shard_map/while/body/eval_jaxpr/add | solution.py:78
  344.5 44.6 %add.542 = f32[4,12,196,196]{3,2,1,0:T(8,128)} reshape(f32[4,12,14,14,14,14]{5,4,3,2,1,0:T(8,128)} %add.541) | data formatting | bytes 14751744 | tf_op jit(solution)/shard_map/while/body/eval_jaxpr/add | solution.py:78
  430.0 26.0 %add.539 = f32[4,12,14,14,14,14]{5,4,3,2,1,0:T(8,128)} broadcast(f32[4,12,14,14,14]{4,3,2,1,0:T(8,128)} %copy.323), dimensions={0,1,2,3,5} | broadcast | bytes 7902720 | tf_op jit(solution)/shard_map/while/body/eval_jaxpr/add | solution.py:78
  456.0 44.6 %add.540 = f32[4,12,196,196]{3,2,1,0:T(8,128)} reshape(f32[4,12,14,14,14,14]{5,4,3,2,1,0:T(8,128)} %add.539) | data formatting | bytes 14751744 | tf_op jit(solution)/shard_map/while/body/eval_jaxpr/add | solution.py:78
  514.2 25.3 %add.541 = f32[4,12,14,14,14,14]{5,4,3,2,1,0:T(8,128)} broadcast(f32[4,12,14,14,14]{4,3,2,1,0:T(8,128)S(1)} %copy.325), dimensions={0,1,2,3,4} | broadcast | bytes 7902720 | tf_op jit(solution)/shard_map/while/body/eval_jaxpr/add | solution.py:78
  539.4 44.6 %add.542 = f32[4,12,196,196]{3,2,1,0:T(8,128)} reshape(f32[4,12,14,14,14,14]{5,4,3,2,1,0:T(8,128)} %add.541) | data formatting | bytes 14751744 | tf_op jit(solution)/shard_map/while/body/eval_jaxpr/add | solution.py:78
  631.4 52.7 %fusion.94 = (bf16[1568,3072]{1,0:T(8,128)(2,1)}, f32[1568,3072]{1,0:T(8,128)}) fusion(f32[3072]{0:T(1024)S(1)} %bitcast.276, bf16[768,3072]{1,0:T(8,128)(2,1)} %all-gather.10.cloned.1.call-done, f32[1568,768]{1,0:T(8,128)} %copy-done.5, f32[768]{0:T(1024)S(1)} %copy-done.52, f32[768]{0:T(1024)S(1)} %copy-done.41, f32[1568]{0:T(1024)S(1)} %add_rsqrt_fusion, ...), kind=kOutput, calls=%fused_computation.83 | convolution fusion | flops 7722688512 | bytes 38467840 | tf_op jit(solution)/shard_map/dot_general | solution.py:190
  701.0 38.8 %all-reduce.19 = (f32[]{:T(128)}, f32[]{:T(128)}) all-reduce(f32[]{:T(128)} %get-tuple-element.418, f32[]{:T(128)} %get-tuple-element.409), channel_id=1, replica_groups=mesh['rep'=4,'fsdp'=8] {'rep','fsdp'}, use_global_device_ids=true, to_apply=%region_9.10 | all-reduce | flops 2 | bytes 16 | tf_op jit(solution)/shard_map/psum | solution.py:200
  815.9 737.5 %while.31 = (s32[]{:T(128)}, bf16[2,4,196,12,64]{2,4,3,1,0:T(8,128)(2,1)}, bf16[2,4,196,12,64]{2,1,0,4,3:T(4,128)(2,1)}, bf16[2,4,196,12,64]{2,4,3,1,0:T(8,128)(...) while((s32[]{:T(128)}, ...), condition=%wide.region_18.19_spmd, body=%wide.region_14.18_spmd.sunk | while | flops 1644546560 | bytes 329321856 | solution.py:307
  825.8 26.2 %add.546 = f32[4,12,14,14,14,14]{5,4,3,2,1,0:T(8,128)} broadcast(f32[4,12,14,14,14]{4,3,2,1,0:T(8,128)} %copy.335), dimensions={0,1,2,3,5} | broadcast | bytes 7902720 | tf_op jit(solution)/shard_map/while/body/eval_jaxpr/add | solution.py:78
  852.0 44.6 %add.547 = f32[4,12,196,196]{3,2,1,0:T(8,128)} reshape(f32[4,12,14,14,14,14]{5,4,3,2,1,0:T(8,128)} %add.546) | data formatting | bytes 14751744 | tf_op jit(solution)/shard_map/while/body/eval_jaxpr/add | solution.py:78
  910.1 25.3 %add.548 = f32[4,12,14,14,14,14]{5,4,3,2,1,0:T(8,128)} broadcast(f32[4,12,14,14,14]{4,3,2,1,0:T(8,128)S(1)} %copy.337), dimensions={0,1,2,3,4} | broadcast | bytes 7902720 | tf_op jit(solution)/shard_map/while/body/eval_jaxpr/add | solution.py:78
  935.4 44.6 %add.549 = f32[4,12,196,196]{3,2,1,0:T(8,128)} reshape(f32[4,12,14,14,14,14]{5,4,3,2,1,0:T(8,128)} %add.548) | data formatting | bytes 14751744 | tf_op jit(solution)/shard_map/while/body/eval_jaxpr/add | solution.py:78
  1039.0 43.0 %reshape.425 = f32[4,12,14,14,14,14]{5,4,3,2,1,0:T(8,128)} reshape(f32[4,12,196,196]{3,2,1,0:T(8,128)} %copy.340) | data formatting | bytes 14751744 | tf_op jit(solution)/shard_map/while/body/eval_jaxpr/convert_element_type | solution.py:284
  1082.0 30.2 %fusion.235 = (f32[4,12,14,14,14]{4,3,2,1,0:T(8,128)}, f32[4,12,14,14,14]{4,3,2,1,0:T(8,128)}) fusion(f32[4,12,14,14,14,14]{5,4,3,2,1,0:T(8,128)} %reshape.425), kind=kLoop, calls=%fused_computation.184.clone.1 | loop fusion | flops 3424512 | bytes 8429568 | tf_op jit(solution)/shard_map/while/body/eval_jaxpr/reduce_sum | solution.py:284
  1191.4 26.1 %add.546 = f32[4,12,14,14,14,14]{5,4,3,2,1,0:T(8,128)} broadcast(f32[4,12,14,14,14]{4,3,2,1,0:T(8,128)} %copy.335), dimensions={0,1,2,3,5} | broadcast | bytes 7902720 | tf_op jit(solution)/shard_map/while/body/eval_jaxpr/add | solution.py:78
  1217.5 44.6 %add.547 = f32[4,12,196,196]{3,2,1,0:T(8,128)} reshape(f32[4,12,14,14,14,14]{5,4,3,2,1,0:T(8,128)} %add.546) | data formatting | bytes 14751744 | tf_op jit(solution)/shard_map/while/body/eval_jaxpr/add | solution.py:78
  1275.7 25.3 %add.548 = f32[4,12,14,14,14,14]{5,4,3,2,1,0:T(8,128)} broadcast(f32[4,12,14,14,14]{4,3,2,1,0:T(8,128)S(1)} %copy.337), dimensions={0,1,2,3,4} | broadcast | bytes 7902720 | tf_op jit(solution)/shard_map/while/body/eval_jaxpr/add | solution.py:78
  1301.0 44.6 %add.549 = f32[4,12,196,196]{3,2,1,0:T(8,128)} reshape(f32[4,12,14,14,14,14]{5,4,3,2,1,0:T(8,128)} %add.548) | data formatting | bytes 14751744 | tf_op jit(solution)/shard_map/while/body/eval_jaxpr/add | solution.py:78
  1404.4 43.0 %reshape.425 = f32[4,12,14,14,14,14]{5,4,3,2,1,0:T(8,128)} reshape(f32[4,12,196,196]{3,2,1,0:T(8,128)} %copy.340) | data formatting | bytes 14751744 | tf_op jit(solution)/shard_map/while/body/eval_jaxpr/convert_element_type | solution.py:284
  1447.4 30.2 %fusion.235 = (f32[4,12,14,14,14]{4,3,2,1,0:T(8,128)}, f32[4,12,14,14,14]{4,3,2,1,0:T(8,128)}) fusion(f32[4,12,14,14,14,14]{5,4,3,2,1,0:T(8,128)} %reshape.425), kind=kLoop, calls=%fused_computation.184.clone.1 | loop fusion | flops 3424512 | bytes 8429568 | tf_op jit(solution)/shard_map/while/body/eval_jaxpr/reduce_sum | solution.py:284
  1650.4 39.0 %all-reduce.20 = (bf16[768]{0:T(1024)(128)(2,1)S(1)}, bf16[768]{0:T(1024)(128)(2,1)S(1)}, bf16[768]{0:T(1024)(128)(2,1)S(1)}, bf16[768]{0:T(1024)(128)(2,1)S(1)}...) all-reduce(bf16[768]{0:T(1024)(128)(2,1)S(1)} %get-tuple-element.31, ...), channel_id=2, replica_groups=mesh['rep'=4,'fsdp'=8] {'fsdp'}, use_global_device_ids=true, to_apply=%region_22.23.clone | all-reduce | flops 12672 | bytes 50688
  1702.1 24.4 %reduce-scatter.5.cloned.1.call-done = bf16[96,2304]{1,0:T(8,128)(2,1)} async-done(((bf16[768,2304]{1,0:T(8,128)(2,1)}), bf16[96,2304]{1,0:T(8,128)(2,1)}) %reduce-scatter.5.cloned.1.call-update) | async-done | bytes 442384 | tf_op jit(solution)/shard_map/reduce_scatter | solution.py:330
  1726.5 98.5 %reduce-scatter.9.cloned.1.call-done = bf16[96,3072]{1,0:T(8,128)(2,1)} async-done(((bf16[768,3072]{1,0:T(8,128)(2,1)}), bf16[96,3072]{1,0:T(8,128)(2,1)}) %reduce-scatter.9.cloned.1.call-update) | async-done | bytes 589840 | tf_op jit(solution)/shard_map/reduce_scatter | solution.py:234
  1825.0 98.9 %reduce-scatter.11.cloned.1.call-done = bf16[384,768]{1,0:T(8,128)(2,1)} async-done(((bf16[3072,768]{1,0:T(8,128)(2,1)}), bf16[384,768]{1,0:T(8,128)(2,1)}) %reduce-scatter.11.cloned.1.call-update) | async-done | bytes 589840 | tf_op jit(solution)/shard_map/reduce_scatter | solution.py:237
  (439 shorter events, 780.0 us)
Async XLA Ops:
  7.2 151.6 %all-gather.6.cloned.1.call-start = ((), (), s32[]{:S(2)}) async-start(), calls=%async_computation.4 | async-start | bytes 3981312 | tf_op jit(solution)/shard_map/all_gather | solution.py:120
  7.9 614.4 %all-gather.8.cloned.1.call-start = ((), (), s32[]{:S(2)}) async-start(), calls=%async_computation.5 | async-start | bytes 1327104 | tf_op jit(solution)/shard_map/all_gather | solution.py:121
  8.7 622.7 %all-gather.10.cloned.1.call-start = ((), (), s32[]{:S(2)}) async-start(), calls=%async_computation.6 | async-start | bytes 5308416 | tf_op jit(solution)/shard_map/all_gather | solution.py:131
  9.4 674.7 %all-gather.12.cloned.1.call-start = ((), (), s32[]{:S(2)}) async-start(), calls=%async_computation.7 | async-start | bytes 5308416 | tf_op jit(solution)/shard_map/all_gather | solution.py:132
  10.0 1692.1 %reduce-scatter.7.cloned.1.call-start = ((), (), s32[]{:S(2)}) async-start(), calls=%async_computation.9 | async-start | bytes 1327104 | tf_op jit(solution)/shard_map/reduce_scatter | solution.py:333
  15.3 143.5 %copy-start.28 = (f32[1568]{0:T(1024)}, f32[1568]{0:T(1024)S(1)}, u32[]{:S(2)}) copy-start(f32[1568]{0:T(1024)S(1)} %div.63) | copy-start | bytes 18820
  15.3 49.3 %copy-start.39 = (s32[14,14]{0,1:T(8,128)}, s32[14,14]{0,1:T(8,128)S(1)}, u32[]{:S(2)}) copy-start(s32[14,14]{0,1:T(8,128)S(1)} %subtract_add_fusion) | copy-start | bytes 2356
  58.1 100.7 %copy-start.43 = (f32[768]{0:T(1024)}, f32[768]{0:T(1024)S(1)}, u32[]{:S(2)}) copy-start(f32[768]{0:T(1024)S(1)} %convert_element_type.270) | copy-start | bytes 9220
  58.1 100.7 %copy-start.50 = (f32[768]{0:T(1024)}, f32[768]{0:T(1024)S(1)}, u32[]{:S(2)}) copy-start(f32[768]{0:T(1024)S(1)} %convert_element_type.271) | copy-start | bytes 9220
  58.3 100.5 %copy-start.32 = (f32[1568]{0:T(1024)}, f32[1568]{0:T(1024)S(1)}, u32[]{:S(2)}) copy-start(f32[1568]{0:T(1024)S(1)} %reshape.351) | copy-start | bytes 18820
  58.3 32.4 %copy-start.59 = (bf16[27,8]{0,1:T(8,128)(2,1)S(1)}, bf16[27,8]{0,1:T(8,128)(2,1)}, u32[]{:S(2)}) copy-start(bf16[27,8]{0,1:T(8,128)(2,1)} %param.31) | copy-start | bytes 1300
  58.3 61.9 %copy-start.61 = (bf16[384]{0:T(512)(128)(2,1)S(1)}, bf16[384]{0:T(512)(128)(2,1)}, u32[]{:S(2)}) copy-start(bf16[384]{0:T(512)(128)(2,1)} %param.37) | copy-start | bytes 2308
  58.4 89.3 %copy-start.47 = (s32[8,196]{1,0:T(8,128)S(1)}, s32[8,196]{1,0:T(8,128)}, u32[]{:S(2)}) copy-start(s32[8,196]{1,0:T(8,128)} %param.24) | copy-start | bytes 18820
  64.6 94.2 %copy-start.30 = (f32[1568]{0:T(1024)}, f32[1568]{0:T(1024)S(1)}, u32[]{:S(2)}) copy-start(f32[1568]{0:T(1024)S(1)} %rsqrt.20) | copy-start | bytes 18820
  628.5 153.9 %copy-start.26 = (f32[1568]{0:T(1024)}, f32[1568]{0:T(1024)S(1)}, u32[]{:S(2)}) copy-start(f32[1568]{0:T(1024)S(1)} %broadcast_multiply_fusion.5) | copy-start | bytes 18820
  631.3 151.1 %copy-start.36 = (f32[1568]{0:T(1024)}, f32[1568]{0:T(1024)S(1)}, u32[]{:S(2)}) copy-start(f32[1568]{0:T(1024)S(1)} %add_rsqrt_fusion) | copy-start | bytes 18820
  631.4 52.7 %copy-start.34 = (f32[1568]{0:T(1024)S(1)}, f32[1568]{0:T(1024)}, u32[]{:S(2)}) copy-start(f32[1568]{0:T(1024)} %copy-done.32) | copy-start | bytes 18820
  631.4 52.7 %copy-start.38 = (f32[1568]{0:T(1024)S(1)}, f32[1568]{0:T(1024)}, u32[]{:S(2)}) copy-start(f32[1568]{0:T(1024)} %mul.272) | copy-start | bytes 18820
  631.4 52.7 %copy-start.54 = (f32[768]{0:T(1024)S(1)}, f32[768]{0:T(1024)}, u32[]{:S(2)}) copy-start(f32[768]{0:T(1024)} %convert_element_type.284) | copy-start | bytes 9220
  740.5 25.6 %slice-start.7 = ((s8[4816896]{0:T(1024)(128)(4,1)}), s8[4194304]{0:T(1024)(128)(4,1)S(1)}, s32[]{:S(2)}) async-start(s8[4816896]{0:T(1024)(128)(4,1)} %bitcast.272), calls=%async_computation.20 | async-start | bytes 8388608
  740.5 41.9 %slice-start.5 = ((s8[4816896]{0:T(1024)(128)(4,1)}), s8[4194304]{0:T(1024)(128)(4,1)S(1)}, s32[]{:S(2)}) async-start(s8[4816896]{0:T(1024)(128)(4,1)} %bitcast.270), calls=%async_computation.18 | async-start | bytes 8388608
  740.5 41.9 %slice-start.9 = ((s8[4816896]{0:T(1024)(128)(4,1)}), s8[4194304]{0:T(1024)(128)(4,1)S(1)}, s32[]{:S(2)}) async-start(s8[4816896]{0:T(1024)(128)(4,1)} %bitcast.274), calls=%async_computation.22 | async-start | bytes 8388608
  745.8 20.3 %copy-start.16 = (bf16[1568,768]{1,0:T(8,128)(2,1)}, bf16[1568,768]{1,0:T(8,128)(2,1)S(1)}, u32[]{:S(2)}) copy-start(bf16[1568,768]{1,0:T(8,128)(2,1)S(1)} %get-tuple-element.406) | copy-start | bytes 7225348
  745.8 20.3 %slice-start.8 = ((s8[4816896]{0:T(1024)(128)(4,1)}), s8[622592]{0:T(1024)(128)(4,1)S(1)}, s32[]{:S(2)}) async-start(s8[4816896]{0:T(1024)(128)(4,1)} %bitcast.272), calls=%async_computation.21 | async-start | bytes 1245184
  745.8 36.6 %slice-start.6 = ((s8[4816896]{0:T(1024)(128)(4,1)}), s8[622592]{0:T(1024)(128)(4,1)S(1)}, s32[]{:S(2)}) async-start(s8[4816896]{0:T(1024)(128)(4,1)} %bitcast.270), calls=%async_computation.19 | async-start | bytes 1245184
  745.8 36.6 %slice-start.10 = ((s8[4816896]{0:T(1024)(128)(4,1)}), s8[622592]{0:T(1024)(128)(4,1)S(1)}, s32[]{:S(2)}) async-start(s8[4816896]{0:T(1024)(128)(4,1)} %bitcast.274), calls=%async_computation.23 | async-start | bytes 1245184
  1156.9 16.5 slice-start.3
  1522.5 16.5 slice-start.3
  1579.0 147.4 %reduce-scatter.5.cloned.1.call-start = ((), (), s32[]{:S(2)}) async-start(), calls=%async_computation.8 | async-start | bytes 3981312 | tf_op jit(solution)/shard_map/reduce_scatter | solution.py:330
  1598.3 226.6 %reduce-scatter.9.cloned.1.call-start = ((), (), s32[]{:S(2)}) async-start(), calls=%async_computation.10 | async-start | bytes 5308416 | tf_op jit(solution)/shard_map/reduce_scatter | solution.py:234
  1614.1 309.7 %reduce-scatter.11.cloned.1.call-start = ((), (), s32[]{:S(2)}) async-start(), calls=%async_computation.11 | async-start | bytes 5308416 | tf_op jit(solution)/shard_map/reduce_scatter | solution.py:237
  1627.1 345.7 %all-reduce.26.cloned.1.call-start = ((), (), s32[]{:S(2)}) async-start(), calls=%async_computation.12 | async-start | bytes 3538944 | tf_op jit(solution)/shard_map/psum | solution.py:361
  (75 other events, 575.0 us)
Sparse Core Ops, SparseCore 0:
  10.2 68.4 all-gather.5
  80.9 39.7 all-gather.7
  122.9 78.6 all-gather.9
  203.7 78.0 all-gather.11
  1579.1 64.2 reduce-scatter.6
  1646.8 79.5 reduce-scatter.4
  1730.1 94.7 reduce-scatter.8
  1828.6 95.1 reduce-scatter.10
  1926.4 46.3 all-reduce.25
where the time goes:
time: 2000 us; the launch traced here: 1990 us
  local copies, waits for them, and re-layouts  1010 us (50%)
  matrix products  368 us (18%)
  waiting for transfers between devices  249 us (12%)
  blocking collectives  202 us (10%)
  other arithmetic  128 us (6%)
  between operations  20.4 us (1%)
    add x24, local copies, waits for them, and re-layouts, window_scores(): plain.reshape(group_size, HEADS, WIN, WIN, WIN, WIN) + along_h[..., :, None]  652 us
    convert_element_type x4, local copies, waits for them, and re-layouts, attend_back(): sum_rows = jnp.sum(grid_score, axis=-1, dtype=jnp.float32)  103 us
    reduce_scatter x1, waiting for transfers between devices, body(): lax.psum_scatter(down_weight_grad.astype(jnp.bfloat16), 'fsdp', scatter_d...  98.9 us
    reduce_scatter x1, waiting for transfers between devices, body(): lax.psum_scatter(up_weight_grad.astype(jnp.bfloat16), 'fsdp', scatter_dim...  98.5 us
    unnamed x2, blocking collectives  78.5 us
    reduce_sum x2, other arithmetic, attend_back(): sum_rows = jnp.sum(grid_score, axis=-1, dtype=jnp.float32)  60.4 us
    dot_general x4, matrix products, times_trans(): lax.dot_general(left, right, (((1,), (1,)), ((), ())), preferred_element_...  57.3 us
    dot_general x4, matrix products, window_scores(): jnp.einsum('aihd,ajhd->ahij', query, keys, preferred_element_type=jnp.flo...  54.7 us
  transfers between devices with their start and end apart: 9, of which 4 were waited for; matrix products, arithmetic and copies ran while one was open for 33% of the time, Pallas kernels for 0%

commit v1 on v0

v1 whole, which is shorter than its diff:
```python
import functools
import math

import jax
import jax.numpy as jnp
import numpy as np
from jax import lax
from jax.experimental import pallas as pl
from jax.experimental.pallas import tpu as pltpu
from jax.sharding import PartitionSpec as P

D = 768
HEADS = 12
HEAD_DIM = 64
MLP = 3072
WIN = 14
MAP = 64
SLOTS = WIN * WIN
ROWS = 208
LANES = 256
PAIRS = HEADS // 2
PAIR = 2 * HEAD_DIM
SIDE = (MAP + WIN - 1) // WIN
LN_EPS = 1e-06
F32 = jnp.float32
BF16 = jnp.bfloat16
VMEM_LIMIT = 60 * 1024 * 1024


def nn(left, right):
    return jnp.dot(left, right, preferred_element_type=F32)


def nt(left, right):
    return lax.dot_general(left, right, (((1,), (1,)), ((), ())), preferred_element_type=F32)


def tn(left, right):
    return lax.dot_general(left, right, (((0,), (0,)), ((), ())), preferred_element_type=F32)


def key_places():
    table = np.zeros((ROWS, HEAD_DIM), np.float32)
    for slot in range(SLOTS):
        for base in (0, 32):
            table[slot, base + WIN - 1 - slot // WIN] = 1.0
            table[slot, base + 16 + WIN - 1 - slot % WIN] = 1.0
    return table


def keep_column(base_ref, window):
    slot = lax.broadcasted_iota(jnp.int32, (ROWS, 1), 0)
    row = lax.shift_right_logical(slot * 4682, 16)
    col = slot - row * WIN
    place = lax.rem(base_ref[0] + window, SIDE * SIDE)
    place_row = lax.div(place, SIDE)
    place_col = place - place_row * SIDE
    inside = (slot < SLOTS) & (row + place_row * WIN < MAP) & (col + place_col * WIN < MAP)
    return inside.astype(F32)


def lane_places():
    slot = lax.broadcasted_iota(jnp.int32, (1, LANES), 1)
    row = lax.shift_right_logical(slot * 4682, 16)
    return row, slot - row * WIN


def norm_parts(values):
    mean = jnp.mean(values, axis=-1, keepdims=True)
    centred = values - mean
    inv_std = lax.rsqrt(jnp.mean(centred * centred, axis=-1, keepdims=True) + LN_EPS)
    return centred * inv_std, inv_std


def norm_grad(grad, scaled, inv_std, gain):
    grad_scaled = grad * gain
    first = jnp.mean(grad_scaled, axis=-1, keepdims=True)
    second = jnp.mean(grad_scaled * scaled, axis=-1, keepdims=True)
    return inv_std * (grad_scaled - first - scaled * second)


def up_by(values, amount):
    take = lambda bit: (amount & bit) != 0
    part = jnp.where(take(8), values[8:32], values[0:24])
    part = jnp.where(take(4), pltpu.roll(part, 20, 0), part)
    part = jnp.where(take(2), pltpu.roll(part, 22, 0), part)
    part = jnp.where(take(1), pltpu.roll(part, 23, 0), part)
    return part[0:16]


def down_by(values, amount):
    take = lambda bit: (amount & bit) != 0
    zeros = jnp.zeros((8, values.shape[1]), values.dtype)
    part = jnp.concatenate([values, zeros], axis=0)
    part = jnp.where(take(1), pltpu.roll(part, 1, 0), part)
    part = jnp.where(take(2), pltpu.roll(part, 2, 0), part)
    part = jnp.where(take(4), pltpu.roll(part, 4, 0), part)
    return jnp.where(
        take(8),
        jnp.concatenate([zeros, part], axis=0),
        jnp.concatenate([part, zeros], axis=0),
    )


def fill_rows(values):
    return jnp.concatenate(
        [values, jnp.zeros((LANES - ROWS,) + values.shape[1:], values.dtype)], axis=0
    )


def attend_kernel(
    base_ref, tok_ref, w_ref, bias_ref, gain_ref, shift_ref, rel_ref, place_ref, wp_ref, pb_ref,
    hid_ref, qkv_ref, prob_ref, mix_ref, fin_ref, x_ref,
):
    keep = keep_column(base_ref, pl.program_id(0))
    x_ref[pl.ds(192, 16), :] = jnp.zeros((16, D), F32)
    x_ref[pl.ds(0, SLOTS), :] = tok_ref[0].astype(F32)
    scaled, _ = norm_parts(x_ref[...])
    first_in = (keep * (scaled * gain_ref[...] + shift_ref[...])).astype(BF16)
    fin_ref[0] = first_in
    for part in range(3):
        cols = pl.ds(part * D, D)
        qkv_ref[0, :, cols] = (nn(first_in, w_ref[:, cols]) + bias_ref[:, cols]).astype(BF16)
    lane_row, lane_col = lane_places()
    low_half = lax.broadcasted_iota(jnp.int32, (ROWS, PAIR), 1) < HEAD_DIM
    tail_rows = lax.broadcasted_iota(jnp.int32, (16, LANES), 0) + 192
    places = place_ref[...]
    place_pair = jnp.concatenate([places, places], axis=1)

    def one_pair(pair, carry):
        at = pl.multiple_of(pair * PAIR, PAIR)
        query = qkv_ref[0, :, pl.ds(at, PAIR)]
        keys = qkv_ref[0, :, pl.ds(pl.multiple_of(D + at, PAIR), PAIR)]
        values = qkv_ref[0, :, pl.ds(pl.multiple_of(2 * D + at, PAIR), PAIR)]
        query_t = fill_rows(query).T
        values_t = fill_rows(values).T
        offsets = nn(rel_ref[...], query_t)
        mixed = []
        for head in range(2):
            mine = offsets[head * HEAD_DIM : (head + 1) * HEAD_DIM]
            along = jnp.concatenate(
                [up_by(mine[0:32], lane_row), up_by(mine[32:64], lane_col)], axis=0
            )
            high = along.astype(BF16)
            rest = (along - high.astype(F32)).astype(BF16)
            scaled_q = query_t[head * HEAD_DIM : (head + 1) * HEAD_DIM] * jnp.asarray(
                HEAD_DIM ** (-0.5), BF16
            )
            if head == 0:
                query_ext = jnp.concatenate([scaled_q, high, rest], axis=0)
                keys_ext = jnp.where(low_half, keys, place_pair)
            else:
                query_ext = jnp.concatenate([high, rest, scaled_q], axis=0)
                keys_ext = jnp.where(low_half, place_pair, keys)
            scores = nn(keys_ext, query_ext)
            scores = jnp.concatenate(
                [scores[0:192], jnp.where(tail_rows < SLOTS, scores[192:208], -1e30)], axis=0
            )
            peak = jnp.max(scores, axis=0, keepdims=True)
            expo = jnp.exp(scores - peak)
            total = jnp.sum(expo, axis=0, keepdims=True)
            probs = (expo * (1.0 / total)).astype(BF16)
            prob_ref[0, 2 * pair + head] = probs
            mixed.append(
                nn(values_t[head * HEAD_DIM : (head + 1) * HEAD_DIM], fill_rows(probs)).astype(BF16)
            )
        mix_ref[0, :, pl.ds(at, PAIR)] = jnp.concatenate(mixed, axis=0).T[0:ROWS]
        return carry

    lax.fori_loop(0, PAIRS, one_pair, 0)
    attn_out = nn(mix_ref[0], wp_ref[...]) + pb_ref[...]
    hid_ref[0] = keep * (x_ref[...] + attn_out)


def gelu_parts(pre):
    bell = jnp.exp(pre * pre * (-0.5))
    steps = 1.0 / (1.0 + (0.3275911 * math.sqrt(0.5)) * jnp.abs(pre))
    poly = steps * (
        0.5 * 0.254829592
        + steps
        * (
            0.5 * -0.284496736
            + steps * (0.5 * 1.421413741 + steps * (0.5 * -1.453152027 + steps * (0.5 * 1.061405429)))
        )
    )
    tail = poly * bell
    cumulative = jnp.where(pre > 0, 1.0 - tail, tail)
    return pre * cumulative, cumulative + pre * (bell * 0.3989422804014327)


def mlp_kernel(
    coef_ref, hid_ref, teach_ref, aux_ref, gain_ref, shift_ref, up_ref, ub_ref, down_ref, db_ref,
    out_ref, gh_ref, si_ref, act_ref, gd_ref, gu_ref, sums_ref, usum_ref, slope_ref, t_ref, *, group
):
    step = pl.program_id(0)
    rows = group * ROWS

    @pl.when(step == 0)
    def _():
        sums_ref[...] = jnp.zeros_like(sums_ref)
        usum_ref[...] = jnp.zeros_like(usum_ref)

    hidden = hid_ref[...].reshape(rows, D)
    aux = aux_ref[...].reshape(rows, 2)
    keep, valid = aux[:, 0:1], aux[:, 1:2]
    scaled, inv_std = norm_parts(hidden)
    second_in = (scaled * gain_ref[...] + shift_ref[...]).astype(BF16)
    si_ref[...] = second_in.reshape(group, ROWS, D)
    chunk = D

    def forward(part, total):
        cols = pl.ds(pl.multiple_of(part * chunk, chunk), chunk)
        pre = nn(second_in, up_ref[:, cols]) + ub_ref[:, cols]
        act, slope = gelu_parts(pre)
        slope_ref[:, cols] = slope
        low = act.astype(BF16)
        act_ref[:, :, cols] = low.reshape(group, ROWS, chunk)
        return total + nn(low, down_ref[cols, :])

    down = lax.fori_loop(0, MLP // chunk, forward, jnp.zeros((rows, D), F32))
    final = keep * (hidden + (down + db_ref[...]))
    for at in range(group):
        out_ref[at] = final[at * ROWS : at * ROWS + SLOTS].astype(BF16)
        t_ref[at, pl.ds(192, 16), :] = jnp.zeros((16, D), F32)
        t_ref[at, pl.ds(0, SLOTS), :] = teach_ref[at].astype(F32)
    error = final - t_ref[...].reshape(rows, D)
    weighted = valid * error
    grad_final = coef_ref[0] * weighted
    grad_down = grad_final.astype(BF16)
    gd_ref[...] = grad_down.reshape(group, ROWS, D)
    sums_ref[0:1, :] += jnp.sum(weighted * error, axis=0, keepdims=True)
    sums_ref[1:2, :] += jnp.sum(grad_down.astype(F32), axis=0, keepdims=True)

    def backward(part, total):
        cols = pl.ds(pl.multiple_of(part * chunk, chunk), chunk)
        grad_up = (nt(grad_down, down_ref[cols, :]) * slope_ref[:, cols]).astype(BF16)
        gu_ref[:, :, cols] = grad_up.reshape(group, ROWS, chunk)
        usum_ref[:, cols] += jnp.sum(grad_up.astype(F32), axis=0, keepdims=True)
        return total + nt(grad_up, up_ref[:, cols])

    grad_second = lax.fori_loop(0, MLP // chunk, backward, jnp.zeros((rows, D), F32))
    sums_ref[2:3, :] += jnp.sum(grad_second * scaled, axis=0, keepdims=True)
    sums_ref[3:4, :] += jnp.sum(grad_second, axis=0, keepdims=True)
    grad_hidden = grad_final + norm_grad(grad_second, scaled, inv_std, gain_ref[...])
    gh_ref[...] = (keep * grad_hidden).reshape(group, ROWS, D)


def attend_back_kernel(
    gh_ref, wp_ref, qkv_ref, prob_ref, rel_ref, relt_ref, place_ref, placet_ref,
    dqkv_ref, ga_ref, rg_ref, sums_ref, qsum_ref, gm_ref,
):
    @pl.when(pl.program_id(0) == 0)
    def _():
        rg_ref[...] = jnp.zeros_like(rg_ref)
        sums_ref[...] = jnp.zeros_like(sums_ref)
        qsum_ref[...] = jnp.zeros_like(qsum_ref)
        gm_ref[pl.ds(ROWS, LANES - ROWS), :] = jnp.zeros((LANES - ROWS, D), BF16)

    grad_attn = gh_ref[0].astype(BF16)
    ga_ref[0] = grad_attn
    sums_ref[...] += jnp.sum(grad_attn.astype(F32), axis=0, keepdims=True)
    gm_ref[pl.ds(0, ROWS), :] = nt(grad_attn, wp_ref[...]).astype(BF16)
    lane_row, lane_col = lane_places()
    low_half = lax.broadcasted_iota(jnp.int32, (ROWS, PAIR), 1) < HEAD_DIM
    low_full = lax.broadcasted_iota(jnp.int32, (LANES, PAIR), 1) < HEAD_DIM
    blank = jnp.zeros((), BF16)
    scale = HEAD_DIM ** (-0.5)

    def one_pair(pair, carry):
        at = pl.multiple_of(pair * PAIR, PAIR)
        q_at = pl.ds(at, PAIR)
        k_at = pl.ds(pl.multiple_of(D + at, PAIR), PAIR)
        v_at = pl.ds(pl.multiple_of(2 * D + at, PAIR), PAIR)
        query = fill_rows(qkv_ref[0, :, q_at])
        keys_t = fill_rows(qkv_ref[0, :, k_at]).T
        values = qkv_ref[0, :, v_at]
        grad_out = gm_ref[:, q_at]
        stacked = jnp.concatenate(
            [jnp.where(low_half, values, blank), jnp.where(low_half, blank, values)], axis=0
        )
        grad_probs = nt(stacked, grad_out)
        grad_values = jnp.zeros((ROWS, PAIR), F32)
        grad_keys = jnp.zeros((ROWS, PAIR), F32)
        spread, plain = [], []
        for head in range(2):
            own = (lambda full: jnp.where(low_full, full, blank)) if head == 0 else (
                lambda full: jnp.where(low_full, blank, full)
            )
            low = prob_ref[0, 2 * pair + head]
            probs = low.astype(F32)
            grad_p = grad_probs[head * ROWS : (head + 1) * ROWS]
            row_dot = jnp.sum(probs * grad_p, axis=0, keepdims=True)
            grad_score = (probs * (grad_p - row_dot)).astype(BF16)
            grad_values = grad_values + nn(low, own(grad_out))
            grad_keys = grad_keys + nn(grad_score, own(query))
            keys_ext = jnp.concatenate(
                [keys_t[head * HEAD_DIM : (head + 1) * HEAD_DIM], placet_ref[...]], axis=0
            )
            grad_ext = nn(keys_ext, fill_rows(grad_score))
            plain.append(grad_ext[0:64])
            spread.append(down_by(grad_ext[64:80], lane_row))
            spread.append(down_by(grad_ext[80:96], lane_col))
        spread = jnp.concatenate(spread, axis=0).astype(BF16)
        grad_query = jnp.concatenate(plain, axis=0) * scale + nn(relt_ref[...], spread)
        rg_ref[...] += nn(spread, query)
        grad_query = grad_query.astype(BF16).T[0:ROWS]
        grad_keys = (grad_keys * scale).astype(BF16)
        grad_values = grad_values.astype(BF16)
        dqkv_ref[0, :, q_at] = grad_query
        dqkv_ref[0, :, k_at] = grad_keys
        dqkv_ref[0, :, v_at] = grad_values
        qsum_ref[0:1, q_at] += jnp.sum(grad_query.astype(F32), axis=0, keepdims=True)
        qsum_ref[1:2, q_at] += jnp.sum(grad_values.astype(F32), axis=0, keepdims=True)
        return carry

    lax.fori_loop(0, PAIRS, one_pair, 0)


def input_kernel(
    base_ref, dqkv_ref, w_ref, tok_ref, gh_ref, gain_ref, out_ref, sums_ref, x_ref, *, group
):
    step = pl.program_id(0)

    @pl.when(step == 0)
    def _():
        sums_ref[...] = jnp.zeros_like(sums_ref)

    for at in range(group):
        keep = keep_column(base_ref, step * group + at)
        grad_first = keep * nt(dqkv_ref[at], w_ref[...])
        x_ref[pl.ds(192, 16), :] = jnp.zeros((16, D), F32)
        x_ref[pl.ds(0, SLOTS), :] = tok_ref[at].astype(F32)
        scaled, inv_std = norm_parts(x_ref[...])
        sums_ref[0:1, :] += jnp.sum(grad_first * scaled, axis=0, keepdims=True)
        sums_ref[1:2, :] += jnp.sum(grad_first, axis=0, keepdims=True)
        total = gh_ref[at] + norm_grad(grad_first, scaled, inv_std, gain_ref[...])
        out_ref[at] = total[0:SLOTS]


def whole(shape):
    zeros = (0,) * len(shape)
    return pl.BlockSpec(shape, lambda *_: zeros)


def per_window(shape):
    tail = (0,) * (len(shape) - 1)
    return pl.BlockSpec(shape, lambda step, *_: (step,) + tail)


SMEM = pl.BlockSpec(memory_space=pltpu.SMEM)


def params():
    return pltpu.CompilerParams(
        vmem_limit_bytes=VMEM_LIMIT, dimension_semantics=("arbitrary",)
    )


def shape_of(shape, dtype):
    return jax.ShapeDtypeStruct(shape, dtype)


def attend(base, tokens, weight, bias, gain, shift, rel, places, proj, proj_bias):
    count = tokens.shape[0]
    return pl.pallas_call(
        attend_kernel,
        grid=(count,),
        in_specs=[
            SMEM, per_window((1, SLOTS, D)), whole((D, 3 * D)), whole((1, 3 * D)), whole((1, D)),
            whole((1, D)), whole((PAIR, PAIR)), whole((ROWS, HEAD_DIM)), whole((D, D)), whole((1, D)),
        ],
        out_specs=[
            per_window((1, ROWS, D)), per_window((1, ROWS, 3 * D)),
            per_window((1, HEADS, ROWS, LANES)), per_window((1, ROWS, D)), per_window((1, ROWS, D)),
        ],
        out_shape=[
            shape_of((count, ROWS, D), F32), shape_of((count, ROWS, 3 * D), BF16),
            shape_of((count, HEADS, ROWS, LANES), BF16), shape_of((count, ROWS, D), BF16),
            shape_of((count, ROWS, D), BF16),
        ],
        scratch_shapes=[pltpu.VMEM((ROWS, D), F32)],
        compiler_params=params(),
        cost_estimate=pl.CostEstimate(
            flops=count * 3_500_000_000 // 2, bytes_accessed=40_000_000, transcendentals=0
        ),
        name="attend",
    )(base, tokens, weight, bias, gain, shift, rel, places, proj, proj_bias)


def mlp(coef, hidden, teacher, aux, gain, shift, up, up_bias, down, down_bias):
    count = hidden.shape[0]
    group = math.gcd(count, 2)
    win = lambda width: per_window((group, ROWS, width))
    arr = lambda width, dtype: shape_of((count, ROWS, width), dtype)
    return pl.pallas_call(
        functools.partial(mlp_kernel, group=group),
        grid=(count // group,),
        in_specs=[
            SMEM, win(D), per_window((group, SLOTS, D)), win(2), whole((1, D)), whole((1, D)),
            whole((D, MLP)), whole((1, MLP)), whole((MLP, D)), whole((1, D)),
        ],
        out_specs=[
            per_window((group, SLOTS, D)), win(D), win(D), win(MLP), win(D), win(MLP),
            whole((4, D)), whole((1, MLP)),
        ],
        out_shape=[
            shape_of((count, SLOTS, D), BF16), arr(D, F32), arr(D, BF16), arr(MLP, BF16),
            arr(D, BF16), arr(MLP, BF16), shape_of((4, D), F32), shape_of((1, MLP), F32),
        ],
        scratch_shapes=[pltpu.VMEM((group * ROWS, MLP), F32), pltpu.VMEM((group, ROWS, D), F32)],
        compiler_params=params(),
        cost_estimate=pl.CostEstimate(
            flops=count * 8 * ROWS * D * MLP, bytes_accessed=60_000_000, transcendentals=0
        ),
        name="mlp",
    )(coef, hidden, teacher, aux, gain, shift, up, up_bias, down, down_bias)


def attend_back(grad_hidden, proj, qkv, probs, rel, rel_t, places, places_t):
    count = grad_hidden.shape[0]
    return pl.pallas_call(
        attend_back_kernel,
        grid=(count,),
        in_specs=[
            per_window((1, ROWS, D)), whole((D, D)), per_window((1, ROWS, 3 * D)),
            per_window((1, HEADS, ROWS, LANES)), whole((PAIR, PAIR)), whole((PAIR, PAIR)),
            whole((ROWS, HEAD_DIM)), whole((32, LANES)),
        ],
        out_specs=[
            per_window((1, ROWS, 3 * D)), per_window((1, ROWS, D)), whole((PAIR, PAIR)),
            whole((1, D)), whole((2, D)),
        ],
        out_shape=[
            shape_of((count, ROWS, 3 * D), BF16), shape_of((count, ROWS, D), BF16),
            shape_of((PAIR, PAIR), F32), shape_of((1, D), F32), shape_of((2, D), F32),
        ],
        scratch_shapes=[pltpu.VMEM((LANES, D), BF16)],
        compiler_params=params(),
        cost_estimate=pl.CostEstimate(
            flops=count * 5_000_000_000 // 2, bytes_accessed=40_000_000, transcendentals=0
        ),
        name="attend_back",
    )(grad_hidden, proj, qkv, probs, rel, rel_t, places, places_t)


def input_back(base, dqkv, weight, tokens, grad_hidden, gain):
    count = tokens.shape[0]
    group = math.gcd(count, 2)
    return pl.pallas_call(
        functools.partial(input_kernel, group=group),
        grid=(count // group,),
        in_specs=[
            SMEM, per_window((group, ROWS, 3 * D)), whole((D, 3 * D)),
            per_window((group, SLOTS, D)), per_window((group, ROWS, D)), whole((1, D)),
        ],
        out_specs=[per_window((group, SLOTS, D)), whole((2, D))],
        out_shape=[shape_of((count, SLOTS, D), F32), shape_of((2, D), F32)],
        scratch_shapes=[pltpu.VMEM((ROWS, D), F32)],
        compiler_params=params(),
        cost_estimate=pl.CostEstimate(
            flops=count * 6 * ROWS * D * D, bytes_accessed=25_000_000, transcendentals=0
        ),
        name="input_back",
    )(base, dqkv, weight, tokens, grad_hidden, gain)


def split_small(packed, parts, width):
    pieces, at = [], 0
    for size in width:
        pieces.append(packed[:, at : at + size])
        at += size
    return pieces


def body(
    tokens, teacher, valid_mask, attn_gain, attn_shift, qkv_weight, query_bias, value_bias,
    rel_pos_h, rel_pos_w, proj_weight, proj_bias, mlp_gain, mlp_shift, up_weight, up_bias,
    down_weight, down_bias,
):
    count = tokens.shape[0]
    parts = lax.axis_size("fsdp")
    copies = lax.axis_size("rep")
    device = lax.axis_index("rep") * parts + lax.axis_index("fsdp")
    base = (device * count).astype(jnp.int32).reshape(1)
    window_ids = device * count + jnp.arange(count, dtype=jnp.int32)
    place = window_ids % (SIDE * SIDE)
    cells = jnp.arange(SLOTS, dtype=jnp.int32)
    inside = ((place // SIDE)[:, None] * WIN + (cells // WIN)[None, :] < MAP) & (
        (place % SIDE)[:, None] * WIN + (cells % WIN)[None, :] < MAP
    )
    keep = inside.astype(F32)
    valid = valid_mask.astype(F32) * keep
    valid_total = lax.psum(jnp.sum(valid), ("rep", "fsdp"))
    aux = jnp.pad(jnp.stack([keep, valid], axis=-1), ((0, 0), (0, ROWS - SLOTS), (0, 0)))

    small = [attn_gain, attn_shift, query_bias, value_bias, proj_bias, mlp_gain, mlp_shift,
             down_bias, up_bias, rel_pos_h, rel_pos_w]
    packed = lax.all_gather(jnp.concatenate([v.reshape(-1) for v in small]), "fsdp")
    pieces = split_small(packed, parts, [v.size for v in small])
    rows = [p.reshape(1, -1).astype(F32) for p in pieces[:9]]
    gain1, shift1, qb, vb, pb, gain2, shift2, db, ub = rows
    offsets = rel_pos_h.shape[0]
    tables = [
        p.reshape(parts, offsets, -1).transpose(1, 0, 2).reshape(offsets, HEAD_DIM)
        for p in pieces[9:]
    ]
    gap = jnp.zeros((32 - offsets, HEAD_DIM), BF16)
    table = jnp.concatenate([tables[0], gap, tables[1], gap], axis=0)
    hole = jnp.zeros((HEAD_DIM, HEAD_DIM), BF16)
    rel = jnp.concatenate(
        [jnp.concatenate([table, hole], axis=1), jnp.concatenate([hole, table], axis=1)], axis=0
    )
    rel_t = rel.T
    bias = jnp.concatenate([qb, jnp.zeros((1, D), F32), vb], axis=1)
    places = jnp.asarray(key_places(), BF16)
    places_t = jnp.asarray(np.pad(key_places().T[0:32], ((0, 0), (0, LANES - ROWS))), BF16)

    gather = lambda v: lax.all_gather(v, "fsdp", axis=0, tiled=True)
    w_qkv, w_proj, w_up, w_down = (
        gather(qkv_weight), gather(proj_weight), gather(up_weight), gather(down_weight)
    )
    hidden, qkv, probs, mixed, first_in = attend(
        base, tokens, w_qkv, bias, gain1, shift1, rel, places, w_proj, pb
    )
    loss_scale = 64.0 * D * count * copies * parts
    coef = (loss_scale * 2.0 / (valid_total * D)).reshape(1)
    out, grad_hidden, second_in, act, grad_down, grad_up, sums2, up_sum = mlp(
        coef, hidden, teacher, aux, gain2, shift2, w_up, ub, w_down, db
    )
    flat = lambda v: v.reshape(count * ROWS, v.shape[-1])
    scatter = lambda v: lax.psum(
        lax.psum_scatter(v.astype(BF16), "fsdp", scatter_dimension=0, tiled=True), "rep"
    ).astype(F32)
    d_down = scatter(tn(flat(act), flat(grad_down)))
    d_up = scatter(tn(flat(second_in), flat(grad_up)))
    dqkv, grad_attn, rel_grad, proj_sum, qv_sum = attend_back(
        grad_hidden, w_proj, qkv, probs, rel, rel_t, places, places_t
    )
    d_proj = scatter(tn(flat(mixed), flat(grad_attn)))
    d_qkv = scatter(tn(flat(first_in), flat(dqkv)))
    input_grad, sums1 = input_back(base, dqkv, w_qkv, tokens, grad_hidden, gain1)
    rel_sum = rel_grad[0:64, 0:64] + rel_grad[64:128, 64:128]
    loss_part = jnp.sum(sums2[0])
    vectors = [sums1[0], sums1[1], qv_sum[0], qv_sum[1], proj_sum[0], sums2[2], sums2[3], sums2[1],
               up_sum[0]]
    own = [
        jnp.concatenate([v.reshape(parts, -1) for v in vectors], axis=1),
        rel_sum[0:offsets].reshape(offsets, parts, -1).transpose(1, 0, 2).reshape(parts, -1),
        rel_sum[32 : 32 + offsets].reshape(offsets, parts, -1).transpose(1, 0, 2).reshape(parts, -1),
        jnp.broadcast_to(loss_part, (parts, 1)),
    ]
    totals = lax.psum(jnp.concatenate(own, axis=1), ("rep", "fsdp"))
    mine = lax.dynamic_index_in_dim(totals, lax.axis_index("fsdp"), 0, keepdims=False)
    outs, at = [], 0
    for v in [v for v in small]:
        outs.append(mine[at : at + v.size].reshape(v.shape))
        at += v.size
    (g_gain1, g_shift1, g_qb, g_vb, g_pb, g_gain2, g_shift2, g_db, g_ub, g_rh, g_rw) = outs
    loss = mine[at] / (valid_total * D)
    return (
        out, loss, input_grad, g_gain1, g_shift1, d_qkv, g_qb, g_vb, g_rh, g_rw, d_proj, g_pb,
        g_gain2, g_shift2, d_up, g_ub, d_down, g_db,
    )


def solution(mesh):
    windows = P(("rep", "fsdp"), None, None)
    vector = P("fsdp")
    matrix = P("fsdp", None)
    table = P(None, "fsdp")
    in_specs = (
        windows, windows, P(("rep", "fsdp"), None), vector, vector, matrix, vector, vector, table,
        table, matrix, vector, vector, vector, matrix, vector, matrix, vector,
    )
    out_specs = (windows, P(), windows) + in_specs[3:]
    return jax.shard_map(body, mesh=mesh, in_specs=in_specs, out_specs=out_specs, check_vma=False)
```

time: 2000 us -> 814 us (0.41)
  local copies, waits for them, and re-layouts: 1010 us -> 39.8 us
  matrix products: 368 us -> 42.7 us
  Pallas kernels: 0 us -> 187 us
  waiting for transfers between devices: 249 us -> 395 us
  other arithmetic: 128 us -> 10.5 us
  blocking collectives: 202 us -> 121 us
    add x26 -> x0, local copies, waits for them, and re-layouts: 662 us -> none  [the longest x24 652 us: window_scores(): plain.reshape(group_size, HEADS, WIN, WIN, WIN, WIN) + along_h[..., :, None]]
    dot_general x46 -> x4, matrix products: 368 us -> 42.7 us  [tn(): lax.dot_general(left, right, (((0,), (0,)), ((), ())), preferred_element_...]
    pallas_call x0 -> x4, Pallas kernels: none -> 187 us  [the longest x1 74.2 us: mlp(): pl.pallas_call(functools.partial(mlp_kernel, group=group), grid=(count //...]
    convert_element_type x9 -> x8, local copies, waits for them, and re-layouts: 123 us -> 4.12 us  [body(): rows = [p.reshape(1, -1).astype(F32) for p in pieces[:9]]]
    all_gather x4, waiting for transfers between devices: 0.06 us -> 114 us  [body(): gather = lambda v: lax.all_gather(v, 'fsdp', axis=0, tiled=True)]
    reduce_sum x14 -> x1, other arithmetic: 82.2 us -> 0.62 us  [body(): loss_part = jnp.sum(sums2[0])]
    all_gather x3 -> x0, blocking collectives: 78.3 us -> none  [the longest x1 26.2 us: body(): lax.all_gather(up_bias, 'fsdp', axis=0, tiled=True)]
    reshape x12 -> x8, local copies, waits for them, and re-layouts: 69.6 us -> 0.83 us  [the longest x2 0.24 us: body(): p.reshape(parts, offsets, -1).transpose(1, 0, 2).reshape(offsets, HEAD_DIM)]
  transfers between devices with their start and end apart: 9 -> 9, of which waited for: 4 -> 6; matrix products, arithmetic and copies ran while one was open for 33% -> 10% of each run, Pallas kernels for 0% -> 8%
where the time goes in v1:
time: 814 us
  waiting for transfers between devices  395 us (49%)
  Pallas kernels  187 us (23%)
  blocking collectives  121 us (15%)
  matrix products  42.7 us (5%)
  local copies, waits for them, and re-layouts  39.8 us (5%)
  between operations  17.3 us (2%)
  other arithmetic  10.5 us (1%)
    reduce_scatter x4, waiting for transfers between devices, body(): lax.psum_scatter(v.astype(BF16), 'fsdp', scatter_dimension=0, tiled=True)  278 us
    all_gather x4, waiting for transfers between devices, body(): gather = lambda v: lax.all_gather(v, 'fsdp', axis=0, tiled=True)  114 us
    pallas_call x1, Pallas kernels, mlp(): pl.pallas_call(functools.partial(mlp_kernel, group=group), grid=(count //...  74.2 us
    pallas_call x1, Pallas kernels, attend(): pl.pallas_call(attend_kernel, grid=(count,), in_specs=[SMEM, per_window((...  51 us
    pallas_call x1, Pallas kernels, attend_back(): pl.pallas_call(attend_back_kernel, grid=(count,), in_specs=[per_window((1...  46.3 us
    dot_general x4, matrix products, tn(): lax.dot_general(left, right, (((0,), (0,)), ((), ())), preferred_element_...  42.7 us
    psum x1, blocking collectives, body(): valid_total = lax.psum(jnp.sum(valid), ('rep', 'fsdp'))  42.4 us
    psum x1, blocking collectives, body(): totals = lax.psum(jnp.concatenate(own, axis=1), ('rep', 'fsdp'))  41.4 us
  transfers between devices with their start and end apart: 9, of which 6 were waited for; matrix products, arithmetic and copies ran while one was open for 10% of the time, Pallas kernels for 8%

profile of v1, /device:TPU:0, one launch (start us, length us, event | category | flops | bytes accessed | tf_op | source)
XLA Modules:
  0.0 813.6 jit_solution(10603263985327057046)
XLA Ops:
  10.1 1.4 fusion.7
  11.5 42.4 %psum.42 = f32[]{:T(128)} all-reduce(f32[]{:T(128)} %get-tuple-element.149), channel_id=1, replica_groups=mesh['rep'=4,'fsdp'=8] {'rep','fsdp'}, use_global_device_ids=true, to_apply=%region_1.2 | all-reduce | flops 1 | bytes 8 | tf_op jit(solution)/shard_map/psum | solution.py:493
  53.8 0.8 copy.67
  54.7 0.8 copy.68
  55.6 1.2 dynamic-slice
  57.5 6.1 concatenate.21
  63.9 37.6 %all-reduce.3 = bf16[12672]{0:T(1024)(128)(2,1)S(1)} all-reduce(bf16[12672]{0:T(1024)(128)(2,1)S(1)} %dynamic-update-slice), channel_id=2, replica_groups=mesh['rep'=4,'fsdp'=8] {'fsdp'}, use_global_device_ids=true, to_apply=%add.3 | all-reduce | flops 12672 | bytes 50688
  106.0 1.9 copy.71.tok_ref
  110.9 3.6 copy.74.teach_ref
  114.5 1.0 pad.6.aux_ref
  116.8 4.0 all-gather.6.cloned.1.call-done.w_ref
  120.7 51.0 %attend.1 = (f32[8,208,768]{2,1,0:T(8,128)}, bf16[8,208,2304]{2,1,0:T(8,128)(2,1)}, bf16[8,12,208,256]{3,2,1,0:T(8,128)(2,1)}, bf16[8,208,768]{2,1,0:T(8,128)(2,1)}, bf16[8,208,768]{2,1,0:T(8,128)(2,1)}) custom-call(s32[1]{0:T(128)} %bitcast.1.base_ref, bf16[8,196,768]{2,1,0:T(8,128)(2,1)} %copy.71.tok_ref, ...), custom_call_target="tpu_custom_call" | custom-call | flops 14000000000 | bytes 40000000 | tf_op jit(solution)/shard_map/attend/pallas_call | solution.py:365
  171.7 29.9 %all-gather.10.cloned.1.call-done.up_ref = bf16[768,3072]{1,0:T(8,128)(2,1)} async-done(((bf16[96,3072]{1,0:T(8,128)(2,1)}), bf16[768,3072]{1,0:T(8,128)(2,1)}) %all-gather.10.cloned.1.call-update) | async-done | bytes 4718608 | tf_op jit(solution)/shard_map/all_gather | solution.py:518
  201.7 80.1 %all-gather.12.cloned.1.call-done.down_ref = bf16[3072,768]{1,0:T(8,128)(2,1)} async-done(((bf16[384,768]{1,0:T(8,128)(2,1)}), bf16[3072,768]{1,0:T(8,128)(2,1)}) %all-gather.12.cloned.1.call-update) | async-done | bytes 4718608 | tf_op jit(solution)/shard_map/all_gather | solution.py:518
  281.7 74.2 %mlp.1 = (bf16[8,196,768]{2,1,0:T(8,128)(2,1)}, f32[8,208,768]{2,1,0:T(8,128)}, bf16[8,208,768]{2,1,0:T(8,128)(2,1)}, bf16[8,208,3072]{2,1,0:T(8,128)(2,1)}, bf1...) custom-call(f32[1]{0:T(128)} %bitcast.coef_ref, ...), custom_call_target="tpu_custom_call" | custom-call | flops 31406948352 | bytes 60000000 | tf_op jit(solution)/shard_map/mlp/pallas_call | solution.py:395
  355.9 46.3 %attend_back.1 = (bf16[8,208,2304]{2,1,0:T(8,128)(2,1)}, bf16[8,208,768]{2,1,0:T(8,128)(2,1)}, f32[128,128]{1,0:T(8,128)}, f32[1,768]{1,0:T(1,128)}, f32[2,768]{1,0:T(2,128)}) custom-call(f32[8,208,768]{2,1,0:T(8,128)} %get-tuple-element.40.gh_ref, bf16[768,768]{1,0:T(8,128)(2,1)} %all-gather.8.cloned.1.call-done.wp_ref, ...), custom_call_target="tpu_custom_call" | custom-call | flops 20000000000 | bytes 40000000 | tf_op jit(solution)/shard_map/attend_back/pallas_call | solution.py:421
  402.3 5.1 bitcast_convert_fusion.3
  407.4 11.7 %bitcast_convert_fusion.2 = bf16[768,2304]{1,0:T(8,128)(2,1)} fusion(bf16[8,208,768]{2,1,0:T(8,128)(2,1)} %get-tuple-element.51, bf16[8,208,2304]{2,1,0:T(8,128)(2,1)} %get-tuple-element.43.dqkv_ref), kind=kOutput, calls=%fused_computation.2 | convolution fusion | flops 5890572288 | bytes 13762560 | tf_op jit(solution)/shard_map/dot_general | solution.py:39
  419.2 1.6 copy-done.12
  420.8 13.0 %bitcast_convert_fusion = bf16[3072,768]{1,0:T(8,128)(2,1)} fusion(bf16[8,208,3072]{2,1,0:T(8,128)(2,1)} %get-tuple-element.56, bf16[8,208,768]{2,1,0:T(8,128)(2,1)S(1)} %copy-done.12), kind=kOutput, calls=%fused_computation | convolution fusion | flops 7854096384 | bytes 17498112 | tf_op jit(solution)/shard_map/dot_general | solution.py:39
  433.9 1.7 copy-done.11
  435.6 12.9 %bitcast_convert_fusion.1 = bf16[768,3072]{1,0:T(8,128)(2,1)} fusion(bf16[8,208,768]{2,1,0:T(8,128)(2,1)S(1)} %copy-done.11, bf16[8,208,3072]{2,1,0:T(8,128)(2,1)} %get-tuple-element.55), kind=kOutput, calls=%fused_computation.1 | convolution fusion | flops 7854096384 | bytes 17498112 | tf_op jit(solution)/shard_map/dot_general | solution.py:39
  448.5 15.2 %input_back.1 = (f32[8,196,768]{2,1,0:T(8,128)}, f32[2,768]{1,0:T(2,128)}) custom-call(s32[1]{0:T(128)} %bitcast.1.base_ref, bf16[8,208,2304]{2,1,0:T(8,128)(2,1)} %get-tuple-element.43.dqkv_ref, bf16[768,2304]{1,0:T(8,128)(2,1)} %all-gather.6.cloned.1.call-done.w_ref, bf16[8,196,768]{2,1,0:T(8,128)(2,1)} %copy.71.tok_ref, ...), custom_call_target="tpu_custom_call" | custom-call | flops 5888802816 | bytes 25000000 | tf_op jit(solution)/shard_map/input_back/pallas_call | solution.py:449
  463.7 6.2 copy.82
  470.0 81.2 %reduce-scatter.5.cloned.1.call-done = bf16[96,2304]{1,0:T(8,128)(2,1)} async-done(((bf16[768,2304]{1,0:T(8,128)(2,1)}), bf16[96,2304]{1,0:T(8,128)(2,1)}) %reduce-scatter.5.cloned.1.call-update) | async-done | bytes 442384 | tf_op jit(solution)/shard_map/reduce_scatter | solution.py:532
  551.1 98.5 %reduce-scatter.11.cloned.1.call-done = bf16[384,768]{1,0:T(8,128)(2,1)} async-done(((bf16[3072,768]{1,0:T(8,128)(2,1)}), bf16[384,768]{1,0:T(8,128)(2,1)}) %reduce-scatter.11.cloned.1.call-update) | async-done | bytes 589840 | tf_op jit(solution)/shard_map/reduce_scatter | solution.py:532
  649.6 98.7 %reduce-scatter.9.cloned.1.call-done = bf16[96,3072]{1,0:T(8,128)(2,1)} async-done(((bf16[768,3072]{1,0:T(8,128)(2,1)}), bf16[96,3072]{1,0:T(8,128)(2,1)}) %reduce-scatter.9.cloned.1.call-update) | async-done | bytes 589840 | tf_op jit(solution)/shard_map/reduce_scatter | solution.py:532
  752.4 41.4 %psum.43 = f32[8,1585]{1,0:T(8,128)S(1)} all-reduce(f32[8,1585]{1,0:T(8,128)S(1)} %concatenate.27), channel_id=1, replica_groups=mesh['rep'=4,'fsdp'=8] {'rep','fsdp'}, use_global_device_ids=true, to_apply=%region_3.4 | all-reduce | flops 12680 | bytes 101440 | tf_op jit(solution)/shard_map/psum | solution.py:552
  796.6 1.9 copy.81
  799.8 2.2 convert_element_type.127
  802.0 2.2 convert_element_type.129
  804.2 1.0 convert_element_type.123
  (112 shorter events, 19.8 us)
Async XLA Ops:
  7.2 98.8 %copy-start.1 = (bf16[8,196,768]{2,0,1:T(8,128)(2,1)S(1)}, bf16[8,196,768]{2,0,1:T(8,128)(2,1)}, u32[]{:S(2)}) copy-start(bf16[8,196,768]{2,0,1:T(8,128)(2,1)} %param.20) | copy-start | bytes 7225348
  7.2 109.6 %all-gather.8.cloned.1.call-start = ((), (), s32[]{:S(2)}) async-start(), calls=%async_computation.5 | async-start | bytes 1327104 | tf_op jit(solution)/shard_map/all_gather | solution.py:518
  7.9 112.8 %all-gather.6.cloned.1.call-start = ((), (), s32[]{:S(2)}) async-start(), calls=%async_computation.4 | async-start | bytes 3981312 | tf_op jit(solution)/shard_map/all_gather | solution.py:518
  8.7 193.0 %all-gather.10.cloned.1.call-start = ((), (), s32[]{:S(2)}) async-start(), calls=%async_computation.6 | async-start | bytes 5308416 | tf_op jit(solution)/shard_map/all_gather | solution.py:518
  9.4 272.3 %all-gather.12.cloned.1.call-start = ((), (), s32[]{:S(2)}) async-start(), calls=%async_computation.7 | async-start | bytes 5308416 | tf_op jit(solution)/shard_map/all_gather | solution.py:518
  10.0 460.0 %reduce-scatter.7.cloned.1.call-start = ((), (), s32[]{:S(2)}) async-start(), calls=%async_computation.9 | async-start | bytes 1327104 | tf_op jit(solution)/shard_map/reduce_scatter | solution.py:532
  355.9 46.3 %copy-start.10 = (bf16[8,208,768]{2,1,0:T(8,128)(2,1)S(1)}, bf16[8,208,768]{2,1,0:T(8,128)(2,1)}, u32[]{:S(2)}) copy-start(bf16[8,208,768]{2,1,0:T(8,128)(2,1)} %get-tuple-element.52) | copy-start | bytes 7667716
  407.4 143.8 %reduce-scatter.5.cloned.1.call-start = ((), (), s32[]{:S(2)}) async-start(), calls=%async_computation.8 | async-start | bytes 3981312 | tf_op jit(solution)/shard_map/reduce_scatter | solution.py:532
  419.1 1.7 copy-start.12
  419.1 230.5 %reduce-scatter.11.cloned.1.call-start = ((), (), s32[]{:S(2)}) async-start(), calls=%async_computation.11 | async-start | bytes 5308416 | tf_op jit(solution)/shard_map/reduce_scatter | solution.py:532
  433.8 1.7 copy-start.11
  433.9 314.5 %reduce-scatter.9.cloned.1.call-start = ((), (), s32[]{:S(2)}) async-start(), calls=%async_computation.10 | async-start | bytes 5308416 | tf_op jit(solution)/shard_map/reduce_scatter | solution.py:532
  448.5 351.3 %all-reduce.7.cloned.1.call-start = ((), (), s32[]{:S(2)}) async-start(), calls=%async_computation.12 | async-start | bytes 3538944 | tf_op jit(solution)/shard_map/psum | solution.py:531
  463.7 284.7 %copy-start.8 = (f32[2,768]{1,0:T(2,128)S(1)}, f32[2,768]{1,0:T(2,128)}, u32[]{:S(2)}) copy-start(f32[2,768]{1,0:T(2,128)} %get-tuple-element.44) | copy-start | bytes 18436
  463.7 284.8 %copy-start.4 = (f32[128,128]{1,0:T(8,128)S(1)}, f32[128,128]{1,0:T(8,128)}, u32[]{:S(2)}) copy-start(f32[128,128]{1,0:T(8,128)} %get-tuple-element.49) | copy-start | bytes 196612
  469.9 279.4 %copy-start.7 = (f32[2,768]{1,0:T(2,128)S(1)}, f32[2,768]{1,0:T(2,128)}, u32[]{:S(2)}) copy-start(f32[2,768]{1,0:T(2,128)} %get-tuple-element.45) | copy-start | bytes 18436
  469.9 279.6 %copy-start.9 = (f32[1,768]{1,0:T(1,128)S(1)}, f32[1,768]{1,0:T(1,128)}, u32[]{:S(2)}) copy-start(f32[1,768]{1,0:T(1,128)} %get-tuple-element.46) | copy-start | bytes 9220
  469.9 279.6 %copy-start.6 = (f32[4,768]{1,0:T(4,128)S(1)}, f32[4,768]{1,0:T(4,128)}, u32[]{:S(2)}) copy-start(f32[4,768]{1,0:T(4,128)} %get-tuple-element.47) | copy-start | bytes 36868
  469.9 281.0 %copy-start.5 = (f32[1,3072]{1,0:T(1,128)S(1)}, f32[1,3072]{1,0:T(1,128)}, u32[]{:S(2)}) copy-start(f32[1,3072]{1,0:T(1,128)} %get-tuple-element.48) | copy-start | bytes 36868
  469.9 326.7 %copy-start = (bf16[8,196,768]{2,1,0:T(8,128)(2,1)S(1)}, bf16[8,196,768]{2,1,0:T(8,128)(2,1)}, u32[]{:S(2)}) copy-start(bf16[8,196,768]{2,1,0:T(8,128)(2,1)} %get-tuple-element.94) | copy-start | bytes 7225348
  799.8 4.4 copy-start.2
  799.8 5.4 copy-start.3
Sparse Core Ops, SparseCore 0:
  10.2 43.8 all-gather.7
  56.3 64.4 all-gather.5
  122.9 78.7 all-gather.9
  203.7 78.0 all-gather.11
  407.5 62.2 reduce-scatter.6
  473.2 77.8 reduce-scatter.4
  554.8 94.7 reduce-scatter.10
  653.3 95.0 reduce-scatter.8
  750.9 47.4 all-reduce.6

commit v2 on v1

v2 whole, which is shorter than its diff:
```python
import functools
import math

import jax
import jax.numpy as jnp
import numpy as np
from jax import lax
from jax.experimental import pallas as pl
from jax.experimental.pallas import tpu as pltpu
from jax.sharding import PartitionSpec as P

D = 768
HEADS = 12
HEAD_DIM = 64
MLP = 3072
WIN = 14
MAP = 64
SLOTS = WIN * WIN
ROWS = 208
LANES = 256
PAIRS = HEADS // 2
PAIR = 2 * HEAD_DIM
SIDE = (MAP + WIN - 1) // WIN
LN_EPS = 1e-06
F32 = jnp.float32
BF16 = jnp.bfloat16
VMEM_LIMIT = 60 * 1024 * 1024
QKV_HALF = 3 * D // 2
NOTES = 128
STEPS = (1, 2, 4, 1)
BACK_STEPS = (1, 5, 2)


def nn(left, right):
    return jnp.dot(left, right, preferred_element_type=F32)


def nt(left, right):
    return lax.dot_general(left, right, (((1,), (1,)), ((), ())), preferred_element_type=F32)


def tn(left, right):
    return lax.dot_general(left, right, (((0,), (0,)), ((), ())), preferred_element_type=F32)


def key_places():
    table = np.zeros((ROWS, HEAD_DIM), np.float32)
    for slot in range(SLOTS):
        for base in (0, 32):
            table[slot, base + WIN - 1 - slot // WIN] = 1.0
            table[slot, base + 16 + WIN - 1 - slot % WIN] = 1.0
    return table


def keep_column(base_ref, window):
    slot = lax.broadcasted_iota(jnp.int32, (ROWS, 1), 0)
    row = lax.shift_right_logical(slot * 4682, 16)
    col = slot - row * WIN
    place = lax.rem(base_ref[2] + window, SIDE * SIDE)
    place_row = lax.div(place, SIDE)
    place_col = place - place_row * SIDE
    inside = (slot < SLOTS) & (row + place_row * WIN < MAP) & (col + place_col * WIN < MAP)
    return inside.astype(F32)


def lane_places():
    slot = lax.broadcasted_iota(jnp.int32, (1, LANES), 1)
    row = lax.shift_right_logical(slot * 4682, 16)
    return row, slot - row * WIN


def norm_parts(values):
    mean = jnp.mean(values, axis=-1, keepdims=True)
    centred = values - mean
    inv_std = lax.rsqrt(jnp.mean(centred * centred, axis=-1, keepdims=True) + LN_EPS)
    return centred * inv_std, inv_std


def norm_grad(grad, scaled, inv_std, gain):
    grad_scaled = grad * gain
    first = jnp.mean(grad_scaled, axis=-1, keepdims=True)
    second = jnp.mean(grad_scaled * scaled, axis=-1, keepdims=True)
    return inv_std * (grad_scaled - first - scaled * second)


def up_by(values, amount):
    take = lambda bit: (amount & bit) != 0
    part = jnp.where(take(8), values[8:32], values[0:24])
    part = jnp.where(take(4), pltpu.roll(part, 20, 0), part)
    part = jnp.where(take(2), pltpu.roll(part, 22, 0), part)
    part = jnp.where(take(1), pltpu.roll(part, 23, 0), part)
    return part[0:16]


def down_by(values, amount):
    take = lambda bit: (amount & bit) != 0
    zeros = jnp.zeros((8, values.shape[1]), values.dtype)
    part = jnp.concatenate([values, zeros], axis=0)
    part = jnp.where(take(1), pltpu.roll(part, 1, 0), part)
    part = jnp.where(take(2), pltpu.roll(part, 2, 0), part)
    part = jnp.where(take(4), pltpu.roll(part, 4, 0), part)
    return jnp.where(
        take(8),
        jnp.concatenate([zeros, part], axis=0),
        jnp.concatenate([part, zeros], axis=0),
    )


def fill_rows(values):
    return jnp.concatenate(
        [values, jnp.zeros((LANES - ROWS,) + values.shape[1:], values.dtype)], axis=0
    )


def chunk_place(me_ref, index, far_y, along_y):
    mid, plane = index // 2, index % 2
    dist_x, dist_y = (far_y, mid) if along_y else (mid, far_y)
    plane = plane * 2 + (0 if along_y else 4)
    return (me_ref[0] // 2) ^ dist_x, me_ref[1] ^ (plane + dist_y)


ARRIVED = tuple((half, along_y, other) for other in (0, 1) for along_y in (True, False) for half in (0, 1))


def load_first(me_ref, parts, full, sem):
    core = me_ref[0] % 2
    for ref, (half, along_y, other) in zip(parts, ARRIVED):

        def start(index, carry, ref=ref, half=half, along_y=along_y, other=other):
            far_x, owner = chunk_place(me_ref, index, half, along_y)
            pltpu.make_async_copy(
                ref.at[index, :, pl.ds(0, QKV_HALF)],
                full.at[
                    pl.ds(pl.multiple_of(owner * 96 + far_x * 48, 16), 48),
                    pl.ds(pl.multiple_of((core ^ other) * QKV_HALF, 128), QKV_HALF),
                ],
                sem.at[0],
            ).start()
            return carry

        lax.fori_loop(0, 4, start, 0)
    pltpu.make_async_copy(full, full, sem.at[0]).wait()


def piece_place(me_ref, index):
    group, high, mid, plane = index // 8, (index // 4) % 2, (index // 2) % 2, index % 2
    dist_x = jnp.where(group == 0, high, mid)
    dist_y = jnp.where(group == 0, mid, high)
    return (me_ref[0] // 2) ^ dist_x, me_ref[1] ^ (group * 4 + plane * 2 + dist_y)


def spread_rows(notes_of, owner_of, width, total):
    row = lax.broadcasted_iota(jnp.int32, (128, total), 0)
    col = lax.broadcasted_iota(jnp.int32, (128, total), 1)
    acc = None
    for at in range(8):
        put = ((row < width) & (col == row + owner_of(at) * width)).astype(BF16)
        part = nn(notes_of(at), put)
        acc = part if acc is None else acc + part
    return acc


def notes_kernel(me_ref, a_ref, b_ref, c_ref, vec_ref, rel_ref, relt_ref):
    picks = [(a_ref, at, at % 2 * 2 + at // 2) for at in range(4)]
    picks += [(b_ref, at, 4 + at * 2) for at in range(2)] + [(c_ref, at, 5 + at * 2) for at in range(2)]
    owner_of = lambda at: me_ref[1] ^ picks[at][2]
    lanes = pl.ds(QKV_HALF, NOTES)
    vec_ref[...] = spread_rows(
        lambda at: picks[at][0][picks[at][1], 0:16, lanes], owner_of, 96, D
    )[0:8]
    row = lax.broadcasted_iota(jnp.int32, (128, 128), 0)
    col = lax.broadcasted_iota(jnp.int32, (128, 128), 1)
    halves = []
    for which in range(2):
        acc = jnp.zeros((32, 128), F32)
        for at in range(8):
            lane = row - 8 * which
            place = lane + owner_of(at) * 8
            put = ((lane >= 0) & (lane < 8) & ((col == place) | (col == place + 64))).astype(BF16)
            acc = acc + nn(picks[at][0][picks[at][1], 16:48, lanes], put)
        halves.append(acc)
    table = jnp.concatenate(halves * 2, axis=0)
    table = jnp.where((row < 64) == (col < 64), table, 0.0).astype(BF16)
    rel_ref[...] = table
    relt_ref[...] = table.T


def attend_kernel(*refs, first, pieces, earlier):
    base_ref, tok_ref = refs[0:2]
    at = 2 + max(pieces, 1)
    vec_ref, rel_ref, place_ref = refs[at : at + 3]
    at += 3 + earlier
    qkv_ref, prob_ref, mix_ref, fin_ref = refs[at : at + 4]
    if pieces:
        w_ref, x_ref, sem = refs[at + 4 :]

        @pl.when(pl.program_id(0) == 0)
        def _():
            load_first(base_ref, refs[2 : 2 + pieces], w_ref, sem)
    else:
        w_ref, x_ref = refs[2], refs[at + 4]
    keep = keep_column(base_ref, pl.program_id(0) + first)
    x_ref[pl.ds(192, 16), :] = jnp.zeros((16, D), F32)
    x_ref[pl.ds(0, SLOTS), :] = tok_ref[0].astype(F32)
    scaled, _ = norm_parts(x_ref[...])
    first_in = (keep * (scaled * vec_ref[0:1, :] + vec_ref[1:2, :])).astype(BF16)
    fin_ref[0] = first_in
    for part in range(3):
        cols = pl.ds(part * D, D)
        total = nn(first_in, w_ref[:, cols])
        if part != 1:
            total = total + vec_ref[2 + part // 2 : 3 + part // 2, :]
        qkv_ref[0, :, cols] = total.astype(BF16)
    lane_row, lane_col = lane_places()
    low_half = lax.broadcasted_iota(jnp.int32, (ROWS, PAIR), 1) < HEAD_DIM
    tail_rows = lax.broadcasted_iota(jnp.int32, (16, LANES), 0) + 192
    places = place_ref[...]
    place_pair = jnp.concatenate([places, places], axis=1)

    def one_pair(pair, carry):
        at = pl.multiple_of(pair * PAIR, PAIR)
        query = qkv_ref[0, :, pl.ds(at, PAIR)]
        keys = qkv_ref[0, :, pl.ds(pl.multiple_of(D + at, PAIR), PAIR)]
        values = qkv_ref[0, :, pl.ds(pl.multiple_of(2 * D + at, PAIR), PAIR)]
        query_t = fill_rows(query).T
        values_t = fill_rows(values).T
        offsets = nn(rel_ref[...], query_t)
        mixed = []
        for head in range(2):
            mine = offsets[head * HEAD_DIM : (head + 1) * HEAD_DIM]
            along = jnp.concatenate(
                [up_by(mine[0:32], lane_row), up_by(mine[32:64], lane_col)], axis=0
            )
            high = along.astype(BF16)
            rest = (along - high.astype(F32)).astype(BF16)
            scaled_q = query_t[head * HEAD_DIM : (head + 1) * HEAD_DIM] * jnp.asarray(
                HEAD_DIM ** (-0.5), BF16
            )
            if head == 0:
                query_ext = jnp.concatenate([scaled_q, high, rest], axis=0)
                keys_ext = jnp.where(low_half, keys, place_pair)
            else:
                query_ext = jnp.concatenate([high, rest, scaled_q], axis=0)
                keys_ext = jnp.where(low_half, place_pair, keys)
            scores = nn(keys_ext, query_ext)
            scores = jnp.concatenate(
                [scores[0:192], jnp.where(tail_rows < SLOTS, scores[192:208], -1e30)], axis=0
            )
            peak = jnp.max(scores, axis=0, keepdims=True)
            expo = jnp.exp(scores - peak)
            total = jnp.sum(expo, axis=0, keepdims=True)
            probs = (expo * (1.0 / total)).astype(BF16)
            prob_ref[0, 2 * pair + head] = probs
            mixed.append(
                nn(values_t[head * HEAD_DIM : (head + 1) * HEAD_DIM], fill_rows(probs)).astype(BF16)
            )
        mix_ref[0, :, pl.ds(at, PAIR)] = jnp.concatenate(mixed, axis=0).T[0:ROWS]
        return carry

    lax.fori_loop(0, PAIRS, one_pair, 0)


def gelu_parts(pre):
    bell = jnp.exp(pre * pre * (-0.5))
    steps = 1.0 / (1.0 + (0.3275911 * math.sqrt(0.5)) * jnp.abs(pre))
    poly = steps * (
        0.5 * 0.254829592
        + steps
        * (
            0.5 * -0.284496736
            + steps * (0.5 * 1.421413741 + steps * (0.5 * -1.453152027 + steps * (0.5 * 1.061405429)))
        )
    )
    tail = poly * bell
    cumulative = jnp.where(pre > 0, 1.0 - tail, tail)
    return pre * cumulative, cumulative + pre * (bell * 0.3989422804014327)


def load_mlp(me_ref, pieces, up, down, proj, notes, sem):
    core = me_ref[0] % 2
    for array, (ref, (half, along_y, other)) in enumerate(zip(pieces, ARRIVED)):

        def start(index, carry, ref=ref, half=half, along_y=along_y, far_core=core ^ other, array=array):
            far_x, owner = chunk_place(me_ref, index, half, along_y)
            rows = pl.ds(pl.multiple_of(owner * 96 + far_x * 48, 16), 48)
            for block in range(2):
                cols = pl.ds(pl.multiple_of(far_core * 1536 + block * D, 128), D)
                pltpu.make_async_copy(ref.at[index, block], up.at[rows, cols], sem.at[0]).start()
            place = owner * 8 + far_core * 4 + far_x * 2
            pltpu.make_async_copy(
                ref.at[index, pl.ds(2, 2)], down.at[pl.ds(place, 2)], sem.at[1]
            ).start()
            cols = pl.ds(pl.multiple_of(far_core * 384, 128), 384)
            pltpu.make_async_copy(
                ref.at[index, 4, :, pl.ds(0, 384)], proj.at[rows, cols], sem.at[2]
            ).start()
            pltpu.make_async_copy(
                ref.at[index, 4, pl.ds(0, 16), pl.ds(384, 384)], notes.at[array * 4 + index], sem.at[3]
            ).start()
            return carry

        lax.fori_loop(0, 4, start, 0)
    for at, full in ((3, notes), (2, proj), (0, up), (1, down)):
        pltpu.make_async_copy(full, full, sem.at[at]).wait()


def mlp_kernel(*refs, group, pieces, scale):
    step = pl.program_id(0)
    rows = group * ROWS
    me_ref, tok_ref, mix_ref, teach_ref, aux_ref = refs[0:5]
    at = 5 + (pieces or 6)
    (out_ref, gh_ref, ga_ref, si_ref, act_ref, gd_ref, gu_ref, sums_ref, usum_ref) = refs[at : at + 9]
    at += 9
    if pieces:
        wp_ref, slope_ref, t_ref, up_ref, down3_ref, notes, vec_ref, ub_ref, total_ref, sem = refs[at:]

        @pl.when(step == 0)
        def _():
            load_mlp(me_ref, refs[5 : 5 + pieces], up_ref, down3_ref, wp_ref, notes, sem)
            picks = [(at, at % 2 * 2 + at // 2) for at in range(4)]
            picks += [(8 + at, 4 + at * 2) for at in range(2)] + [(12 + at, 5 + at * 2) for at in range(2)]
            owner_of = lambda at: me_ref[1] ^ picks[at][1]
            vec_ref[...] = spread_rows(lambda at: notes[picks[at][0], :, 0:128], owner_of, 96, D)
            for at in range(8):
                lanes = pl.ds(pl.multiple_of(owner_of(at) * 384, 128), 384)
                ub_ref[:, lanes] = notes[picks[at][0], 0:16, :].astype(F32)[4:5, :]
            counts = notes[0].astype(F32)
            for at in range(1, 32):
                counts = counts + notes[at].astype(F32)
            counts = counts[5:6, 0:128]
            lane = lax.broadcasted_iota(jnp.int32, (1, 128), 1)
            weight = jnp.where(lane == 0, 128.0, jnp.where(lane == 1, 1.0, 0.0))
            total_ref[...] = jnp.sum(counts * weight, axis=1, keepdims=True)

        down_rows = lambda part: down3_ref[pl.ds(part * 16, 16)].reshape(D, D)
    else:
        wp_ref, up_ref, down_ref, vec_ref, ub_ref, total_ref = refs[5:11]
        slope_ref, t_ref = refs[at:]
        down_rows = lambda part: down_ref[pl.ds(pl.multiple_of(part * D, D), D), :]
    pb_row, gain_row, shift_row, db_row = [vec_ref[at : at + 1, :] for at in range(4)]
    coef = scale / total_ref[...]

    @pl.when(step == 0)
    def _():
        sums_ref[...] = jnp.zeros_like(sums_ref)
        sums_ref[5:6, :] = jnp.broadcast_to(total_ref[...], (1, D))
        usum_ref[...] = jnp.zeros_like(usum_ref)

    aux = aux_ref[...].reshape(rows, 2)
    keep, valid = aux[:, 0:1], aux[:, 1:2]
    for at in range(group):
        t_ref[at, pl.ds(192, 16), :] = jnp.zeros((16, D), F32)
        t_ref[at, pl.ds(0, SLOTS), :] = tok_ref[at].astype(F32)
    attn_out = nn(mix_ref[...].reshape(rows, D), wp_ref[...]) + pb_row
    hidden = keep * (t_ref[...].reshape(rows, D) + attn_out)
    scaled, inv_std = norm_parts(hidden)
    second_in = (scaled * gain_row + shift_row).astype(BF16)
    si_ref[...] = second_in.reshape(group, ROWS, D)
    chunk = D

    def forward(part, total):
        cols = pl.ds(pl.multiple_of(part * chunk, chunk), chunk)
        pre = nn(second_in, up_ref[:, cols]) + ub_ref[:, cols]
        act, slope = gelu_parts(pre)
        slope_ref[:, cols] = slope
        low = act.astype(BF16)
        act_ref[:, :, cols] = low.reshape(group, ROWS, chunk)
        return total + nn(low, down_rows(part))

    down = lax.fori_loop(0, MLP // chunk, forward, jnp.zeros((rows, D), F32))
    final = keep * (hidden + (down + db_row))
    for at in range(group):
        out_ref[at] = final[at * ROWS : at * ROWS + SLOTS].astype(BF16)
        t_ref[at, pl.ds(192, 16), :] = jnp.zeros((16, D), F32)
        t_ref[at, pl.ds(0, SLOTS), :] = teach_ref[at].astype(F32)
    error = final - t_ref[...].reshape(rows, D)
    weighted = valid * error
    grad_final = coef * weighted
    grad_down = grad_final.astype(BF16)
    gd_ref[...] = grad_down.reshape(group, ROWS, D)
    sums_ref[0:1, :] += jnp.sum(weighted * error, axis=0, keepdims=True)
    sums_ref[1:2, :] += jnp.sum(grad_down.astype(F32), axis=0, keepdims=True)

    def backward(part, total):
        cols = pl.ds(pl.multiple_of(part * chunk, chunk), chunk)
        grad_up = (nt(grad_down, down_rows(part)) * slope_ref[:, cols]).astype(BF16)
        gu_ref[:, :, cols] = grad_up.reshape(group, ROWS, chunk)
        usum_ref[:, cols] += jnp.sum(grad_up.astype(F32), axis=0, keepdims=True)
        return total + nt(grad_up, up_ref[:, cols])

    grad_second = lax.fori_loop(0, MLP // chunk, backward, jnp.zeros((rows, D), F32))
    sums_ref[2:3, :] += jnp.sum(grad_second * scaled, axis=0, keepdims=True)
    sums_ref[3:4, :] += jnp.sum(grad_second, axis=0, keepdims=True)
    grad_hidden = grad_final + norm_grad(grad_second, scaled, inv_std, gain_row)
    grad_hidden = keep * grad_hidden
    gh_ref[...] = grad_hidden.reshape(group, ROWS, D)
    grad_attn = grad_hidden.astype(BF16)
    ga_ref[...] = grad_attn.reshape(group, ROWS, D)
    sums_ref[4:5, :] += jnp.sum(grad_attn.astype(F32), axis=0, keepdims=True)


def attend_back_kernel(*refs, earlier):
    ga_ref, wp_ref, qkv_ref, prob_ref, relt_ref, placet_ref = refs[0:6]
    dqkv_ref, rg_ref, qsum_ref, gm_ref = refs[6 + earlier :]

    @pl.when(pl.program_id(0) == 0)
    def _():
        rg_ref[...] = refs[7][...] if earlier else jnp.zeros_like(rg_ref)
        qsum_ref[...] = refs[8][...] if earlier else jnp.zeros_like(qsum_ref)
        gm_ref[pl.ds(ROWS, LANES - ROWS), :] = jnp.zeros((LANES - ROWS, D), BF16)

    gm_ref[pl.ds(0, ROWS), :] = nt(ga_ref[0], wp_ref[...]).astype(BF16)
    lane_row, lane_col = lane_places()
    low_half = lax.broadcasted_iota(jnp.int32, (ROWS, PAIR), 1) < HEAD_DIM
    low_full = lax.broadcasted_iota(jnp.int32, (LANES, PAIR), 1) < HEAD_DIM
    blank = jnp.zeros((), BF16)
    scale = HEAD_DIM ** (-0.5)

    def one_pair(pair, carry):
        at = pl.multiple_of(pair * PAIR, PAIR)
        q_at = pl.ds(at, PAIR)
        k_at = pl.ds(pl.multiple_of(D + at, PAIR), PAIR)
        v_at = pl.ds(pl.multiple_of(2 * D + at, PAIR), PAIR)
        query = fill_rows(qkv_ref[0, :, q_at])
        keys_t = fill_rows(qkv_ref[0, :, k_at]).T
        values = qkv_ref[0, :, v_at]
        grad_out = gm_ref[:, q_at]
        stacked = jnp.concatenate(
            [jnp.where(low_half, values, blank), jnp.where(low_half, blank, values)], axis=0
        )
        grad_probs = nt(stacked, grad_out)
        grad_values = jnp.zeros((ROWS, PAIR), F32)
        grad_keys = jnp.zeros((ROWS, PAIR), F32)
        spread, plain = [], []
        for head in range(2):
            own = (lambda full: jnp.where(low_full, full, blank)) if head == 0 else (
                lambda full: jnp.where(low_full, blank, full)
            )
            low = prob_ref[0, 2 * pair + head]
            probs = low.astype(F32)
            grad_p = grad_probs[head * ROWS : (head + 1) * ROWS]
            row_dot = jnp.sum(probs * grad_p, axis=0, keepdims=True)
            grad_score = (probs * (grad_p - row_dot)).astype(BF16)
            grad_values = grad_values + nn(low, own(grad_out))
            grad_keys = grad_keys + nn(grad_score, own(query))
            keys_ext = jnp.concatenate(
                [keys_t[head * HEAD_DIM : (head + 1) * HEAD_DIM], placet_ref[...]], axis=0
            )
            grad_ext = nn(keys_ext, fill_rows(grad_score))
            plain.append(grad_ext[0:64])
            spread.append(down_by(grad_ext[64:80], lane_row))
            spread.append(down_by(grad_ext[80:96], lane_col))
        spread = jnp.concatenate(spread, axis=0).astype(BF16)
        grad_query = jnp.concatenate(plain, axis=0) * scale + nn(relt_ref[...], spread)
        rg_ref[...] += nn(spread, query)
        grad_query = grad_query.astype(BF16).T[0:ROWS]
        grad_keys = (grad_keys * scale).astype(BF16)
        grad_values = grad_values.astype(BF16)
        dqkv_ref[0, :, q_at] = grad_query
        dqkv_ref[0, :, k_at] = grad_keys
        dqkv_ref[0, :, v_at] = grad_values
        qsum_ref[0:1, q_at] += jnp.sum(grad_query.astype(F32), axis=0, keepdims=True)
        qsum_ref[1:2, q_at] += jnp.sum(grad_values.astype(F32), axis=0, keepdims=True)
        return carry

    lax.fori_loop(0, PAIRS, one_pair, 0)


def input_kernel(
    base_ref, dqkv_ref, w_ref, tok_ref, gh_ref, vec_ref, *refs, group, first, earlier
):
    step = pl.program_id(0)
    out_ref, sums_ref, x_ref = refs[earlier:]

    @pl.when(step == 0)
    def _():
        sums_ref[...] = refs[1][...] if earlier else jnp.zeros_like(sums_ref)

    for at in range(group):
        keep = keep_column(base_ref, first + step * group + at)
        grad_first = keep * nt(dqkv_ref[at], w_ref[...])
        x_ref[pl.ds(192, 16), :] = jnp.zeros((16, D), F32)
        x_ref[pl.ds(0, SLOTS), :] = tok_ref[at].astype(F32)
        scaled, inv_std = norm_parts(x_ref[...])
        sums_ref[0:1, :] += jnp.sum(grad_first * scaled, axis=0, keepdims=True)
        sums_ref[1:2, :] += jnp.sum(grad_first, axis=0, keepdims=True)
        total = gh_ref[at] + norm_grad(grad_first, scaled, inv_std, vec_ref[0:1, :])
        out_ref[at] = total[0:SLOTS]


def weight_grad_kernel(*refs):
    left_ref, right_ref, out_ref = refs
    out_ref[...] = tn(left_ref[...], right_ref[...]).astype(BF16)


def qkv_grad_kernel(me_ref, left_ref, right_ref, keep_ref, send_ref, full, sem):
    step = pl.program_id(0)
    cols = pl.ds(pl.multiple_of(step * D, D), D)
    full[:, cols] = tn(left_ref[...], right_ref[...]).astype(BF16)

    @pl.when(step == pl.num_programs(0) - 1)
    def _():
        core = me_ref[0] % 2
        for at, (ref, far_core) in enumerate(((send_ref, 1 - core), (keep_ref, core))):

            def start(index, carry, ref=ref, far_core=far_core, at=at):
                far_x, owner = piece_place(me_ref, index)
                pltpu.make_async_copy(
                    full.at[
                        pl.ds(pl.multiple_of(owner * 96 + far_x * 48, 16), 48),
                        pl.ds(pl.multiple_of(far_core * QKV_HALF, 128), QKV_HALF),
                    ],
                    ref.at[index],
                    sem.at[at],
                ).start()
                return carry

            lax.fori_loop(0, 16, start, 0)
        for at, ref in enumerate((send_ref, keep_ref)):
            pltpu.make_async_copy(ref, ref, sem.at[at]).wait()


def up_grad_kernel(me_ref, left_ref, right_ref, keep_ref, send_ref, full, sem):
    step = pl.program_id(0)
    full[step] = tn(left_ref[...], right_ref[...]).astype(BF16)
    mine = (step // 2) == me_ref[0] % 2

    def send_to(ref, at):
        def start(index, carry):
            far_x, owner = piece_place(me_ref, index)
            rows = pl.ds(pl.multiple_of(owner * 96 + far_x * 48, 16), 48)
            pltpu.make_async_copy(
                full.at[step, rows], ref.at[index, step % 2], sem.at[at]
            ).start()
            return carry

        lax.fori_loop(0, 16, start, 0)

    @pl.when(mine)
    def _():
        send_to(keep_ref, 0)

    @pl.when(jnp.logical_not(mine))
    def _():
        send_to(send_ref, 1)

    @pl.when(step == pl.num_programs(0) - 1)
    def _():
        pltpu.make_async_copy(keep_ref, keep_ref, sem.at[0]).wait()
        pltpu.make_async_copy(send_ref, send_ref, sem.at[1]).wait()


def down_grad_kernel(
    me_ref, act_ref, gd_ref, mix_ref, ga_ref, keep_ref, send_ref, full, half, sem
):
    step = pl.program_id(0)
    last = pl.num_programs(0) - 1

    @pl.when(step < last)
    def _():
        full[step] = tn(act_ref[...], gd_ref[...]).astype(BF16).reshape(16, 48, D)

    @pl.when(step == last)
    def _():
        total = tn(mix_ref[...], ga_ref[...]).astype(BF16)
        for core in range(2):
            half[core] = total[:, core * 384 : core * 384 + 384]

    core = me_ref[0] % 2
    for ref, far_core, at in ((keep_ref, core, 0), (send_ref, 1 - core, 1)):

        def start_down(index, carry, ref=ref, far_core=far_core, at=at):
            far_x, owner = piece_place(me_ref, index)

            @pl.when(owner // 2 == step)
            def _():
                place = (owner % 2) * 8 + far_core * 4 + far_x * 2
                pltpu.make_async_copy(
                    full.at[step, pl.ds(place, 2)], ref.at[index, pl.ds(0, 2)], sem.at[at]
                ).start()

            return carry

        def start_proj(index, carry, ref=ref, far_core=far_core, at=at):
            far_x, owner = piece_place(me_ref, index)
            rows = pl.ds(pl.multiple_of(owner * 96 + far_x * 48, 16), 48)
            for col in (0, 384):
                pltpu.make_async_copy(
                    half.at[far_core, rows], ref.at[index, 2, :, pl.ds(col, 384)], sem.at[at]
                ).start()
            return carry

        @pl.when(step < last)
        def _(start_down=start_down):
            lax.fori_loop(0, 16, start_down, 0)

        @pl.when(step == last)
        def _(start_proj=start_proj):
            lax.fori_loop(0, 16, start_proj, 0)

    @pl.when(step == last)
    def _():
        pltpu.make_async_copy(keep_ref, keep_ref, sem.at[0]).wait()
        pltpu.make_async_copy(send_ref, send_ref, sem.at[1]).wait()


def whole(shape):
    zeros = (0,) * len(shape)
    return pl.BlockSpec(shape, lambda *_: zeros)


def windows_from(first, shape):
    tail = (0,) * (len(shape) - 1)
    return pl.BlockSpec(shape, lambda step: (step + first,) + tail)


SMEM = pl.BlockSpec(memory_space=pltpu.SMEM)
ANY = pl.BlockSpec(memory_space=pl.ANY)


def params():
    return pltpu.CompilerParams(
        vmem_limit_bytes=VMEM_LIMIT, dimension_semantics=("arbitrary",)
    )


def shape_of(shape, dtype):
    return jax.ShapeDtypeStruct(shape, dtype)


def cost(flops, moved):
    return pl.CostEstimate(flops=int(flops), bytes_accessed=int(moved), transcendentals=0)


def notes_of(me, near, far_x, far_y):
    return pl.pallas_call(
        notes_kernel,
        in_specs=[SMEM] + [whole(v.shape) for v in (near, far_x, far_y)],
        out_specs=[whole((8, D)), whole((PAIR, PAIR)), whole((PAIR, PAIR))],
        out_shape=[shape_of((8, D), F32)] + [shape_of((PAIR, PAIR), BF16)] * 2,
        grid=(1,),
        compiler_params=params(),
        cost_estimate=cost(1e9, 1e6),
        name="notes",
    )(me, near, far_x, far_y)


def attend(me, tokens, weight, vec, rel, places, first, number, earlier=()):
    count = tokens.shape[0]
    win = lambda shape: windows_from(first, shape)
    pieces = len(weight) if isinstance(weight, tuple) else 0
    weights = weight if pieces else (weight,)
    weight_specs = [ANY] * pieces if pieces else [whole((D, 3 * D))]
    out_specs = [win((1, ROWS, 3 * D)), win((1, HEADS, ROWS, LANES)), win((1, ROWS, D)),
                 win((1, ROWS, D))]
    out_shape = [
        shape_of((count, ROWS, 3 * D), BF16), shape_of((count, HEADS, ROWS, LANES), BF16),
        shape_of((count, ROWS, D), BF16), shape_of((count, ROWS, D), BF16),
    ]
    scratch = [pltpu.VMEM((ROWS, D), F32)]
    if pieces:
        out_specs.append(whole((D, 3 * D)))
        out_shape.append(shape_of((D, 3 * D), BF16))
        scratch.append(pltpu.SemaphoreType.DMA((1,)))
    inputs = 5 + len(weights)
    return pl.pallas_call(
        functools.partial(attend_kernel, first=first, pieces=pieces, earlier=len(earlier)),
        grid=(number,),
        in_specs=[
            SMEM, win((1, SLOTS, D)), *weight_specs, whole((8, D)),
            whole((PAIR, PAIR)), whole((ROWS, HEAD_DIM)), *([ANY] * len(earlier)),
        ],
        out_specs=out_specs,
        out_shape=out_shape,
        scratch_shapes=scratch,
        input_output_aliases={inputs + at: at for at in range(len(earlier))},
        compiler_params=params(),
        cost_estimate=cost(number * 6e9, number * 2e6),
        name="attend",
    )(me, tokens, *weights, vec, rel, places, *earlier)


def mlp(me, tokens, mixed, teacher, aux, weights, scale, chunked):
    count = tokens.shape[0]
    group = math.gcd(count, 2)
    win = lambda width: windows_from(0, (group, ROWS, width))
    plain = windows_from(0, (group, SLOTS, D))
    arr = lambda width, dtype: shape_of((count, ROWS, width), dtype)
    pieces = len(weights) if chunked else 0
    weight_specs = [ANY] * pieces if pieces else [whole(v.shape) for v in weights]
    out_specs = [plain, win(D), win(D), win(D), win(MLP), win(D), win(MLP), whole((6, D)),
                 whole((1, MLP))]
    out_shape = [
        shape_of((count, SLOTS, D), BF16), arr(D, F32), arr(D, BF16), arr(D, BF16), arr(MLP, BF16),
        arr(D, BF16), arr(MLP, BF16), shape_of((6, D), F32), shape_of((1, MLP), F32),
    ]
    scratch = [pltpu.VMEM((group * ROWS, MLP), F32), pltpu.VMEM((group, ROWS, D), F32)]
    if pieces:
        out_specs.append(whole((D, D)))
        out_shape.append(shape_of((D, D), BF16))
        scratch += [pltpu.VMEM((D, MLP), BF16), pltpu.VMEM((MLP // 48, 48, D), BF16),
                    pltpu.VMEM((32, 16, 384), BF16), pltpu.VMEM((16, D), F32),
                    pltpu.VMEM((1, MLP), F32), pltpu.VMEM((1, 1), F32),
                    pltpu.SemaphoreType.DMA((4,))]
    return pl.pallas_call(
        functools.partial(mlp_kernel, group=group, pieces=pieces, scale=scale),
        grid=(count // group,),
        in_specs=[SMEM, plain, win(D), plain, win(2), *weight_specs],
        out_specs=out_specs,
        out_shape=out_shape,
        scratch_shapes=scratch,
        compiler_params=params(),
        cost_estimate=cost(count * 8e9, 60e6),
        name="mlp",
    )(me, tokens, mixed, teacher, aux, *weights)


def attend_back(grad_attn, proj, qkv, probs, rel_t, places_t, first, number, earlier=()):
    count = grad_attn.shape[0]
    win = lambda shape: windows_from(first, shape)
    before = [ANY, whole((PAIR, PAIR)), whole((2, D))] if earlier else []
    return pl.pallas_call(
        functools.partial(attend_back_kernel, earlier=len(earlier)),
        grid=(number,),
        in_specs=[
            win((1, ROWS, D)), whole((D, D)), win((1, ROWS, 3 * D)), win((1, HEADS, ROWS, LANES)),
            whole((PAIR, PAIR)), whole((32, LANES)), *before,
        ],
        out_specs=[win((1, ROWS, 3 * D)), whole((PAIR, PAIR)), whole((2, D))],
        out_shape=[
            shape_of((count, ROWS, 3 * D), BF16), shape_of((PAIR, PAIR), F32),
            shape_of((2, D), F32),
        ],
        scratch_shapes=[pltpu.VMEM((LANES, D), BF16)],
        input_output_aliases={6: 0} if earlier else {},
        compiler_params=params(),
        cost_estimate=cost(number * 6e9, number * 2e6),
        name="attend_back",
    )(grad_attn, proj, qkv, probs, rel_t, places_t, *earlier)


def input_back(me, dqkv, weight, tokens, grad_hidden, vec, first, number, earlier=()):
    count = tokens.shape[0]
    group = math.gcd(math.gcd(first, number), 2)
    win = lambda shape: windows_from(first // group, shape)
    before = [ANY, whole((2, D))] if earlier else []
    return pl.pallas_call(
        functools.partial(input_kernel, group=group, first=first, earlier=len(earlier)),
        grid=(number // group,),
        in_specs=[
            SMEM, win((group, ROWS, 3 * D)), whole((D, 3 * D)), win((group, SLOTS, D)),
            win((group, ROWS, D)), whole((8, D)), *before,
        ],
        out_specs=[win((group, SLOTS, D)), whole((2, D))],
        out_shape=[shape_of((count, SLOTS, D), F32), shape_of((2, D), F32)],
        scratch_shapes=[pltpu.VMEM((ROWS, D), F32)],
        input_output_aliases={6: 0} if earlier else {},
        compiler_params=params(),
        cost_estimate=cost(number * 2e9, 25e6),
        name="input_back",
    )(me, dqkv, weight, tokens, grad_hidden, vec, *earlier)


def pick(left, right):
    return jnp.dot(left, right, preferred_element_type=F32, precision=lax.Precision.HIGHEST)


def pack_kernel(me_ref, one_ref, qv_ref, two_ref, up_ref, rel_ref, out_ref):
    vectors = jnp.concatenate(
        [one_ref[0:2], qv_ref[0:2], two_ref[4:5], two_ref[2:4], two_ref[1:2]], axis=0
    )
    error = jnp.sum(two_ref[0:1, :], axis=1, keepdims=True)
    tables = rel_ref[0:64, 0:64] + rel_ref[64:128, 64:128]
    row = lax.broadcasted_iota(jnp.int32, (D, 128), 0)
    col = lax.broadcasted_iota(jnp.int32, (D, 128), 1)
    small_row = lax.broadcasted_iota(jnp.int32, (64, 128), 0)
    small_col = lax.broadcasted_iota(jnp.int32, (64, 128), 1)
    for at in range(8):
        owner = me_ref[1] ^ ((at % 4) * 2 + at // 4)
        own = pick(vectors, ((col < 96) & (row == col + owner * 96)).astype(F32))
        total = jnp.concatenate([own, jnp.zeros((24, 128), F32)], axis=0)
        for which in range(2):
            lane = small_col - 96 - 8 * which
            put = ((lane >= 0) & (lane < 8) & (small_row == lane + owner * 8)).astype(F32)
            total = total + pick(tables[32 * which : 32 * which + 32], put)
        out_ref[at] = total
        for part in range(3):
            lanes = pl.ds(pl.multiple_of(owner * 384 + part * 128, 128), 128)
            out_ref[at, 27 + part : 28 + part, :] = up_ref[:, lanes]
        out_ref[at, 30:31, :] = jnp.broadcast_to(error, (1, 128))


def pack(me, *sums):
    return pl.pallas_call(
        pack_kernel,
        grid=(1,),
        in_specs=[SMEM] + [whole(v.shape) for v in sums],
        out_specs=whole((8, 32, 128)),
        out_shape=shape_of((8, 32, 128), F32),
        compiler_params=params(),
        cost_estimate=cost(1e9, 1e6),
        name="pack",
    )(me, *sums)


def shard_kernel(me_ref, *refs, split):
    quarters, outs = refs[0:4], refs[4:]
    core, far_x = me_ref[0] % 2, me_ref[0] // 2
    for at, ref in enumerate(quarters):
        this_core, this_x = core ^ (at // 2), far_x ^ (at % 2)
        rows = pl.ds(pl.multiple_of(this_x * 48, 16), 48)
        if not split:
            cols = pl.ds(pl.multiple_of(this_core * QKV_HALF, 128), QKV_HALF)
            outs[0][rows, cols] = ref[...].astype(F32)
            continue
        up_ref, down_ref, proj_ref = outs
        for block in range(2):
            cols = pl.ds(pl.multiple_of(this_core * 1536 + block * D, 128), D)
            up_ref[rows, cols] = ref[block].astype(F32)
            at_row = this_core * 192 + this_x * 96 + block * 48
            down_ref[pl.ds(pl.multiple_of(at_row, 16), 48), :] = ref[2 + block].astype(F32)
        cols = pl.ds(pl.multiple_of(this_core * 384, 128), 384)
        proj_ref[rows, cols] = ref[4, :, 0:384].astype(F32)


def shard(me, quarters, split):
    shapes = [(96, MLP), (384, D), (96, D)] if split else [(96, 3 * D)]
    return pl.pallas_call(
        functools.partial(shard_kernel, split=split),
        grid=(1,),
        in_specs=[SMEM] + [whole(v.shape) for v in quarters],
        out_specs=[whole(s) for s in shapes],
        out_shape=[shape_of(s, F32) for s in shapes],
        compiler_params=params(),
        cost_estimate=cost(1e9, 5e6),
        name="shard",
    )(me, *quarters)


def column_blocks(rows):
    return pl.BlockSpec((rows, D), lambda step: (0, step))


def weight_grad(left, right, by_rows=False):
    rows = left.shape[0]
    blocks = (left if by_rows else right).shape[1] // D
    moving, still = column_blocks(rows), whole((rows, D))
    return pl.pallas_call(
        weight_grad_kernel,
        grid=(blocks,),
        in_specs=[moving, still] if by_rows else [still, moving],
        out_specs=pl.BlockSpec((D, D), (lambda s: (s, 0)) if by_rows else (lambda s: (0, s))),
        out_shape=shape_of((left.shape[1], right.shape[1]), BF16),
        compiler_params=params(),
        name="weight_grad",
    )(left, right)


def qkv_grad(me, left, right):
    rows = left.shape[0]
    return pl.pallas_call(
        qkv_grad_kernel,
        grid=(3,),
        in_specs=[SMEM, whole((rows, D)), column_blocks(rows)],
        out_specs=[ANY] * 2,
        out_shape=[shape_of((16, 48, QKV_HALF), BF16)] * 2,
        scratch_shapes=[pltpu.VMEM((D, 3 * D), BF16), pltpu.SemaphoreType.DMA((2,))],
        compiler_params=params(),
        cost_estimate=cost(12e9, 18e6),
        name="qkv_grad",
    )(me, left, right)


def up_grad(me, left, right):
    rows = left.shape[0]
    return pl.pallas_call(
        up_grad_kernel,
        grid=(4,),
        in_specs=[SMEM, whole((rows, D)), column_blocks(rows)],
        out_specs=[ANY] * 2,
        out_shape=[shape_of((16, 2, 48, D), BF16)] * 2,
        scratch_shapes=[pltpu.VMEM((4, D, D), BF16), pltpu.SemaphoreType.DMA((2,))],
        compiler_params=params(),
        cost_estimate=cost(14e9, 18e6),
        name="up_grad",
    )(me, left, right)


def down_grad(me, act, grad_down, mixed, grad_attn):
    rows = act.shape[0]
    return pl.pallas_call(
        down_grad_kernel,
        grid=(5,),
        in_specs=[
            SMEM, pl.BlockSpec((rows, D), lambda step: (0, jnp.minimum(step, 3))),
            whole((rows, D)), whole((rows, D)), whole((rows, D)),
        ],
        out_specs=[ANY] * 2,
        out_shape=[shape_of((16, 3, 48, D), BF16)] * 2,
        scratch_shapes=[
            pltpu.VMEM((4, 16, 48, D), BF16), pltpu.VMEM((2, D, 384), BF16),
            pltpu.SemaphoreType.DMA((2,)),
        ],
        compiler_params=params(),
        cost_estimate=cost(18e9, 22e6),
        name="down_grad",
    )(me, act, grad_down, mixed, grad_attn)


def swap(values, axis, mask):
    size = lax.axis_size(axis)
    return lax.ppermute(values, axis, [(at, at ^ mask) for at in range(size)])


def joined(stack, axis, mask):
    return jnp.concatenate([stack, swap(stack, axis, mask)], axis=0)


def added(one, two):
    return (one.astype(F32) + two.astype(F32)).astype(BF16)


def tied(*values):
    return lax.optimization_barrier(values)


def cut(values, row, col, rows, cols):
    return lax.dynamic_slice(values, (row, col), (rows, cols))


def body(
    tokens, teacher, valid_mask, attn_gain, attn_shift, qkv_weight, query_bias, value_bias,
    rel_pos_h, rel_pos_w, proj_weight, proj_bias, mlp_gain, mlp_shift, up_weight, up_bias,
    down_weight, down_bias,
):
    count = tokens.shape[0]
    parts = lax.axis_size("fsdp")
    copies = lax.axis_size("rep")
    in_pieces = (copies, parts) == (4, 8)
    rep_at, part_at = lax.axis_index("rep"), lax.axis_index("fsdp")
    device = rep_at * parts + part_at
    core, far_x = rep_at % 2, rep_at // 2
    me = jnp.stack([rep_at, part_at, device * count]).astype(jnp.int32)
    window_ids = device * count + jnp.arange(count, dtype=jnp.int32)
    place = window_ids % (SIDE * SIDE)
    cells = jnp.arange(SLOTS, dtype=jnp.int32)
    inside = ((place // SIDE)[:, None] * WIN + (cells // WIN)[None, :] < MAP) & (
        (place % SIDE)[:, None] * WIN + (cells % WIN)[None, :] < MAP
    )
    keep = inside.astype(F32)
    valid = valid_mask.astype(F32) * keep
    counted = jnp.sum(valid_mask * inside.astype(jnp.int32))
    aux = jnp.pad(jnp.stack([keep, valid], axis=-1), ((0, 0), (0, ROWS - SLOTS), (0, 0)))

    small = [attn_gain, attn_shift, query_bias, value_bias, proj_bias, mlp_gain, mlp_shift,
             down_bias, up_bias, rel_pos_h, rel_pos_w]
    places = jnp.asarray(key_places(), BF16)
    places_t = jnp.asarray(np.pad(key_places().T[0:32], ((0, 0), (0, LANES - ROWS))), BF16)
    counted = jnp.stack([counted // 128, counted % 128]).astype(BF16)
    loss_scale = 64.0 * D * count * copies * parts

    def noted(shape, *entries):
        total = jnp.zeros(shape, BF16)
        for values, row, col in entries:
            if values.ndim == 1:
                values = values[None]
            high, wide = values.shape
            total = total + jnp.pad(
                values, ((row, shape[0] - row - high), (col, shape[1] - col - wide))
            )
        return total

    if in_pieces:
        rect = cut(qkv_weight, far_x * 48, core * QKV_HALF, 48, QKV_HALF)
        notes = noted(
            (48, NOTES), *[(v, at, 0) for at, v in enumerate(small[0:4])],
            (rel_pos_h, 16, 0), (rel_pos_w, 16, 8),
        )
        rect = jnp.concatenate([rect, notes], axis=1)
        near = [rect] + [swap(rect, "fsdp", mask) for mask in (2, 4, 6)]
        up_rect = cut(up_weight, far_x * 48, core * 1536, 48, 1536)
        down_rect = cut(down_weight, core * 192 + far_x * 96, 0, 96, D)
        proj_rect = cut(proj_weight, far_x * 48, core * 384, 48, 384)
        notes = noted(
            (48, 384), *[(v, at, 0) for at, v in enumerate(small[4:8])], (up_bias, 4, 0),
            (counted, 5, 0),
        )
        rects = jnp.concatenate(
            [up_rect.reshape(48, 2, D).transpose(1, 0, 2), down_rect.reshape(2, 48, D),
             jnp.concatenate([proj_rect, notes], axis=1)[None]], axis=0,
        )
        *near, rects, aux = tied(*near, rects, aux)
        near_a, near_b = jnp.stack(near[0:2]), jnp.stack(near[2:4])
        from_a, from_b = swap(near_a, "fsdp", 1), swap(near_b, "rep", 2)
        planes = [rects] + [swap(rects, "fsdp", mask) for mask in (2, 4, 6)]
        near_a = jnp.concatenate([near_a, from_a])
        near_b = jnp.concatenate([near_b, from_b])
        far_a, far_b = swap(near_a, "rep", 2), swap(near_b, "fsdp", 1)
        own = (near_a, far_a, near_b, far_b)
        own = tied(*own)
        other = tuple(swap(v, "rep", 1) for v in own)
        vec, rel, rel_t = notes_of(me, own[0], own[2], own[3])
        vec, rel, rel_t, *other = tied(vec, rel, rel_t, *other)
        *state, w_qkv = attend(me, tokens, own + tuple(other), vec, rel, places, 0, STEPS[0])
        *planes, s0 = tied(*planes, state[0])
        state[0] = s0
        near_a, near_b = jnp.stack(planes[0:2]), jnp.stack(planes[2:4])
        near_a, near_b, *state = tied(near_a, near_b, *state)
        from_a, from_b = swap(near_a, "fsdp", 1), swap(near_b, "rep", 2)
        state = attend(me, tokens, w_qkv, vec, rel, places, STEPS[0], STEPS[1], tuple(state))
        from_a, from_b, *state = tied(from_a, from_b, *state)
        near_a = jnp.concatenate([near_a, from_a])
        near_b = jnp.concatenate([near_b, from_b])
        near_a, near_b, *state = tied(near_a, near_b, *state)
        far_a, far_b = swap(near_a, "rep", 2), swap(near_b, "fsdp", 1)
        core_a, core_b = swap(near_a, "rep", 1), swap(near_b, "rep", 1)
        state = attend(
            me, tokens, w_qkv, vec, rel, places, sum(STEPS[:2]), STEPS[2], tuple(state)
        )
        far_a, far_b, core_a, core_b, *state = tied(far_a, far_b, core_a, core_b, *state)
        own = (near_a, far_a, near_b, far_b)
        other = (core_a, swap(far_a, "rep", 1), core_b, swap(far_b, "rep", 1))
        state = attend(
            me, tokens, w_qkv, vec, rel, places, sum(STEPS[:3]), STEPS[3], tuple(state)
        )
        weights = own + other
    else:
        gather = lambda v: lax.all_gather(v, "fsdp", axis=0, tiled=True)
        w_qkv, w_proj = gather(qkv_weight), gather(proj_weight)
        packed = gather(jnp.concatenate([v.reshape(-1) for v in small] + [counted])[None])
        pieces, at = [], 0
        for v in small:
            pieces.append(packed[:, at : at + v.size])
            at += v.size
        rows = [p.reshape(1, -1).astype(F32) for p in pieces[:9]]
        offsets = rel_pos_h.shape[0]
        tables = [
            p.reshape(parts, offsets, -1).transpose(1, 0, 2).reshape(offsets, HEAD_DIM)
            for p in pieces[9:]
        ]
        gap = jnp.zeros((32 - offsets, HEAD_DIM), BF16)
        table = jnp.concatenate([tables[0], gap, tables[1], gap], axis=0)
        hole = jnp.zeros((HEAD_DIM, HEAD_DIM), BF16)
        rel = jnp.concatenate(
            [jnp.concatenate([table, hole], axis=1), jnp.concatenate([hole, table], axis=1)],
            axis=0,
        )
        rel_t = rel.T
        fill = jnp.zeros((4, D), F32)
        vec = jnp.concatenate(rows[0:4] + [fill])
        counts = lax.psum(jnp.sum(valid), ("rep", "fsdp")).reshape(1, 1)
        weights = (w_proj, gather(up_weight), gather(down_weight),
                   jnp.concatenate(rows[4:8] + [fill]), rows[8], counts)
        state = attend(me, tokens, w_qkv, vec, rel, places, 0, count)
    qkv, probs, mixed, first_in = state
    out, grad_hidden, grad_attn, second_in, act, grad_down, grad_up, sums2, up_sum, *rest = mlp(
        me, tokens, mixed, teacher, aux, weights, loss_scale * 2.0 / D, in_pieces
    )
    valid_total = sums2[5, 0]
    w_proj = rest[0] if in_pieces else w_proj
    flat = lambda v: v.reshape(count * ROWS, v.shape[-1])
    if in_pieces:
        keep_d, send_d = down_grad(me, flat(act), flat(grad_down), flat(mixed), flat(grad_attn))
        send_d, second_in = tied(send_d, second_in)
        from_d = swap(send_d, "rep", 1)
        keep_u, send_u = up_grad(me, flat(second_in), flat(grad_up))
        from_d, keep_u, send_u, grad_attn = tied(from_d, keep_u, send_u, grad_attn)
        from_u = swap(send_u, "rep", 1)
        back = (grad_attn, w_proj, qkv, probs, rel_t, places_t)
        ends = (0,) + tuple(sum(BACK_STEPS[: at + 1]) for at in range(3))
        state = attend_back(*back, 0, BACK_STEPS[0])
        both = lambda at, to: jnp.concatenate(
            [added(keep_u[at:to], from_u[at:to]), added(keep_d[at:to], from_d[at:to])], axis=1
        )
        from_u, *state = tied(from_u, *state)
        send_a, send_b = both(4, 8), both(12, 16)
        send_a, send_b, *state = tied(send_a, send_b, *state)
        from_a, from_b = swap(send_a, "rep", 2), swap(send_b, "fsdp", 1)
        state = attend_back(*back, ends[1], BACK_STEPS[1], tuple(state))
        from_a, from_b, *state = tied(from_a, from_b, *state)
        sum_a, sum_b = added(both(0, 4), from_a), added(both(8, 12), from_b)
        send_a, send_b = sum_a[2:4], sum_b[2:4]
        send_a, send_b, *state = tied(send_a, send_b, *state)
        from_a, from_b = swap(send_a, "fsdp", 1), swap(send_b, "rep", 2)
        state = attend_back(*back, ends[2], BACK_STEPS[2], tuple(state))
        from_a, from_b, *state = tied(from_a, from_b, *state)
        sum_a, sum_b = added(sum_a[0:2], from_a), added(sum_b[0:2], from_b)
        sends = (sum_a[0], sum_a[1], sum_b[0], sum_b[1])
        *sends, dqkv, rel_grad, qv_sum = tied(*sends, *state)
        from_z = [swap(v, "fsdp", mask) for v, mask in zip(sends[1:], (2, 4, 6))]
        keep, send = qkv_grad(me, flat(first_in), flat(dqkv))
        half = count // 2
        keep, send, dqkv = tied(keep, send, dqkv)
        from_core = swap(send, "rep", 1)
        state = input_back(me, dqkv, w_qkv, tokens, grad_hidden, vec, 0, half)
        from_core, *state = tied(from_core, *state)
        both = lambda at, to: added(keep[at:to], from_core[at:to])
        send_a, send_b = both(4, 8), both(12, 16)
        send_a, send_b, *state = tied(send_a, send_b, *state)
        from_a, from_b = swap(send_a, "rep", 2), swap(send_b, "fsdp", 1)
        input_grad, sums1 = input_back(
            me, dqkv, w_qkv, tokens, grad_hidden, vec, half, count - half, tuple(state)
        )
        *from_z, from_a, from_b, sums1 = tied(*from_z, from_a, from_b, sums1)
        sum_a, sum_b = added(both(0, 4), from_a), added(both(8, 12), from_b)
        from_a, from_b = swap(sum_a[2:4], "fsdp", 1), swap(sum_b[2:4], "rep", 2)
        own = sends[0].astype(F32)
        for v in from_z:
            own = own + v.astype(F32)
        own = own.astype(BF16)
        from_x = swap(own, "rep", 2)
        notes = pack(me, sums1, qv_sum, sums2, up_sum, rel_grad)
        from_a, from_b, notes = tied(from_a, from_b, notes)
        sum_a, sum_b = added(sum_a[0:2], from_a), added(sum_b[0:2], from_b)
        from_z = [swap(v, "fsdp", mask) for v, mask in
                  ((sum_a[1], 2), (sum_b[0], 4), (sum_b[1], 6))]
        notes = notes + swap(notes, "rep", 1)
        notes = notes + swap(notes, "rep", 2)
        notes = notes[0:4] + swap(notes[4:8], "fsdp", 1)
        d_up, d_down, d_proj = shard(
            me, (own, from_x, swap(own, "rep", 1), swap(from_x, "rep", 1)), True
        )
        mine = notes[0]
        for at, mask in ((1, 2), (2, 4), (3, 6)):
            mine = mine + swap(notes[at], "fsdp", mask)
        own = sum_a[0].astype(F32)
        for v in from_z:
            own = own + v.astype(F32)
        own = own.astype(BF16)
        from_x = swap(own, "rep", 2)
        (d_qkv,) = shard(
            me, (own, from_x, swap(own, "rep", 1), swap(from_x, "rep", 1)), False
        )
        lanes = tokens.shape[2] // parts
        vectors = [mine[at, 0:lanes] for at in range(8)]
        tables = [mine[0:27, 96 + 8 * at : 104 + 8 * at] for at in range(2)]
        outs = vectors + [mine[27:30].reshape(-1)] + tables
        loss = mine[30, 0] / (valid_total * D)
    else:
        scatter = lambda v: lax.psum(
            lax.psum_scatter(v, "fsdp", scatter_dimension=0, tiled=True), "rep"
        ).astype(F32)
        d_down = scatter(weight_grad(flat(act), flat(grad_down), True))
        d_up = scatter(weight_grad(flat(second_in), flat(grad_up)))
        d_proj = scatter(weight_grad(flat(mixed), flat(grad_attn)))
        back = (grad_attn, w_proj, qkv, probs, rel_t, places_t)
        dqkv, rel_grad, qv_sum = attend_back(*back, 0, count)
        d_qkv = scatter(weight_grad(flat(first_in), flat(dqkv)))
        input_grad, sums1 = input_back(me, dqkv, w_qkv, tokens, grad_hidden, vec, 0, count)
        offsets = rel_pos_h.shape[0]
        rel_sum = rel_grad[0:64, 0:64] + rel_grad[64:128, 64:128]
        vectors = [sums1[0], sums1[1], qv_sum[0], qv_sum[1], sums2[4], sums2[2], sums2[3],
                   sums2[1], up_sum[0]]
        own = jnp.concatenate(
            [v.reshape(parts, -1) for v in vectors]
            + [
                rel_sum[at : at + offsets].reshape(offsets, parts, -1).transpose(1, 0, 2)
                .reshape(parts, -1) for at in (0, 32)
            ]
            + [jnp.broadcast_to(jnp.sum(sums2[0]), (parts, 1))],
            axis=1,
        )
        mine = lax.dynamic_index_in_dim(
            lax.psum(own, ("rep", "fsdp")), part_at, 0, keepdims=False
        )
        outs, at = [], 0
        for v in small:
            outs.append(mine[at : at + v.size].reshape(v.shape))
            at += v.size
        loss = mine[at] / (valid_total * D)
    (g_gain1, g_shift1, g_qb, g_vb, g_pb, g_gain2, g_shift2, g_db, g_ub, g_rh, g_rw) = outs
    return (
        out, loss, input_grad, g_gain1, g_shift1, d_qkv, g_qb, g_vb, g_rh, g_rw, d_proj, g_pb,
        g_gain2, g_shift2, d_up, g_ub, d_down, g_db,
    )


def solution(mesh):
    windows = P(("rep", "fsdp"), None, None)
    vector = P("fsdp")
    matrix = P("fsdp", None)
    table = P(None, "fsdp")
    in_specs = (
        windows, windows, P(("rep", "fsdp"), None), vector, vector, matrix, vector, vector, table,
        table, matrix, vector, vector, vector, matrix, vector, matrix, vector,
    )
    out_specs = (windows, P(), windows) + in_specs[3:]
    return jax.shard_map(body, mesh=mesh, in_specs=in_specs, out_specs=out_specs, check_vma=False)
```

time: 814 us -> 457 us (0.56); the launches traced: 814 us -> 448 us
  waiting for transfers between devices: 395 us -> 62.3 us
  blocking collectives: 121 us -> 0 us
  Pallas kernels: 187 us -> 270 us
  starting transfers between devices: 0.36 us -> 56.3 us
  matrix products: 42.7 us -> 0 us
  other arithmetic: 10.5 us -> 23.3 us
  between operations: 17.3 us -> 6.73 us
  local copies, waits for them, and re-layouts: 39.8 us -> 29.4 us
    reduce_scatter x4 -> x0, waiting for transfers between devices: 278 us -> none  [body(): lax.psum_scatter(v.astype(BF16), 'fsdp', scatter_dimension=0, tiled=True)]
    all_gather x4 -> x0, waiting for transfers between devices: 114 us -> none  [body(): gather = lambda v: lax.all_gather(v, 'fsdp', axis=0, tiled=True)]
    psum x2 -> x0, blocking collectives: 83.7 us -> none  [the longest x1 42.4 us: body(): valid_total = lax.psum(jnp.sum(valid), ('rep', 'fsdp'))]
    pallas_call x4 -> x17, Pallas kernels: 187 us -> 270 us  [the longest x1 79.1 us: mlp(): pl.pallas_call(functools.partial(mlp_kernel, group=group, pieces=pieces,...]
    ppermute x0 -> x51, waiting for transfers between devices: none -> 62.3 us  [swap(): return lax.ppermute(values, axis, [(at, at ^ mask) for at in range(size)])]
    ppermute x0 -> x51, starting transfers between devices: none -> 56.3 us  [swap(): return lax.ppermute(values, axis, [(at, at ^ mask) for at in range(size)])]
    dot_general x4 -> x0, matrix products: 42.7 us -> none  [tn(): lax.dot_general(left, right, (((0,), (0,)), ((), ())), preferred_element_...]
    unnamed x1 -> x0, blocking collectives: 37.6 us -> none
  transfers between devices with their start and end apart: 9 -> 51, of which waited for: 6 -> 20; matrix products, arithmetic and copies ran while one was open for 10% -> 6% of each run, Pallas kernels for 8% -> 35%
where the time goes in v2:
time: 457 us; the launch traced here: 448 us
  Pallas kernels  270 us (59%)
  waiting for transfers between devices  62.3 us (14%)
  starting transfers between devices  56.3 us (12%)
  local copies, waits for them, and re-layouts  29.4 us (6%)
  other arithmetic  23.3 us (5%)
  between operations  6.73 us (1%)
    pallas_call x1, Pallas kernels, mlp(): pl.pallas_call(functools.partial(mlp_kernel, group=group, pieces=pieces,...  79.1 us
    ppermute x51, waiting for transfers between devices, swap(): return lax.ppermute(values, axis, [(at, at ^ mask) for at in range(size)])  62.3 us
    pallas_call x4, Pallas kernels, attend(): pl.pallas_call(functools.partial(attend_kernel, first=first, pieces=piece...  59.6 us
    ppermute x51, starting transfers between devices, swap(): return lax.ppermute(values, axis, [(at, at ^ mask) for at in range(size)])  56.3 us
    pallas_call x3, Pallas kernels, attend_back(): pl.pallas_call(functools.partial(attend_back_kernel, earlier=len(earlier)...  52.3 us
    pallas_call x1, Pallas kernels, down_grad(): pl.pallas_call(down_grad_kernel, grid=(5,), in_specs=[SMEM, pl.BlockSpec(...  22.1 us
    pallas_call x2, Pallas kernels, input_back(): pl.pallas_call(functools.partial(input_kernel, group=group, first=first,...  20 us
    unnamed x80, local copies, waits for them, and re-layouts  18.1 us
  transfers between devices with their start and end apart: 51, of which 20 were waited for; matrix products, arithmetic and copies ran while one was open for 6% of the time, Pallas kernels for 35%

profile of v2, /device:TPU:0, one launch (start us, length us, event | category | flops | bytes accessed | tf_op | source)
XLA Modules:
  0.0 448.2 jit_solution(12025894873546715577)
XLA Ops:
  4.0 5.1 %collective-permute-start.2 = (bf16[48,1280]{1,0:T(8,128)(2,1)S(1)}, bf16[48,1280]{1,0:T(8,128)(2,1)S(1)}, u32[]{:S(2)}, u32[]{:S(2)}) collective-permute-start(bf16[48,1280]{1,0:T(8,128)(2,1)S(1)} %pad_maximum_fusion.11), channel_id=1, source_target_pairs={{0,6},{1,7},{2,4},{3,5},{4,2},{5,3},{6,0},{7,1},{8,14},{9,15},{10,... | collective-permute-start | bytes 368648 | tf_op jit(solution)/shard_map/ppermute | solution.py:912
  22.7 3.9 collective-permute-done.3
  29.9 8.6 %collective-permute-done.4.refs_3_ = bf16[4,48,1280]{2,1,0:T(8,128)(2,1)S(1)} collective-permute-done((bf16[4,48,1280]{2,1,0:T(8,128)(2,1)S(1)}, bf16[4,48,1280]{2,1,0:T(8,128)(2,1)S(1)}, u32[]{:S(2)}, u32[]{:S(2)}) %collective-permute-start.4) | collective-permute-done | bytes 491552 | tf_op jit(solution)/shard_map/ppermute | solution.py:912
  43.0 3.2 collective-permute-start.13
  46.3 2.4 notes.1
  49.8 10.8 %attend.4 = (bf16[8,208,2304]{2,1,0:T(8,128)(2,1)}, bf16[8,12,208,256]{3,2,1,0:T(8,128)(2,1)}, bf16[8,208,768]{2,1,0:T(8,128)(2,1)}, bf16[8,208,768]{2,1,0:T(8,128)(2,1)}, bf16[768,2304]{1,0:T(8,128)(2,1)}) custom-call(s32[3]{0:T(128)} %pad_add_fusion.1.me_ref.refs_0_.base_ref, bf16[8,196,768]{2,1,0:T(8,128)(2,1)} %copy.91.refs_1_.tok_ref, ...), custom_call_target="tpu_custom_call" | custom-call | flops 6000000000 | bytes 2000000 | tf_op jit(solution)/shard_map/attend/pallas_call | solution.py:666
  60.6 17.5 %collective-permute-done.12 = bf16[5,48,768]{2,1,0:T(8,128)(2,1)S(1)} collective-permute-done((bf16[5,48,768]{2,1,0:T(8,128)(2,1)S(1)}, bf16[5,48,768]{2,1,0:T(8,128)(2,1)S(1)}, u32[]{:S(2)}, u32[]{:S(2)}) %collective-permute-start.12) | collective-permute-done | bytes 368672 | tf_op jit(solution)/shard_map/ppermute | solution.py:912
  80.4 14.7 %attend.5 = (bf16[8,208,2304]{2,1,0:T(8,128)(2,1)}, bf16[8,12,208,256]{3,2,1,0:T(8,128)(2,1)}, bf16[8,208,768]{2,1,0:T(8,128)(2,1)}, bf16[8,208,768]{2,1,0:T(8,128)(2,1)}) custom-call(s32[3]{0:T(128)} %pad_add_fusion.1.me_ref.refs_0_.base_ref, ...), custom_call_target="tpu_custom_call", output_to_operand_aliasing={{0}: (6, {}), {1}: (7, {}), {2}: (8, {}), {3}: (9, {})} | custom-call | flops 12000000000 | bytes 4000000 | tf_op jit(solution)/shard_map/attend/pallas_call | solution.py:666
  102.4 25.7 %attend.6 = (bf16[8,208,2304]{2,1,0:T(8,128)(2,1)}, bf16[8,12,208,256]{3,2,1,0:T(8,128)(2,1)}, bf16[8,208,768]{2,1,0:T(8,128)(2,1)}, bf16[8,208,768]{2,1,0:T(8,128)(2,1)}) custom-call(s32[3]{0:T(128)} %pad_add_fusion.1.me_ref.refs_0_.base_ref, ...), custom_call_target="tpu_custom_call", output_to_operand_aliasing={{0}: (6, {}), {1}: (7, {}), {2}: (8, {}), {3}: (9, {})} | custom-call | flops 24000000000 | bytes 8000000 | tf_op jit(solution)/shard_map/attend/pallas_call | solution.py:666
  128.1 7.2 %collective-permute-done.16.refs_6_ = bf16[4,5,48,768]{3,2,1,0:T(8,128)(2,1)} collective-permute-done((bf16[4,5,48,768]{3,2,1,0:T(8,128)(2,1)S(1)}, bf16[4,5,48,768]{3,2,1,0:T(8,128)(2,1)}, u32[]{:S(2)}, u32[]{:S(2)}) %collective-permute-start.16) | collective-permute-done | bytes 1474592 | tf_op jit(solution)/shard_map/ppermute | solution.py:912
  136.5 2.0 copy.92.refs_3_
  138.5 8.5 %attend.7 = (bf16[8,208,2304]{2,1,0:T(8,128)(2,1)}, bf16[8,12,208,256]{3,2,1,0:T(8,128)(2,1)}, bf16[8,208,768]{2,1,0:T(8,128)(2,1)}, bf16[8,208,768]{2,1,0:T(8,128)(2,1)}) custom-call(s32[3]{0:T(128)} %pad_add_fusion.1.me_ref.refs_0_.base_ref, ...), custom_call_target="tpu_custom_call", output_to_operand_aliasing={{0}: (6, {}), {1}: (7, {}), {2}: (8, {}), {3}: (9, {})} | custom-call | flops 6000000000 | bytes 2000000 | tf_op jit(solution)/shard_map/attend/pallas_call | solution.py:666
  148.2 79.1 %mlp.1 = (bf16[8,196,768]{2,1,0:T(8,128)(2,1)}, f32[8,208,768]{2,1,0:T(8,128)}, bf16[8,208,768]{2,1,0:T(8,128)(2,1)}, bf16[8,208,768]{2,1,0:T(8,128)(2,1)}, bf16...) custom-call(s32[3]{0:T(128)} %pad_add_fusion.1.me_ref.refs_0_.base_r, ...), custom_call_target="tpu_custom_call" | custom-call | flops 64000000000 | bytes 60000000 | tf_op jit(solution)/shard_map/mlp/pallas_call | solution.py:705
  227.3 22.1 %down_grad.1 = (bf16[16,3,48,768]{3,2,1,0:T(8,128)(2,1)}, bf16[16,3,48,768]{3,2,1,0:T(8,128)(2,1)}) custom-call(s32[3]{0:T(128)} %pad_add_fusion.1.me_ref.refs_0_.base_ref, bf16[1664,3072]{1,0:T(8,128)(2,1)} %bitcast.121, bf16[1664,768]{1,0:T(8,128)(2,1)} %bitcast.125, bf16[1664,768]{1,0:T(8,128)(2,1)} %bitcast.95, bf16[1664,768]{1,0:T(8,128)(2,1)} %bitcast.123), custom_call_target="tpu_custom_call" | custom-call | flops 17999998976 | bytes 22000000 | tf_op jit(solution)/shard_map/down_grad/pallas_call | solution.py:891
  249.5 14.9 %up_grad.1 = (bf16[16,2,48,768]{3,2,1,0:T(8,128)(2,1)}, bf16[16,2,48,768]{3,2,1,0:T(8,128)(2,1)}) custom-call(s32[3]{0:T(128)} %pad_add_fusion.1.me_ref.refs_0_.base_ref, bf16[1664,768]{1,0:T(8,128)(2,1)} %bitcast.124, bf16[1664,3072]{1,0:T(8,128)(2,1)} %bitcast.120), custom_call_target="tpu_custom_call" | custom-call | flops 14000000000 | bytes 18000000 | tf_op jit(solution)/shard_map/up_grad/pallas_call | solution.py:876
  264.9 4.3 add_convert_fusion.2
  269.3 8.4 %attend_back.3 = (bf16[8,208,2304]{2,1,0:T(8,128)(2,1)}, f32[128,128]{1,0:T(8,128)}, f32[2,768]{1,0:T(2,128)}) custom-call(bf16[8,208,768]{2,1,0:T(8,128)(2,1)} %get-tuple-element.252.refs_0_, bf16[768,768]{1,0:T(8,128)(2,1)} %get-tuple-element.253.refs_1_, bf16[8,208,2304]{2,1,0:T(8,128)(2,1)} %get-tuple-element.254.refs_2_, ...), custom_call_target="tpu_custom_call" | custom-call | flops 6000000000 | bytes 2000000 | tf_op jit(solution)/shard_map/attend_back/pallas_call | solution.py:722
  277.7 2.3 add_convert_fusion.8
  284.7 29.9 %attend_back.4 = (bf16[8,208,2304]{2,1,0:T(8,128)(2,1)}, f32[128,128]{1,0:T(8,128)}, f32[2,768]{1,0:T(2,128)}) custom-call(bf16[8,208,768]{2,1,0:T(8,128)(2,1)} %get-tuple-element.252.refs_0_, bf16[768,768]{1,0:T(8,128)(2,1)} %get-tuple-element.253.refs_1_, bf16[8,208,2304]{2,1,0:T(8,128)(2,1)} %get-tuple-element.254.refs_2_, ...), custom_call_target="tpu_custom_call", output_to_operand_aliasing={{0}: (6, {})} | custom-call | flops 30000001024 | bytes 10000000 | tf_op jit(solution)/shard_map/attend_back/pallas_call | solution.py:722
  314.6 2.5 collective-permute-done.24
  324.9 13.9 %attend_back.5 = (bf16[8,208,2304]{2,1,0:T(8,128)(2,1)}, f32[128,128]{1,0:T(8,128)}, f32[2,768]{1,0:T(2,128)}) custom-call(bf16[8,208,768]{2,1,0:T(8,128)(2,1)} %get-tuple-element.252.refs_0_, bf16[768,768]{1,0:T(8,128)(2,1)} %get-tuple-element.253.refs_1_, bf16[8,208,2304]{2,1,0:T(8,128)(2,1)} %get-tuple-element.254.refs_2_, ...), custom_call_target="tpu_custom_call", output_to_operand_aliasing={{0}: (6, {})} | custom-call | flops 12000000000 | bytes 4000000 | tf_op jit(solution)/shard_map/attend_back/pallas_call | solution.py:722
  345.1 11.4 %qkv_grad.1 = (bf16[16,48,1152]{2,1,0:T(8,128)(2,1)}, bf16[16,48,1152]{2,1,0:T(8,128)(2,1)}) custom-call(s32[3]{0:T(128)} %pad_add_fusion.1.me_ref.refs_0_.base_ref, bf16[1664,768]{1,0:T(8,128)(2,1)} %bitcast.96, bf16[1664,2304]{1,0:T(8,128)(2,1)} %bitcast.122), custom_call_target="tpu_custom_call" | custom-call | flops 12000000000 | bytes 18000000 | tf_op jit(solution)/shard_map/qkv_grad/pallas_call | solution.py:861
  356.6 2.9 collective-permute-start.30
  361.0 9.9 %input_back.2 = (f32[8,196,768]{2,1,0:T(8,128)}, f32[2,768]{1,0:T(2,128)}) custom-call(s32[3]{0:T(128)} %pad_add_fusion.1.me_ref.refs_0_.base_ref, bf16[8,208,2304]{2,1,0:T(8,128)(2,1)} %get-tuple-element.297.dqkv_ref, bf16[768,2304]{1,0:T(8,128)(2,1)} %get-tuple-element.191.refs_2_.w_ref, bf16[8,196,768]{2,1,0:T(8,128)(2,1)} %copy.91.refs_1_.tok_ref, ...), custom_call_target="tpu_custom_call" | custom-call | flops 8000000000 | bytes 25000000 | tf_op jit(solution)/shard_map/input_back/pallas_call | solution.py:747
  374.3 10.0 %input_back.3 = (f32[8,196,768]{2,1,0:T(8,128)}, f32[2,768]{1,0:T(2,128)}) custom-call(s32[3]{0:T(128)} %pad_add_fusion.1.me_ref.refs_0_.base_ref, bf16[8,208,2304]{2,1,0:T(8,128)(2,1)} %get-tuple-element.297.dqkv_ref, bf16[768,2304]{1,0:T(8,128)(2,1)} %get-tuple-element.191.refs_2_.w_ref, ...), custom_call_target="tpu_custom_call", output_to_operand_aliasing={{0}: (6, {})} | custom-call | flops 8000000000 | bytes 25000000 | tf_op jit(solution)/shard_map/input_back/pallas_call | solution.py:747
  389.2 3.5 pack.1
  393.9 8.5 %collective-permute-start.42 = (bf16[48,1152]{1,0:T(8,128)(2,1)S(1)}, bf16[48,1152]{1,0:T(8,128)(2,1)S(1)}, u32[]{:S(2)}, u32[]{:S(2)}) collective-permute-start(bf16[48,1152]{1,0:T(8,128)(2,1)S(1)} %slice_bitcast_fusion.6), channel_id=1, source_target_pairs={{0,2},{1,3},{2,0},{3,1},{4,6},{5,7},{6,4},{7,5},{8,10},{9,11},{10,... | collective-permute-start | bytes 331784 | tf_op jit(solution)/shard_map/ppermute | solution.py:912
  408.5 3.8 collective-permute-done.43
  413.9 6.6 %collective-permute-done.37 = f32[8,32,128]{2,1,0:T(8,128)S(1)} collective-permute-done((f32[8,32,128]{2,1,0:T(8,128)S(1)}, f32[8,32,128]{2,1,0:T(8,128)S(1)}, u32[]{:S(2)}, u32[]{:S(2)}) %collective-permute-start.37) | collective-permute-done | bytes 131104 | tf_op jit(solution)/shard_map/ppermute | solution.py:912
  425.6 3.7 copy.96
  434.4 2.0 shard.2
  443.6 3.0 shard.3
  (229 shorter events, 89.0 us)
Async XLA Ops:
  4.0 15.3 %collective-permute-start.2 = (bf16[48,1280]{1,0:T(8,128)(2,1)S(1)}, bf16[48,1280]{1,0:T(8,128)(2,1)S(1)}, u32[]{:S(2)}, u32[]{:S(2)}) collective-permute-start(bf16[48,1280]{1,0:T(8,128)(2,1)S(1)} %pad_maximum_fusion.11), channel_id=1, source_target_pairs={{0,6},{1,7},{2,4},{3,5},{4,2},{5,3},{6,0},{7,1},{8,14},{9,15},{10,... | collective-permute-start | bytes 368648 | tf_op jit(solution)/shard_map/ppermute | solution.py:912
  26.7 11.8 %collective-permute-start.4 = (bf16[4,48,1280]{2,1,0:T(8,128)(2,1)S(1)}, bf16[4,48,1280]{2,1,0:T(8,128)(2,1)S(1)}, u32[]{:S(2)}, u32[]{:S(2)}) collective-permute-start(bf16[4,48,1280]{2,1,0:T(8,128)(2,1)S(1)} %pad_maximum_fusion.6.a_ref.refs_2_), channel_id=1, source_target_pairs={{0,16},{8,24},{16,0},{24,8},{1,17},{9,25},{17,1},{25,9},{2,18},{10... | collective-permute-start | bytes 1474568 | tf_op jit(solution)/shard_map/ppermute | solution.py:912
  28.3 11.1 %collective-permute-start.6 = (bf16[4,48,1280]{2,1,0:T(8,128)(2,1)S(1)}, bf16[4,48,1280]{2,1,0:T(8,128)(2,1)S(1)}, u32[]{:S(2)}, u32[]{:S(2)}) collective-permute-start(bf16[4,48,1280]{2,1,0:T(8,128)(2,1)S(1)} %pad_maximum_fusion.7.b_ref.refs_4_), channel_id=1, source_target_pairs={{0,1},{1,0},{2,3},{3,2},{4,5},{5,4},{6,7},{7,6},{8,9},{9,8},{10,11... | collective-permute-start | bytes 1474568 | tf_op jit(solution)/shard_map/ppermute | solution.py:912
  43.0 17.6 %collective-permute-start.13 = (bf16[5,48,768]{2,1,0:T(8,128)(2,1)S(1)}, bf16[5,48,768]{2,1,0:T(8,128)(2,1)S(1)}, u32[]{:S(2)}, u32[]{:S(2)}) collective-permute-start(bf16[5,48,768]{2,1,0:T(8,128)(2,1)S(1)} %pad_maximum_fusion.8), channel_id=1, source_target_pairs={{0,6},{1,7},{2,4},{3,5},{4,2},{5,3},{6,0},{7,1},{8,14},{9,15},{10,... | collective-permute-start | bytes 1105928 | tf_op jit(solution)/shard_map/ppermute | solution.py:912
  48.6 29.5 %collective-permute-start.12 = (bf16[5,48,768]{2,1,0:T(8,128)(2,1)S(1)}, bf16[5,48,768]{2,1,0:T(8,128)(2,1)S(1)}, u32[]{:S(2)}, u32[]{:S(2)}) collective-permute-start(bf16[5,48,768]{2,1,0:T(8,128)(2,1)S(1)} %pad_maximum_fusion.8), channel_id=1, source_target_pairs={{0,4},{1,5},{2,6},{3,7},{4,0},{5,1},{6,2},{7,3},{8,12},{9,13},{10,... | collective-permute-start | bytes 1105928 | tf_op jit(solution)/shard_map/ppermute | solution.py:912
  48.6 29.5 %collective-permute-start.11 = (bf16[5,48,768]{2,1,0:T(8,128)(2,1)S(1)}, bf16[5,48,768]{2,1,0:T(8,128)(2,1)S(1)}, u32[]{:S(2)}, u32[]{:S(2)}) collective-permute-start(bf16[5,48,768]{2,1,0:T(8,128)(2,1)S(1)} %pad_maximum_fusion.8), channel_id=1, source_target_pairs={{0,2},{1,3},{2,0},{3,1},{4,6},{5,7},{6,4},{7,5},{8,10},{9,11},{10,... | collective-permute-start | bytes 1105928 | tf_op jit(solution)/shard_map/ppermute | solution.py:912
  78.3 17.6 %collective-permute-start.14 = (bf16[2,5,48,768]{3,2,1,0:T(8,128)(2,1)S(1)}, bf16[2,5,48,768]{3,2,1,0:T(8,128)(2,1)S(1)}, u32[]{:S(2)}, u32[]{:S(2)}) collective-permute-start(bf16[2,5,48,768]{3,2,1,0:T(8,128)(2,1)S(1)} %pad_maximum_fusion.4), channel_id=1, source_target_pairs={{0,1},{1,0},{2,3},{3,2},{4,5},{5,4},{6,7},{7,6},{8,9},{9,8},{10,11... | collective-permute-start | bytes 2211848 | tf_op jit(solution)/shard_map/ppermute | solution.py:912
  79.8 17.3 %collective-permute-start.15 = (bf16[2,5,48,768]{3,2,1,0:T(8,128)(2,1)S(1)}, bf16[2,5,48,768]{3,2,1,0:T(8,128)(2,1)S(1)}, u32[]{:S(2)}, u32[]{:S(2)}) collective-permute-start(bf16[2,5,48,768]{3,2,1,0:T(8,128)(2,1)S(1)} %pad_maximum_fusion.5), channel_id=1, source_target_pairs={{0,16},{8,24},{16,0},{24,8},{1,17},{9,25},{17,1},{25,9},{2,18},{10... | collective-permute-start | bytes 2211848 | tf_op jit(solution)/shard_map/ppermute | solution.py:912
  100.5 27.6 %collective-permute-start.18 = (bf16[4,5,48,768]{3,2,1,0:T(8,128)(2,1)S(1)}, bf16[4,5,48,768]{3,2,1,0:T(8,128)(2,1)}, u32[]{:S(2)}, u32[]{:S(2)}) collective-permute-start(bf16[4,5,48,768]{3,2,1,0:T(8,128)(2,1)S(1)} %pad_maximum_fusion.refs_5_), channel_id=1, source_target_pairs={{0,8},{8,0},{16,24},{24,16},{1,9},{9,1},{17,25},{25,17},{2,10},{10... | collective-permute-start | bytes 4423688 | tf_op jit(solution)/shard_map/ppermute | solution.py:912
  100.5 34.8 %collective-permute-start.16 = (bf16[4,5,48,768]{3,2,1,0:T(8,128)(2,1)S(1)}, bf16[4,5,48,768]{3,2,1,0:T(8,128)(2,1)}, u32[]{:S(2)}, u32[]{:S(2)}) collective-permute-start(bf16[4,5,48,768]{3,2,1,0:T(8,128)(2,1)S(1)} %pad_maximum_fusion.refs_5_), channel_id=1, source_target_pairs={{0,16},{8,24},{16,0},{24,8},{1,17},{9,25},{17,1},{25,9},{2,18},{10... | collective-permute-start | bytes 4423688 | tf_op jit(solution)/shard_map/ppermute | solution.py:912
  101.0 34.3 %collective-permute-start.19 = (bf16[4,5,48,768]{3,2,1,0:T(8,128)(2,1)}, bf16[4,5,48,768]{3,2,1,0:T(8,128)(2,1)}, u32[]{:S(2)}, u32[]{:S(2)}) collective-permute-start(bf16[4,5,48,768]{3,2,1,0:T(8,128)(2,1)} %pad_maximum_fusion.1.refs_7_), channel_id=1, source_target_pairs={{0,8},{8,0},{16,24},{24,16},{1,9},{9,1},{17,25},{25,17},{2,10},{10... | collective-permute-start | bytes 4423688 | tf_op jit(solution)/shard_map/ppermute | solution.py:912
  101.2 34.8 %collective-permute-start.17 = (bf16[4,5,48,768]{3,2,1,0:T(8,128)(2,1)}, bf16[4,5,48,768]{3,2,1,0:T(8,128)(2,1)}, u32[]{:S(2)}, u32[]{:S(2)}) collective-permute-start(bf16[4,5,48,768]{3,2,1,0:T(8,128)(2,1)} %pad_maximum_fusion.1.refs_7_), channel_id=1, source_target_pairs={{0,1},{1,0},{2,3},{3,2},{4,5},{5,4},{6,7},{7,6},{8,9},{9,8},{10,11... | collective-permute-start | bytes 4423688 | tf_op jit(solution)/shard_map/ppermute | solution.py:912
  136.0 11.0 %collective-permute-start.20 = (bf16[4,5,48,768]{3,2,1,0:T(8,128)(2,1)}, bf16[4,5,48,768]{3,2,1,0:T(8,128)(2,1)S(1)}, u32[]{:S(2)}, u32[]{:S(2)}) collective-permute-start(bf16[4,5,48,768]{3,2,1,0:T(8,128)(2,1)} %collective-permute-done.16.refs_6_), channel_id=1, source_target_pairs={{0,8},{8,0},{16,24},{24,16},{1,9},{9,1},{17,25},{25,17},{2,10},{10... | collective-permute-start | bytes 4423688 | tf_op jit(solution)/shard_map/ppermute | solution.py:912
  136.0 11.0 %collective-permute-start.21 = (bf16[4,5,48,768]{3,2,1,0:T(8,128)(2,1)}, bf16[4,5,48,768]{3,2,1,0:T(8,128)(2,1)}, u32[]{:S(2)}, u32[]{:S(2)}) collective-permute-start(bf16[4,5,48,768]{3,2,1,0:T(8,128)(2,1)} %collective-permute-done.17.refs_8_), channel_id=1, source_target_pairs={{0,8},{8,0},{16,24},{24,16},{1,9},{9,1},{17,25},{25,17},{2,10},{10... | collective-permute-start | bytes 4423688 | tf_op jit(solution)/shard_map/ppermute | solution.py:912
  249.4 15.0 %collective-permute-start.22 = (bf16[16,3,48,768]{3,2,1,0:T(8,128)(2,1)}, bf16[16,3,48,768]{3,2,1,0:T(8,128)(2,1)}, u32[]{:S(2)}, u32[]{:S(2)}) collective-permute-start(bf16[16,3,48,768]{3,2,1,0:T(8,128)(2,1)} %get-tuple-element.245), channel_id=1, source_target_pairs={{0,8},{8,0},{16,24},{24,16},{1,9},{9,1},{17,25},{25,17},{2,10},{10... | collective-permute-start | bytes 10616840 | tf_op jit(solution)/shard_map/ppermute | solution.py:912
  264.4 13.3 %collective-permute-start.23 = (bf16[16,2,48,768]{3,2,1,0:T(8,128)(2,1)}, bf16[16,2,48,768]{3,2,1,0:T(8,128)(2,1)}, u32[]{:S(2)}, u32[]{:S(2)}) collective-permute-start(bf16[16,2,48,768]{3,2,1,0:T(8,128)(2,1)} %get-tuple-element.251), channel_id=1, source_target_pairs={{0,8},{8,0},{16,24},{24,16},{1,9},{9,1},{17,25},{25,17},{2,10},{10... | collective-permute-start | bytes 7077896 | tf_op jit(solution)/shard_map/ppermute | solution.py:912
  282.7 34.4 %collective-permute-start.24 = (bf16[4,5,48,768]{3,2,1,0:T(8,128)(2,1)}, bf16[4,5,48,768]{3,2,1,0:T(8,128)(2,1)S(1)}, u32[]{:S(2)}, u32[]{:S(2)}) collective-permute-start(bf16[4,5,48,768]{3,2,1,0:T(8,128)(2,1)} %pad_maximum_fusion.2), channel_id=1, source_target_pairs={{0,16},{8,24},{16,0},{24,8},{1,17},{9,25},{17,1},{25,9},{2,18},{10... | collective-permute-start | bytes 4423688 | tf_op jit(solution)/shard_map/ppermute | solution.py:912
  284.2 34.3 %collective-permute-start.25 = (bf16[4,5,48,768]{3,2,1,0:T(8,128)(2,1)}, bf16[4,5,48,768]{3,2,1,0:T(8,128)(2,1)}, u32[]{:S(2)}, u32[]{:S(2)}) collective-permute-start(bf16[4,5,48,768]{3,2,1,0:T(8,128)(2,1)} %pad_maximum_fusion.3), channel_id=1, source_target_pairs={{0,1},{1,0},{2,3},{3,2},{4,5},{5,4},{6,7},{7,6},{8,9},{9,8},{10,11... | collective-permute-start | bytes 4423688 | tf_op jit(solution)/shard_map/ppermute | solution.py:912
  323.1 17.7 %collective-permute-start.26 = (bf16[2,5,48,768]{3,2,1,0:T(8,128)(2,1)}, bf16[2,5,48,768]{3,2,1,0:T(8,128)(2,1)S(1)}, u32[]{:S(2)}, u32[]{:S(2)}) collective-permute-start(bf16[2,5,48,768]{3,2,1,0:T(8,128)(2,1)} %slice.237), channel_id=1, source_target_pairs={{0,1},{1,0},{2,3},{3,2},{4,5},{5,4},{6,7},{7,6},{8,9},{9,8},{10,11... | collective-permute-start | bytes 2211848 | tf_op jit(solution)/shard_map/ppermute | solution.py:912
  324.0 17.7 %collective-permute-start.27 = (bf16[2,5,48,768]{3,2,1,0:T(8,128)(2,1)}, bf16[2,5,48,768]{3,2,1,0:T(8,128)(2,1)}, u32[]{:S(2)}, u32[]{:S(2)}) collective-permute-start(bf16[2,5,48,768]{3,2,1,0:T(8,128)(2,1)} %slice.238), channel_id=1, source_target_pairs={{0,16},{8,24},{16,0},{24,8},{1,17},{9,25},{17,1},{25,9},{2,18},{10... | collective-permute-start | bytes 2211848 | tf_op jit(solution)/shard_map/ppermute | solution.py:912
  356.5 14.5 %collective-permute-start.28 = (bf16[16,48,1152]{2,1,0:T(8,128)(2,1)}, bf16[16,48,1152]{2,1,0:T(8,128)(2,1)S(1)}, u32[]{:S(2)}, u32[]{:S(2)}) collective-permute-start(bf16[16,48,1152]{2,1,0:T(8,128)(2,1)} %get-tuple-element.296), channel_id=1, source_target_pairs={{0,8},{8,0},{16,24},{24,16},{1,9},{9,1},{17,25},{25,17},{2,10},{10... | collective-permute-start | bytes 5308424 | tf_op jit(solution)/shard_map/ppermute | solution.py:912
  356.6 27.8 %collective-permute-start.29 = (bf16[5,48,768]{2,1,0:T(8,128)(2,1)}, bf16[5,48,768]{2,1,0:T(8,128)(2,1)}, u32[]{:S(2)}, u32[]{:S(2)}) collective-permute-start(bf16[5,48,768]{2,1,0:T(8,128)(2,1)} %get-tuple-element.302), channel_id=1, source_target_pairs={{0,2},{1,3},{2,0},{3,1},{4,6},{5,7},{6,4},{7,5},{8,10},{9,11},{10,... | collective-permute-start | bytes 1105928 | tf_op jit(solution)/shard_map/ppermute | solution.py:912
  356.6 28.5 %collective-permute-start.30 = (bf16[5,48,768]{2,1,0:T(8,128)(2,1)}, bf16[5,48,768]{2,1,0:T(8,128)(2,1)}, u32[]{:S(2)}, u32[]{:S(2)}) collective-permute-start(bf16[5,48,768]{2,1,0:T(8,128)(2,1)} %get-tuple-element.303), channel_id=1, source_target_pairs={{0,4},{1,5},{2,6},{3,7},{4,0},{5,1},{6,2},{7,3},{8,12},{9,13},{10,... | collective-permute-start | bytes 1105928 | tf_op jit(solution)/shard_map/ppermute | solution.py:912
  359.6 25.6 %collective-permute-start.31 = (bf16[5,48,768]{2,1,0:T(8,128)(2,1)}, bf16[5,48,768]{2,1,0:T(8,128)(2,1)}, u32[]{:S(2)}, u32[]{:S(2)}) collective-permute-start(bf16[5,48,768]{2,1,0:T(8,128)(2,1)} %get-tuple-element.304), channel_id=1, source_target_pairs={{0,6},{1,7},{2,4},{3,5},{4,2},{5,3},{6,0},{7,1},{8,14},{9,15},{10,... | collective-permute-start | bytes 1105928 | tf_op jit(solution)/shard_map/ppermute | solution.py:912
  371.9 13.2 %collective-permute-start.32 = (bf16[4,48,1152]{2,1,0:T(8,128)(2,1)}, bf16[4,48,1152]{2,1,0:T(8,128)(2,1)}, u32[]{:S(2)}, u32[]{:S(2)}) collective-permute-start(bf16[4,48,1152]{2,1,0:T(8,128)(2,1)} %get-tuple-element.307), channel_id=1, source_target_pairs={{0,16},{8,24},{16,0},{24,8},{1,17},{9,25},{17,1},{25,9},{2,18},{10... | collective-permute-start | bytes 1327112 | tf_op jit(solution)/shard_map/ppermute | solution.py:912
  372.8 12.4 %collective-permute-start.33 = (bf16[4,48,1152]{2,1,0:T(8,128)(2,1)S(1)}, bf16[4,48,1152]{2,1,0:T(8,128)(2,1)}, u32[]{:S(2)}, u32[]{:S(2)}) collective-permute-start(bf16[4,48,1152]{2,1,0:T(8,128)(2,1)S(1)} %get-tuple-element.308), channel_id=1, source_target_pairs={{0,1},{1,0},{2,3},{3,2},{4,5},{5,4},{6,7},{7,6},{8,9},{9,8},{10,11... | collective-permute-start | bytes 1327112 | tf_op jit(solution)/shard_map/ppermute | solution.py:912
  393.9 14.6 %collective-permute-start.42 = (bf16[48,1152]{1,0:T(8,128)(2,1)S(1)}, bf16[48,1152]{1,0:T(8,128)(2,1)S(1)}, u32[]{:S(2)}, u32[]{:S(2)}) collective-permute-start(bf16[48,1152]{1,0:T(8,128)(2,1)S(1)} %slice_bitcast_fusion.6), channel_id=1, source_target_pairs={{0,2},{1,3},{2,0},{3,1},{4,6},{5,7},{6,4},{7,5},{8,10},{9,11},{10,... | collective-permute-start | bytes 331784 | tf_op jit(solution)/shard_map/ppermute | solution.py:912
  406.3 23.5 %collective-permute-start.48 = (bf16[5,48,768]{2,1,0:T(8,128)(2,1)S(1)}, bf16[5,48,768]{2,1,0:T(8,128)(2,1)S(1)}, u32[]{:S(2)}, u32[]{:S(2)}) collective-permute-start(bf16[5,48,768]{2,1,0:T(8,128)(2,1)S(1)} %add_convert_fusion.18.refs_0_), channel_id=1, source_target_pairs={{0,16},{8,24},{16,0},{24,8},{1,17},{9,25},{17,1},{25,9},{2,18},{10... | collective-permute-start | bytes 1105928 | tf_op jit(solution)/shard_map/ppermute | solution.py:912
  407.9 12.7 %collective-permute-start.37 = (f32[8,32,128]{2,1,0:T(8,128)S(1)}, f32[8,32,128]{2,1,0:T(8,128)S(1)}, u32[]{:S(2)}, u32[]{:S(2)}) collective-permute-start(f32[8,32,128]{2,1,0:T(8,128)S(1)} %add.346), channel_id=1, source_target_pairs={{0,16},{8,24},{16,0},{24,8},{1,17},{9,25},{17,1},{25,9},{2,18},{10... | collective-permute-start | bytes 393224 | tf_op jit(solution)/shard_map/ppermute | solution.py:912
  412.4 17.5 %collective-permute-start.45 = (bf16[48,1152]{1,0:T(8,128)(2,1)S(1)}, bf16[48,1152]{1,0:T(8,128)(2,1)S(1)}, u32[]{:S(2)}, u32[]{:S(2)}) collective-permute-start(bf16[48,1152]{1,0:T(8,128)(2,1)S(1)} %fusion.2.refs_0_), channel_id=1, source_target_pairs={{0,16},{8,24},{16,0},{24,8},{1,17},{9,25},{17,1},{25,9},{2,18},{10... | collective-permute-start | bytes 331784 | tf_op jit(solution)/shard_map/ppermute | solution.py:912
  429.3 12.9 %collective-permute-start.49 = (bf16[5,48,768]{2,1,0:T(8,128)(2,1)S(1)}, bf16[5,48,768]{2,1,0:T(8,128)(2,1)S(1)}, u32[]{:S(2)}, u32[]{:S(2)}) collective-permute-start(bf16[5,48,768]{2,1,0:T(8,128)(2,1)S(1)} %add_convert_fusion.18.refs_0_), channel_id=1, source_target_pairs={{0,8},{8,0},{16,24},{24,16},{1,9},{9,1},{17,25},{25,17},{2,10},{10... | collective-permute-start | bytes 1105928 | tf_op jit(solution)/shard_map/ppermute | solution.py:912
  429.8 12.4 %collective-permute-start.50 = (bf16[5,48,768]{2,1,0:T(8,128)(2,1)S(1)}, bf16[5,48,768]{2,1,0:T(8,128)(2,1)S(1)}, u32[]{:S(2)}, u32[]{:S(2)}) collective-permute-start(bf16[5,48,768]{2,1,0:T(8,128)(2,1)S(1)} %collective-permute-done.48.refs_1_), channel_id=1, source_target_pairs={{0,8},{8,0},{16,24},{24,16},{1,9},{9,1},{17,25},{25,17},{2,10},{10... | collective-permute-start | bytes 1105928 | tf_op jit(solution)/shard_map/ppermute | solution.py:912
  (55 other events, 540.2 us)

commit v3 on v2

--- a/solution.py
+++ b/solution.py
@@ -22,13 +22,15 @@
 PAIR = 2 * HEAD_DIM
 SIDE = (MAP + WIN - 1) // WIN
 LN_EPS = 1e-06
+SQRT_HALF = 0.7071067811865476
+INV_ROOT_TAU = 0.3989422804014327
 F32 = jnp.float32
 BF16 = jnp.bfloat16
-VMEM_LIMIT = 60 * 1024 * 1024
 QKV_HALF = 3 * D // 2
 NOTES = 128
-STEPS = (1, 2, 4, 1)
-BACK_STEPS = (1, 5, 2)
+STEPS = (3, 4, 1)
+COST = 1e8
+BACK_STEPS = (2, 4, 2)
 
 
 def nn(left, right):
@@ -124,10 +126,11 @@
 
 def load_first(me_ref, parts, full, sem):
     core = me_ref[0] % 2
-    for ref, (half, along_y, other) in zip(parts, ARRIVED):
-
-        def start(index, carry, ref=ref, half=half, along_y=along_y, other=other):
-            far_x, owner = chunk_place(me_ref, index, half, along_y)
+    for at, ref in enumerate(parts):
+        along_y, other = at % 2 == 0, at // 2
+
+        def start(index, carry, ref=ref, along_y=along_y, other=other):
+            far_x, owner = chunk_place(me_ref, index % 4, index // 4, along_y)
             pltpu.make_async_copy(
                 ref.at[index, :, pl.ds(0, QKV_HALF)],
                 full.at[
@@ -138,7 +141,7 @@
             ).start()
             return carry
 
-        lax.fori_loop(0, 4, start, 0)
+        lax.fori_loop(0, 8, start, 0)
     pltpu.make_async_copy(full, full, sem.at[0]).wait()
 
 
@@ -147,6 +150,15 @@
     dist_x = jnp.where(group == 0, high, mid)
     dist_y = jnp.where(group == 0, mid, high)
     return (me_ref[0] // 2) ^ dist_x, me_ref[1] ^ (group * 4 + plane * 2 + dist_y)
+
+
+def piece_index(me_ref, far_x, owner):
+    dist = me_ref[1] ^ owner
+    dist_x = (me_ref[0] // 2) ^ far_x
+    dist_y, plane, group = dist % 2, (dist // 2) % 2, dist // 4
+    high = jnp.where(group == 0, dist_x, dist_y)
+    mid = jnp.where(group == 0, dist_y, dist_x)
+    return group * 8 + high * 4 + mid * 2 + plane
 
 
 def spread_rows(notes_of, owner_of, width, total):
@@ -223,7 +235,6 @@
         keys = qkv_ref[0, :, pl.ds(pl.multiple_of(D + at, PAIR), PAIR)]
         values = qkv_ref[0, :, pl.ds(pl.multiple_of(2 * D + at, PAIR), PAIR)]
         query_t = fill_rows(query).T
-        values_t = fill_rows(values).T
         offsets = nn(rel_ref[...], query_t)
         mixed = []
         for head in range(2):
@@ -251,76 +262,75 @@
             total = jnp.sum(expo, axis=0, keepdims=True)
             probs = (expo * (1.0 / total)).astype(BF16)
             prob_ref[0, 2 * pair + head] = probs
-            mixed.append(
-                nn(values_t[head * HEAD_DIM : (head + 1) * HEAD_DIM], fill_rows(probs)).astype(BF16)
-            )
-        mix_ref[0, :, pl.ds(at, PAIR)] = jnp.concatenate(mixed, axis=0).T[0:ROWS]
+            mixed.append(tn(probs, values)[0:ROWS].astype(BF16))
+        mix_ref[0, :, pl.ds(at, PAIR)] = jnp.where(low_half, mixed[0], mixed[1])
         return carry
 
-    lax.fori_loop(0, PAIRS, one_pair, 0)
+    lax.fori_loop(0, PAIRS, one_pair, 0, unroll=PAIRS)
 
 
 def gelu_parts(pre):
+    cumulative = 0.5 + 0.5 * lax.erf(pre * SQRT_HALF)
     bell = jnp.exp(pre * pre * (-0.5))
-    steps = 1.0 / (1.0 + (0.3275911 * math.sqrt(0.5)) * jnp.abs(pre))
-    poly = steps * (
-        0.5 * 0.254829592
-        + steps
-        * (
-            0.5 * -0.284496736
-            + steps * (0.5 * 1.421413741 + steps * (0.5 * -1.453152027 + steps * (0.5 * 1.061405429)))
-        )
-    )
-    tail = poly * bell
-    cumulative = jnp.where(pre > 0, 1.0 - tail, tail)
-    return pre * cumulative, cumulative + pre * (bell * 0.3989422804014327)
-
-
-def load_mlp(me_ref, pieces, up, down, proj, notes, sem):
+    return pre * cumulative, cumulative + pre * (bell * INV_ROOT_TAU)
+
+
+def load_up(me_ref, pieces, up, proj, notes, sem):
     core = me_ref[0] % 2
     for array, (ref, (half, along_y, other)) in enumerate(zip(pieces, ARRIVED)):
 
         def start(index, carry, ref=ref, half=half, along_y=along_y, far_core=core ^ other, array=array):
             far_x, owner = chunk_place(me_ref, index, half, along_y)
             rows = pl.ds(pl.multiple_of(owner * 96 + far_x * 48, 16), 48)
+            cols = pl.ds(pl.multiple_of(far_core * 384, 128), 384)
+            pltpu.make_async_copy(
+                ref.at[index, 2, :, pl.ds(0, 384)], proj.at[rows, cols], sem.at[1]
+            ).start()
+            pltpu.make_async_copy(
+                ref.at[index, 2, pl.ds(0, 16), pl.ds(384, 384)], notes.at[array * 4 + index], sem.at[2]
+            ).start()
             for block in range(2):
                 cols = pl.ds(pl.multiple_of(far_core * 1536 + block * D, 128), D)
                 pltpu.make_async_copy(ref.at[index, block], up.at[rows, cols], sem.at[0]).start()
+            return carry
+
+        lax.fori_loop(0, 4, start, 0)
+    for at, full in ((2, notes), (1, proj), (0, up)):
+        pltpu.make_async_copy(full, full, sem.at[at]).wait()
+
+
+def load_down(me_ref, pieces, down, sem):
+    core = me_ref[0] % 2
+    for ref, (half, along_y, other) in zip(pieces, ARRIVED):
+
+        def start(index, carry, ref=ref, half=half, along_y=along_y, far_core=core ^ other):
+            far_x, owner = chunk_place(me_ref, index, half, along_y)
             place = owner * 8 + far_core * 4 + far_x * 2
-            pltpu.make_async_copy(
-                ref.at[index, pl.ds(2, 2)], down.at[pl.ds(place, 2)], sem.at[1]
-            ).start()
-            cols = pl.ds(pl.multiple_of(far_core * 384, 128), 384)
-            pltpu.make_async_copy(
-                ref.at[index, 4, :, pl.ds(0, 384)], proj.at[rows, cols], sem.at[2]
-            ).start()
-            pltpu.make_async_copy(
-                ref.at[index, 4, pl.ds(0, 16), pl.ds(384, 384)], notes.at[array * 4 + index], sem.at[3]
-            ).start()
+            pltpu.make_async_copy(ref.at[index], down.at[pl.ds(place, 2)], sem.at[0]).start()
             return carry
 
         lax.fori_loop(0, 4, start, 0)
-    for at, full in ((3, notes), (2, proj), (0, up), (1, down)):
-        pltpu.make_async_copy(full, full, sem.at[at]).wait()
-
-
-def mlp_kernel(*refs, group, pieces, scale):
-    step = pl.program_id(0)
+    pltpu.make_async_copy(down, down, sem.at[0]).wait()
+
+
+def up_kernel(*refs, group, pieces):
     rows = group * ROWS
-    me_ref, tok_ref, mix_ref, teach_ref, aux_ref = refs[0:5]
-    at = 5 + (pieces or 6)
-    (out_ref, gh_ref, ga_ref, si_ref, act_ref, gd_ref, gu_ref, sums_ref, usum_ref) = refs[at : at + 9]
-    at += 9
+    me_ref, tok_ref, mix_ref, keep_ref = refs[0:4]
+    at = 4 + (pieces or 4)
+    hid_ref, si_ref, act_ref, slope_ref = refs[at : at + 4]
+    at += 4
     if pieces:
-        wp_ref, slope_ref, t_ref, up_ref, down3_ref, notes, vec_ref, ub_ref, total_ref, sem = refs[at:]
-
-        @pl.when(step == 0)
+        up_ref, wp_ref, vec_ref, ub_ref, total_ref, t_ref, notes, sem = refs[at:]
+
+        @pl.when(pl.program_id(0) == 0)
         def _():
-            load_mlp(me_ref, refs[5 : 5 + pieces], up_ref, down3_ref, wp_ref, notes, sem)
+            load_up(me_ref, refs[4 : 4 + pieces], up_ref, wp_ref, notes, sem)
             picks = [(at, at % 2 * 2 + at // 2) for at in range(4)]
             picks += [(8 + at, 4 + at * 2) for at in range(2)] + [(12 + at, 5 + at * 2) for at in range(2)]
             owner_of = lambda at: me_ref[1] ^ picks[at][1]
-            vec_ref[...] = spread_rows(lambda at: notes[picks[at][0], :, 0:128], owner_of, 96, D)
+            vec_ref[...] = spread_rows(
+                lambda at: notes[picks[at][0], :, 0:128], owner_of, 96, D
+            )[0:8]
             for at in range(8):
                 lanes = pl.ds(pl.multiple_of(owner_of(at) * 384, 128), 384)
                 ub_ref[:, lanes] = notes[picks[at][0], 0:16, :].astype(F32)[4:5, :]
@@ -330,45 +340,62 @@
             counts = counts[5:6, 0:128]
             lane = lax.broadcasted_iota(jnp.int32, (1, 128), 1)
             weight = jnp.where(lane == 0, 128.0, jnp.where(lane == 1, 1.0, 0.0))
-            total_ref[...] = jnp.sum(counts * weight, axis=1, keepdims=True)
-
-        down_rows = lambda part: down3_ref[pl.ds(part * 16, 16)].reshape(D, D)
+            total_ref[...] = jnp.broadcast_to(
+                jnp.sum(counts * weight, axis=1, keepdims=True), (1, 128)
+            )
     else:
-        wp_ref, up_ref, down_ref, vec_ref, ub_ref, total_ref = refs[5:11]
-        slope_ref, t_ref = refs[at:]
-        down_rows = lambda part: down_ref[pl.ds(pl.multiple_of(part * D, D), D), :]
-    pb_row, gain_row, shift_row, db_row = [vec_ref[at : at + 1, :] for at in range(4)]
-    coef = scale / total_ref[...]
-
-    @pl.when(step == 0)
-    def _():
-        sums_ref[...] = jnp.zeros_like(sums_ref)
-        sums_ref[5:6, :] = jnp.broadcast_to(total_ref[...], (1, D))
-        usum_ref[...] = jnp.zeros_like(usum_ref)
-
-    aux = aux_ref[...].reshape(rows, 2)
-    keep, valid = aux[:, 0:1], aux[:, 1:2]
+        wp_ref, up_ref, vec_ref, ub_ref = refs[4:8]
+        t_ref = refs[at]
+    pb_row, gain_row, shift_row = [vec_ref[at : at + 1, :] for at in range(3)]
+    keep = keep_ref[...].reshape(rows, 2)[:, 0:1]
     for at in range(group):
         t_ref[at, pl.ds(192, 16), :] = jnp.zeros((16, D), F32)
         t_ref[at, pl.ds(0, SLOTS), :] = tok_ref[at].astype(F32)
     attn_out = nn(mix_ref[...].reshape(rows, D), wp_ref[...]) + pb_row
     hidden = keep * (t_ref[...].reshape(rows, D) + attn_out)
-    scaled, inv_std = norm_parts(hidden)
+    hid_ref[...] = hidden.reshape(group, ROWS, D)
+    scaled, _ = norm_parts(hidden)
     second_in = (scaled * gain_row + shift_row).astype(BF16)
     si_ref[...] = second_in.reshape(group, ROWS, D)
-    chunk = D
-
-    def forward(part, total):
-        cols = pl.ds(pl.multiple_of(part * chunk, chunk), chunk)
-        pre = nn(second_in, up_ref[:, cols]) + ub_ref[:, cols]
-        act, slope = gelu_parts(pre)
-        slope_ref[:, cols] = slope
-        low = act.astype(BF16)
-        act_ref[:, :, cols] = low.reshape(group, ROWS, chunk)
-        return total + nn(low, down_rows(part))
-
-    down = lax.fori_loop(0, MLP // chunk, forward, jnp.zeros((rows, D), F32))
-    final = keep * (hidden + (down + db_row))
+    for part in range(MLP // D):
+        cols = slice(part * D, part * D + D)
+        act, slope = gelu_parts(nn(second_in, up_ref[:, cols]) + ub_ref[:, cols])
+        slope_ref[:, :, cols] = slope.astype(BF16).reshape(group, ROWS, D)
+        act_ref[:, :, cols] = act.astype(BF16).reshape(group, ROWS, D)
+
+
+def down_kernel(*refs, group, pieces, scale):
+    step = pl.program_id(0)
+    rows = group * ROWS
+    me_ref, hid_ref, act_ref, slope_ref, teach_ref, aux_ref, up_ref, vec_ref, total_ref = refs[0:9]
+    at = 9 + (pieces or 1)
+    out_ref, gh_ref, ga_ref, gd_ref, gu_ref, sums_ref, usum_ref, t_ref = refs[at : at + 8]
+    if pieces:
+        down3_ref, sem = refs[at + 8 :]
+
+        @pl.when(step == 0)
+        def _():
+            load_down(me_ref, refs[9 : 9 + pieces], down3_ref, sem)
+
+        down_rows = lambda part: down3_ref[pl.ds(part * 16, 16)].reshape(D, D)
+    else:
+        down_rows = lambda part: refs[9][pl.ds(part * D, D), :]
+
+    @pl.when(step == 0)
+    def _():
+        sums_ref[...] = jnp.zeros_like(sums_ref)
+        usum_ref[...] = jnp.zeros_like(usum_ref)
+
+    gain_row, db_row = vec_ref[1:2, :], vec_ref[3:4, :]
+    coef = scale / total_ref[:, 0:1]
+    aux = aux_ref[...].reshape(rows, 2)
+    keep, valid = aux[:, 0:1], aux[:, 1:2]
+    hidden = hid_ref[...].reshape(rows, D)
+    down = db_row
+    for part in range(MLP // D):
+        cols = slice(part * D, part * D + D)
+        down = down + nn(act_ref[:, :, cols].reshape(rows, D), down_rows(part))
+    final = keep * (hidden + down)
     for at in range(group):
         out_ref[at] = final[at * ROWS : at * ROWS + SLOTS].astype(BF16)
         t_ref[at, pl.ds(192, 16), :] = jnp.zeros((16, D), F32)
@@ -380,19 +407,17 @@
     gd_ref[...] = grad_down.reshape(group, ROWS, D)
     sums_ref[0:1, :] += jnp.sum(weighted * error, axis=0, keepdims=True)
     sums_ref[1:2, :] += jnp.sum(grad_down.astype(F32), axis=0, keepdims=True)
-
-    def backward(part, total):
-        cols = pl.ds(pl.multiple_of(part * chunk, chunk), chunk)
-        grad_up = (nt(grad_down, down_rows(part)) * slope_ref[:, cols]).astype(BF16)
-        gu_ref[:, :, cols] = grad_up.reshape(group, ROWS, chunk)
+    for part in range(MLP // D):
+        cols = slice(part * D, part * D + D)
+        slope = slope_ref[:, :, cols].reshape(rows, D).astype(F32)
+        grad_up = (nt(grad_down, down_rows(part)) * slope).astype(BF16)
+        gu_ref[:, :, cols] = grad_up.reshape(group, ROWS, D)
         usum_ref[:, cols] += jnp.sum(grad_up.astype(F32), axis=0, keepdims=True)
-        return total + nt(grad_up, up_ref[:, cols])
-
-    grad_second = lax.fori_loop(0, MLP // chunk, backward, jnp.zeros((rows, D), F32))
+    grad_second = nt(gu_ref[...].reshape(rows, MLP), up_ref[...])
+    scaled, inv_std = norm_parts(hidden)
     sums_ref[2:3, :] += jnp.sum(grad_second * scaled, axis=0, keepdims=True)
     sums_ref[3:4, :] += jnp.sum(grad_second, axis=0, keepdims=True)
-    grad_hidden = grad_final + norm_grad(grad_second, scaled, inv_std, gain_row)
-    grad_hidden = keep * grad_hidden
+    grad_hidden = keep * (grad_final + norm_grad(grad_second, scaled, inv_std, gain_row))
     gh_ref[...] = grad_hidden.reshape(group, ROWS, D)
     grad_attn = grad_hidden.astype(BF16)
     ga_ref[...] = grad_attn.reshape(group, ROWS, D)
@@ -463,7 +488,7 @@
         qsum_ref[1:2, q_at] += jnp.sum(grad_values.astype(F32), axis=0, keepdims=True)
         return carry
 
-    lax.fori_loop(0, PAIRS, one_pair, 0)
+    lax.fori_loop(0, PAIRS, one_pair, 0, unroll=PAIRS)
 
 
 def input_kernel(
@@ -520,66 +545,55 @@
             pltpu.make_async_copy(ref, ref, sem.at[at]).wait()
 
 
-def up_grad_kernel(me_ref, left_ref, right_ref, keep_ref, send_ref, full, sem):
+def up_grad_kernel(me_ref, left_ref, right_ref, out_ref, full, sem):
     step = pl.program_id(0)
     full[step] = tn(left_ref[...], right_ref[...]).astype(BF16)
-    mine = (step // 2) == me_ref[0] % 2
-
-    def send_to(ref, at):
-        def start(index, carry):
-            far_x, owner = piece_place(me_ref, index)
-            rows = pl.ds(pl.multiple_of(owner * 96 + far_x * 48, 16), 48)
-            pltpu.make_async_copy(
-                full.at[step, rows], ref.at[index, step % 2], sem.at[at]
-            ).start()
-            return carry
-
-        lax.fori_loop(0, 16, start, 0)
-
-    @pl.when(mine)
-    def _():
-        send_to(keep_ref, 0)
-
-    @pl.when(jnp.logical_not(mine))
-    def _():
-        send_to(send_ref, 1)
+    cols = pl.ds(pl.multiple_of((step % 2) * 384, 128), 384)
+
+    def start(index, carry):
+        far_x, owner = piece_place(me_ref, index)
+        rows = pl.ds(pl.multiple_of(owner * 96 + far_x * 48, 16), 48)
+        pltpu.make_async_copy(
+            full.at[step, rows], out_ref.at[index, step // 2, :, cols], sem.at[0]
+        ).start()
+        return carry
+
+    lax.fori_loop(0, 16, start, 0)
 
     @pl.when(step == pl.num_programs(0) - 1)
     def _():
-        pltpu.make_async_copy(keep_ref, keep_ref, sem.at[0]).wait()
-        pltpu.make_async_copy(send_ref, send_ref, sem.at[1]).wait()
+        pltpu.make_async_copy(out_ref, out_ref, sem.at[0]).wait()
 
 
 def down_grad_kernel(
-    me_ref, act_ref, gd_ref, mix_ref, ga_ref, keep_ref, send_ref, full, half, sem
+    me_ref, act_ref, gd_ref, mix_any, ga_any, keep_ref, send_ref, full, half, mix_ref, ga_ref, sem
 ):
     step = pl.program_id(0)
     last = pl.num_programs(0) - 1
+    fetches = [
+        pltpu.make_async_copy(mix_any, mix_ref, sem.at[2]),
+        pltpu.make_async_copy(ga_any, ga_ref, sem.at[3]),
+    ]
+
+    @pl.when(step == 0)
+    def _():
+        for fetch in fetches:
+            fetch.start()
 
     @pl.when(step < last)
     def _():
-        full[step] = tn(act_ref[...], gd_ref[...]).astype(BF16).reshape(16, 48, D)
+        full[step] = tn(act_ref[...], gd_ref[...]).astype(BF16).reshape(8, 48, D)
 
     @pl.when(step == last)
     def _():
+        for fetch in fetches:
+            fetch.wait()
         total = tn(mix_ref[...], ga_ref[...]).astype(BF16)
         for core in range(2):
             half[core] = total[:, core * 384 : core * 384 + 384]
 
     core = me_ref[0] % 2
     for ref, far_core, at in ((keep_ref, core, 0), (send_ref, 1 - core, 1)):
-
-        def start_down(index, carry, ref=ref, far_core=far_core, at=at):
-            far_x, owner = piece_place(me_ref, index)
-
-            @pl.when(owner // 2 == step)
-            def _():
-                place = (owner % 2) * 8 + far_core * 4 + far_x * 2
-                pltpu.make_async_copy(
-                    full.at[step, pl.ds(place, 2)], ref.at[index, pl.ds(0, 2)], sem.at[at]
-                ).start()
-
-            return carry
 
         def start_proj(index, carry, ref=ref, far_core=far_core, at=at):
             far_x, owner = piece_place(me_ref, index)
@@ -591,8 +605,13 @@
             return carry
 
         @pl.when(step < last)
-        def _(start_down=start_down):
-            lax.fori_loop(0, 16, start_down, 0)
+        def _(ref=ref, far_core=far_core, at=at):
+            for far_x in range(2):
+                pltpu.make_async_copy(
+                    full.at[step, pl.ds(far_core * 4 + far_x * 2, 2)],
+                    ref.at[piece_index(me_ref, far_x, step), pl.ds(0, 2)],
+                    sem.at[at],
+                ).start()
 
         @pl.when(step == last)
         def _(start_proj=start_proj):
@@ -606,6 +625,11 @@
 
 def whole(shape):
     zeros = (0,) * len(shape)
+    return pl.BlockSpec(shape, lambda *_: zeros, pipeline_mode=pl.Buffered(1))
+
+
+def whole_out(shape):
+    zeros = (0,) * len(shape)
     return pl.BlockSpec(shape, lambda *_: zeros)
 
 
@@ -618,9 +642,9 @@
 ANY = pl.BlockSpec(memory_space=pl.ANY)
 
 
-def params():
+def params(mebibytes=32):
     return pltpu.CompilerParams(
-        vmem_limit_bytes=VMEM_LIMIT, dimension_semantics=("arbitrary",)
+        vmem_limit_bytes=mebibytes * 1024 * 1024, dimension_semantics=("arbitrary",)
     )
 
 
@@ -636,11 +660,11 @@
     return pl.pallas_call(
         notes_kernel,
         in_specs=[SMEM] + [whole(v.shape) for v in (near, far_x, far_y)],
-        out_specs=[whole((8, D)), whole((PAIR, PAIR)), whole((PAIR, PAIR))],
+        out_specs=[whole_out((8, D)), whole_out((PAIR, PAIR)), whole_out((PAIR, PAIR))],
         out_shape=[shape_of((8, D), F32)] + [shape_of((PAIR, PAIR), BF16)] * 2,
         grid=(1,),
         compiler_params=params(),
-        cost_estimate=cost(1e9, 1e6),
+        cost_estimate=cost(COST, 1e5),
         name="notes",
     )(me, near, far_x, far_y)
 
@@ -659,7 +683,7 @@
     ]
     scratch = [pltpu.VMEM((ROWS, D), F32)]
     if pieces:
-        out_specs.append(whole((D, 3 * D)))
+        out_specs.append(whole_out((D, 3 * D)))
         out_shape.append(shape_of((D, 3 * D), BF16))
         scratch.append(pltpu.SemaphoreType.DMA((1,)))
     inputs = 5 + len(weights)
@@ -675,44 +699,65 @@
         scratch_shapes=scratch,
         input_output_aliases={inputs + at: at for at in range(len(earlier))},
         compiler_params=params(),
-        cost_estimate=cost(number * 6e9, number * 2e6),
+        cost_estimate=cost(COST, 1e5),
         name="attend",
     )(me, tokens, *weights, vec, rel, places, *earlier)
 
 
-def mlp(me, tokens, mixed, teacher, aux, weights, scale, chunked):
+def mlp_up(me, tokens, mixed, aux, weights, chunked):
     count = tokens.shape[0]
+    group = math.gcd(count, 2)
+    win = lambda width: windows_from(0, (group, ROWS, width))
+    arr = lambda width, dtype: shape_of((count, ROWS, width), dtype)
+    pieces = len(weights) if chunked else 0
+    out_specs = [win(D), win(D), win(MLP), win(MLP)]
+    out_shape = [arr(D, F32), arr(D, BF16), arr(MLP, BF16), arr(MLP, BF16)]
+    scratch = [pltpu.VMEM((group, ROWS, D), F32)]
+    if pieces:
+        shapes = [((D, MLP), BF16), ((D, D), BF16), ((8, D), F32), ((1, MLP), F32), ((1, 128), F32)]
+        out_specs += [whole_out(s) for s, _ in shapes]
+        out_shape += [shape_of(s, t) for s, t in shapes]
+        scratch += [pltpu.VMEM((32, 16, 384), BF16), pltpu.SemaphoreType.DMA((3,))]
+    return pl.pallas_call(
+        functools.partial(up_kernel, group=group, pieces=pieces),
+        grid=(count // group,),
+        in_specs=[SMEM, windows_from(0, (group, SLOTS, D)), win(D), win(2)]
+        + ([ANY] * pieces if pieces else [whole(v.shape) for v in weights]),
+        out_specs=out_specs,
+        out_shape=out_shape,
+        scratch_shapes=scratch,
+        compiler_params=params(44),
+        cost_estimate=cost(COST * count, 1e5),
+        name="mlp_up",
+    )(me, tokens, mixed, aux, *weights)
+
+
+def mlp_down(me, hidden, act, slope, teacher, aux, up, vec, total, weights, scale, chunked):
+    count = hidden.shape[0]
     group = math.gcd(count, 2)
     win = lambda width: windows_from(0, (group, ROWS, width))
     plain = windows_from(0, (group, SLOTS, D))
     arr = lambda width, dtype: shape_of((count, ROWS, width), dtype)
     pieces = len(weights) if chunked else 0
-    weight_specs = [ANY] * pieces if pieces else [whole(v.shape) for v in weights]
-    out_specs = [plain, win(D), win(D), win(D), win(MLP), win(D), win(MLP), whole((6, D)),
-                 whole((1, MLP))]
-    out_shape = [
-        shape_of((count, SLOTS, D), BF16), arr(D, F32), arr(D, BF16), arr(D, BF16), arr(MLP, BF16),
-        arr(D, BF16), arr(MLP, BF16), shape_of((6, D), F32), shape_of((1, MLP), F32),
-    ]
-    scratch = [pltpu.VMEM((group * ROWS, MLP), F32), pltpu.VMEM((group, ROWS, D), F32)]
+    scratch = [pltpu.VMEM((group, ROWS, D), F32)]
     if pieces:
-        out_specs.append(whole((D, D)))
-        out_shape.append(shape_of((D, D), BF16))
-        scratch += [pltpu.VMEM((D, MLP), BF16), pltpu.VMEM((MLP // 48, 48, D), BF16),
-                    pltpu.VMEM((32, 16, 384), BF16), pltpu.VMEM((16, D), F32),
-                    pltpu.VMEM((1, MLP), F32), pltpu.VMEM((1, 1), F32),
-                    pltpu.SemaphoreType.DMA((4,))]
+        scratch += [pltpu.VMEM((MLP // 48, 48, D), BF16), pltpu.SemaphoreType.DMA((1,))]
     return pl.pallas_call(
-        functools.partial(mlp_kernel, group=group, pieces=pieces, scale=scale),
+        functools.partial(down_kernel, group=group, pieces=pieces, scale=scale),
         grid=(count // group,),
-        in_specs=[SMEM, plain, win(D), plain, win(2), *weight_specs],
-        out_specs=out_specs,
-        out_shape=out_shape,
+        in_specs=[SMEM, win(D), win(MLP), win(MLP), plain, win(2), whole((D, MLP)), whole((8, D)),
+                  whole((1, 128))]
+        + ([ANY] * pieces if pieces else [whole(v.shape) for v in weights]),
+        out_specs=[plain, win(D), win(D), win(D), win(MLP), whole_out((5, D)), whole_out((1, MLP))],
+        out_shape=[
+            shape_of((count, SLOTS, D), BF16), arr(D, F32), arr(D, BF16), arr(D, BF16),
+            arr(MLP, BF16), shape_of((5, D), F32), shape_of((1, MLP), F32),
+        ],
         scratch_shapes=scratch,
-        compiler_params=params(),
-        cost_estimate=cost(count * 8e9, 60e6),
-        name="mlp",
-    )(me, tokens, mixed, teacher, aux, *weights)
+        compiler_params=params(48),
+        cost_estimate=cost(COST * count, 1e5),
+        name="mlp_down",
+    )(me, hidden, act, slope, teacher, aux, up, vec, total, *weights)
 
 
 def attend_back(grad_attn, proj, qkv, probs, rel_t, places_t, first, number, earlier=()):
@@ -726,7 +771,7 @@
             win((1, ROWS, D)), whole((D, D)), win((1, ROWS, 3 * D)), win((1, HEADS, ROWS, LANES)),
             whole((PAIR, PAIR)), whole((32, LANES)), *before,
         ],
-        out_specs=[win((1, ROWS, 3 * D)), whole((PAIR, PAIR)), whole((2, D))],
+        out_specs=[win((1, ROWS, 3 * D)), whole_out((PAIR, PAIR)), whole_out((2, D))],
         out_shape=[
             shape_of((count, ROWS, 3 * D), BF16), shape_of((PAIR, PAIR), F32),
             shape_of((2, D), F32),
@@ -734,7 +779,7 @@
         scratch_shapes=[pltpu.VMEM((LANES, D), BF16)],
         input_output_aliases={6: 0} if earlier else {},
         compiler_params=params(),
-        cost_estimate=cost(number * 6e9, number * 2e6),
+        cost_estimate=cost(COST, 1e5),
         name="attend_back",
     )(grad_attn, proj, qkv, probs, rel_t, places_t, *earlier)
 
@@ -751,12 +796,12 @@
             SMEM, win((group, ROWS, 3 * D)), whole((D, 3 * D)), win((group, SLOTS, D)),
             win((group, ROWS, D)), whole((8, D)), *before,
         ],
-        out_specs=[win((group, SLOTS, D)), whole((2, D))],
+        out_specs=[win((group, SLOTS, D)), whole_out((2, D))],
         out_shape=[shape_of((count, SLOTS, D), F32), shape_of((2, D), F32)],
         scratch_shapes=[pltpu.VMEM((ROWS, D), F32)],
         input_output_aliases={6: 0} if earlier else {},
         compiler_params=params(),
-        cost_estimate=cost(number * 2e9, 25e6),
+        cost_estimate=cost(COST, 1e5),
         name="input_back",
     )(me, dqkv, weight, tokens, grad_hidden, vec, *earlier)
 
@@ -795,10 +840,10 @@
         pack_kernel,
         grid=(1,),
         in_specs=[SMEM] + [whole(v.shape) for v in sums],
-        out_specs=whole((8, 32, 128)),
+        out_specs=whole_out((8, 32, 128)),
         out_shape=shape_of((8, 32, 128), F32),
         compiler_params=params(),
-        cost_estimate=cost(1e9, 1e6),
+        cost_estimate=cost(COST, 1e5),
         name="pack",
     )(me, *sums)
 
@@ -829,10 +874,10 @@
         functools.partial(shard_kernel, split=split),
         grid=(1,),
         in_specs=[SMEM] + [whole(v.shape) for v in quarters],
-        out_specs=[whole(s) for s in shapes],
+        out_specs=[whole_out(s) for s in shapes],
         out_shape=[shape_of(s, F32) for s in shapes],
         compiler_params=params(),
-        cost_estimate=cost(1e9, 5e6),
+        cost_estimate=cost(COST, 1e5),
         name="shard",
     )(me, *quarters)
 
@@ -851,7 +896,7 @@
         in_specs=[moving, still] if by_rows else [still, moving],
         out_specs=pl.BlockSpec((D, D), (lambda s: (s, 0)) if by_rows else (lambda s: (0, s))),
         out_shape=shape_of((left.shape[1], right.shape[1]), BF16),
-        compiler_params=params(),
+        compiler_params=params(44),
         name="weight_grad",
     )(left, right)
 
@@ -866,22 +911,28 @@
         out_shape=[shape_of((16, 48, QKV_HALF), BF16)] * 2,
         scratch_shapes=[pltpu.VMEM((D, 3 * D), BF16), pltpu.SemaphoreType.DMA((2,))],
         compiler_params=params(),
-        cost_estimate=cost(12e9, 18e6),
+        cost_estimate=cost(COST, 1e5),
         name="qkv_grad",
     )(me, left, right)
 
 
-def up_grad(me, left, right):
+def up_grad(me, left, right, other):
     rows = left.shape[0]
     return pl.pallas_call(
         up_grad_kernel,
-        grid=(4,),
-        in_specs=[SMEM, whole((rows, D)), column_blocks(rows)],
-        out_specs=[ANY] * 2,
-        out_shape=[shape_of((16, 2, 48, D), BF16)] * 2,
-        scratch_shapes=[pltpu.VMEM((4, D, D), BF16), pltpu.SemaphoreType.DMA((2,))],
+        grid_spec=pltpu.PrefetchScalarGridSpec(
+            num_scalar_prefetch=1,
+            grid=(4,),
+            in_specs=[
+                whole((rows, D)),
+                pl.BlockSpec((rows, 384), lambda step, me: (0, ((me[0] % 2) ^ other) * 4 + step)),
+            ],
+            out_specs=ANY,
+            scratch_shapes=[pltpu.VMEM((4, D, 384), BF16), pltpu.SemaphoreType.DMA((1,))],
+        ),
+        out_shape=shape_of((16, 2, 48, D), BF16),
         compiler_params=params(),
-        cost_estimate=cost(14e9, 18e6),
+        cost_estimate=cost(COST, 1e5),
         name="up_grad",
     )(me, left, right)
 
@@ -890,19 +941,20 @@
     rows = act.shape[0]
     return pl.pallas_call(
         down_grad_kernel,
-        grid=(5,),
+        grid=(9,),
         in_specs=[
-            SMEM, pl.BlockSpec((rows, D), lambda step: (0, jnp.minimum(step, 3))),
-            whole((rows, D)), whole((rows, D)), whole((rows, D)),
+            SMEM, pl.BlockSpec((rows, 384), lambda step: (0, jnp.minimum(step, 7))),
+            whole((rows, D)), ANY, ANY,
         ],
         out_specs=[ANY] * 2,
         out_shape=[shape_of((16, 3, 48, D), BF16)] * 2,
         scratch_shapes=[
-            pltpu.VMEM((4, 16, 48, D), BF16), pltpu.VMEM((2, D, 384), BF16),
-            pltpu.SemaphoreType.DMA((2,)),
+            pltpu.VMEM((8, 8, 48, D), BF16), pltpu.VMEM((2, D, 384), BF16),
+            pltpu.VMEM((rows, D), BF16), pltpu.VMEM((rows, D), BF16),
+            pltpu.SemaphoreType.DMA((4,)),
         ],
         compiler_params=params(),
-        cost_estimate=cost(18e9, 22e6),
+        cost_estimate=cost(COST, 1e5),
         name="down_grad",
     )(me, act, grad_down, mixed, grad_attn)
 
@@ -986,44 +1038,63 @@
             (counted, 5, 0),
         )
         rects = jnp.concatenate(
-            [up_rect.reshape(48, 2, D).transpose(1, 0, 2), down_rect.reshape(2, 48, D),
+            [up_rect.reshape(48, 2, D).transpose(1, 0, 2),
              jnp.concatenate([proj_rect, notes], axis=1)[None]], axis=0,
         )
-        *near, rects, aux = tied(*near, rects, aux)
+        down_rect = down_rect.reshape(2, 48, D)
+        *near, rects, down_rect, aux = tied(*near, rects, down_rect, aux)
+        planes = [rects] + [swap(rects, "fsdp", mask) for mask in (2, 4, 6)]
         near_a, near_b = jnp.stack(near[0:2]), jnp.stack(near[2:4])
         from_a, from_b = swap(near_a, "fsdp", 1), swap(near_b, "rep", 2)
-        planes = [rects] + [swap(rects, "fsdp", mask) for mask in (2, 4, 6)]
+        from_a, from_b, planes[1] = tied(from_a, from_b, planes[1])
         near_a = jnp.concatenate([near_a, from_a])
         near_b = jnp.concatenate([near_b, from_b])
         far_a, far_b = swap(near_a, "rep", 2), swap(near_b, "fsdp", 1)
-        own = (near_a, far_a, near_b, far_b)
-        own = tied(*own)
-        other = tuple(swap(v, "rep", 1) for v in own)
-        vec, rel, rel_t = notes_of(me, own[0], own[2], own[3])
-        vec, rel, rel_t, *other = tied(vec, rel, rel_t, *other)
-        *state, w_qkv = attend(me, tokens, own + tuple(other), vec, rel, places, 0, STEPS[0])
-        *planes, s0 = tied(*planes, state[0])
-        state[0] = s0
-        near_a, near_b = jnp.stack(planes[0:2]), jnp.stack(planes[2:4])
-        near_a, near_b, *state = tied(near_a, near_b, *state)
-        from_a, from_b = swap(near_a, "fsdp", 1), swap(near_b, "rep", 2)
+        far_a, far_b, planes[2] = tied(far_a, far_b, planes[2])
+        all_a, all_b = jnp.concatenate([near_a, far_a]), jnp.concatenate([near_b, far_b])
+        other_a, other_b = swap(all_a, "rep", 1), swap(all_b, "rep", 1)
+        vec, rel, rel_t = notes_of(me, near_a, near_b, far_b)
+        vec, rel, rel_t, other_a, other_b, planes[3] = tied(
+            vec, rel, rel_t, other_a, other_b, planes[3]
+        )
+        up_a, up_b = jnp.stack(planes[0:2]), jnp.stack(planes[2:4])
+        up_a, up_b, vec = tied(up_a, up_b, vec)
+        from_a, from_b = swap(up_a, "fsdp", 1), swap(up_b, "rep", 2)
+        planes = [down_rect] + [swap(down_rect, "fsdp", mask) for mask in (2, 4, 6)]
+        *state, w_qkv = attend(
+            me, tokens, (all_a, all_b, other_a, other_b), vec, rel, places, 0, STEPS[0]
+        )
+        from_a, from_b, *rest = tied(from_a, from_b, *planes[1:], *state)
+        planes, state = [down_rect] + rest[0:3], rest[3:]
+        up_a, up_b = jnp.concatenate([up_a, from_a]), jnp.concatenate([up_b, from_b])
+        down_a, down_b = jnp.stack(planes[0:2]), jnp.stack(planes[2:4])
+        up_a, up_b, down_a, down_b, *state = tied(up_a, up_b, down_a, down_b, *state)
+        far_up_a, far_up_b = swap(up_a, "rep", 2), swap(up_b, "fsdp", 1)
+        core_up_a, core_up_b = swap(up_a, "rep", 1), swap(up_b, "rep", 1)
         state = attend(me, tokens, w_qkv, vec, rel, places, STEPS[0], STEPS[1], tuple(state))
-        from_a, from_b, *state = tied(from_a, from_b, *state)
-        near_a = jnp.concatenate([near_a, from_a])
-        near_b = jnp.concatenate([near_b, from_b])
-        near_a, near_b, *state = tied(near_a, near_b, *state)
-        far_a, far_b = swap(near_a, "rep", 2), swap(near_b, "fsdp", 1)
-        core_a, core_b = swap(near_a, "rep", 1), swap(near_b, "rep", 1)
-        state = attend(
-            me, tokens, w_qkv, vec, rel, places, sum(STEPS[:2]), STEPS[2], tuple(state)
-        )
-        far_a, far_b, core_a, core_b, *state = tied(far_a, far_b, core_a, core_b, *state)
-        own = (near_a, far_a, near_b, far_b)
-        other = (core_a, swap(far_a, "rep", 1), core_b, swap(far_b, "rep", 1))
-        state = attend(
-            me, tokens, w_qkv, vec, rel, places, sum(STEPS[:3]), STEPS[3], tuple(state)
-        )
-        weights = own + other
+        far_up_a, far_up_b, core_up_a, core_up_b, *state = tied(
+            far_up_a, far_up_b, core_up_a, core_up_b, *state
+        )
+        from_a, from_b = swap(down_a, "fsdp", 1), swap(down_b, "rep", 2)
+        core_far_a, core_far_b = swap(far_up_a, "rep", 1), swap(far_up_b, "rep", 1)
+        state = attend(me, tokens, w_qkv, vec, rel, places, sum(STEPS[:2]), STEPS[2], tuple(state))
+        from_a, from_b, core_far_a, core_far_b, *state = tied(
+            from_a, from_b, core_far_a, core_far_b, *state
+        )
+        up_pieces = (up_a, far_up_a, up_b, far_up_b, core_up_a, core_far_a, core_up_b, core_far_b)
+        down_a, down_b = jnp.concatenate([down_a, from_a]), jnp.concatenate([down_b, from_b])
+        down_a, down_b, *state = tied(down_a, down_b, *state)
+        far_a, far_b = swap(down_a, "rep", 2), swap(down_b, "fsdp", 1)
+        core_a, core_b = swap(down_a, "rep", 1), swap(down_b, "rep", 1)
+        qkv, probs, mixed, first_in = state
+        hidden, second_in, act, slope, w_up, w_proj, vec2, _, total = mlp_up(
+            me, tokens, mixed, aux, up_pieces, True
+        )
+        far_a, far_b, core_a, core_b, hidden = tied(far_a, far_b, core_a, core_b, hidden)
+        down_pieces = (
+            down_a, far_a, down_b, far_b,
+            core_a, swap(far_a, "rep", 1), core_b, swap(far_b, "rep", 1),
+        )
     else:
         gather = lambda v: lax.all_gather(v, "fsdp", axis=0, tiled=True)
         w_qkv, w_proj = gather(qkv_weight), gather(proj_weight)
@@ -1049,77 +1120,97 @@
         fill = jnp.zeros((4, D), F32)
         vec = jnp.concatenate(rows[0:4] + [fill])
         counts = lax.psum(jnp.sum(valid), ("rep", "fsdp")).reshape(1, 1)
-        weights = (w_proj, gather(up_weight), gather(down_weight),
-                   jnp.concatenate(rows[4:8] + [fill]), rows[8], counts)
-        state = attend(me, tokens, w_qkv, vec, rel, places, 0, count)
-    qkv, probs, mixed, first_in = state
-    out, grad_hidden, grad_attn, second_in, act, grad_down, grad_up, sums2, up_sum, *rest = mlp(
-        me, tokens, mixed, teacher, aux, weights, loss_scale * 2.0 / D, in_pieces
+        vec2 = jnp.concatenate(rows[4:8] + [fill])
+        total = jnp.broadcast_to(counts, (1, 128))
+        w_up, down_pieces = gather(up_weight), (gather(down_weight),)
+        qkv, probs, mixed, first_in = attend(me, tokens, w_qkv, vec, rel, places, 0, count)
+        hidden, second_in, act, slope = mlp_up(
+            me, tokens, mixed, aux, (w_proj, w_up, vec2, rows[8]), False
+        )
+    out, grad_hidden, grad_attn, grad_down, grad_up, sums2, up_sum = mlp_down(
+        me, hidden, act, slope, teacher, aux, w_up, vec2, total, down_pieces,
+        loss_scale * 2.0 / D, in_pieces,
     )
-    valid_total = sums2[5, 0]
-    w_proj = rest[0] if in_pieces else w_proj
+    valid_total = total[0, 0]
     flat = lambda v: v.reshape(count * ROWS, v.shape[-1])
     if in_pieces:
+        back_ends = (0, BACK_STEPS[0], BACK_STEPS[0] + BACK_STEPS[1])
+        parts_of = lambda keep, come: lambda at, to: added(keep[at:to], come[at:to])
         keep_d, send_d = down_grad(me, flat(act), flat(grad_down), flat(mixed), flat(grad_attn))
-        send_d, second_in = tied(send_d, second_in)
+        send_d, second_in = tied(send_d, flat(second_in))
         from_d = swap(send_d, "rep", 1)
-        keep_u, send_u = up_grad(me, flat(second_in), flat(grad_up))
-        from_d, keep_u, send_u, grad_attn = tied(from_d, keep_u, send_u, grad_attn)
+        send_u = up_grad(me, second_in, flat(grad_up), 1)
+        from_d, send_u, second_in = tied(from_d, send_u, second_in)
+        sum_d = parts_of(keep_d, from_d)
+        send_a, send_b = sum_d(4, 8), sum_d(12, 16)
+        send_a, send_b, send_u, second_in = tied(send_a, send_b, send_u, second_in)
         from_u = swap(send_u, "rep", 1)
+        from_a, from_b = swap(send_a, "rep", 2), swap(send_b, "fsdp", 1)
+        keep_u = up_grad(me, second_in, flat(grad_up), 0)
+        from_u, keep_u, grad_attn = tied(from_u, keep_u, grad_attn)
+        sum_u = parts_of(keep_u, from_u)
+        send_ua, send_ub = sum_u(4, 8), sum_u(12, 16)
+        send_ua, send_ub, grad_attn = tied(send_ua, send_ub, grad_attn)
         back = (grad_attn, w_proj, qkv, probs, rel_t, places_t)
-        ends = (0,) + tuple(sum(BACK_STEPS[: at + 1]) for at in range(3))
         state = attend_back(*back, 0, BACK_STEPS[0])
-        both = lambda at, to: jnp.concatenate(
-            [added(keep_u[at:to], from_u[at:to]), added(keep_d[at:to], from_d[at:to])], axis=1
-        )
-        from_u, *state = tied(from_u, *state)
-        send_a, send_b = both(4, 8), both(12, 16)
-        send_a, send_b, *state = tied(send_a, send_b, *state)
-        from_a, from_b = swap(send_a, "rep", 2), swap(send_b, "fsdp", 1)
-        state = attend_back(*back, ends[1], BACK_STEPS[1], tuple(state))
         from_a, from_b, *state = tied(from_a, from_b, *state)
-        sum_a, sum_b = added(both(0, 4), from_a), added(both(8, 12), from_b)
-        send_a, send_b = sum_a[2:4], sum_b[2:4]
+        d_a, d_b = added(sum_d(0, 4), from_a), added(sum_d(8, 12), from_b)
+        send_a, send_b = d_a[2:4], d_b[2:4]
         send_a, send_b, *state = tied(send_a, send_b, *state)
         from_a, from_b = swap(send_a, "fsdp", 1), swap(send_b, "rep", 2)
-        state = attend_back(*back, ends[2], BACK_STEPS[2], tuple(state))
-        from_a, from_b, *state = tied(from_a, from_b, *state)
-        sum_a, sum_b = added(sum_a[0:2], from_a), added(sum_b[0:2], from_b)
-        sends = (sum_a[0], sum_a[1], sum_b[0], sum_b[1])
-        *sends, dqkv, rel_grad, qv_sum = tied(*sends, *state)
-        from_z = [swap(v, "fsdp", mask) for v, mask in zip(sends[1:], (2, 4, 6))]
+        from_ua, from_ub = swap(send_ua, "rep", 2), swap(send_ub, "fsdp", 1)
+        state = attend_back(*back, back_ends[1], BACK_STEPS[1], tuple(state))
+        from_a, from_b, from_ua, from_ub, *state = tied(from_a, from_b, from_ua, from_ub, *state)
+        d_a, d_b = added(d_a[0:2], from_a), added(d_b[0:2], from_b)
+        u_a, u_b = added(sum_u(0, 4), from_ua), added(sum_u(8, 12), from_ub)
+        sends_d = (d_a[0], d_a[1], d_b[0], d_b[1])
+        send_ua, send_ub = u_a[2:4], u_b[2:4]
+        *sends_d, send_ua, send_ub, s0, s1, s2 = tied(*sends_d, send_ua, send_ub, *state)
+        from_z = [swap(v, "fsdp", mask) for v, mask in zip(sends_d[1:], (2, 4, 6))]
+        from_ua, from_ub = swap(send_ua, "fsdp", 1), swap(send_ub, "rep", 2)
+        state = attend_back(*back, back_ends[2], BACK_STEPS[2], (s0, s1, s2))
+        from_ua, from_ub, from_z[0], dqkv, rel_grad, qv_sum = tied(
+            from_ua, from_ub, from_z[0], *state
+        )
         keep, send = qkv_grad(me, flat(first_in), flat(dqkv))
         half = count // 2
-        keep, send, dqkv = tied(keep, send, dqkv)
+        from_z[1], from_z[2], keep, send, dqkv = tied(from_z[1], from_z[2], keep, send, dqkv)
+        own_d = sends_d[0].astype(F32)
+        for v in from_z:
+            own_d = own_d + v.astype(F32)
+        u_a, u_b = added(u_a[0:2], from_ua), added(u_b[0:2], from_ub)
+        sends_u = (u_a[0], u_a[1], u_b[0], u_b[1])
+        *sends_u, send, dqkv = tied(*sends_u, send, dqkv)
         from_core = swap(send, "rep", 1)
+        from_z = [swap(v, "fsdp", mask) for v, mask in zip(sends_u[1:], (2, 4, 6))]
         state = input_back(me, dqkv, w_qkv, tokens, grad_hidden, vec, 0, half)
-        from_core, *state = tied(from_core, *state)
-        both = lambda at, to: added(keep[at:to], from_core[at:to])
+        from_core, *rest = tied(from_core, *from_z, *state)
+        from_z, state = rest[0:3], rest[3:]
+        both = parts_of(keep, from_core)
         send_a, send_b = both(4, 8), both(12, 16)
-        send_a, send_b, *state = tied(send_a, send_b, *state)
+        own_u = sends_u[0].astype(F32)
+        for v in from_z:
+            own_u = own_u + v.astype(F32)
+        own = jnp.concatenate([own_u.astype(BF16), own_d.astype(BF16)], axis=0)
+        send_a, send_b, own, *state = tied(send_a, send_b, own, *state)
         from_a, from_b = swap(send_a, "rep", 2), swap(send_b, "fsdp", 1)
+        from_x = swap(own, "rep", 2)
         input_grad, sums1 = input_back(
             me, dqkv, w_qkv, tokens, grad_hidden, vec, half, count - half, tuple(state)
         )
-        *from_z, from_a, from_b, sums1 = tied(*from_z, from_a, from_b, sums1)
+        from_a, from_b, from_x, sums1 = tied(from_a, from_b, from_x, sums1)
         sum_a, sum_b = added(both(0, 4), from_a), added(both(8, 12), from_b)
         from_a, from_b = swap(sum_a[2:4], "fsdp", 1), swap(sum_b[2:4], "rep", 2)
-        own = sends[0].astype(F32)
-        for v in from_z:
-            own = own + v.astype(F32)
-        own = own.astype(BF16)
-        from_x = swap(own, "rep", 2)
+        core_own, core_x = swap(own, "rep", 1), swap(from_x, "rep", 1)
         notes = pack(me, sums1, qv_sum, sums2, up_sum, rel_grad)
-        from_a, from_b, notes = tied(from_a, from_b, notes)
+        from_a, from_b, notes, core_own, core_x = tied(from_a, from_b, notes, core_own, core_x)
         sum_a, sum_b = added(sum_a[0:2], from_a), added(sum_b[0:2], from_b)
         from_z = [swap(v, "fsdp", mask) for v, mask in
                   ((sum_a[1], 2), (sum_b[0], 4), (sum_b[1], 6))]
         notes = notes + swap(notes, "rep", 1)
         notes = notes + swap(notes, "rep", 2)
         notes = notes[0:4] + swap(notes[4:8], "fsdp", 1)
-        d_up, d_down, d_proj = shard(
-            me, (own, from_x, swap(own, "rep", 1), swap(from_x, "rep", 1)), True
-        )
+        d_up, d_down, d_proj = shard(me, (own, from_x, core_own, core_x), True)
         mine = notes[0]
         for at, mask in ((1, 2), (2, 4), (3, 6)):
             mine = mine + swap(notes[at], "fsdp", mask)

time: 457 us -> 395 us (0.86); the launches traced: 448 us -> 391 us
  Pallas kernels: 270 us -> 210 us
  waiting for transfers between devices: 62.3 us -> 43.1 us
  starting transfers between devices: 56.3 us -> 73.3 us
  local copies, waits for them, and re-layouts: 29.4 us -> 43.6 us
  other arithmetic: 23.3 us -> 14.9 us
    pallas_call x3, Pallas kernels: 52.3 us -> 31.4 us  [attend_back(): pl.pallas_call(functools.partial(attend_back_kernel, earlier=len(earlier)...]
    pallas_call x4 -> x3, Pallas kernels: 59.6 us -> 38.8 us  [attend(): pl.pallas_call(functools.partial(attend_kernel, first=first, pieces=piece...]
    unnamed x80 -> x84, local copies, waits for them, and re-layouts: 18.1 us -> 37.9 us
    ppermute x51 -> x67, waiting for transfers between devices: 62.3 us -> 43.1 us  [swap(): return lax.ppermute(values, axis, [(at, at ^ mask) for at in range(size)])]
    ppermute x51 -> x67, starting transfers between devices: 56.3 us -> 73.3 us  [swap(): return lax.ppermute(values, axis, [(at, at ^ mask) for at in range(size)])]
    pallas_call x3 -> x5, Pallas kernels: 116 us -> 108 us  [the longest x1 41.3 us: mlp_down(): pl.pallas_call(functools.partial(down_kernel, group=group, pieces=pieces,...]
    pallas_call x2, Pallas kernels: 20 us -> 14 us  [input_back(): pl.pallas_call(functools.partial(input_kernel, group=group, first=first,...]
    convert_element_type x10 -> x12, other arithmetic: 12.9 us -> 9.78 us  [added(): return (one.astype(F32) + two.astype(F32)).astype(BF16)]
  transfers between devices with their start and end apart: 51 -> 67, of which waited for: 20 -> 12; matrix products, arithmetic and copies ran while one was open for 6% -> 5% of each run, Pallas kernels for 35% -> 38%
where the time goes in v3:
time: 395 us; the launch traced here: 391 us
  Pallas kernels  210 us (53%)
  starting transfers between devices  73.3 us (19%)
  local copies, waits for them, and re-layouts  43.6 us (11%)
  waiting for transfers between devices  43.1 us (11%)
  other arithmetic  14.9 us (4%)
  between operations  6.38 us (2%)
    ppermute x67, starting transfers between devices, swap(): return lax.ppermute(values, axis, [(at, at ^ mask) for at in range(size)])  73.3 us
    ppermute x67, waiting for transfers between devices, swap(): return lax.ppermute(values, axis, [(at, at ^ mask) for at in range(size)])  43.1 us
    pallas_call x1, Pallas kernels, mlp_down(): pl.pallas_call(functools.partial(down_kernel, group=group, pieces=pieces,...  41.3 us
    pallas_call x3, Pallas kernels, attend(): pl.pallas_call(functools.partial(attend_kernel, first=first, pieces=piece...  38.8 us
    unnamed x84, local copies, waits for them, and re-layouts  37.9 us
    pallas_call x3, Pallas kernels, attend_back(): pl.pallas_call(functools.partial(attend_back_kernel, earlier=len(earlier)...  31.4 us
    pallas_call x1, Pallas kernels, mlp_up(): pl.pallas_call(functools.partial(up_kernel, group=group, pieces=pieces),...  25.4 us
    pallas_call x1, Pallas kernels, down_grad(): pl.pallas_call(down_grad_kernel, grid=(9,), in_specs=[SMEM, pl.BlockSpec(...  21 us
  transfers between devices with their start and end apart: 67, of which 12 were waited for; matrix products, arithmetic and copies ran while one was open for 5% of the time, Pallas kernels for 38%

profile of v3, /device:TPU:0, one launch (start us, length us, event | category | flops | bytes accessed | tf_op | source)
XLA Modules:
  0.0 390.8 jit_solution(13315905308025094138)
XLA Ops:
  4.0 3.1 collective-permute-start
  24.5 4.1 %collective-permute-done.5 = bf16[3,48,768]{2,1,0:T(8,128)(2,1)S(1)} collective-permute-done((bf16[3,48,768]{2,1,0:T(8,128)(2,1)S(1)}, bf16[3,48,768]{2,1,0:T(8,128)(2,1)S(1)}, u32[]{:S(2)}, u32[]{:S(2)}) %collective-permute-start.5) | collective-permute-done | bytes 221216 | tf_op jit(solution)/shard_map/ppermute | solution.py:964
  29.8 2.9 collective-permute-start.8
  32.7 7.4 %collective-permute-done.8 = bf16[3,48,768]{2,1,0:T(8,128)(2,1)S(1)} collective-permute-done((bf16[3,48,768]{2,1,0:T(8,128)(2,1)S(1)}, bf16[3,48,768]{2,1,0:T(8,128)(2,1)S(1)}, u32[]{:S(2)}, u32[]{:S(2)}) %collective-permute-start.8) | collective-permute-done | bytes 221216 | tf_op jit(solution)/shard_map/ppermute | solution.py:964
  44.9 5.5 %collective-permute-done.11 = bf16[3,48,768]{2,1,0:T(8,128)(2,1)S(1)} collective-permute-done((bf16[3,48,768]{2,1,0:T(8,128)(2,1)S(1)}, bf16[3,48,768]{2,1,0:T(8,128)(2,1)S(1)}, u32[]{:S(2)}, u32[]{:S(2)}) %collective-permute-start.11) | collective-permute-done | bytes 221216 | tf_op jit(solution)/shard_map/ppermute | solution.py:964
  53.3 3.2 collective-permute-start.14
  59.7 15.8 %attend.3 = (bf16[8,208,2304]{2,1,0:T(8,128)(2,1)S(1)}, bf16[8,12,208,256]{3,2,1,0:T(8,128)(2,1)}, bf16[8,208,768]{2,1,0:T(8,128)(2,1)S(1)}, bf16[8,208,768]{2,1,0:T(8,128)(2,1)S(1)}, bf16[768,2304]{1,0:T(8,128)(2,1)S(1)}) custom-call(s32[3]{0:T(128)S(1)} %pad_add_fusion.1.me_ref.refs_0_.base_ref, bf16[8,196,768]{2,1,0:T(8,128)(2,1)S(1)} %copy.81.refs_1_.tok_ref, ...), custom_call_target="tpu_custom_call" | custom-call | flops 100000000 | bytes 100000 | tf_op jit(solution)/shard_map/attend/pallas_call | solution.py:690
  78.6 17.7 %attend.4 = (bf16[8,208,2304]{2,1,0:T(8,128)(2,1)S(1)}, bf16[8,12,208,256]{3,2,1,0:T(8,128)(2,1)}, bf16[8,208,768]{2,1,0:T(8,128)(2,1)S(1)}, bf16[8,208,768]{2,1,0:T(8,128)(2,1)S(1)}) custom-call(s32[3]{0:T(128)S(1)} %pad_add_fusion.1.me_ref.refs_0_.base_ref, ...), custom_call_target="tpu_custom_call", output_to_operand_aliasing={{0}: (6, {}), {1}: (7, {}), {2}: (8, {}), {3}: (9, {})} | custom-call | flops 100000000 | bytes 100000 | tf_op jit(solution)/shard_map/attend/pallas_call | solution.py:690
  98.7 5.4 %attend.5 = (bf16[8,208,2304]{2,1,0:T(8,128)(2,1)S(1)}, bf16[8,12,208,256]{3,2,1,0:T(8,128)(2,1)}, bf16[8,208,768]{2,1,0:T(8,128)(2,1)S(1)}, bf16[8,208,768]{2,1,0:T(8,128)(2,1)S(1)}) custom-call(s32[3]{0:T(128)S(1)} %pad_add_fusion.1.me_ref.refs_0_.base_ref, ...), custom_call_target="tpu_custom_call", output_to_operand_aliasing={{0}: (6, {}), {1}: (7, {}), {2}: (8, {}), {3}: (9, {})} | custom-call | flops 100000000 | bytes 100000 | tf_op jit(solution)/shard_map/attend/pallas_call | solution.py:690
  110.5 25.4 %mlp_up.1 = (f32[8,208,768]{2,1,0:T(8,128)}, bf16[8,208,768]{2,1,0:T(8,128)(2,1)}, bf16[8,208,3072]{2,1,0:T(8,128)(2,1)}, bf16[8,208,3072]{2,1,0:T(8,128)(2,1)},...) custom-call(s32[3]{0:T(128)S(1)} %pad_add_fusion.1.me_ref.refs_0_.ba, ...), custom_call_target="tpu_custom_call" | custom-call | flops 800000000 | bytes 100000 | tf_op jit(solution)/shard_map/mlp_up/pallas_call | solution.py:721
  136.6 4.3 %copy.85.refs_4_ = bf16[8,196,768]{2,1,0:T(8,128)(2,1)} copy(bf16[8,196,768]{2,0,1:T(8,128)(2,1)} %param.21) | data formatting | bytes 4816896 | tf_op args[1]
  146.0 41.3 %mlp_down.1 = (bf16[8,196,768]{2,1,0:T(8,128)(2,1)}, f32[8,208,768]{2,1,0:T(8,128)}, bf16[8,208,768]{2,1,0:T(8,128)(2,1)}, bf16[8,208,768]{2,1,0:T(8,128)(2,1)},...) custom-call(s32[3]{0:T(128)S(1)} %pad_add_fusion.1.me_ref.refs_0_.base_ref, ...), custom_call_target="tpu_custom_call" | custom-call | flops 800000000 | bytes 100000 | tf_op jit(solution)/shard_map/mlp_down/pallas_call | solution.py:745
  190.8 21.0 %down_grad.1 = (bf16[16,3,48,768]{3,2,1,0:T(8,128)(2,1)S(1)}, bf16[16,3,48,768]{3,2,1,0:T(8,128)(2,1)}) custom-call(s32[3]{0:T(128)S(1)} %pad_add_fusion.1.me_ref.refs_0_.base_ref, bf16[1664,3072]{1,0:T(8,128)(2,1)} %bitcast.116, bf16[1664,768]{1,0:T(8,128)(2,1)S(1)} %bitcast.114, bf16[1664,768]{1,0:T(8,128)(2,1)S(1)} %bitcast.107, ...), custom_call_target="tpu_custom_call" | custom-call | flops 100000000 | bytes 100000 | tf_op jit(solution)/shard_map/down_grad/pallas_call | solution.py:942
  211.9 3.9 copy-done.10
  215.8 10.4 %up_grad.2 = bf16[16,2,48,768]{3,2,1,0:T(8,128)(2,1)S(1)} custom-call(s32[3]{0:T(128)S(1)} %pad_add_fusion.1.me_ref.refs_0_.base_ref, bf16[1664,768]{1,0:T(8,128)(2,1)S(1)} %bitcast.112, bf16[1664,3072]{1,0:T(8,128)(2,1)S(1)} %bitcast.108), custom_call_target="tpu_custom_call" | custom-call | flops 100000000 | bytes 100000 | tf_op jit(solution)/shard_map/up_grad/pallas_call | solution.py:921
  226.2 3.1 add_convert_fusion.3
  231.1 10.4 %up_grad.3 = bf16[16,2,48,768]{3,2,1,0:T(8,128)(2,1)S(1)} custom-call(s32[3]{0:T(128)S(1)} %pad_add_fusion.1.me_ref.refs_0_.base_ref, bf16[1664,768]{1,0:T(8,128)(2,1)S(1)} %bitcast.113, bf16[1664,3072]{1,0:T(8,128)(2,1)S(1)} %bitcast.109), custom_call_target="tpu_custom_call" | custom-call | flops 100000000 | bytes 100000 | tf_op jit(solution)/shard_map/up_grad/pallas_call | solution.py:921
  243.6 8.1 %attend_back.3 = (bf16[8,208,2304]{2,1,0:T(8,128)(2,1)S(1)}, f32[128,128]{1,0:T(8,128)S(1)}, f32[2,768]{1,0:T(2,128)S(1)}) custom-call(bf16[8,208,768]{2,1,0:T(8,128)(2,1)S(1)} %copy-done.12, bf16[768,768]{1,0:T(8,128)(2,1)S(1)} %copy-done.17, bf16[8,208,2304]{2,1,0:T(8,128)(2,1)S(1)} %get-tuple-element.318.refs_2_, ...), custom_call_target="tpu_custom_call" | custom-call | flops 100000000 | bytes 100000 | tf_op jit(solution)/shard_map/attend_back/pallas_call | solution.py:767
  258.5 15.2 %attend_back.4 = (bf16[8,208,2304]{2,1,0:T(8,128)(2,1)S(1)}, f32[128,128]{1,0:T(8,128)S(1)}, f32[2,768]{1,0:T(2,128)S(1)}) custom-call(bf16[8,208,768]{2,1,0:T(8,128)(2,1)S(1)} %copy-done.12, bf16[768,768]{1,0:T(8,128)(2,1)S(1)} %copy-done.17, bf16[8,208,2304]{2,1,0:T(8,128)(2,1)S(1)} %get-tuple-element.318.refs_2_, ...), custom_call_target="tpu_custom_call", output_to_operand_aliasing={{0}: (6, {})} | custom-call | flops 100000000 | bytes 100000 | tf_op jit(solution)/shard_map/attend_back/pallas_call | solution.py:767
  273.7 3.5 collective-permute-done.35
  285.4 8.1 %attend_back.5 = (bf16[8,208,2304]{2,1,0:T(8,128)(2,1)S(1)}, f32[128,128]{1,0:T(8,128)S(1)}, f32[2,768]{1,0:T(2,128)S(1)}) custom-call(bf16[8,208,768]{2,1,0:T(8,128)(2,1)S(1)} %copy-done.12, bf16[768,768]{1,0:T(8,128)(2,1)S(1)} %copy-done.17, bf16[8,208,2304]{2,1,0:T(8,128)(2,1)S(1)} %get-tuple-element.318.refs_2_, ...), custom_call_target="tpu_custom_call", output_to_operand_aliasing={{0}: (6, {})} | custom-call | flops 100000000 | bytes 100000 | tf_op jit(solution)/shard_map/attend_back/pallas_call | solution.py:767
  293.5 3.1 copy-done.2
  296.7 3.2 copy-done.3
  299.9 9.7 %qkv_grad.1 = (bf16[16,48,1152]{2,1,0:T(8,128)(2,1)S(1)}, bf16[16,48,1152]{2,1,0:T(8,128)(2,1)S(1)}) custom-call(s32[3]{0:T(128)S(1)} %pad_add_fusion.1.me_ref.refs_0_.base_ref, bf16[1664,768]{1,0:T(8,128)(2,1)S(1)} %bitcast.111, bf16[1664,2304]{1,0:T(8,128)(2,1)S(1)} %bitcast.106), custom_call_target="tpu_custom_call" | custom-call | flops 100000000 | bytes 100000 | tf_op jit(solution)/shard_map/qkv_grad/pallas_call | solution.py:906
  310.0 2.9 collective-permute-start.46
  316.8 7.1 %input_back.2 = (f32[8,196,768]{2,1,0:T(8,128)S(1)}, f32[2,768]{1,0:T(2,128)S(1)}) custom-call(s32[3]{0:T(128)S(1)} %pad_add_fusion.1.me_ref.refs_0_.base_ref, bf16[8,208,2304]{2,1,0:T(8,128)(2,1)} %copy-done.2, bf16[768,2304]{1,0:T(8,128)(2,1)S(1)} %copy-done.7, bf16[8,196,768]{2,1,0:T(8,128)(2,1)S(1)} %copy-done.5, f32[8,208,768]{2,1,0:T(8,128)S(1)} %copy-done.15, ...), custom_call_target="tpu_custom_call" | custom-call | flops 100000000 | bytes 100000 | tf_op jit(solution)/shard_map/input_back/pallas_call | solution.py:792
  327.4 6.9 %input_back.3 = (f32[8,196,768]{2,1,0:T(8,128)S(1)}, f32[2,768]{1,0:T(2,128)S(1)}) custom-call(s32[3]{0:T(128)S(1)} %pad_add_fusion.1.me_ref.refs_0_.base_ref, bf16[8,208,2304]{2,1,0:T(8,128)(2,1)} %copy-done.2, bf16[768,2304]{1,0:T(8,128)(2,1)S(1)} %copy-done.7, bf16[8,196,768]{2,1,0:T(8,128)(2,1)S(1)} %copy-done.5, ...), custom_call_target="tpu_custom_call", output_to_operand_aliasing={{0}: (6, {})} | custom-call | flops 100000000 | bytes 100000 | tf_op jit(solution)/shard_map/input_back/pallas_call | solution.py:792
  334.3 9.8 %collective-permute-done.50.refs_1_ = bf16[5,48,768]{2,1,0:T(8,128)(2,1)S(1)} collective-permute-done((bf16[5,48,768]{2,1,0:T(8,128)(2,1)S(1)}, bf16[5,48,768]{2,1,0:T(8,128)(2,1)S(1)}, u32[]{:S(2)}, u32[]{:S(2)}) %collective-permute-start.50) | collective-permute-done | bytes 368672 | tf_op jit(solution)/shard_map/ppermute | solution.py:964
  349.4 3.0 collective-permute-done.51
  353.1 3.1 collective-permute-start.61
  360.5 7.1 %collective-permute-done.62 = bf16[48,1152]{1,0:T(8,128)(2,1)S(1)} collective-permute-done((bf16[48,1152]{1,0:T(8,128)(2,1)S(1)}, bf16[48,1152]{1,0:T(8,128)(2,1)S(1)}, u32[]{:S(2)}, u32[]{:S(2)}) %collective-permute-start.62) | collective-permute-done | bytes 110624 | tf_op jit(solution)/shard_map/ppermute | solution.py:964
  372.4 3.7 copy.89
  (276 shorter events, 105.1 us)
Async XLA Ops:
  4.0 14.3 %collective-permute-start = (bf16[48,1280]{1,0:T(8,128)(2,1)S(1)}, bf16[48,1280]{1,0:T(8,128)(2,1)S(1)}, u32[]{:S(2)}, u32[]{:S(2)}) collective-permute-start(bf16[48,1280]{1,0:T(8,128)(2,1)S(1)} %pad_maximum_fusion.16), channel_id=1, source_target_pairs={{0,2},{1,3},{2,0},{3,1},{4,6},{5,7},{6,4},{7,5},{8,10},{9,11},{10,... | collective-permute-start | bytes 368648 | tf_op jit(solution)/shard_map/ppermute | solution.py:964
  50.4 25.0 %collective-permute-start.12 = (bf16[2,3,48,768]{3,2,1,0:T(8,128)(2,1)S(1)}, bf16[2,3,48,768]{3,2,1,0:T(8,128)(2,1)S(1)}, u32[]{:S(2)}, u32[]{:S(2)}) collective-permute-start(bf16[2,3,48,768]{3,2,1,0:T(8,128)(2,1)S(1)} %pad_maximum_fusion.8), channel_id=1, source_target_pairs={{0,1},{1,0},{2,3},{3,2},{4,5},{5,4},{6,7},{7,6},{8,9},{9,8},{10,11... | collective-permute-start | bytes 1327112 | tf_op jit(solution)/shard_map/ppermute | solution.py:964
  51.8 23.7 %collective-permute-start.13 = (bf16[2,3,48,768]{3,2,1,0:T(8,128)(2,1)S(1)}, bf16[2,3,48,768]{3,2,1,0:T(8,128)(2,1)S(1)}, u32[]{:S(2)}, u32[]{:S(2)}) collective-permute-start(bf16[2,3,48,768]{3,2,1,0:T(8,128)(2,1)S(1)} %pad_maximum_fusion.9), channel_id=1, source_target_pairs={{0,16},{8,24},{16,0},{24,8},{1,17},{9,25},{17,1},{25,9},{2,18},{10... | collective-permute-start | bytes 1327112 | tf_op jit(solution)/shard_map/ppermute | solution.py:964
  53.3 22.2 %collective-permute-start.14 = (bf16[2,48,768]{2,1,0:T(8,128)(2,1)S(1)}, bf16[2,48,768]{2,1,0:T(8,128)(2,1)S(1)}, u32[]{:S(2)}, u32[]{:S(2)}) collective-permute-start(bf16[2,48,768]{2,1,0:T(8,128)(2,1)S(1)} %bitcast.132), channel_id=1, source_target_pairs={{0,2},{1,3},{2,0},{3,1},{4,6},{5,7},{6,4},{7,5},{8,10},{9,11},{10,... | collective-permute-start | bytes 442376 | tf_op jit(solution)/shard_map/ppermute | solution.py:964
  56.5 18.9 %collective-permute-start.15 = (bf16[2,48,768]{2,1,0:T(8,128)(2,1)S(1)}, bf16[2,48,768]{2,1,0:T(8,128)(2,1)S(1)}, u32[]{:S(2)}, u32[]{:S(2)}) collective-permute-start(bf16[2,48,768]{2,1,0:T(8,128)(2,1)S(1)} %bitcast.133), channel_id=1, source_target_pairs={{0,4},{1,5},{2,6},{3,7},{4,0},{5,1},{6,2},{7,3},{8,12},{9,13},{10,... | collective-permute-start | bytes 442376 | tf_op jit(solution)/shard_map/ppermute | solution.py:964
  57.7 17.8 %collective-permute-start.16 = (bf16[2,48,768]{2,1,0:T(8,128)(2,1)S(1)}, bf16[2,48,768]{2,1,0:T(8,128)(2,1)S(1)}, u32[]{:S(2)}, u32[]{:S(2)}) collective-permute-start(bf16[2,48,768]{2,1,0:T(8,128)(2,1)S(1)} %bitcast.134), channel_id=1, source_target_pairs={{0,6},{1,7},{2,4},{3,5},{4,2},{5,3},{6,0},{7,1},{8,14},{9,15},{10,... | collective-permute-start | bytes 442376 | tf_op jit(solution)/shard_map/ppermute | solution.py:964
  75.8 20.5 %collective-permute-start.19 = (bf16[4,3,48,768]{3,2,1,0:T(8,128)(2,1)S(1)}, bf16[4,3,48,768]{3,2,1,0:T(8,128)(2,1)S(1)}, u32[]{:S(2)}, u32[]{:S(2)}) collective-permute-start(bf16[4,3,48,768]{3,2,1,0:T(8,128)(2,1)S(1)} %pad_maximum_fusion.2.refs_4_), channel_id=1, source_target_pairs={{0,16},{8,24},{16,0},{24,8},{1,17},{9,25},{17,1},{25,9},{2,18},{10... | collective-permute-start | bytes 2654216 | tf_op jit(solution)/shard_map/ppermute | solution.py:964
  77.3 19.4 %collective-permute-start.20 = (bf16[4,3,48,768]{3,2,1,0:T(8,128)(2,1)S(1)}, bf16[4,3,48,768]{3,2,1,0:T(8,128)(2,1)S(1)}, u32[]{:S(2)}, u32[]{:S(2)}) collective-permute-start(bf16[4,3,48,768]{3,2,1,0:T(8,128)(2,1)S(1)} %pad_maximum_fusion.3.refs_6_), channel_id=1, source_target_pairs={{0,1},{1,0},{2,3},{3,2},{4,5},{5,4},{6,7},{7,6},{8,9},{9,8},{10,11... | collective-permute-start | bytes 2654216 | tf_op jit(solution)/shard_map/ppermute | solution.py:964
  78.1 18.7 %collective-permute-start.21 = (bf16[4,3,48,768]{3,2,1,0:T(8,128)(2,1)S(1)}, bf16[4,3,48,768]{3,2,1,0:T(8,128)(2,1)S(1)}, u32[]{:S(2)}, u32[]{:S(2)}) collective-permute-start(bf16[4,3,48,768]{3,2,1,0:T(8,128)(2,1)S(1)} %pad_maximum_fusion.2.refs_4_), channel_id=1, source_target_pairs={{0,8},{8,0},{16,24},{24,16},{1,9},{9,1},{17,25},{25,17},{2,10},{10... | collective-permute-start | bytes 2654216 | tf_op jit(solution)/shard_map/ppermute | solution.py:964
  78.1 18.7 %collective-permute-start.22 = (bf16[4,3,48,768]{3,2,1,0:T(8,128)(2,1)S(1)}, bf16[4,3,48,768]{3,2,1,0:T(8,128)(2,1)S(1)}, u32[]{:S(2)}, u32[]{:S(2)}) collective-permute-start(bf16[4,3,48,768]{3,2,1,0:T(8,128)(2,1)S(1)} %pad_maximum_fusion.3.refs_6_), channel_id=1, source_target_pairs={{0,8},{8,0},{16,24},{24,16},{1,9},{9,1},{17,25},{25,17},{2,10},{10... | collective-permute-start | bytes 2654216 | tf_op jit(solution)/shard_map/ppermute | solution.py:964
  107.2 28.7 %collective-permute-start.25 = (bf16[4,2,48,768]{3,2,1,0:T(8,128)(2,1)S(1)}, bf16[4,2,48,768]{3,2,1,0:T(8,128)(2,1)S(1)}, u32[]{:S(2)}, u32[]{:S(2)}) collective-permute-start(bf16[4,2,48,768]{3,2,1,0:T(8,128)(2,1)S(1)} %pad_maximum_fusion.4.refs_9_), channel_id=1, source_target_pairs={{0,16},{8,24},{16,0},{24,8},{1,17},{9,25},{17,1},{25,9},{2,18},{10... | collective-permute-start | bytes 1769480 | tf_op jit(solution)/shard_map/ppermute | solution.py:964
  108.8 27.2 %collective-permute-start.26 = (bf16[4,2,48,768]{3,2,1,0:T(8,128)(2,1)S(1)}, bf16[4,2,48,768]{3,2,1,0:T(8,128)(2,1)S(1)}, u32[]{:S(2)}, u32[]{:S(2)}) collective-permute-start(bf16[4,2,48,768]{3,2,1,0:T(8,128)(2,1)S(1)} %pad_maximum_fusion.5.refs_11_), channel_id=1, source_target_pairs={{0,1},{1,0},{2,3},{3,2},{4,5},{5,4},{6,7},{7,6},{8,9},{9,8},{10,11... | collective-permute-start | bytes 1769480 | tf_op jit(solution)/shard_map/ppermute | solution.py:964
  110.0 26.0 %collective-permute-start.27 = (bf16[4,2,48,768]{3,2,1,0:T(8,128)(2,1)S(1)}, bf16[4,2,48,768]{3,2,1,0:T(8,128)(2,1)S(1)}, u32[]{:S(2)}, u32[]{:S(2)}) collective-permute-start(bf16[4,2,48,768]{3,2,1,0:T(8,128)(2,1)S(1)} %pad_maximum_fusion.4.refs_9_), channel_id=1, source_target_pairs={{0,8},{8,0},{16,24},{24,16},{1,9},{9,1},{17,25},{25,17},{2,10},{10... | collective-permute-start | bytes 1769480 | tf_op jit(solution)/shard_map/ppermute | solution.py:964
  110.0 26.0 %collective-permute-start.28 = (bf16[4,2,48,768]{3,2,1,0:T(8,128)(2,1)S(1)}, bf16[4,2,48,768]{3,2,1,0:T(8,128)(2,1)}, u32[]{:S(2)}, u32[]{:S(2)}) collective-permute-start(bf16[4,2,48,768]{3,2,1,0:T(8,128)(2,1)S(1)} %pad_maximum_fusion.5.refs_11_), channel_id=1, source_target_pairs={{0,8},{8,0},{16,24},{24,16},{1,9},{9,1},{17,25},{25,17},{2,10},{10... | collective-permute-start | bytes 1769480 | tf_op jit(solution)/shard_map/ppermute | solution.py:964
  211.8 14.4 %collective-permute-start.31 = (bf16[16,3,48,768]{3,2,1,0:T(8,128)(2,1)}, bf16[16,3,48,768]{3,2,1,0:T(8,128)(2,1)}, u32[]{:S(2)}, u32[]{:S(2)}) collective-permute-start(bf16[16,3,48,768]{3,2,1,0:T(8,128)(2,1)} %get-tuple-element.303), channel_id=1, source_target_pairs={{0,8},{8,0},{16,24},{24,16},{1,9},{9,1},{17,25},{25,17},{2,10},{10... | collective-permute-start | bytes 10616840 | tf_op jit(solution)/shard_map/ppermute | solution.py:964
  229.8 21.9 %collective-permute-start.32 = (bf16[4,3,48,768]{3,2,1,0:T(8,128)(2,1)}, bf16[4,3,48,768]{3,2,1,0:T(8,128)(2,1)S(1)}, u32[]{:S(2)}, u32[]{:S(2)}) collective-permute-start(bf16[4,3,48,768]{3,2,1,0:T(8,128)(2,1)} %get-tuple-element.309), channel_id=1, source_target_pairs={{0,16},{8,24},{16,0},{24,8},{1,17},{9,25},{17,1},{25,9},{2,18},{10... | collective-permute-start | bytes 2654216 | tf_op jit(solution)/shard_map/ppermute | solution.py:964
  230.3 21.6 %collective-permute-start.33 = (bf16[4,3,48,768]{3,2,1,0:T(8,128)(2,1)}, bf16[4,3,48,768]{3,2,1,0:T(8,128)(2,1)}, u32[]{:S(2)}, u32[]{:S(2)}) collective-permute-start(bf16[4,3,48,768]{3,2,1,0:T(8,128)(2,1)} %get-tuple-element.310), channel_id=1, source_target_pairs={{0,1},{1,0},{2,3},{3,2},{4,5},{5,4},{6,7},{7,6},{8,9},{9,8},{10,11... | collective-permute-start | bytes 2654216 | tf_op jit(solution)/shard_map/ppermute | solution.py:964
  251.9 25.3 %collective-permute-start.37 = (bf16[4,2,48,768]{3,2,1,0:T(8,128)(2,1)S(1)}, bf16[4,2,48,768]{3,2,1,0:T(8,128)(2,1)S(1)}, u32[]{:S(2)}, u32[]{:S(2)}) collective-permute-start(bf16[4,2,48,768]{3,2,1,0:T(8,128)(2,1)S(1)} %get-tuple-element.331), channel_id=1, source_target_pairs={{0,16},{8,24},{16,0},{24,8},{1,17},{9,25},{17,1},{25,9},{2,18},{10... | collective-permute-start | bytes 1769480 | tf_op jit(solution)/shard_map/ppermute | solution.py:964
  253.4 23.8 %collective-permute-start.38 = (bf16[4,2,48,768]{3,2,1,0:T(8,128)(2,1)S(1)}, bf16[4,2,48,768]{3,2,1,0:T(8,128)(2,1)S(1)}, u32[]{:S(2)}, u32[]{:S(2)}) collective-permute-start(bf16[4,2,48,768]{3,2,1,0:T(8,128)(2,1)S(1)} %get-tuple-element.332), channel_id=1, source_target_pairs={{0,1},{1,0},{2,3},{3,2},{4,5},{5,4},{6,7},{7,6},{8,9},{9,8},{10,11... | collective-permute-start | bytes 1769480 | tf_op jit(solution)/shard_map/ppermute | solution.py:964
  256.9 20.3 %collective-permute-start.35 = (bf16[2,3,48,768]{3,2,1,0:T(8,128)(2,1)S(1)}, bf16[2,3,48,768]{3,2,1,0:T(8,128)(2,1)S(1)}, u32[]{:S(2)}, u32[]{:S(2)}) collective-permute-start(bf16[2,3,48,768]{3,2,1,0:T(8,128)(2,1)S(1)} %slice.269), channel_id=1, source_target_pairs={{0,1},{1,0},{2,3},{3,2},{4,5},{5,4},{6,7},{7,6},{8,9},{9,8},{10,11... | collective-permute-start | bytes 1327112 | tf_op jit(solution)/shard_map/ppermute | solution.py:964
  257.9 19.3 %collective-permute-start.36 = (bf16[2,3,48,768]{3,2,1,0:T(8,128)(2,1)S(1)}, bf16[2,3,48,768]{3,2,1,0:T(8,128)(2,1)S(1)}, u32[]{:S(2)}, u32[]{:S(2)}) collective-permute-start(bf16[2,3,48,768]{3,2,1,0:T(8,128)(2,1)S(1)} %slice.270), channel_id=1, source_target_pairs={{0,16},{8,24},{16,0},{24,8},{1,17},{9,25},{17,1},{25,9},{2,18},{10... | collective-permute-start | bytes 1327112 | tf_op jit(solution)/shard_map/ppermute | solution.py:964
  279.2 17.4 %collective-permute-start.41 = (bf16[2,2,48,768]{3,2,1,0:T(8,128)(2,1)S(1)}, bf16[2,2,48,768]{3,2,1,0:T(8,128)(2,1)S(1)}, u32[]{:S(2)}, u32[]{:S(2)}) collective-permute-start(bf16[2,2,48,768]{3,2,1,0:T(8,128)(2,1)S(1)} %slice.276), channel_id=1, source_target_pairs={{0,1},{1,0},{2,3},{3,2},{4,5},{5,4},{6,7},{7,6},{8,9},{9,8},{10,11... | collective-permute-start | bytes 884744 | tf_op jit(solution)/shard_map/ppermute | solution.py:964
  280.5 16.2 %collective-permute-start.42 = (bf16[2,2,48,768]{3,2,1,0:T(8,128)(2,1)S(1)}, bf16[2,2,48,768]{3,2,1,0:T(8,128)(2,1)S(1)}, u32[]{:S(2)}, u32[]{:S(2)}) collective-permute-start(bf16[2,2,48,768]{3,2,1,0:T(8,128)(2,1)S(1)} %slice.277), channel_id=1, source_target_pairs={{0,16},{8,24},{16,0},{24,8},{1,17},{9,25},{17,1},{25,9},{2,18},{10... | collective-permute-start | bytes 884744 | tf_op jit(solution)/shard_map/ppermute | solution.py:964
  281.0 15.6 %collective-permute-start.43 = (bf16[3,48,768]{2,1,0:T(8,128)(2,1)S(1)}, bf16[3,48,768]{2,1,0:T(8,128)(2,1)S(1)}, u32[]{:S(2)}, u32[]{:S(2)}) collective-permute-start(bf16[3,48,768]{2,1,0:T(8,128)(2,1)S(1)} %get-tuple-element.351), channel_id=1, source_target_pairs={{0,2},{1,3},{2,0},{3,1},{4,6},{5,7},{6,4},{7,5},{8,10},{9,11},{10,... | collective-permute-start | bytes 663560 | tf_op jit(solution)/shard_map/ppermute | solution.py:964
  281.9 27.8 %collective-permute-start.39 = (bf16[3,48,768]{2,1,0:T(8,128)(2,1)S(1)}, bf16[3,48,768]{2,1,0:T(8,128)(2,1)S(1)}, u32[]{:S(2)}, u32[]{:S(2)}) collective-permute-start(bf16[3,48,768]{2,1,0:T(8,128)(2,1)S(1)} %get-tuple-element.346), channel_id=1, source_target_pairs={{0,4},{1,5},{2,6},{3,7},{4,0},{5,1},{6,2},{7,3},{8,12},{9,13},{10,... | collective-permute-start | bytes 663560 | tf_op jit(solution)/shard_map/ppermute | solution.py:964
  283.9 25.7 %collective-permute-start.40 = (bf16[3,48,768]{2,1,0:T(8,128)(2,1)S(1)}, bf16[3,48,768]{2,1,0:T(8,128)(2,1)S(1)}, u32[]{:S(2)}, u32[]{:S(2)}) collective-permute-start(bf16[3,48,768]{2,1,0:T(8,128)(2,1)S(1)} %get-tuple-element.347), channel_id=1, source_target_pairs={{0,6},{1,7},{2,4},{3,5},{4,2},{5,3},{6,0},{7,1},{8,14},{9,15},{10,... | collective-permute-start | bytes 663560 | tf_op jit(solution)/shard_map/ppermute | solution.py:964
  309.9 14.2 %collective-permute-start.44 = (bf16[16,48,1152]{2,1,0:T(8,128)(2,1)S(1)}, bf16[16,48,1152]{2,1,0:T(8,128)(2,1)S(1)}, u32[]{:S(2)}, u32[]{:S(2)}) collective-permute-start(bf16[16,48,1152]{2,1,0:T(8,128)(2,1)S(1)} %get-tuple-element.366), channel_id=1, source_target_pairs={{0,8},{8,0},{16,24},{24,16},{1,9},{9,1},{17,25},{25,17},{2,10},{10... | collective-permute-start | bytes 5308424 | tf_op jit(solution)/shard_map/ppermute | solution.py:964
  309.9 14.1 %collective-permute-start.45 = (bf16[2,48,768]{2,1,0:T(8,128)(2,1)S(1)}, bf16[2,48,768]{2,1,0:T(8,128)(2,1)S(1)}, u32[]{:S(2)}, u32[]{:S(2)}) collective-permute-start(bf16[2,48,768]{2,1,0:T(8,128)(2,1)S(1)} %get-tuple-element.367), channel_id=1, source_target_pairs={{0,2},{1,3},{2,0},{3,1},{4,6},{5,7},{6,4},{7,5},{8,10},{9,11},{10,... | collective-permute-start | bytes 442376 | tf_op jit(solution)/shard_map/ppermute | solution.py:964
  324.5 19.6 %collective-permute-start.48 = (bf16[4,48,1152]{2,1,0:T(8,128)(2,1)S(1)}, bf16[4,48,1152]{2,1,0:T(8,128)(2,1)S(1)}, u32[]{:S(2)}, u32[]{:S(2)}) collective-permute-start(bf16[4,48,1152]{2,1,0:T(8,128)(2,1)S(1)} %get-tuple-element.385), channel_id=1, source_target_pairs={{0,16},{8,24},{16,0},{24,8},{1,17},{9,25},{17,1},{25,9},{2,18},{10... | collective-permute-start | bytes 1327112 | tf_op jit(solution)/shard_map/ppermute | solution.py:964
  326.0 18.1 %collective-permute-start.49 = (bf16[4,48,1152]{2,1,0:T(8,128)(2,1)S(1)}, bf16[4,48,1152]{2,1,0:T(8,128)(2,1)S(1)}, u32[]{:S(2)}, u32[]{:S(2)}) collective-permute-start(bf16[4,48,1152]{2,1,0:T(8,128)(2,1)S(1)} %get-tuple-element.386), channel_id=1, source_target_pairs={{0,1},{1,0},{2,3},{3,2},{4,5},{5,4},{6,7},{7,6},{8,9},{9,8},{10,11... | collective-permute-start | bytes 1327112 | tf_op jit(solution)/shard_map/ppermute | solution.py:964
  326.9 17.2 %collective-permute-start.50 = (bf16[5,48,768]{2,1,0:T(8,128)(2,1)S(1)}, bf16[5,48,768]{2,1,0:T(8,128)(2,1)S(1)}, u32[]{:S(2)}, u32[]{:S(2)}) collective-permute-start(bf16[5,48,768]{2,1,0:T(8,128)(2,1)S(1)} %pad_maximum_fusion.10.refs_0_), channel_id=1, source_target_pairs={{0,16},{8,24},{16,0},{24,8},{1,17},{9,25},{17,1},{25,9},{2,18},{10... | collective-permute-start | bytes 1105928 | tf_op jit(solution)/shard_map/ppermute | solution.py:964
  327.4 22.0 %collective-permute-start.53 = (bf16[5,48,768]{2,1,0:T(8,128)(2,1)S(1)}, bf16[5,48,768]{2,1,0:T(8,128)(2,1)S(1)}, u32[]{:S(2)}, u32[]{:S(2)}) collective-permute-start(bf16[5,48,768]{2,1,0:T(8,128)(2,1)S(1)} %pad_maximum_fusion.10.refs_0_), channel_id=1, source_target_pairs={{0,8},{8,0},{16,24},{24,16},{1,9},{9,1},{17,25},{25,17},{2,10},{10... | collective-permute-start | bytes 1105928 | tf_op jit(solution)/shard_map/ppermute | solution.py:964
  (73 other events, 767.2 us)

commit v4 on v3

--- a/solution.py
+++ b/solution.py
@@ -204,17 +204,15 @@
     at += 3 + earlier
     qkv_ref, prob_ref, mix_ref, fin_ref = refs[at : at + 4]
     if pieces:
-        w_ref, x_ref, sem = refs[at + 4 :]
+        w_ref, sem = refs[at + 4 :]
 
         @pl.when(pl.program_id(0) == 0)
         def _():
             load_first(base_ref, refs[2 : 2 + pieces], w_ref, sem)
     else:
-        w_ref, x_ref = refs[2], refs[at + 4]
+        w_ref = refs[2]
     keep = keep_column(base_ref, pl.program_id(0) + first)
-    x_ref[pl.ds(192, 16), :] = jnp.zeros((16, D), F32)
-    x_ref[pl.ds(0, SLOTS), :] = tok_ref[0].astype(F32)
-    scaled, _ = norm_parts(x_ref[...])
+    scaled, _ = norm_parts(tok_ref[0].astype(F32))
     first_in = (keep * (scaled * vec_ref[0:1, :] + vec_ref[1:2, :])).astype(BF16)
     fin_ref[0] = first_in
     for part in range(3):
@@ -320,7 +318,7 @@
     hid_ref, si_ref, act_ref, slope_ref = refs[at : at + 4]
     at += 4
     if pieces:
-        up_ref, wp_ref, vec_ref, ub_ref, total_ref, t_ref, notes, sem = refs[at:]
+        up_ref, wp_ref, vec_ref, ub_ref, total_ref, notes, sem = refs[at:]
 
         @pl.when(pl.program_id(0) == 0)
         def _():
@@ -345,14 +343,10 @@
             )
     else:
         wp_ref, up_ref, vec_ref, ub_ref = refs[4:8]
-        t_ref = refs[at]
     pb_row, gain_row, shift_row = [vec_ref[at : at + 1, :] for at in range(3)]
     keep = keep_ref[...].reshape(rows, 2)[:, 0:1]
-    for at in range(group):
-        t_ref[at, pl.ds(192, 16), :] = jnp.zeros((16, D), F32)
-        t_ref[at, pl.ds(0, SLOTS), :] = tok_ref[at].astype(F32)
     attn_out = nn(mix_ref[...].reshape(rows, D), wp_ref[...]) + pb_row
-    hidden = keep * (t_ref[...].reshape(rows, D) + attn_out)
+    hidden = keep * (tok_ref[...].reshape(rows, D).astype(F32) + attn_out)
     hid_ref[...] = hidden.reshape(group, ROWS, D)
     scaled, _ = norm_parts(hidden)
     second_in = (scaled * gain_row + shift_row).astype(BF16)
@@ -369,9 +363,9 @@
     rows = group * ROWS
     me_ref, hid_ref, act_ref, slope_ref, teach_ref, aux_ref, up_ref, vec_ref, total_ref = refs[0:9]
     at = 9 + (pieces or 1)
-    out_ref, gh_ref, ga_ref, gd_ref, gu_ref, sums_ref, usum_ref, t_ref = refs[at : at + 8]
+    out_ref, gh_ref, ga_ref, gd_ref, gu_ref, sums_ref, usum_ref = refs[at : at + 7]
     if pieces:
-        down3_ref, sem = refs[at + 8 :]
+        down3_ref, sem = refs[at + 7 :]
 
         @pl.when(step == 0)
         def _():
@@ -398,9 +392,7 @@
     final = keep * (hidden + down)
     for at in range(group):
         out_ref[at] = final[at * ROWS : at * ROWS + SLOTS].astype(BF16)
-        t_ref[at, pl.ds(192, 16), :] = jnp.zeros((16, D), F32)
-        t_ref[at, pl.ds(0, SLOTS), :] = teach_ref[at].astype(F32)
-    error = final - t_ref[...].reshape(rows, D)
+    error = final - teach_ref[...].reshape(rows, D).astype(F32)
     weighted = valid * error
     grad_final = coef * weighted
     grad_down = grad_final.astype(BF16)
@@ -495,7 +487,7 @@
     base_ref, dqkv_ref, w_ref, tok_ref, gh_ref, vec_ref, *refs, group, first, earlier
 ):
     step = pl.program_id(0)
-    out_ref, sums_ref, x_ref = refs[earlier:]
+    out_ref, sums_ref = refs[earlier:]
 
     @pl.when(step == 0)
     def _():
@@ -504,13 +496,11 @@
     for at in range(group):
         keep = keep_column(base_ref, first + step * group + at)
         grad_first = keep * nt(dqkv_ref[at], w_ref[...])
-        x_ref[pl.ds(192, 16), :] = jnp.zeros((16, D), F32)
-        x_ref[pl.ds(0, SLOTS), :] = tok_ref[at].astype(F32)
-        scaled, inv_std = norm_parts(x_ref[...])
+        scaled, inv_std = norm_parts(tok_ref[at].astype(F32))
         sums_ref[0:1, :] += jnp.sum(grad_first * scaled, axis=0, keepdims=True)
         sums_ref[1:2, :] += jnp.sum(grad_first, axis=0, keepdims=True)
         total = gh_ref[at] + norm_grad(grad_first, scaled, inv_std, vec_ref[0:1, :])
-        out_ref[at] = total[0:SLOTS]
+        out_ref[:, first + step * group + at, :] = total[0:SLOTS]
 
 
 def weight_grad_kernel(*refs):
@@ -518,44 +508,36 @@
     out_ref[...] = tn(left_ref[...], right_ref[...]).astype(BF16)
 
 
-def qkv_grad_kernel(me_ref, left_ref, right_ref, keep_ref, send_ref, full, sem):
-    step = pl.program_id(0)
-    cols = pl.ds(pl.multiple_of(step * D, D), D)
-    full[:, cols] = tn(left_ref[...], right_ref[...]).astype(BF16)
-
-    @pl.when(step == pl.num_programs(0) - 1)
-    def _():
-        core = me_ref[0] % 2
-        for at, (ref, far_core) in enumerate(((send_ref, 1 - core), (keep_ref, core))):
-
-            def start(index, carry, ref=ref, far_core=far_core, at=at):
-                far_x, owner = piece_place(me_ref, index)
-                pltpu.make_async_copy(
-                    full.at[
-                        pl.ds(pl.multiple_of(owner * 96 + far_x * 48, 16), 48),
-                        pl.ds(pl.multiple_of(far_core * QKV_HALF, 128), QKV_HALF),
-                    ],
-                    ref.at[index],
-                    sem.at[at],
-                ).start()
-                return carry
-
-            lax.fori_loop(0, 16, start, 0)
-        for at, ref in enumerate((send_ref, keep_ref)):
-            pltpu.make_async_copy(ref, ref, sem.at[at]).wait()
+def qkv_grad_kernel(me_ref, left_ref, right_ref, notes_ref, out_ref, full, sem, *, other):
+    full[...] = tn(left_ref[...], right_ref[...]).astype(BF16)
+    core = (me_ref[0] % 2) ^ other
+
+    def start(index, carry):
+        far_x, owner = piece_place(me_ref, index)
+        pltpu.make_async_copy(
+            full.at[pl.ds(pl.multiple_of(owner * 96 + far_x * 48, 16), 48)],
+            out_ref.at[index, :, pl.ds(0, QKV_HALF)],
+            sem.at[0],
+        ).start()
+        pltpu.make_async_copy(
+            notes_ref.at[core * 2 + far_x, owner],
+            out_ref.at[index, :, pl.ds(QKV_HALF, NOTES)],
+            sem.at[0],
+        ).start()
+        return carry
+
+    lax.fori_loop(0, 16, start, 0)
+    pltpu.make_async_copy(out_ref, out_ref, sem.at[0]).wait()
 
 
 def up_grad_kernel(me_ref, left_ref, right_ref, out_ref, full, sem):
     step = pl.program_id(0)
     full[step] = tn(left_ref[...], right_ref[...]).astype(BF16)
-    cols = pl.ds(pl.multiple_of((step % 2) * 384, 128), 384)
 
     def start(index, carry):
         far_x, owner = piece_place(me_ref, index)
         rows = pl.ds(pl.multiple_of(owner * 96 + far_x * 48, 16), 48)
-        pltpu.make_async_copy(
-            full.at[step, rows], out_ref.at[index, step // 2, :, cols], sem.at[0]
-        ).start()
+        pltpu.make_async_copy(full.at[step, rows], out_ref.at[index, step], sem.at[0]).start()
         return carry
 
     lax.fori_loop(0, 16, start, 0)
@@ -582,7 +564,7 @@
 
     @pl.when(step < last)
     def _():
-        full[step] = tn(act_ref[...], gd_ref[...]).astype(BF16).reshape(8, 48, D)
+        full[step] = tn(act_ref[...], gd_ref[...]).astype(BF16).reshape(16, 48, D)
 
     @pl.when(step == last)
     def _():
@@ -606,10 +588,11 @@
 
         @pl.when(step < last)
         def _(ref=ref, far_core=far_core, at=at):
-            for far_x in range(2):
+            for place in range(4):
+                which, far_x = place // 2, place % 2
                 pltpu.make_async_copy(
-                    full.at[step, pl.ds(far_core * 4 + far_x * 2, 2)],
-                    ref.at[piece_index(me_ref, far_x, step), pl.ds(0, 2)],
+                    full.at[step, pl.ds(which * 8 + far_core * 4 + far_x * 2, 2)],
+                    ref.at[piece_index(me_ref, far_x, step * 2 + which), pl.ds(0, 2)],
                     sem.at[at],
                 ).start()
 
@@ -681,7 +664,7 @@
         shape_of((count, ROWS, 3 * D), BF16), shape_of((count, HEADS, ROWS, LANES), BF16),
         shape_of((count, ROWS, D), BF16), shape_of((count, ROWS, D), BF16),
     ]
-    scratch = [pltpu.VMEM((ROWS, D), F32)]
+    scratch = []
     if pieces:
         out_specs.append(whole_out((D, 3 * D)))
         out_shape.append(shape_of((D, 3 * D), BF16))
@@ -691,14 +674,14 @@
         functools.partial(attend_kernel, first=first, pieces=pieces, earlier=len(earlier)),
         grid=(number,),
         in_specs=[
-            SMEM, win((1, SLOTS, D)), *weight_specs, whole((8, D)),
+            SMEM, win((1, ROWS, D)), *weight_specs, whole((8, D)),
             whole((PAIR, PAIR)), whole((ROWS, HEAD_DIM)), *([ANY] * len(earlier)),
         ],
         out_specs=out_specs,
         out_shape=out_shape,
         scratch_shapes=scratch,
         input_output_aliases={inputs + at: at for at in range(len(earlier))},
-        compiler_params=params(),
+        compiler_params=params(54),
         cost_estimate=cost(COST, 1e5),
         name="attend",
     )(me, tokens, *weights, vec, rel, places, *earlier)
@@ -712,7 +695,7 @@
     pieces = len(weights) if chunked else 0
     out_specs = [win(D), win(D), win(MLP), win(MLP)]
     out_shape = [arr(D, F32), arr(D, BF16), arr(MLP, BF16), arr(MLP, BF16)]
-    scratch = [pltpu.VMEM((group, ROWS, D), F32)]
+    scratch = []
     if pieces:
         shapes = [((D, MLP), BF16), ((D, D), BF16), ((8, D), F32), ((1, MLP), F32), ((1, 128), F32)]
         out_specs += [whole_out(s) for s, _ in shapes]
@@ -721,12 +704,12 @@
     return pl.pallas_call(
         functools.partial(up_kernel, group=group, pieces=pieces),
         grid=(count // group,),
-        in_specs=[SMEM, windows_from(0, (group, SLOTS, D)), win(D), win(2)]
+        in_specs=[SMEM, win(D), win(D), win(2)]
         + ([ANY] * pieces if pieces else [whole(v.shape) for v in weights]),
         out_specs=out_specs,
         out_shape=out_shape,
         scratch_shapes=scratch,
-        compiler_params=params(44),
+        compiler_params=params(60),
         cost_estimate=cost(COST * count, 1e5),
         name="mlp_up",
     )(me, tokens, mixed, aux, *weights)
@@ -739,13 +722,13 @@
     plain = windows_from(0, (group, SLOTS, D))
     arr = lambda width, dtype: shape_of((count, ROWS, width), dtype)
     pieces = len(weights) if chunked else 0
-    scratch = [pltpu.VMEM((group, ROWS, D), F32)]
+    scratch = []
     if pieces:
         scratch += [pltpu.VMEM((MLP // 48, 48, D), BF16), pltpu.SemaphoreType.DMA((1,))]
     return pl.pallas_call(
         functools.partial(down_kernel, group=group, pieces=pieces, scale=scale),
         grid=(count // group,),
-        in_specs=[SMEM, win(D), win(MLP), win(MLP), plain, win(2), whole((D, MLP)), whole((8, D)),
+        in_specs=[SMEM, win(D), win(MLP), win(MLP), win(D), win(2), whole((D, MLP)), whole((8, D)),
                   whole((1, 128))]
         + ([ANY] * pieces if pieces else [whole(v.shape) for v in weights]),
         out_specs=[plain, win(D), win(D), win(D), win(MLP), whole_out((5, D)), whole_out((1, MLP))],
@@ -754,7 +737,7 @@
             arr(MLP, BF16), shape_of((5, D), F32), shape_of((1, MLP), F32),
         ],
         scratch_shapes=scratch,
-        compiler_params=params(48),
+        compiler_params=params(60),
         cost_estimate=cost(COST * count, 1e5),
         name="mlp_down",
     )(me, hidden, act, slope, teacher, aux, up, vec, total, *weights)
@@ -778,7 +761,7 @@
         ],
         scratch_shapes=[pltpu.VMEM((LANES, D), BF16)],
         input_output_aliases={6: 0} if earlier else {},
-        compiler_params=params(),
+        compiler_params=params(48),
         cost_estimate=cost(COST, 1e5),
         name="attend_back",
     )(grad_attn, proj, qkv, probs, rel_t, places_t, *earlier)
@@ -793,14 +776,13 @@
         functools.partial(input_kernel, group=group, first=first, earlier=len(earlier)),
         grid=(number // group,),
         in_specs=[
-            SMEM, win((group, ROWS, 3 * D)), whole((D, 3 * D)), win((group, SLOTS, D)),
+            SMEM, win((group, ROWS, 3 * D)), whole((D, 3 * D)), win((group, ROWS, D)),
             win((group, ROWS, D)), whole((8, D)), *before,
         ],
-        out_specs=[win((group, SLOTS, D)), whole_out((2, D))],
-        out_shape=[shape_of((count, SLOTS, D), F32), shape_of((2, D), F32)],
-        scratch_shapes=[pltpu.VMEM((ROWS, D), F32)],
+        out_specs=[whole_out((SLOTS, count, D)), whole_out((2, D))],
+        out_shape=[shape_of((SLOTS, count, D), F32), shape_of((2, D), F32)],
         input_output_aliases={6: 0} if earlier else {},
-        compiler_params=params(),
+        compiler_params=params(44),
         cost_estimate=cost(COST, 1e5),
         name="input_back",
     )(me, dqkv, weight, tokens, grad_hidden, vec, *earlier)
@@ -815,24 +797,32 @@
         [one_ref[0:2], qv_ref[0:2], two_ref[4:5], two_ref[2:4], two_ref[1:2]], axis=0
     )
     error = jnp.sum(two_ref[0:1, :], axis=1, keepdims=True)
+    high = error.astype(BF16).astype(F32)
+    middle = (error - high).astype(BF16).astype(F32)
+    lane = lax.broadcasted_iota(jnp.int32, (1, 128), 1) - 3 * (me_ref[0] * 8 + me_ref[1])
+    error = jnp.where(
+        lane == 0, high, jnp.where(lane == 1, middle, jnp.where(lane == 2, error - high - middle, 0.0))
+    )
     tables = rel_ref[0:64, 0:64] + rel_ref[64:128, 64:128]
     row = lax.broadcasted_iota(jnp.int32, (D, 128), 0)
     col = lax.broadcasted_iota(jnp.int32, (D, 128), 1)
-    small_row = lax.broadcasted_iota(jnp.int32, (64, 128), 0)
-    small_col = lax.broadcasted_iota(jnp.int32, (64, 128), 1)
-    for at in range(8):
-        owner = me_ref[1] ^ ((at % 4) * 2 + at // 4)
+    small_row = lax.broadcasted_iota(jnp.int32, (32, 128), 0)
+    lanes_row = lax.broadcasted_iota(jnp.int32, (64, 128), 0)
+    lanes_col = lax.broadcasted_iota(jnp.int32, (64, 128), 1)
+    out_ref[...] = jnp.zeros_like(out_ref)
+    for owner in range(8):
         own = pick(vectors, ((col < 96) & (row == col + owner * 96)).astype(F32))
         total = jnp.concatenate([own, jnp.zeros((24, 128), F32)], axis=0)
         for which in range(2):
-            lane = small_col - 96 - 8 * which
-            put = ((lane >= 0) & (lane < 8) & (small_row == lane + owner * 8)).astype(F32)
+            lane = lanes_col - 96 - 8 * which
+            put = ((lane >= 0) & (lane < 8) & (lanes_row == lane + owner * 8)).astype(F32)
             total = total + pick(tables[32 * which : 32 * which + 32], put)
-        out_ref[at] = total
         for part in range(3):
-            lanes = pl.ds(pl.multiple_of(owner * 384 + part * 128, 128), 128)
-            out_ref[at, 27 + part : 28 + part, :] = up_ref[:, lanes]
-        out_ref[at, 30:31, :] = jnp.broadcast_to(error, (1, 128))
+            at = owner * 384 + part * 128
+            total = jnp.where(small_row == 27 + part, up_ref[:, at : at + 128], total)
+        total = jnp.where(small_row == 30, error, total).astype(BF16)
+        for quarter in range(4):
+            out_ref[quarter, owner, 0:8] = total[quarter * 8 : quarter * 8 + 8]
 
 
 def pack(me, *sums):
@@ -840,25 +830,48 @@
         pack_kernel,
         grid=(1,),
         in_specs=[SMEM] + [whole(v.shape) for v in sums],
-        out_specs=whole_out((8, 32, 128)),
-        out_shape=shape_of((8, 32, 128), F32),
+        out_specs=whole_out((4, 8, 48, NOTES)),
+        out_shape=shape_of((4, 8, 48, NOTES), BF16),
         compiler_params=params(),
         cost_estimate=cost(COST, 1e5),
         name="pack",
     )(me, *sums)
 
 
-def shard_kernel(me_ref, *refs, split):
-    quarters, outs = refs[0:4], refs[4:]
+def qkv_shard_kernel(me_ref, total_ref, *refs):
+    quarters, out_ref, notes_ref = refs[0:4], refs[4], refs[5]
     core, far_x = me_ref[0] % 2, me_ref[0] // 2
     for at, ref in enumerate(quarters):
         this_core, this_x = core ^ (at // 2), far_x ^ (at % 2)
         rows = pl.ds(pl.multiple_of(this_x * 48, 16), 48)
-        if not split:
-            cols = pl.ds(pl.multiple_of(this_core * QKV_HALF, 128), QKV_HALF)
-            outs[0][rows, cols] = ref[...].astype(F32)
-            continue
-        up_ref, down_ref, proj_ref = outs
+        cols = pl.ds(pl.multiple_of(this_core * QKV_HALF, 128), QKV_HALF)
+        out_ref[rows, cols] = ref[:, 0:QKV_HALF].astype(F32)
+        here = pl.ds(pl.multiple_of((this_core * 2 + this_x) * 8, 8), 8)
+        notes_ref[here, :] = ref[0:16, QKV_HALF : QKV_HALF + NOTES].astype(F32)[0:8]
+    errors = jnp.sum(notes_ref[30:31, :], axis=1, keepdims=True)
+    notes_ref[31:32, :] = errors / (total_ref[...] * D)
+
+
+def qkv_shard(me, total, quarters):
+    shapes = [(96, 3 * D), (32, 128)]
+    return pl.pallas_call(
+        qkv_shard_kernel,
+        grid=(1,),
+        in_specs=[SMEM, whole((1, 128))] + [whole(v.shape) for v in quarters],
+        out_specs=[whole_out(shape) for shape in shapes],
+        out_shape=[shape_of(shape, F32) for shape in shapes],
+        compiler_params=params(),
+        cost_estimate=cost(COST, 1e5),
+        name="qkv_shard",
+    )(me, total, *quarters)
+
+
+def shard_kernel(me_ref, *refs):
+    quarters, (up_ref, down_ref, proj_ref) = refs[0:4], refs[4:]
+    core, far_x = me_ref[0] % 2, me_ref[0] // 2
+    for at, ref in enumerate(quarters):
+        this_core, this_x = core ^ (at // 2), far_x ^ (at % 2)
+        rows = pl.ds(pl.multiple_of(this_x * 48, 16), 48)
         for block in range(2):
             cols = pl.ds(pl.multiple_of(this_core * 1536 + block * D, 128), D)
             up_ref[rows, cols] = ref[block].astype(F32)
@@ -868,14 +881,14 @@
         proj_ref[rows, cols] = ref[4, :, 0:384].astype(F32)
 
 
-def shard(me, quarters, split):
-    shapes = [(96, MLP), (384, D), (96, D)] if split else [(96, 3 * D)]
+def shard(me, quarters):
+    shapes = [(96, MLP), (384, D), (96, D)]
     return pl.pallas_call(
-        functools.partial(shard_kernel, split=split),
+        shard_kernel,
         grid=(1,),
         in_specs=[SMEM] + [whole(v.shape) for v in quarters],
-        out_specs=[whole_out(s) for s in shapes],
-        out_shape=[shape_of(s, F32) for s in shapes],
+        out_specs=[whole_out(shape) for shape in shapes],
+        out_shape=[shape_of(shape, F32) for shape in shapes],
         compiler_params=params(),
         cost_estimate=cost(COST, 1e5),
         name="shard",
@@ -901,19 +914,26 @@
     )(left, right)
 
 
-def qkv_grad(me, left, right):
+def qkv_grad(me, left, right, notes, other):
     rows = left.shape[0]
     return pl.pallas_call(
-        qkv_grad_kernel,
-        grid=(3,),
-        in_specs=[SMEM, whole((rows, D)), column_blocks(rows)],
-        out_specs=[ANY] * 2,
-        out_shape=[shape_of((16, 48, QKV_HALF), BF16)] * 2,
-        scratch_shapes=[pltpu.VMEM((D, 3 * D), BF16), pltpu.SemaphoreType.DMA((2,))],
-        compiler_params=params(),
+        functools.partial(qkv_grad_kernel, other=other),
+        grid_spec=pltpu.PrefetchScalarGridSpec(
+            num_scalar_prefetch=1,
+            grid=(1,),
+            in_specs=[
+                whole((rows, D)),
+                pl.BlockSpec((rows, QKV_HALF), lambda step, me: (0, (me[0] % 2) ^ other)),
+                whole((4, 8, 48, NOTES)),
+            ],
+            out_specs=ANY,
+            scratch_shapes=[pltpu.VMEM((D, QKV_HALF), BF16), pltpu.SemaphoreType.DMA((1,))],
+        ),
+        out_shape=shape_of((16, 48, QKV_HALF + NOTES), BF16),
+        compiler_params=params(60),
         cost_estimate=cost(COST, 1e5),
         name="qkv_grad",
-    )(me, left, right)
+    )(me, left, right, notes)
 
 
 def up_grad(me, left, right, other):
@@ -922,16 +942,16 @@
         up_grad_kernel,
         grid_spec=pltpu.PrefetchScalarGridSpec(
             num_scalar_prefetch=1,
-            grid=(4,),
+            grid=(2,),
             in_specs=[
                 whole((rows, D)),
-                pl.BlockSpec((rows, 384), lambda step, me: (0, ((me[0] % 2) ^ other) * 4 + step)),
+                pl.BlockSpec((rows, D), lambda step, me: (0, ((me[0] % 2) ^ other) * 2 + step)),
             ],
             out_specs=ANY,
-            scratch_shapes=[pltpu.VMEM((4, D, 384), BF16), pltpu.SemaphoreType.DMA((1,))],
+            scratch_shapes=[pltpu.VMEM((2, D, D), BF16), pltpu.SemaphoreType.DMA((1,))],
         ),
         out_shape=shape_of((16, 2, 48, D), BF16),
-        compiler_params=params(),
+        compiler_params=params(60),
         cost_estimate=cost(COST, 1e5),
         name="up_grad",
     )(me, left, right)
@@ -941,19 +961,19 @@
     rows = act.shape[0]
     return pl.pallas_call(
         down_grad_kernel,
-        grid=(9,),
+        grid=(5,),
         in_specs=[
-            SMEM, pl.BlockSpec((rows, 384), lambda step: (0, jnp.minimum(step, 7))),
+            SMEM, pl.BlockSpec((rows, D), lambda step: (0, jnp.minimum(step, 3))),
             whole((rows, D)), ANY, ANY,
         ],
         out_specs=[ANY] * 2,
         out_shape=[shape_of((16, 3, 48, D), BF16)] * 2,
         scratch_shapes=[
-            pltpu.VMEM((8, 8, 48, D), BF16), pltpu.VMEM((2, D, 384), BF16),
+            pltpu.VMEM((4, 16, 48, D), BF16), pltpu.VMEM((2, D, 384), BF16),
             pltpu.VMEM((rows, D), BF16), pltpu.VMEM((rows, D), BF16),
             pltpu.SemaphoreType.DMA((4,)),
         ],
-        compiler_params=params(),
+        compiler_params=params(60),
         cost_estimate=cost(COST, 1e5),
         name="down_grad",
     )(me, act, grad_down, mixed, grad_attn)
@@ -1002,7 +1022,9 @@
     keep = inside.astype(F32)
     valid = valid_mask.astype(F32) * keep
     counted = jnp.sum(valid_mask * inside.astype(jnp.int32))
-    aux = jnp.pad(jnp.stack([keep, valid], axis=-1), ((0, 0), (0, ROWS - SLOTS), (0, 0)))
+    fill = ((0, 0), (0, ROWS - SLOTS), (0, 0))
+    aux = jnp.pad(jnp.stack([keep, valid], axis=-1), fill)
+    tokens, teacher = jnp.pad(tokens, fill), jnp.pad(teacher, fill)
 
     small = [attn_gain, attn_shift, query_bias, value_bias, proj_bias, mlp_gain, mlp_shift,
              down_bias, up_bias, rel_pos_h, rel_pos_w]
@@ -1046,11 +1068,11 @@
         planes = [rects] + [swap(rects, "fsdp", mask) for mask in (2, 4, 6)]
         near_a, near_b = jnp.stack(near[0:2]), jnp.stack(near[2:4])
         from_a, from_b = swap(near_a, "fsdp", 1), swap(near_b, "rep", 2)
-        from_a, from_b, planes[1] = tied(from_a, from_b, planes[1])
+        from_a, from_b, planes[1], tokens = tied(from_a, from_b, planes[1], tokens)
         near_a = jnp.concatenate([near_a, from_a])
         near_b = jnp.concatenate([near_b, from_b])
         far_a, far_b = swap(near_a, "rep", 2), swap(near_b, "fsdp", 1)
-        far_a, far_b, planes[2] = tied(far_a, far_b, planes[2])
+        far_a, far_b, planes[2], teacher = tied(far_a, far_b, planes[2], teacher)
         all_a, all_b = jnp.concatenate([near_a, far_a]), jnp.concatenate([near_b, far_b])
         other_a, other_b = swap(all_a, "rep", 1), swap(all_b, "rep", 1)
         vec, rel, rel_t = notes_of(me, near_a, near_b, far_b)
@@ -1172,61 +1194,56 @@
         from_ua, from_ub, from_z[0], dqkv, rel_grad, qv_sum = tied(
             from_ua, from_ub, from_z[0], *state
         )
-        keep, send = qkv_grad(me, flat(first_in), flat(dqkv))
-        half = count // 2
-        from_z[1], from_z[2], keep, send, dqkv = tied(from_z[1], from_z[2], keep, send, dqkv)
+        input_grad, sums1 = input_back(me, dqkv, w_qkv, tokens, grad_hidden, vec, 0, count)
+        from_z[1], from_z[2], sums1, dqkv = tied(from_z[1], from_z[2], sums1, dqkv)
         own_d = sends_d[0].astype(F32)
         for v in from_z:
             own_d = own_d + v.astype(F32)
         u_a, u_b = added(u_a[0:2], from_ua), added(u_b[0:2], from_ub)
+        notes = pack(me, sums1, qv_sum, sums2, up_sum, rel_grad)
         sends_u = (u_a[0], u_a[1], u_b[0], u_b[1])
-        *sends_u, send, dqkv = tied(*sends_u, send, dqkv)
+        own_d, *sends_u, notes = tied(own_d.astype(BF16), *sends_u, notes)
+        from_z = [swap(v, "fsdp", mask) for v, mask in zip(sends_u[1:], (2, 4, 6))]
+        first_in, dqkv = flat(first_in), flat(dqkv)
+        send = qkv_grad(me, first_in, dqkv, notes, 1)
+        from_z[0], send, first_in, input_grad = tied(from_z[0], send, first_in, input_grad)
         from_core = swap(send, "rep", 1)
-        from_z = [swap(v, "fsdp", mask) for v, mask in zip(sends_u[1:], (2, 4, 6))]
-        state = input_back(me, dqkv, w_qkv, tokens, grad_hidden, vec, 0, half)
-        from_core, *rest = tied(from_core, *from_z, *state)
-        from_z, state = rest[0:3], rest[3:]
+        keep = qkv_grad(me, first_in, dqkv, notes, 0)
+        from_core, keep = tied(from_core, keep)
         both = parts_of(keep, from_core)
         send_a, send_b = both(4, 8), both(12, 16)
+        send_a, send_b = tied(send_a, send_b)
+        from_a, from_b = swap(send_a, "rep", 2), swap(send_b, "fsdp", 1)
+        from_a, from_b, *from_z = tied(from_a, from_b, *from_z)
+        sum_a, sum_b = added(both(0, 4), from_a), added(both(8, 12), from_b)
         own_u = sends_u[0].astype(F32)
         for v in from_z:
             own_u = own_u + v.astype(F32)
-        own = jnp.concatenate([own_u.astype(BF16), own_d.astype(BF16)], axis=0)
-        send_a, send_b, own, *state = tied(send_a, send_b, own, *state)
-        from_a, from_b = swap(send_a, "rep", 2), swap(send_b, "fsdp", 1)
+        own = jnp.concatenate([own_u.astype(BF16), own_d], axis=0)
+        from_a, from_b = swap(sum_a[2:4], "fsdp", 1), swap(sum_b[2:4], "rep", 2)
+        from_a, from_b = tied(from_a, from_b)
+        sum_a, sum_b = added(sum_a[0:2], from_a), added(sum_b[0:2], from_b)
+        sends = (sum_a[0], sum_a[1], sum_b[0], sum_b[1])
+        *sends, own = tied(*sends, own)
+        from_z = [swap(v, "fsdp", mask) for v, mask in zip(sends[1:], (2, 4, 6))]
         from_x = swap(own, "rep", 2)
-        input_grad, sums1 = input_back(
-            me, dqkv, w_qkv, tokens, grad_hidden, vec, half, count - half, tuple(state)
-        )
-        from_a, from_b, from_x, sums1 = tied(from_a, from_b, from_x, sums1)
-        sum_a, sum_b = added(both(0, 4), from_a), added(both(8, 12), from_b)
-        from_a, from_b = swap(sum_a[2:4], "fsdp", 1), swap(sum_b[2:4], "rep", 2)
-        core_own, core_x = swap(own, "rep", 1), swap(from_x, "rep", 1)
-        notes = pack(me, sums1, qv_sum, sums2, up_sum, rel_grad)
-        from_a, from_b, notes, core_own, core_x = tied(from_a, from_b, notes, core_own, core_x)
-        sum_a, sum_b = added(sum_a[0:2], from_a), added(sum_b[0:2], from_b)
-        from_z = [swap(v, "fsdp", mask) for v, mask in
-                  ((sum_a[1], 2), (sum_b[0], 4), (sum_b[1], 6))]
-        notes = notes + swap(notes, "rep", 1)
-        notes = notes + swap(notes, "rep", 2)
-        notes = notes[0:4] + swap(notes[4:8], "fsdp", 1)
-        d_up, d_down, d_proj = shard(me, (own, from_x, core_own, core_x), True)
-        mine = notes[0]
-        for at, mask in ((1, 2), (2, 4), (3, 6)):
-            mine = mine + swap(notes[at], "fsdp", mask)
-        own = sum_a[0].astype(F32)
+        *from_z, from_x = tied(*from_z, from_x)
+        own_q = sends[0].astype(F32)
         for v in from_z:
-            own = own + v.astype(F32)
-        own = own.astype(BF16)
-        from_x = swap(own, "rep", 2)
-        (d_qkv,) = shard(
-            me, (own, from_x, swap(own, "rep", 1), swap(from_x, "rep", 1)), False
-        )
-        lanes = tokens.shape[2] // parts
-        vectors = [mine[at, 0:lanes] for at in range(8)]
+            own_q = own_q + v.astype(F32)
+        own_q = own_q.astype(BF16)
+        from_xq = swap(own_q, "rep", 2)
+        d_up, d_down, d_proj = shard(
+            me, (own, from_x, swap(own, "rep", 1), swap(from_x, "rep", 1))
+        )
+        from_xq, d_up = tied(from_xq, d_up)
+        d_qkv, mine = qkv_shard(
+            me, total, (own_q, from_xq, swap(own_q, "rep", 1), swap(from_xq, "rep", 1))
+        )
+        vectors = [mine[at, 0:96] for at in range(8)]
         tables = [mine[0:27, 96 + 8 * at : 104 + 8 * at] for at in range(2)]
         outs = vectors + [mine[27:30].reshape(-1)] + tables
-        loss = mine[30, 0] / (valid_total * D)
+        loss = mine[31, 0]
     else:
         scatter = lambda v: lax.psum(
             lax.psum_scatter(v, "fsdp", scatter_dimension=0, tiled=True), "rep"
@@ -1261,7 +1278,7 @@
         loss = mine[at] / (valid_total * D)
     (g_gain1, g_shift1, g_qb, g_vb, g_pb, g_gain2, g_shift2, g_db, g_ub, g_rh, g_rw) = outs
     return (
-        out, loss, input_grad, g_gain1, g_shift1, d_qkv, g_qb, g_vb, g_rh, g_rw, d_proj, g_pb,
+        out, loss, input_grad.transpose(1, 0, 2), g_gain1, g_shift1, d_qkv, g_qb, g_vb, g_rh, g_rw, d_proj, g_pb,
         g_gain2, g_shift2, d_up, g_ub, d_down, g_db,
     )
 

time: 395 us -> 371 us (0.939)
  local copies, waits for them, and re-layouts: 43.6 us -> 22.3 us
  Pallas kernels: 210 us -> 221 us
  starting transfers between devices: 73.3 us -> 62.5 us
    unnamed x84 -> x93, local copies, waits for them, and re-layouts: 37.9 us -> 12.4 us
    ppermute x67 -> x61, starting transfers between devices: 73.3 us -> 62.5 us  [swap(): return lax.ppermute(values, axis, [(at, at ^ mask) for at in range(size)])]
    pallas_call x3, Pallas kernels: 38.8 us -> 45.2 us  [attend(): pl.pallas_call(functools.partial(attend_kernel, first=first, pieces=piece...]
    pad x1 -> x3, local copies, waits for them, and re-layouts: 0.06 us -> 4.28 us  [the longest x2 3.27 us: body(): tokens, teacher = (jnp.pad(tokens, fill), jnp.pad(teacher, fill))]
    pallas_call x3, Pallas kernels: 31.4 us -> 35.3 us  [attend_back(): pl.pallas_call(functools.partial(attend_back_kernel, earlier=len(earlier)...]
    pallas_call x4 -> x5, Pallas kernels: 34.5 us -> 37.8 us  [the longest x2 17.4 us: qkv_grad(): pl.pallas_call(functools.partial(qkv_grad_kernel, other=other), grid_spec...]
    pallas_call x2 -> x1, Pallas kernels: 14 us -> 16.5 us  [input_back(): pl.pallas_call(functools.partial(input_kernel, group=group, first=first,...]
    ppermute x67 -> x61, waiting for transfers between devices: 43.1 us -> 41.3 us  [swap(): return lax.ppermute(values, axis, [(at, at ^ mask) for at in range(size)])]
  transfers between devices with their start and end apart: 67 -> 61, of which waited for: 12 -> 15; matrix products, arithmetic and copies ran while one was open for 5% -> 5% of each run, Pallas kernels for 38% -> 44%
where the time goes in v4:
time: 371 us; the launch traced here: 367 us
  Pallas kernels  221 us (60%)
  starting transfers between devices  62.5 us (17%)
  waiting for transfers between devices  41.3 us (11%)
  local copies, waits for them, and re-layouts  22.3 us (6%)
  other arithmetic  15.3 us (4%)
  between operations  4.55 us (1%)
    ppermute x61, starting transfers between devices, swap(): return lax.ppermute(values, axis, [(at, at ^ mask) for at in range(size)])  62.5 us
    pallas_call x3, Pallas kernels, attend(): pl.pallas_call(functools.partial(attend_kernel, first=first, pieces=piece...  45.2 us
    ppermute x61, waiting for transfers between devices, swap(): return lax.ppermute(values, axis, [(at, at ^ mask) for at in range(size)])  41.3 us
    pallas_call x1, Pallas kernels, mlp_down(): pl.pallas_call(functools.partial(down_kernel, group=group, pieces=pieces,...  37.9 us
    pallas_call x3, Pallas kernels, attend_back(): pl.pallas_call(functools.partial(attend_back_kernel, earlier=len(earlier)...  35.3 us
    pallas_call x1, Pallas kernels, mlp_up(): pl.pallas_call(functools.partial(up_kernel, group=group, pieces=pieces),...  26.1 us
    pallas_call x2, Pallas kernels, up_grad(): pl.pallas_call(up_grad_kernel, grid_spec=pltpu.PrefetchScalarGridSpec(num...  19.5 us
    pallas_call x2, Pallas kernels, qkv_grad(): pl.pallas_call(functools.partial(qkv_grad_kernel, other=other), grid_spec...  17.4 us
  transfers between devices with their start and end apart: 61, of which 15 were waited for; matrix products, arithmetic and copies ran while one was open for 5% of the time, Pallas kernels for 44%

profile of v4, /device:TPU:0, one launch (start us, length us, event | category | flops | bytes accessed | tf_op | source)
XLA Modules:
  0.0 367.2 jit_solution(12940087840680512438)
XLA Ops:
  4.0 5.1 %collective-permute-start.2 = (bf16[48,1280]{1,0:T(8,128)(2,1)S(1)}, bf16[48,1280]{1,0:T(8,128)(2,1)S(1)}, u32[]{:S(2)}, u32[]{:S(2)}) collective-permute-start(bf16[48,1280]{1,0:T(8,128)(2,1)S(1)} %pad_maximum_fusion.16), channel_id=1, source_target_pairs={{0,6},{1,7},{2,4},{3,5},{4,2},{5,3},{6,0},{7,1},{8,14},{9,15},{10,... | collective-permute-start | bytes 368648 | tf_op jit(solution)/shard_map/ppermute | solution.py:984
  23.9 2.1 copy.68
  30.2 2.2 collective-permute-start.8
  34.5 6.0 %collective-permute-done.8 = bf16[3,48,768]{2,1,0:T(8,128)(2,1)S(1)} collective-permute-done((bf16[3,48,768]{2,1,0:T(8,128)(2,1)S(1)}, bf16[3,48,768]{2,1,0:T(8,128)(2,1)S(1)}, u32[]{:S(2)}, u32[]{:S(2)}) %collective-permute-start.8) | collective-permute-done | bytes 221216 | tf_op jit(solution)/shard_map/ppermute | solution.py:984
  41.3 3.2 collective-permute-start.11
  46.9 3.8 %collective-permute-done.11 = bf16[3,48,768]{2,1,0:T(8,128)(2,1)S(1)} collective-permute-done((bf16[3,48,768]{2,1,0:T(8,128)(2,1)S(1)}, bf16[3,48,768]{2,1,0:T(8,128)(2,1)S(1)}, u32[]{:S(2)}, u32[]{:S(2)}) %collective-permute-start.11) | collective-permute-done | bytes 221216 | tf_op jit(solution)/shard_map/ppermute | solution.py:984
  53.3 3.3 collective-permute-start.16
  58.1 18.3 %attend.3 = (bf16[8,208,2304]{2,1,0:T(8,128)(2,1)}, bf16[8,12,208,256]{3,2,1,0:T(8,128)(2,1)}, bf16[8,208,768]{2,1,0:T(8,128)(2,1)}, bf16[8,208,768]{2,1,0:T(8,128)(2,1)}, bf16[768,2304]{1,0:T(8,128)(2,1)}) custom-call(s32[3]{0:T(128)} %copy-done.11, bf16[8,208,768]{2,1,0:T(8,128)(2,1)} %pad.72.refs_1_.tok_ref, bf16[8,48,1280]{2,1,0:T(8,128)(2,1)} %copy-done.19, ...), custom_call_target="tpu_custom_call" | custom-call | flops 100000000 | bytes 100000 | tf_op jit(solution)/shard_map/attend/pallas_call | solution.py:673
  79.5 19.8 %attend.4 = (bf16[8,208,2304]{2,1,0:T(8,128)(2,1)}, bf16[8,12,208,256]{3,2,1,0:T(8,128)(2,1)}, bf16[8,208,768]{2,1,0:T(8,128)(2,1)}, bf16[8,208,768]{2,1,0:T(8,128)(2,1)}) custom-call(s32[3]{0:T(128)} %copy-done.11, bf16[8,208,768]{2,1,0:T(8,128)(2,1)} %pad.72.refs_1_.tok_ref, ...), custom_call_target="tpu_custom_call", output_to_operand_aliasing={{0}: (6, {}), {1}: (7, {}), {2}: (8, {}), {3}: (9, {})} | custom-call | flops 100000000 | bytes 100000 | tf_op jit(solution)/shard_map/attend/pallas_call | solution.py:673
  102.5 7.0 %attend.5 = (bf16[8,208,2304]{2,1,0:T(8,128)(2,1)}, bf16[8,12,208,256]{3,2,1,0:T(8,128)(2,1)}, bf16[8,208,768]{2,1,0:T(8,128)(2,1)}, bf16[8,208,768]{2,1,0:T(8,128)(2,1)}) custom-call(s32[3]{0:T(128)} %copy-done.11, bf16[8,208,768]{2,1,0:T(8,128)(2,1)} %pad.72.refs_1_.tok_ref, ...), custom_call_target="tpu_custom_call", output_to_operand_aliasing={{0}: (6, {}), {1}: (7, {}), {2}: (8, {}), {3}: (9, {})} | custom-call | flops 100000000 | bytes 100000 | tf_op jit(solution)/shard_map/attend/pallas_call | solution.py:673
  112.8 26.1 %mlp_up.1 = (f32[8,208,768]{2,1,0:T(8,128)}, bf16[8,208,768]{2,1,0:T(8,128)(2,1)}, bf16[8,208,3072]{2,1,0:T(8,128)(2,1)}, bf16[8,208,3072]{2,1,0:T(8,128)(2,1)},...) custom-call(s32[3]{0:T(128)} %copy-done.11, ...), custom_call_target="tpu_custom_call" | custom-call | flops 800000000 | bytes 100000 | tf_op jit(solution)/shard_map/mlp_up/pallas_call | solution.py:704
  142.8 37.9 %mlp_down.1 = (bf16[8,196,768]{2,1,0:T(8,128)(2,1)}, f32[8,208,768]{2,1,0:T(8,128)}, bf16[8,208,768]{2,1,0:T(8,128)(2,1)}, bf16[8,208,768]{2,1,0:T(8,128)(2,1)},...) custom-call(s32[3]{0:T(128)} %copy-done.11, f32[8,208,768]{2,1,0:T(8,128)} %get-tuple-element.293.refs_1_, ...), custom_call_target="tpu_custom_call" | custom-call | flops 800000000 | bytes 100000 | tf_op jit(solution)/shard_map/mlp_down/pallas_call | solution.py:728
  180.7 16.7 %down_grad.1 = (bf16[16,3,48,768]{3,2,1,0:T(8,128)(2,1)}, bf16[16,3,48,768]{3,2,1,0:T(8,128)(2,1)}) custom-call(s32[3]{0:T(128)} %copy-done.11, bf16[1664,3072]{1,0:T(8,128)(2,1)} %bitcast.94, bf16[1664,768]{1,0:T(8,128)(2,1)} %bitcast.100, bf16[1664,768]{1,0:T(8,128)(2,1)} %bitcast.95, bf16[1664,768]{1,0:T(8,128)(2,1)} %bitcast.89), custom_call_target="tpu_custom_call" | custom-call | flops 100000000 | bytes 100000 | tf_op jit(solution)/shard_map/down_grad/pallas_call | solution.py:962
  197.6 9.9 %up_grad.2 = bf16[16,2,48,768]{3,2,1,0:T(8,128)(2,1)} custom-call(s32[3]{0:T(128)} %copy-done.11, bf16[1664,768]{1,0:T(8,128)(2,1)} %bitcast.98, bf16[1664,3072]{1,0:T(8,128)(2,1)} %bitcast.92), custom_call_target="tpu_custom_call" | custom-call | flops 100000000 | bytes 100000 | tf_op jit(solution)/shard_map/up_grad/pallas_call | solution.py:941
  207.5 3.1 add_convert_fusion.3
  213.2 9.6 %up_grad.3 = bf16[16,2,48,768]{3,2,1,0:T(8,128)(2,1)} custom-call(s32[3]{0:T(128)} %copy-done.11, bf16[1664,768]{1,0:T(8,128)(2,1)} %bitcast.99, bf16[1664,3072]{1,0:T(8,128)(2,1)} %bitcast.93), custom_call_target="tpu_custom_call" | custom-call | flops 100000000 | bytes 100000 | tf_op jit(solution)/shard_map/up_grad/pallas_call | solution.py:941
  226.5 9.4 %attend_back.3 = (bf16[8,208,2304]{2,1,0:T(8,128)(2,1)}, f32[128,128]{1,0:T(8,128)S(1)}, f32[2,768]{1,0:T(2,128)S(1)}) custom-call(bf16[8,208,768]{2,1,0:T(8,128)(2,1)S(1)} %copy-done.3, bf16[768,768]{1,0:T(8,128)(2,1)S(1)} %copy-done.5, bf16[8,208,2304]{2,1,0:T(8,128)(2,1)} %get-tuple-element.325.refs_2_, ...), custom_call_target="tpu_custom_call" | custom-call | flops 100000000 | bytes 100000 | tf_op jit(solution)/shard_map/attend_back/pallas_call | solution.py:750
  235.9 2.6 add_convert_fusion
  240.9 16.4 %attend_back.4 = (bf16[8,208,2304]{2,1,0:T(8,128)(2,1)}, f32[128,128]{1,0:T(8,128)S(1)}, f32[2,768]{1,0:T(2,128)S(1)}) custom-call(bf16[8,208,768]{2,1,0:T(8,128)(2,1)S(1)} %copy-done.3, bf16[768,768]{1,0:T(8,128)(2,1)S(1)} %copy-done.5, bf16[8,208,2304]{2,1,0:T(8,128)(2,1)} %get-tuple-element.325.refs_2_, ...), custom_call_target="tpu_custom_call", output_to_operand_aliasing={{0}: (6, {})} | custom-call | flops 100000000 | bytes 100000 | tf_op jit(solution)/shard_map/attend_back/pallas_call | solution.py:750
  261.3 1.9 collective-permute-start.41
  265.7 9.5 %attend_back.5 = (bf16[8,208,2304]{2,1,0:T(8,128)(2,1)}, f32[128,128]{1,0:T(8,128)S(1)}, f32[2,768]{1,0:T(2,128)S(1)}) custom-call(bf16[8,208,768]{2,1,0:T(8,128)(2,1)S(1)} %copy-done.3, bf16[768,768]{1,0:T(8,128)(2,1)S(1)} %copy-done.5, bf16[8,208,2304]{2,1,0:T(8,128)(2,1)} %get-tuple-element.325.refs_2_, ...), custom_call_target="tpu_custom_call", output_to_operand_aliasing={{0}: (6, {})} | custom-call | flops 100000000 | bytes 100000 | tf_op jit(solution)/shard_map/attend_back/pallas_call | solution.py:750
  276.0 16.5 %input_back.1 = (f32[196,8,768]{2,1,0:T(8,128)}, f32[2,768]{1,0:T(2,128)S(1)}) custom-call(s32[3]{0:T(128)S(1)} %copy-done.12, bf16[8,208,2304]{2,1,0:T(8,128)(2,1)} %get-tuple-element.380.dqkv_ref, bf16[768,2304]{1,0:T(8,128)(2,1)S(1)} %copy-done.4, bf16[8,208,768]{2,1,0:T(8,128)(2,1)S(1)} %copy-done.2, f32[8,208,768]{2,1,0:T(8,128)} %get-tuple-element.367.gh_ref, ...), custom_call_target="tpu_custom_call" | custom-call | flops 100000000 | bytes 100000 | tf_op jit(solution)/shard_map/input_back/pallas_call | solution.py:775
  292.6 2.0 pack.1.notes_ref
  296.4 8.7 %qkv_grad.2 = bf16[16,48,1280]{2,1,0:T(8,128)(2,1)} custom-call(s32[3]{0:T(128)} %copy-done.11, bf16[1664,768]{1,0:T(8,128)(2,1)} %bitcast.96, bf16[1664,2304]{1,0:T(8,128)(2,1)} %bitcast.90, bf16[4,8,48,128]{3,2,1,0:T(8,128)(2,1)} %copy-done.6), custom_call_target="tpu_custom_call" | custom-call | flops 100000000 | bytes 100000 | tf_op jit(solution)/shard_map/qkv_grad/pallas_call | solution.py:919
  305.2 8.7 %qkv_grad.3 = bf16[16,48,1280]{2,1,0:T(8,128)(2,1)} custom-call(s32[3]{0:T(128)} %copy-done.11, bf16[1664,768]{1,0:T(8,128)(2,1)} %bitcast.97, bf16[1664,2304]{1,0:T(8,128)(2,1)} %bitcast.91, bf16[4,8,48,128]{3,2,1,0:T(8,128)(2,1)} %copy-done.6), custom_call_target="tpu_custom_call" | custom-call | flops 100000000 | bytes 100000 | tf_op jit(solution)/shard_map/qkv_grad/pallas_call | solution.py:919
  321.2 10.1 %collective-permute-done.48 = bf16[2,48,768]{2,1,0:T(8,128)(2,1)S(1)} collective-permute-done((bf16[2,48,768]{2,1,0:T(8,128)(2,1)S(1)}, bf16[2,48,768]{2,1,0:T(8,128)(2,1)S(1)}, u32[]{:S(2)}, u32[]{:S(2)}) %collective-permute-start.48) | collective-permute-done | bytes 147488 | tf_op jit(solution)/shard_map/ppermute | solution.py:984
  333.7 5.1 %collective-permute-done.50 = bf16[2,48,1280]{2,1,0:T(8,128)(2,1)S(1)} collective-permute-done((bf16[2,48,1280]{2,1,0:T(8,128)(2,1)S(1)}, bf16[2,48,1280]{2,1,0:T(8,128)(2,1)S(1)}, u32[]{:S(2)}, u32[]{:S(2)}) %collective-permute-start.50) | collective-permute-done | bytes 245792 | tf_op jit(solution)/shard_map/ppermute | solution.py:984
  340.4 3.7 %collective-permute-start.52 = (bf16[48,1280]{1,0:T(8,128)(2,1)S(1)}, bf16[48,1280]{1,0:T(8,128)(2,1)S(1)}, u32[]{:S(2)}, u32[]{:S(2)}) collective-permute-start(bf16[48,1280]{1,0:T(8,128)(2,1)S(1)} %get-tuple-element.402), channel_id=1, source_target_pairs={{0,2},{1,3},{2,0},{3,1},{4,6},{5,7},{6,4},{7,5},{8,10},{9,11},{10,... | collective-permute-start | bytes 368648 | tf_op jit(solution)/shard_map/ppermute | solution.py:984
  347.8 6.9 %collective-permute-done.53 = bf16[48,1280]{1,0:T(8,128)(2,1)S(1)} collective-permute-done((bf16[48,1280]{1,0:T(8,128)(2,1)S(1)}, bf16[48,1280]{1,0:T(8,128)(2,1)S(1)}, u32[]{:S(2)}, u32[]{:S(2)}) %collective-permute-start.53) | collective-permute-done | bytes 122912 | tf_op jit(solution)/shard_map/ppermute | solution.py:984
  356.4 2.2 shard.1
  358.6 2.0 collective-permute-done.56.refs_1_
  360.6 1.9 copy.70
  (269 shorter events, 80.9 us)
Async XLA Ops:
  4.0 15.3 %collective-permute-start.2 = (bf16[48,1280]{1,0:T(8,128)(2,1)S(1)}, bf16[48,1280]{1,0:T(8,128)(2,1)S(1)}, u32[]{:S(2)}, u32[]{:S(2)}) collective-permute-start(bf16[48,1280]{1,0:T(8,128)(2,1)S(1)} %pad_maximum_fusion.16), channel_id=1, source_target_pairs={{0,6},{1,7},{2,4},{3,5},{4,2},{5,3},{6,0},{7,1},{8,14},{9,15},{10,... | collective-permute-start | bytes 368648 | tf_op jit(solution)/shard_map/ppermute | solution.py:984
  28.8 11.8 %collective-permute-start.7 = (bf16[4,48,1280]{2,1,0:T(8,128)(2,1)S(1)}, bf16[4,48,1280]{2,1,0:T(8,128)(2,1)S(1)}, u32[]{:S(2)}, u32[]{:S(2)}) collective-permute-start(bf16[4,48,1280]{2,1,0:T(8,128)(2,1)S(1)} %pad_maximum_fusion.7.b_ref), channel_id=1, source_target_pairs={{0,1},{1,0},{2,3},{3,2},{4,5},{5,4},{6,7},{7,6},{8,9},{9,8},{10,11... | collective-permute-start | bytes 1474568 | tf_op jit(solution)/shard_map/ppermute | solution.py:984
  50.7 25.8 %collective-permute-start.12 = (bf16[2,3,48,768]{3,2,1,0:T(8,128)(2,1)S(1)}, bf16[2,3,48,768]{3,2,1,0:T(8,128)(2,1)S(1)}, u32[]{:S(2)}, u32[]{:S(2)}) collective-permute-start(bf16[2,3,48,768]{3,2,1,0:T(8,128)(2,1)S(1)} %pad_maximum_fusion.8), channel_id=1, source_target_pairs={{0,1},{1,0},{2,3},{3,2},{4,5},{5,4},{6,7},{7,6},{8,9},{9,8},{10,11... | collective-permute-start | bytes 1327112 | tf_op jit(solution)/shard_map/ppermute | solution.py:984
  51.8 24.7 %collective-permute-start.13 = (bf16[2,3,48,768]{3,2,1,0:T(8,128)(2,1)S(1)}, bf16[2,3,48,768]{3,2,1,0:T(8,128)(2,1)S(1)}, u32[]{:S(2)}, u32[]{:S(2)}) collective-permute-start(bf16[2,3,48,768]{3,2,1,0:T(8,128)(2,1)S(1)} %pad_maximum_fusion.9), channel_id=1, source_target_pairs={{0,16},{8,24},{16,0},{24,8},{1,17},{9,25},{17,1},{25,9},{2,18},{10... | collective-permute-start | bytes 1327112 | tf_op jit(solution)/shard_map/ppermute | solution.py:984
  53.3 23.1 %collective-permute-start.16 = (bf16[2,48,768]{2,1,0:T(8,128)(2,1)S(1)}, bf16[2,48,768]{2,1,0:T(8,128)(2,1)S(1)}, u32[]{:S(2)}, u32[]{:S(2)}) collective-permute-start(bf16[2,48,768]{2,1,0:T(8,128)(2,1)S(1)} %bitcast.116), channel_id=1, source_target_pairs={{0,6},{1,7},{2,4},{3,5},{4,2},{5,3},{6,0},{7,1},{8,14},{9,15},{10,... | collective-permute-start | bytes 442376 | tf_op jit(solution)/shard_map/ppermute | solution.py:984
  56.6 19.9 %collective-permute-start.15 = (bf16[2,48,768]{2,1,0:T(8,128)(2,1)S(1)}, bf16[2,48,768]{2,1,0:T(8,128)(2,1)S(1)}, u32[]{:S(2)}, u32[]{:S(2)}) collective-permute-start(bf16[2,48,768]{2,1,0:T(8,128)(2,1)S(1)} %bitcast.117), channel_id=1, source_target_pairs={{0,4},{1,5},{2,6},{3,7},{4,0},{5,1},{6,2},{7,3},{8,12},{9,13},{10,... | collective-permute-start | bytes 442376 | tf_op jit(solution)/shard_map/ppermute | solution.py:984
  58.1 18.4 %collective-permute-start.14 = (bf16[2,48,768]{2,1,0:T(8,128)(2,1)S(1)}, bf16[2,48,768]{2,1,0:T(8,128)(2,1)S(1)}, u32[]{:S(2)}, u32[]{:S(2)}) collective-permute-start(bf16[2,48,768]{2,1,0:T(8,128)(2,1)S(1)} %bitcast.118), channel_id=1, source_target_pairs={{0,2},{1,3},{2,0},{3,1},{4,6},{5,7},{6,4},{7,5},{8,10},{9,11},{10,... | collective-permute-start | bytes 442376 | tf_op jit(solution)/shard_map/ppermute | solution.py:984
  76.8 22.6 %collective-permute-start.21 = (bf16[4,3,48,768]{3,2,1,0:T(8,128)(2,1)S(1)}, bf16[4,3,48,768]{3,2,1,0:T(8,128)(2,1)S(1)}, u32[]{:S(2)}, u32[]{:S(2)}) collective-permute-start(bf16[4,3,48,768]{3,2,1,0:T(8,128)(2,1)S(1)} %pad_maximum_fusion.2.refs_4_), channel_id=1, source_target_pairs={{0,8},{8,0},{16,24},{24,16},{1,9},{9,1},{17,25},{25,17},{2,10},{10... | collective-permute-start | bytes 2654216 | tf_op jit(solution)/shard_map/ppermute | solution.py:984
  76.9 22.5 %collective-permute-start.19 = (bf16[4,3,48,768]{3,2,1,0:T(8,128)(2,1)S(1)}, bf16[4,3,48,768]{3,2,1,0:T(8,128)(2,1)S(1)}, u32[]{:S(2)}, u32[]{:S(2)}) collective-permute-start(bf16[4,3,48,768]{3,2,1,0:T(8,128)(2,1)S(1)} %pad_maximum_fusion.2.refs_4_), channel_id=1, source_target_pairs={{0,16},{8,24},{16,0},{24,8},{1,17},{9,25},{17,1},{25,9},{2,18},{10... | collective-permute-start | bytes 2654216 | tf_op jit(solution)/shard_map/ppermute | solution.py:984
  78.4 21.0 %collective-permute-start.22 = (bf16[4,3,48,768]{3,2,1,0:T(8,128)(2,1)S(1)}, bf16[4,3,48,768]{3,2,1,0:T(8,128)(2,1)S(1)}, u32[]{:S(2)}, u32[]{:S(2)}) collective-permute-start(bf16[4,3,48,768]{3,2,1,0:T(8,128)(2,1)S(1)} %pad_maximum_fusion.3.refs_6_), channel_id=1, source_target_pairs={{0,8},{8,0},{16,24},{24,16},{1,9},{9,1},{17,25},{25,17},{2,10},{10... | collective-permute-start | bytes 2654216 | tf_op jit(solution)/shard_map/ppermute | solution.py:984
  78.5 21.9 %collective-permute-start.20 = (bf16[4,3,48,768]{3,2,1,0:T(8,128)(2,1)S(1)}, bf16[4,3,48,768]{3,2,1,0:T(8,128)(2,1)S(1)}, u32[]{:S(2)}, u32[]{:S(2)}) collective-permute-start(bf16[4,3,48,768]{3,2,1,0:T(8,128)(2,1)S(1)} %pad_maximum_fusion.3.refs_6_), channel_id=1, source_target_pairs={{0,1},{1,0},{2,3},{3,2},{4,5},{5,4},{6,7},{7,6},{8,9},{9,8},{10,11... | collective-permute-start | bytes 2654216 | tf_op jit(solution)/shard_map/ppermute | solution.py:984
  110.7 28.3 %collective-permute-start.27 = (bf16[4,2,48,768]{3,2,1,0:T(8,128)(2,1)S(1)}, bf16[4,2,48,768]{3,2,1,0:T(8,128)(2,1)S(1)}, u32[]{:S(2)}, u32[]{:S(2)}) collective-permute-start(bf16[4,2,48,768]{3,2,1,0:T(8,128)(2,1)S(1)} %pad_maximum_fusion.4.refs_9_), channel_id=1, source_target_pairs={{0,8},{8,0},{16,24},{24,16},{1,9},{9,1},{17,25},{25,17},{2,10},{10... | collective-permute-start | bytes 1769480 | tf_op jit(solution)/shard_map/ppermute | solution.py:984
  110.8 28.2 %collective-permute-start.25 = (bf16[4,2,48,768]{3,2,1,0:T(8,128)(2,1)S(1)}, bf16[4,2,48,768]{3,2,1,0:T(8,128)(2,1)S(1)}, u32[]{:S(2)}, u32[]{:S(2)}) collective-permute-start(bf16[4,2,48,768]{3,2,1,0:T(8,128)(2,1)S(1)} %pad_maximum_fusion.4.refs_9_), channel_id=1, source_target_pairs={{0,16},{8,24},{16,0},{24,8},{1,17},{9,25},{17,1},{25,9},{2,18},{10... | collective-permute-start | bytes 1769480 | tf_op jit(solution)/shard_map/ppermute | solution.py:984
  111.5 27.6 %collective-permute-start.28 = (bf16[4,2,48,768]{3,2,1,0:T(8,128)(2,1)S(1)}, bf16[4,2,48,768]{3,2,1,0:T(8,128)(2,1)S(1)}, u32[]{:S(2)}, u32[]{:S(2)}) collective-permute-start(bf16[4,2,48,768]{3,2,1,0:T(8,128)(2,1)S(1)} %pad_maximum_fusion.5.refs_11_), channel_id=1, source_target_pairs={{0,8},{8,0},{16,24},{24,16},{1,9},{9,1},{17,25},{25,17},{2,10},{10... | collective-permute-start | bytes 1769480 | tf_op jit(solution)/shard_map/ppermute | solution.py:984
  111.8 27.3 %collective-permute-start.26 = (bf16[4,2,48,768]{3,2,1,0:T(8,128)(2,1)S(1)}, bf16[4,2,48,768]{3,2,1,0:T(8,128)(2,1)S(1)}, u32[]{:S(2)}, u32[]{:S(2)}) collective-permute-start(bf16[4,2,48,768]{3,2,1,0:T(8,128)(2,1)S(1)} %pad_maximum_fusion.5.refs_11_), channel_id=1, source_target_pairs={{0,1},{1,0},{2,3},{3,2},{4,5},{5,4},{6,7},{7,6},{8,9},{9,8},{10,11... | collective-permute-start | bytes 1769480 | tf_op jit(solution)/shard_map/ppermute | solution.py:984
  210.6 12.3 %collective-permute-start.34 = (bf16[16,2,48,768]{3,2,1,0:T(8,128)(2,1)}, bf16[16,2,48,768]{3,2,1,0:T(8,128)(2,1)S(1)}, u32[]{:S(2)}, u32[]{:S(2)}) collective-permute-start(bf16[16,2,48,768]{3,2,1,0:T(8,128)(2,1)} %up_grad.2), channel_id=1, source_target_pairs={{0,8},{8,0},{16,24},{24,16},{1,9},{9,1},{17,25},{25,17},{2,10},{10... | collective-permute-start | bytes 7077896 | tf_op jit(solution)/shard_map/ppermute | solution.py:984
  211.0 24.9 %collective-permute-start.32 = (bf16[4,3,48,768]{3,2,1,0:T(8,128)(2,1)}, bf16[4,3,48,768]{3,2,1,0:T(8,128)(2,1)}, u32[]{:S(2)}, u32[]{:S(2)}) collective-permute-start(bf16[4,3,48,768]{3,2,1,0:T(8,128)(2,1)} %get-tuple-element.316), channel_id=1, source_target_pairs={{0,16},{8,24},{16,0},{24,8},{1,17},{9,25},{17,1},{25,9},{2,18},{10... | collective-permute-start | bytes 2654216 | tf_op jit(solution)/shard_map/ppermute | solution.py:984
  212.2 23.6 %collective-permute-start.33 = (bf16[4,3,48,768]{3,2,1,0:T(8,128)(2,1)}, bf16[4,3,48,768]{3,2,1,0:T(8,128)(2,1)}, u32[]{:S(2)}, u32[]{:S(2)}) collective-permute-start(bf16[4,3,48,768]{3,2,1,0:T(8,128)(2,1)} %get-tuple-element.317), channel_id=1, source_target_pairs={{0,1},{1,0},{2,3},{3,2},{4,5},{5,4},{6,7},{7,6},{8,9},{9,8},{10,11... | collective-permute-start | bytes 2654216 | tf_op jit(solution)/shard_map/ppermute | solution.py:984
  224.6 32.8 %collective-permute-start.37 = (bf16[4,2,48,768]{3,2,1,0:T(8,128)(2,1)S(1)}, bf16[4,2,48,768]{3,2,1,0:T(8,128)(2,1)S(1)}, u32[]{:S(2)}, u32[]{:S(2)}) collective-permute-start(bf16[4,2,48,768]{3,2,1,0:T(8,128)(2,1)S(1)} %get-tuple-element.338), channel_id=1, source_target_pairs={{0,16},{8,24},{16,0},{24,8},{1,17},{9,25},{17,1},{25,9},{2,18},{10... | collective-permute-start | bytes 1769480 | tf_op jit(solution)/shard_map/ppermute | solution.py:984
  225.4 31.9 %collective-permute-start.38 = (bf16[4,2,48,768]{3,2,1,0:T(8,128)(2,1)S(1)}, bf16[4,2,48,768]{3,2,1,0:T(8,128)(2,1)S(1)}, u32[]{:S(2)}, u32[]{:S(2)}) collective-permute-start(bf16[4,2,48,768]{3,2,1,0:T(8,128)(2,1)S(1)} %get-tuple-element.339), channel_id=1, source_target_pairs={{0,1},{1,0},{2,3},{3,2},{4,5},{5,4},{6,7},{7,6},{8,9},{9,8},{10,11... | collective-permute-start | bytes 1769480 | tf_op jit(solution)/shard_map/ppermute | solution.py:984
  238.6 18.7 %collective-permute-start.35 = (bf16[2,3,48,768]{3,2,1,0:T(8,128)(2,1)S(1)}, bf16[2,3,48,768]{3,2,1,0:T(8,128)(2,1)S(1)}, u32[]{:S(2)}, u32[]{:S(2)}) collective-permute-start(bf16[2,3,48,768]{3,2,1,0:T(8,128)(2,1)S(1)} %slice.241), channel_id=1, source_target_pairs={{0,1},{1,0},{2,3},{3,2},{4,5},{5,4},{6,7},{7,6},{8,9},{9,8},{10,11... | collective-permute-start | bytes 1327112 | tf_op jit(solution)/shard_map/ppermute | solution.py:984
  239.6 17.7 %collective-permute-start.36 = (bf16[2,3,48,768]{3,2,1,0:T(8,128)(2,1)S(1)}, bf16[2,3,48,768]{3,2,1,0:T(8,128)(2,1)S(1)}, u32[]{:S(2)}, u32[]{:S(2)}) collective-permute-start(bf16[2,3,48,768]{3,2,1,0:T(8,128)(2,1)S(1)} %slice.242), channel_id=1, source_target_pairs={{0,16},{8,24},{16,0},{24,8},{1,17},{9,25},{17,1},{25,9},{2,18},{10... | collective-permute-start | bytes 1327112 | tf_op jit(solution)/shard_map/ppermute | solution.py:984
  259.5 15.8 %collective-permute-start.39 = (bf16[2,2,48,768]{3,2,1,0:T(8,128)(2,1)S(1)}, bf16[2,2,48,768]{3,2,1,0:T(8,128)(2,1)S(1)}, u32[]{:S(2)}, u32[]{:S(2)}) collective-permute-start(bf16[2,2,48,768]{3,2,1,0:T(8,128)(2,1)S(1)} %slice.248), channel_id=1, source_target_pairs={{0,1},{1,0},{2,3},{3,2},{4,5},{5,4},{6,7},{7,6},{8,9},{9,8},{10,11... | collective-permute-start | bytes 884744 | tf_op jit(solution)/shard_map/ppermute | solution.py:984
  260.6 14.7 %collective-permute-start.40 = (bf16[2,2,48,768]{3,2,1,0:T(8,128)(2,1)S(1)}, bf16[2,2,48,768]{3,2,1,0:T(8,128)(2,1)S(1)}, u32[]{:S(2)}, u32[]{:S(2)}) collective-permute-start(bf16[2,2,48,768]{3,2,1,0:T(8,128)(2,1)S(1)} %slice.249), channel_id=1, source_target_pairs={{0,16},{8,24},{16,0},{24,8},{1,17},{9,25},{17,1},{25,9},{2,18},{10... | collective-permute-start | bytes 884744 | tf_op jit(solution)/shard_map/ppermute | solution.py:984
  261.3 13.9 %collective-permute-start.41 = (bf16[3,48,768]{2,1,0:T(8,128)(2,1)S(1)}, bf16[3,48,768]{2,1,0:T(8,128)(2,1)S(1)}, u32[]{:S(2)}, u32[]{:S(2)}) collective-permute-start(bf16[3,48,768]{2,1,0:T(8,128)(2,1)S(1)} %get-tuple-element.356), channel_id=1, source_target_pairs={{0,2},{1,3},{2,0},{3,1},{4,6},{5,7},{6,4},{7,5},{8,10},{9,11},{10,... | collective-permute-start | bytes 663560 | tf_op jit(solution)/shard_map/ppermute | solution.py:984
  263.2 29.2 %collective-permute-start.42 = (bf16[3,48,768]{2,1,0:T(8,128)(2,1)S(1)}, bf16[3,48,768]{2,1,0:T(8,128)(2,1)S(1)}, u32[]{:S(2)}, u32[]{:S(2)}) collective-permute-start(bf16[3,48,768]{2,1,0:T(8,128)(2,1)S(1)} %get-tuple-element.364), channel_id=1, source_target_pairs={{0,4},{1,5},{2,6},{3,7},{4,0},{5,1},{6,2},{7,3},{8,12},{9,13},{10,... | collective-permute-start | bytes 663560 | tf_op jit(solution)/shard_map/ppermute | solution.py:984
  264.6 27.9 %collective-permute-start.43 = (bf16[3,48,768]{2,1,0:T(8,128)(2,1)S(1)}, bf16[3,48,768]{2,1,0:T(8,128)(2,1)S(1)}, u32[]{:S(2)}, u32[]{:S(2)}) collective-permute-start(bf16[3,48,768]{2,1,0:T(8,128)(2,1)S(1)} %get-tuple-element.365), channel_id=1, source_target_pairs={{0,6},{1,7},{2,4},{3,5},{4,2},{5,3},{6,0},{7,1},{8,14},{9,15},{10,... | collective-permute-start | bytes 663560 | tf_op jit(solution)/shard_map/ppermute | solution.py:984
  315.5 15.8 %collective-permute-start.46 = (bf16[4,48,1280]{2,1,0:T(8,128)(2,1)S(1)}, bf16[4,48,1280]{2,1,0:T(8,128)(2,1)S(1)}, u32[]{:S(2)}, u32[]{:S(2)}) collective-permute-start(bf16[4,48,1280]{2,1,0:T(8,128)(2,1)S(1)} %get-tuple-element.387), channel_id=1, source_target_pairs={{0,16},{8,24},{16,0},{24,8},{1,17},{9,25},{17,1},{25,9},{2,18},{10... | collective-permute-start | bytes 1474568 | tf_op jit(solution)/shard_map/ppermute | solution.py:984
  316.8 14.4 %collective-permute-start.47 = (bf16[4,48,1280]{2,1,0:T(8,128)(2,1)S(1)}, bf16[4,48,1280]{2,1,0:T(8,128)(2,1)S(1)}, u32[]{:S(2)}, u32[]{:S(2)}) collective-permute-start(bf16[4,48,1280]{2,1,0:T(8,128)(2,1)S(1)} %get-tuple-element.388), channel_id=1, source_target_pairs={{0,1},{1,0},{2,3},{3,2},{4,5},{5,4},{6,7},{7,6},{8,9},{9,8},{10,11... | collective-permute-start | bytes 1474568 | tf_op jit(solution)/shard_map/ppermute | solution.py:984
  317.9 13.3 %collective-permute-start.48 = (bf16[2,48,768]{2,1,0:T(8,128)(2,1)S(1)}, bf16[2,48,768]{2,1,0:T(8,128)(2,1)S(1)}, u32[]{:S(2)}, u32[]{:S(2)}) collective-permute-start(bf16[2,48,768]{2,1,0:T(8,128)(2,1)S(1)} %get-tuple-element.390), channel_id=1, source_target_pairs={{0,4},{1,5},{2,6},{3,7},{4,0},{5,1},{6,2},{7,3},{8,12},{9,13},{10,... | collective-permute-start | bytes 442376 | tf_op jit(solution)/shard_map/ppermute | solution.py:984
  319.7 11.5 %collective-permute-start.49 = (bf16[2,48,768]{2,1,0:T(8,128)(2,1)S(1)}, bf16[2,48,768]{2,1,0:T(8,128)(2,1)S(1)}, u32[]{:S(2)}, u32[]{:S(2)}) collective-permute-start(bf16[2,48,768]{2,1,0:T(8,128)(2,1)S(1)} %get-tuple-element.391), channel_id=1, source_target_pairs={{0,6},{1,7},{2,4},{3,5},{4,2},{5,3},{6,0},{7,1},{8,14},{9,15},{10,... | collective-permute-start | bytes 442376 | tf_op jit(solution)/shard_map/ppermute | solution.py:984
  339.6 15.1 %collective-permute-start.55 = (bf16[5,48,768]{2,1,0:T(8,128)(2,1)S(1)}, bf16[5,48,768]{2,1,0:T(8,128)(2,1)S(1)}, u32[]{:S(2)}, u32[]{:S(2)}) collective-permute-start(bf16[5,48,768]{2,1,0:T(8,128)(2,1)S(1)} %pad_maximum_fusion.10.refs_0_), channel_id=1, source_target_pairs={{0,16},{8,24},{16,0},{24,8},{1,17},{9,25},{17,1},{25,9},{2,18},{10... | collective-permute-start | bytes 1105928 | tf_op jit(solution)/shard_map/ppermute | solution.py:984
  (72 other events, 642.5 us)

commit v5 on v4

--- a/solution.py
+++ b/solution.py
@@ -172,7 +172,7 @@
     return acc
 
 
-def notes_kernel(me_ref, a_ref, b_ref, c_ref, vec_ref, rel_ref, relt_ref):
+def notes_kernel(me_ref, a_ref, b_ref, c_ref, vec_ref, rel_ref, relt_ref, turn_ref):
     picks = [(a_ref, at, at % 2 * 2 + at // 2) for at in range(4)]
     picks += [(b_ref, at, 4 + at * 2) for at in range(2)] + [(c_ref, at, 5 + at * 2) for at in range(2)]
     owner_of = lambda at: me_ref[1] ^ picks[at][2]
@@ -180,21 +180,16 @@
     vec_ref[...] = spread_rows(
         lambda at: picks[at][0][picks[at][1], 0:16, lanes], owner_of, 96, D
     )[0:8]
+    for at in range(8):
+        both = picks[at][0][picks[at][1], 16:32, lanes].astype(F32)
+        for copy in range(2):
+            place = pl.ds(pl.multiple_of(copy * 64 + owner_of(at) * 8, 8), 8)
+            turn_ref[place, :] = jnp.concatenate([both[0:8, 0:32], both[8:16, 0:32]] * 2, axis=1)
     row = lax.broadcasted_iota(jnp.int32, (128, 128), 0)
     col = lax.broadcasted_iota(jnp.int32, (128, 128), 1)
-    halves = []
-    for which in range(2):
-        acc = jnp.zeros((32, 128), F32)
-        for at in range(8):
-            lane = row - 8 * which
-            place = lane + owner_of(at) * 8
-            put = ((lane >= 0) & (lane < 8) & ((col == place) | (col == place + 64))).astype(BF16)
-            acc = acc + nn(picks[at][0][picks[at][1], 16:48, lanes], put)
-        halves.append(acc)
-    table = jnp.concatenate(halves * 2, axis=0)
-    table = jnp.where((row < 64) == (col < 64), table, 0.0).astype(BF16)
-    rel_ref[...] = table
-    relt_ref[...] = table.T
+    turned = jnp.where((row < 64) == (col < 64), turn_ref[...], 0.0)
+    relt_ref[...] = turned.astype(BF16)
+    rel_ref[...] = turned.T.astype(BF16)
 
 
 def attend_kernel(*refs, first, pieces, earlier):
@@ -204,13 +199,14 @@
     at += 3 + earlier
     qkv_ref, prob_ref, mix_ref, fin_ref = refs[at : at + 4]
     if pieces:
-        w_ref, sem = refs[at + 4 :]
+        w_ref, sem, s_ref = refs[at + 4 :]
 
         @pl.when(pl.program_id(0) == 0)
         def _():
             load_first(base_ref, refs[2 : 2 + pieces], w_ref, sem)
     else:
         w_ref = refs[2]
+        s_ref = refs[at + 4]
     keep = keep_column(base_ref, pl.program_id(0) + first)
     scaled, _ = norm_parts(tok_ref[0].astype(F32))
     first_in = (keep * (scaled * vec_ref[0:1, :] + vec_ref[1:2, :])).astype(BF16)
@@ -251,20 +247,30 @@
             else:
                 query_ext = jnp.concatenate([high, rest, scaled_q], axis=0)
                 keys_ext = jnp.where(low_half, place_pair, keys)
-            scores = nn(keys_ext, query_ext)
-            scores = jnp.concatenate(
-                [scores[0:192], jnp.where(tail_rows < SLOTS, scores[192:208], -1e30)], axis=0
-            )
-            peak = jnp.max(scores, axis=0, keepdims=True)
-            expo = jnp.exp(scores - peak)
-            total = jnp.sum(expo, axis=0, keepdims=True)
-            probs = (expo * (1.0 / total)).astype(BF16)
-            prob_ref[0, 2 * pair + head] = probs
-            mixed.append(tn(probs, values)[0:ROWS].astype(BF16))
+            s_ref[2 * pair + head] = nn(keys_ext, query_ext)
+        return carry
+
+    def soft(head, carry):
+        scores = s_ref[head]
+        scores = jnp.concatenate(
+            [scores[0:192], jnp.where(tail_rows < SLOTS, scores[192:208], -1e30)], axis=0
+        )
+        peak = jnp.max(scores, axis=0, keepdims=True)
+        expo = jnp.exp(scores - peak)
+        total = jnp.sum(expo, axis=0, keepdims=True)
+        prob_ref[0, head] = (expo * (1.0 / total)).astype(BF16)
+        return carry
+
+    def mix(pair, carry):
+        at = pl.multiple_of(pair * PAIR, PAIR)
+        values = qkv_ref[0, :, pl.ds(pl.multiple_of(2 * D + at, PAIR), PAIR)]
+        mixed = [tn(prob_ref[0, 2 * pair + head], values)[0:ROWS].astype(BF16) for head in range(2)]
         mix_ref[0, :, pl.ds(at, PAIR)] = jnp.where(low_half, mixed[0], mixed[1])
         return carry
 
     lax.fori_loop(0, PAIRS, one_pair, 0, unroll=PAIRS)
+    lax.fori_loop(0, HEADS, soft, 0, unroll=HEADS)
+    lax.fori_loop(0, PAIRS, mix, 0, unroll=PAIRS)
 
 
 def gelu_parts(pre):
@@ -277,23 +283,32 @@
     core = me_ref[0] % 2
     for array, (ref, (half, along_y, other)) in enumerate(zip(pieces, ARRIVED)):
 
-        def start(index, carry, ref=ref, half=half, along_y=along_y, far_core=core ^ other, array=array):
+        def start_small(index, carry, ref=ref, half=half, along_y=along_y, far_core=core ^ other, array=array):
             far_x, owner = chunk_place(me_ref, index, half, along_y)
             rows = pl.ds(pl.multiple_of(owner * 96 + far_x * 48, 16), 48)
             cols = pl.ds(pl.multiple_of(far_core * 384, 128), 384)
             pltpu.make_async_copy(
-                ref.at[index, 2, :, pl.ds(0, 384)], proj.at[rows, cols], sem.at[1]
+                ref.at[index, :, pl.ds(1536, 384)], proj.at[rows, cols], sem.at[1]
             ).start()
             pltpu.make_async_copy(
-                ref.at[index, 2, pl.ds(0, 16), pl.ds(384, 384)], notes.at[array * 4 + index], sem.at[2]
+                ref.at[index, pl.ds(0, 16), pl.ds(1920, 128)], notes.at[array * 4 + index], sem.at[2]
             ).start()
-            for block in range(2):
-                cols = pl.ds(pl.multiple_of(far_core * 1536 + block * D, 128), D)
-                pltpu.make_async_copy(ref.at[index, block], up.at[rows, cols], sem.at[0]).start()
             return carry
 
+        lax.fori_loop(0, 4, start_small, 0)
+    for ref, (half, along_y, other) in zip(pieces, ARRIVED):
+
+        def start(index, carry, ref=ref, half=half, along_y=along_y, far_core=core ^ other):
+            far_x, owner = chunk_place(me_ref, index, half, along_y)
+            rows = pl.ds(pl.multiple_of(owner * 96 + far_x * 48, 16), 48)
+            cols = pl.ds(pl.multiple_of(far_core * 1536, 128), 1536)
+            pltpu.make_async_copy(
+                ref.at[index, :, pl.ds(0, 1536)], up.at[rows, cols], sem.at[0]
+            ).start()
+            return carry
+
         lax.fori_loop(0, 4, start, 0)
-    for at, full in ((2, notes), (1, proj), (0, up)):
+    for at, full in ((2, notes), (1, proj)):
         pltpu.make_async_copy(full, full, sem.at[at]).wait()
 
 
@@ -327,15 +342,16 @@
             picks += [(8 + at, 4 + at * 2) for at in range(2)] + [(12 + at, 5 + at * 2) for at in range(2)]
             owner_of = lambda at: me_ref[1] ^ picks[at][1]
             vec_ref[...] = spread_rows(
-                lambda at: notes[picks[at][0], :, 0:128], owner_of, 96, D
+                lambda at: notes[picks[at][0]], owner_of, 96, D
             )[0:8]
             for at in range(8):
                 lanes = pl.ds(pl.multiple_of(owner_of(at) * 384, 128), 384)
-                ub_ref[:, lanes] = notes[picks[at][0], 0:16, :].astype(F32)[4:5, :]
+                own = notes[picks[at][0]].astype(F32)
+                ub_ref[:, lanes] = jnp.concatenate([own[6:7], own[7:8], own[8:9]], axis=1)
             counts = notes[0].astype(F32)
             for at in range(1, 32):
                 counts = counts + notes[at].astype(F32)
-            counts = counts[5:6, 0:128]
+            counts = counts[5:6]
             lane = lax.broadcasted_iota(jnp.int32, (1, 128), 1)
             weight = jnp.where(lane == 0, 128.0, jnp.where(lane == 1, 1.0, 0.0))
             total_ref[...] = jnp.broadcast_to(
@@ -351,6 +367,12 @@
     scaled, _ = norm_parts(hidden)
     second_in = (scaled * gain_row + shift_row).astype(BF16)
     si_ref[...] = second_in.reshape(group, ROWS, D)
+    if pieces:
+
+        @pl.when(pl.program_id(0) == 0)
+        def _():
+            pltpu.make_async_copy(up_ref, up_ref, sem.at[0]).wait()
+
     for part in range(MLP // D):
         cols = slice(part * D, part * D + D)
         act, slope = gelu_parts(nn(second_in, up_ref[:, cols]) + ub_ref[:, cols])
@@ -418,7 +440,7 @@
 
 def attend_back_kernel(*refs, earlier):
     ga_ref, wp_ref, qkv_ref, prob_ref, relt_ref, placet_ref = refs[0:6]
-    dqkv_ref, rg_ref, qsum_ref, gm_ref = refs[6 + earlier :]
+    dqkv_ref, rg_ref, qsum_ref, gm_ref, s_ref, g_ref, e_ref = refs[6 + earlier :]
 
     @pl.when(pl.program_id(0) == 0)
     def _():
@@ -433,37 +455,49 @@
     blank = jnp.zeros((), BF16)
     scale = HEAD_DIM ** (-0.5)
 
-    def one_pair(pair, carry):
-        at = pl.multiple_of(pair * PAIR, PAIR)
-        q_at = pl.ds(at, PAIR)
-        k_at = pl.ds(pl.multiple_of(D + at, PAIR), PAIR)
-        v_at = pl.ds(pl.multiple_of(2 * D + at, PAIR), PAIR)
-        query = fill_rows(qkv_ref[0, :, q_at])
-        keys_t = fill_rows(qkv_ref[0, :, k_at]).T
-        values = qkv_ref[0, :, v_at]
-        grad_out = gm_ref[:, q_at]
+    pair_at = lambda base, pair: pl.ds(base + pair * PAIR, PAIR)
+    own = (
+        lambda full: jnp.where(low_full, full, blank),
+        lambda full: jnp.where(low_full, blank, full),
+    )
+    for pair in range(PAIRS):
+        values = qkv_ref[0, :, pair_at(2 * D, pair)]
         stacked = jnp.concatenate(
             [jnp.where(low_half, values, blank), jnp.where(low_half, blank, values)], axis=0
         )
-        grad_probs = nt(stacked, grad_out)
-        grad_values = jnp.zeros((ROWS, PAIR), F32)
-        grad_keys = jnp.zeros((ROWS, PAIR), F32)
-        spread, plain = [], []
+        grad_probs = nt(stacked, gm_ref[:, pair_at(0, pair)])
+        s_ref[2 * pair] = grad_probs[0:ROWS]
+        s_ref[2 * pair + 1] = grad_probs[ROWS : 2 * ROWS]
+    for head in range(HEADS):
+        probs = prob_ref[0, head].astype(F32)
+        grad_p = s_ref[head]
+        row_dot = jnp.sum(probs * grad_p, axis=0, keepdims=True)
+        g_ref[head] = (probs * (grad_p - row_dot)).astype(BF16)
+    for pair in range(PAIRS):
+        query = fill_rows(qkv_ref[0, :, pair_at(0, pair)])
+        grad_out = gm_ref[:, pair_at(0, pair)]
+        grad_values = nn(prob_ref[0, 2 * pair], own[0](grad_out)) + nn(
+            prob_ref[0, 2 * pair + 1], own[1](grad_out)
+        )
+        grad_keys = nn(g_ref[2 * pair], own[0](query)) + nn(g_ref[2 * pair + 1], own[1](query))
+        grad_values = grad_values.astype(BF16)
+        dqkv_ref[0, :, pair_at(D, pair)] = (grad_keys * scale).astype(BF16)
+        dqkv_ref[0, :, pair_at(2 * D, pair)] = grad_values
+        qsum_ref[1:2, pair_at(0, pair)] += jnp.sum(
+            grad_values.astype(F32), axis=0, keepdims=True
+        )
+    for pair in range(PAIRS):
+        keys_t = fill_rows(qkv_ref[0, :, pair_at(D, pair)]).T
         for head in range(2):
-            own = (lambda full: jnp.where(low_full, full, blank)) if head == 0 else (
-                lambda full: jnp.where(low_full, blank, full)
-            )
-            low = prob_ref[0, 2 * pair + head]
-            probs = low.astype(F32)
-            grad_p = grad_probs[head * ROWS : (head + 1) * ROWS]
-            row_dot = jnp.sum(probs * grad_p, axis=0, keepdims=True)
-            grad_score = (probs * (grad_p - row_dot)).astype(BF16)
-            grad_values = grad_values + nn(low, own(grad_out))
-            grad_keys = grad_keys + nn(grad_score, own(query))
             keys_ext = jnp.concatenate(
                 [keys_t[head * HEAD_DIM : (head + 1) * HEAD_DIM], placet_ref[...]], axis=0
             )
-            grad_ext = nn(keys_ext, fill_rows(grad_score))
+            e_ref[2 * pair + head] = nn(keys_ext, fill_rows(g_ref[2 * pair + head]))
+    for pair in range(PAIRS):
+        query = fill_rows(qkv_ref[0, :, pair_at(0, pair)])
+        plain, spread = [], []
+        for head in range(2):
+            grad_ext = e_ref[2 * pair + head]
             plain.append(grad_ext[0:64])
             spread.append(down_by(grad_ext[64:80], lane_row))
             spread.append(down_by(grad_ext[80:96], lane_col))
@@ -471,16 +505,8 @@
         grad_query = jnp.concatenate(plain, axis=0) * scale + nn(relt_ref[...], spread)
         rg_ref[...] += nn(spread, query)
         grad_query = grad_query.astype(BF16).T[0:ROWS]
-        grad_keys = (grad_keys * scale).astype(BF16)
-        grad_values = grad_values.astype(BF16)
-        dqkv_ref[0, :, q_at] = grad_query
-        dqkv_ref[0, :, k_at] = grad_keys
-        dqkv_ref[0, :, v_at] = grad_values
-        qsum_ref[0:1, q_at] += jnp.sum(grad_query.astype(F32), axis=0, keepdims=True)
-        qsum_ref[1:2, q_at] += jnp.sum(grad_values.astype(F32), axis=0, keepdims=True)
-        return carry
-
-    lax.fori_loop(0, PAIRS, one_pair, 0, unroll=PAIRS)
+        dqkv_ref[0, :, pair_at(0, pair)] = grad_query
+        qsum_ref[0:1, pair_at(0, pair)] += jnp.sum(grad_query.astype(F32), axis=0, keepdims=True)
 
 
 def input_kernel(
@@ -646,6 +672,7 @@
         out_specs=[whole_out((8, D)), whole_out((PAIR, PAIR)), whole_out((PAIR, PAIR))],
         out_shape=[shape_of((8, D), F32)] + [shape_of((PAIR, PAIR), BF16)] * 2,
         grid=(1,),
+        scratch_shapes=[pltpu.VMEM((128, 128), F32)],
         compiler_params=params(),
         cost_estimate=cost(COST, 1e5),
         name="notes",
@@ -664,11 +691,11 @@
         shape_of((count, ROWS, 3 * D), BF16), shape_of((count, HEADS, ROWS, LANES), BF16),
         shape_of((count, ROWS, D), BF16), shape_of((count, ROWS, D), BF16),
     ]
-    scratch = []
+    scratch = [pltpu.VMEM((HEADS, ROWS, LANES), F32)]
     if pieces:
         out_specs.append(whole_out((D, 3 * D)))
         out_shape.append(shape_of((D, 3 * D), BF16))
-        scratch.append(pltpu.SemaphoreType.DMA((1,)))
+        scratch.insert(0, pltpu.SemaphoreType.DMA((1,)))
     inputs = 5 + len(weights)
     return pl.pallas_call(
         functools.partial(attend_kernel, first=first, pieces=pieces, earlier=len(earlier)),
@@ -700,7 +727,7 @@
         shapes = [((D, MLP), BF16), ((D, D), BF16), ((8, D), F32), ((1, MLP), F32), ((1, 128), F32)]
         out_specs += [whole_out(s) for s, _ in shapes]
         out_shape += [shape_of(s, t) for s, t in shapes]
-        scratch += [pltpu.VMEM((32, 16, 384), BF16), pltpu.SemaphoreType.DMA((3,))]
+        scratch += [pltpu.VMEM((32, 16, 128), BF16), pltpu.SemaphoreType.DMA((3,))]
     return pl.pallas_call(
         functools.partial(up_kernel, group=group, pieces=pieces),
         grid=(count // group,),
@@ -759,7 +786,10 @@
             shape_of((count, ROWS, 3 * D), BF16), shape_of((PAIR, PAIR), F32),
             shape_of((2, D), F32),
         ],
-        scratch_shapes=[pltpu.VMEM((LANES, D), BF16)],
+        scratch_shapes=[
+            pltpu.VMEM((LANES, D), BF16), pltpu.VMEM((HEADS, ROWS, LANES), F32),
+            pltpu.VMEM((HEADS, ROWS, LANES), BF16), pltpu.VMEM((HEADS, 96, LANES), F32),
+        ],
         input_output_aliases={6: 0} if earlier else {},
         compiler_params=params(48),
         cost_estimate=cost(COST, 1e5),
@@ -930,7 +960,7 @@
             scratch_shapes=[pltpu.VMEM((D, QKV_HALF), BF16), pltpu.SemaphoreType.DMA((1,))],
         ),
         out_shape=shape_of((16, 48, QKV_HALF + NOTES), BF16),
-        compiler_params=params(60),
+        compiler_params=params(48),
         cost_estimate=cost(COST, 1e5),
         name="qkv_grad",
     )(me, left, right, notes)
@@ -1048,7 +1078,7 @@
         rect = cut(qkv_weight, far_x * 48, core * QKV_HALF, 48, QKV_HALF)
         notes = noted(
             (48, NOTES), *[(v, at, 0) for at, v in enumerate(small[0:4])],
-            (rel_pos_h, 16, 0), (rel_pos_w, 16, 8),
+            (rel_pos_h.T, 16, 0), (rel_pos_w.T, 24, 0),
         )
         rect = jnp.concatenate([rect, notes], axis=1)
         near = [rect] + [swap(rect, "fsdp", mask) for mask in (2, 4, 6)]
@@ -1056,13 +1086,10 @@
         down_rect = cut(down_weight, core * 192 + far_x * 96, 0, 96, D)
         proj_rect = cut(proj_weight, far_x * 48, core * 384, 48, 384)
         notes = noted(
-            (48, 384), *[(v, at, 0) for at, v in enumerate(small[4:8])], (up_bias, 4, 0),
-            (counted, 5, 0),
-        )
-        rects = jnp.concatenate(
-            [up_rect.reshape(48, 2, D).transpose(1, 0, 2),
-             jnp.concatenate([proj_rect, notes], axis=1)[None]], axis=0,
-        )
+            (48, 128), *[(v, at, 0) for at, v in enumerate(small[4:8])],
+            (up_bias.reshape(3, 128), 6, 0), (counted, 5, 0),
+        )
+        rects = jnp.concatenate([up_rect, proj_rect, notes], axis=1)
         down_rect = down_rect.reshape(2, 48, D)
         *near, rects, down_rect, aux = tied(*near, rects, down_rect, aux)
         planes = [rects] + [swap(rects, "fsdp", mask) for mask in (2, 4, 6)]

time: 371 us -> 354 us (0.954)
  Pallas kernels: 221 us -> 203 us
  waiting for transfers between devices: 41.3 us -> 52.8 us
  local copies, waits for them, and re-layouts: 22.3 us -> 16.3 us
    ppermute x61, waiting for transfers between devices: 41.3 us -> 52.8 us  [swap(): return lax.ppermute(values, axis, [(at, at ^ mask) for at in range(size)])]
    pallas_call x3, Pallas kernels: 35.3 us -> 27 us  [attend_back(): pl.pallas_call(functools.partial(attend_back_kernel, earlier=len(earlier)...]
    pallas_call x3, Pallas kernels: 45.2 us -> 38.3 us  [attend(): pl.pallas_call(functools.partial(attend_kernel, first=first, pieces=piece...]
    unnamed x93 -> x89, local copies, waits for them, and re-layouts: 12.4 us -> 7.1 us
  transfers between devices with their start and end apart: 61 -> 61, of which waited for: 15 -> 19; matrix products, arithmetic and copies ran while one was open for 5% -> 5% of each run, Pallas kernels for 44% -> 41%
where the time goes in v5:
time: 354 us; the launch traced here: 350 us
  Pallas kernels  203 us (57%)
  starting transfers between devices  59.4 us (17%)
  waiting for transfers between devices  52.8 us (15%)
  local copies, waits for them, and re-layouts  16.3 us (5%)
  other arithmetic  13.9 us (4%)
  between operations  4.45 us (1%)
    ppermute x61, starting transfers between devices, swap(): return lax.ppermute(values, axis, [(at, at ^ mask) for at in range(size)])  59.4 us
    ppermute x61, waiting for transfers between devices, swap(): return lax.ppermute(values, axis, [(at, at ^ mask) for at in range(size)])  52.8 us
    pallas_call x3, Pallas kernels, attend(): pl.pallas_call(functools.partial(attend_kernel, first=first, pieces=piece...  38.3 us
    pallas_call x1, Pallas kernels, mlp_down(): pl.pallas_call(functools.partial(down_kernel, group=group, pieces=pieces,...  37.9 us
    pallas_call x3, Pallas kernels, attend_back(): pl.pallas_call(functools.partial(attend_back_kernel, earlier=len(earlier)...  27 us
    pallas_call x1, Pallas kernels, mlp_up(): pl.pallas_call(functools.partial(up_kernel, group=group, pieces=pieces),...  25.7 us
    pallas_call x2, Pallas kernels, up_grad(): pl.pallas_call(up_grad_kernel, grid_spec=pltpu.PrefetchScalarGridSpec(num...  19.5 us
    pallas_call x1, Pallas kernels, input_back(): pl.pallas_call(functools.partial(input_kernel, group=group, first=first,...  16.7 us
  transfers between devices with their start and end apart: 61, of which 19 were waited for; matrix products, arithmetic and copies ran while one was open for 5% of the time, Pallas kernels for 41%

profile of v5, /device:TPU:0, one launch (start us, length us, event | category | flops | bytes accessed | tf_op | source)
XLA Modules:
  0.0 350.2 jit_solution(14182477075374576860)
XLA Ops:
  2.4 5.1 %collective-permute-start.2 = (bf16[48,1280]{1,0:T(8,128)(2,1)S(1)}, bf16[48,1280]{1,0:T(8,128)(2,1)S(1)}, u32[]{:S(2)}, u32[]{:S(2)}) collective-permute-start(bf16[48,1280]{1,0:T(8,128)(2,1)S(1)} %pad_maximum_fusion.16), channel_id=1, source_target_pairs={{0,6},{1,7},{2,4},{3,5},{4,2},{5,3},{6,0},{7,1},{8,14},{9,15},{10,... | collective-permute-start | bytes 368648 | tf_op jit(solution)/shard_map/ppermute | solution.py:1014
  23.7 3.1 collective-permute-done.5
  32.2 5.7 %collective-permute-done.8 = bf16[48,2048]{1,0:T(8,128)(2,1)S(1)} collective-permute-done((bf16[48,2048]{1,0:T(8,128)(2,1)S(1)}, bf16[48,2048]{1,0:T(8,128)(2,1)S(1)}, u32[]{:S(2)}, u32[]{:S(2)}) %collective-permute-start.8) | collective-permute-done | bytes 196640 | tf_op jit(solution)/shard_map/ppermute | solution.py:1014
  39.7 2.5 collective-permute-start.11
  44.3 4.2 %collective-permute-done.11 = bf16[48,2048]{1,0:T(8,128)(2,1)S(1)} collective-permute-done((bf16[48,2048]{1,0:T(8,128)(2,1)S(1)}, bf16[48,2048]{1,0:T(8,128)(2,1)S(1)}, u32[]{:S(2)}, u32[]{:S(2)}) %collective-permute-start.11) | collective-permute-done | bytes 196640 | tf_op jit(solution)/shard_map/ppermute | solution.py:1014
  50.0 2.6 collective-permute-start.16
  54.4 15.8 %attend.3 = (bf16[8,208,2304]{2,1,0:T(8,128)(2,1)}, bf16[8,12,208,256]{3,2,1,0:T(8,128)(2,1)}, bf16[8,208,768]{2,1,0:T(8,128)(2,1)}, bf16[8,208,768]{2,1,0:T(8,128)(2,1)}, bf16[768,2304]{1,0:T(8,128)(2,1)}) custom-call(s32[3]{0:T(128)} %copy-done.11, bf16[8,208,768]{2,1,0:T(8,128)(2,1)} %pad.68.refs_1_.tok_ref, bf16[8,48,1280]{2,1,0:T(8,128)(2,1)} %copy-done.17, ...), custom_call_target="tpu_custom_call" | custom-call | flops 100000000 | bytes 100000 | tf_op jit(solution)/shard_map/attend/pallas_call | solution.py:700
  73.6 16.4 %attend.4 = (bf16[8,208,2304]{2,1,0:T(8,128)(2,1)}, bf16[8,12,208,256]{3,2,1,0:T(8,128)(2,1)}, bf16[8,208,768]{2,1,0:T(8,128)(2,1)}, bf16[8,208,768]{2,1,0:T(8,128)(2,1)}) custom-call(s32[3]{0:T(128)} %copy-done.11, bf16[8,208,768]{2,1,0:T(8,128)(2,1)} %pad.68.refs_1_.tok_ref, ...), custom_call_target="tpu_custom_call", output_to_operand_aliasing={{0}: (6, {}), {1}: (7, {}), {2}: (8, {}), {3}: (9, {})} | custom-call | flops 100000000 | bytes 100000 | tf_op jit(solution)/shard_map/attend/pallas_call | solution.py:700
  94.5 6.1 %attend.5 = (bf16[8,208,2304]{2,1,0:T(8,128)(2,1)}, bf16[8,12,208,256]{3,2,1,0:T(8,128)(2,1)}, bf16[8,208,768]{2,1,0:T(8,128)(2,1)}, bf16[8,208,768]{2,1,0:T(8,128)(2,1)}) custom-call(s32[3]{0:T(128)} %copy-done.11, bf16[8,208,768]{2,1,0:T(8,128)(2,1)} %pad.68.refs_1_.tok_ref, ...), custom_call_target="tpu_custom_call", output_to_operand_aliasing={{0}: (6, {}), {1}: (7, {}), {2}: (8, {}), {3}: (9, {})} | custom-call | flops 100000000 | bytes 100000 | tf_op jit(solution)/shard_map/attend/pallas_call | solution.py:700
  104.4 25.7 %mlp_up.1 = (f32[8,208,768]{2,1,0:T(8,128)}, bf16[8,208,768]{2,1,0:T(8,128)(2,1)}, bf16[8,208,3072]{2,1,0:T(8,128)(2,1)}, bf16[8,208,3072]{2,1,0:T(8,128)(2,1)},...) custom-call(s32[3]{0:T(128)} %copy-done.11, ...), custom_call_target="tpu_custom_call" | custom-call | flops 800000000 | bytes 100000 | tf_op jit(solution)/shard_map/mlp_up/pallas_call | solution.py:731
  134.0 37.9 %mlp_down.1 = (bf16[8,196,768]{2,1,0:T(8,128)(2,1)}, f32[8,208,768]{2,1,0:T(8,128)}, bf16[8,208,768]{2,1,0:T(8,128)(2,1)}, bf16[8,208,768]{2,1,0:T(8,128)(2,1)},...) custom-call(s32[3]{0:T(128)} %copy-done.11, f32[8,208,768]{2,1,0:T(8,128)} %get-tuple-element.293.refs_1_, ...), custom_call_target="tpu_custom_call" | custom-call | flops 800000000 | bytes 100000 | tf_op jit(solution)/shard_map/mlp_down/pallas_call | solution.py:755
  171.9 16.7 %down_grad.1 = (bf16[16,3,48,768]{3,2,1,0:T(8,128)(2,1)}, bf16[16,3,48,768]{3,2,1,0:T(8,128)(2,1)}) custom-call(s32[3]{0:T(128)} %copy-done.11, bf16[1664,3072]{1,0:T(8,128)(2,1)} %bitcast.90, bf16[1664,768]{1,0:T(8,128)(2,1)} %bitcast.94, bf16[1664,768]{1,0:T(8,128)(2,1)} %bitcast.91, bf16[1664,768]{1,0:T(8,128)(2,1)} %bitcast.83), custom_call_target="tpu_custom_call" | custom-call | flops 100000000 | bytes 100000 | tf_op jit(solution)/shard_map/down_grad/pallas_call | solution.py:992
  188.8 9.9 %up_grad.2 = bf16[16,2,48,768]{3,2,1,0:T(8,128)(2,1)} custom-call(s32[3]{0:T(128)} %copy-done.11, bf16[1664,768]{1,0:T(8,128)(2,1)} %bitcast.92, bf16[1664,3072]{1,0:T(8,128)(2,1)} %bitcast.88), custom_call_target="tpu_custom_call" | custom-call | flops 100000000 | bytes 100000 | tf_op jit(solution)/shard_map/up_grad/pallas_call | solution.py:971
  198.7 3.1 add_convert_fusion.3
  204.8 9.6 %up_grad.3 = bf16[16,2,48,768]{3,2,1,0:T(8,128)(2,1)} custom-call(s32[3]{0:T(128)} %copy-done.11, bf16[1664,768]{1,0:T(8,128)(2,1)} %bitcast.93, bf16[1664,3072]{1,0:T(8,128)(2,1)} %bitcast.89), custom_call_target="tpu_custom_call" | custom-call | flops 100000000 | bytes 100000 | tf_op jit(solution)/shard_map/up_grad/pallas_call | solution.py:971
  217.7 7.3 %attend_back.3 = (bf16[8,208,2304]{2,1,0:T(8,128)(2,1)}, f32[128,128]{1,0:T(8,128)S(1)}, f32[2,768]{1,0:T(2,128)S(1)}) custom-call(bf16[8,208,768]{2,1,0:T(8,128)(2,1)S(1)} %copy-done.3, bf16[768,768]{1,0:T(8,128)(2,1)S(1)} %copy-done.6, bf16[8,208,2304]{2,1,0:T(8,128)(2,1)} %get-tuple-element.325.refs_2_, ...), custom_call_target="tpu_custom_call" | custom-call | flops 100000000 | bytes 100000 | tf_op jit(solution)/shard_map/attend_back/pallas_call | solution.py:777
  226.3 2.6 add_convert_fusion
  231.2 12.2 %attend_back.4 = (bf16[8,208,2304]{2,1,0:T(8,128)(2,1)}, f32[128,128]{1,0:T(8,128)S(1)}, f32[2,768]{1,0:T(2,128)S(1)}) custom-call(bf16[8,208,768]{2,1,0:T(8,128)(2,1)S(1)} %copy-done.3, bf16[768,768]{1,0:T(8,128)(2,1)S(1)} %copy-done.6, bf16[8,208,2304]{2,1,0:T(8,128)(2,1)} %get-tuple-element.325.refs_2_, ...), custom_call_target="tpu_custom_call", output_to_operand_aliasing={{0}: (6, {})} | custom-call | flops 100000000 | bytes 100000 | tf_op jit(solution)/shard_map/attend_back/pallas_call | solution.py:777
  243.4 3.8 %collective-permute-done.35 = bf16[2,3,48,768]{3,2,1,0:T(8,128)(2,1)S(1)} collective-permute-done((bf16[2,3,48,768]{3,2,1,0:T(8,128)(2,1)S(1)}, bf16[2,3,48,768]{3,2,1,0:T(8,128)(2,1)S(1)}, u32[]{:S(2)}, u32[]{:S(2)}) %collective-permute-start.35) | collective-permute-done | bytes 442400 | tf_op jit(solution)/shard_map/ppermute | solution.py:1014
  250.2 2.0 collective-permute-start.41
  254.6 7.4 %attend_back.5 = (bf16[8,208,2304]{2,1,0:T(8,128)(2,1)}, f32[128,128]{1,0:T(8,128)S(1)}, f32[2,768]{1,0:T(2,128)S(1)}) custom-call(bf16[8,208,768]{2,1,0:T(8,128)(2,1)S(1)} %copy-done.3, bf16[768,768]{1,0:T(8,128)(2,1)S(1)} %copy-done.6, bf16[8,208,2304]{2,1,0:T(8,128)(2,1)} %get-tuple-element.325.refs_2_, ...), custom_call_target="tpu_custom_call", output_to_operand_aliasing={{0}: (6, {})} | custom-call | flops 100000000 | bytes 100000 | tf_op jit(solution)/shard_map/attend_back/pallas_call | solution.py:777
  262.8 16.7 %input_back.1 = (f32[196,8,768]{2,1,0:T(8,128)}, f32[2,768]{1,0:T(2,128)S(1)}) custom-call(s32[3]{0:T(128)S(1)} %copy-done.12, bf16[8,208,2304]{2,1,0:T(8,128)(2,1)} %get-tuple-element.380.dqkv_ref, bf16[768,2304]{1,0:T(8,128)(2,1)S(1)} %copy-done.5, bf16[8,208,768]{2,1,0:T(8,128)(2,1)S(1)} %copy-done.2, f32[8,208,768]{2,1,0:T(8,128)} %get-tuple-element.367.gh_ref, ...), custom_call_target="tpu_custom_call" | custom-call | flops 100000000 | bytes 100000 | tf_op jit(solution)/shard_map/input_back/pallas_call | solution.py:805
  279.7 2.0 pack.1.notes_ref
  282.9 7.6 %qkv_grad.2 = bf16[16,48,1280]{2,1,0:T(8,128)(2,1)S(1)} custom-call(s32[3]{0:T(128)S(1)} %copy-done.12, bf16[1664,768]{1,0:T(8,128)(2,1)S(1)} %bitcast.84, bf16[1664,2304]{1,0:T(8,128)(2,1)} %bitcast.86, bf16[4,8,48,128]{3,2,1,0:T(8,128)(2,1)S(1)} %pack.1.notes_ref), custom_call_target="tpu_custom_call" | custom-call | flops 100000000 | bytes 100000 | tf_op jit(solution)/shard_map/qkv_grad/pallas_call | solution.py:949
  290.6 7.4 %qkv_grad.3 = bf16[16,48,1280]{2,1,0:T(8,128)(2,1)S(1)} custom-call(s32[3]{0:T(128)S(1)} %copy-done.12, bf16[1664,768]{1,0:T(8,128)(2,1)S(1)} %bitcast.85, bf16[1664,2304]{1,0:T(8,128)(2,1)} %bitcast.87, bf16[4,8,48,128]{3,2,1,0:T(8,128)(2,1)S(1)} %pack.1.notes_ref), custom_call_target="tpu_custom_call" | custom-call | flops 100000000 | bytes 100000 | tf_op jit(solution)/shard_map/qkv_grad/pallas_call | solution.py:949
  300.2 2.1 collective-permute-start.48
  303.5 10.1 %collective-permute-done.48 = bf16[2,48,768]{2,1,0:T(8,128)(2,1)S(1)} collective-permute-done((bf16[2,48,768]{2,1,0:T(8,128)(2,1)S(1)}, bf16[2,48,768]{2,1,0:T(8,128)(2,1)S(1)}, u32[]{:S(2)}, u32[]{:S(2)}) %collective-permute-start.48) | collective-permute-done | bytes 147488 | tf_op jit(solution)/shard_map/ppermute | solution.py:1014
  316.3 4.9 %collective-permute-done.50 = bf16[2,48,1280]{2,1,0:T(8,128)(2,1)S(1)} collective-permute-done((bf16[2,48,1280]{2,1,0:T(8,128)(2,1)S(1)}, bf16[2,48,1280]{2,1,0:T(8,128)(2,1)S(1)}, u32[]{:S(2)}, u32[]{:S(2)}) %collective-permute-start.50) | collective-permute-done | bytes 245792 | tf_op jit(solution)/shard_map/ppermute | solution.py:1014
  323.3 3.7 %collective-permute-start.52 = (bf16[48,1280]{1,0:T(8,128)(2,1)S(1)}, bf16[48,1280]{1,0:T(8,128)(2,1)S(1)}, u32[]{:S(2)}, u32[]{:S(2)}) collective-permute-start(bf16[48,1280]{1,0:T(8,128)(2,1)S(1)} %get-tuple-element.402), channel_id=1, source_target_pairs={{0,2},{1,3},{2,0},{3,1},{4,6},{5,7},{6,4},{7,5},{8,10},{9,11},{10,... | collective-permute-start | bytes 368648 | tf_op jit(solution)/shard_map/ppermute | solution.py:1014
  330.8 6.9 %collective-permute-done.53 = bf16[48,1280]{1,0:T(8,128)(2,1)S(1)} collective-permute-done((bf16[48,1280]{1,0:T(8,128)(2,1)S(1)}, bf16[48,1280]{1,0:T(8,128)(2,1)S(1)}, u32[]{:S(2)}, u32[]{:S(2)}) %collective-permute-start.53) | collective-permute-done | bytes 122912 | tf_op jit(solution)/shard_map/ppermute | solution.py:1014
  339.3 2.2 shard.1
  341.5 2.0 collective-permute-done.56.refs_1_
  (262 shorter events, 80.3 us)
Async XLA Ops:
  2.4 14.5 %collective-permute-start.2 = (bf16[48,1280]{1,0:T(8,128)(2,1)S(1)}, bf16[48,1280]{1,0:T(8,128)(2,1)S(1)}, u32[]{:S(2)}, u32[]{:S(2)}) collective-permute-start(bf16[48,1280]{1,0:T(8,128)(2,1)S(1)} %pad_maximum_fusion.16), channel_id=1, source_target_pairs={{0,6},{1,7},{2,4},{3,5},{4,2},{5,3},{6,0},{7,1},{8,14},{9,15},{10,... | collective-permute-start | bytes 368648 | tf_op jit(solution)/shard_map/ppermute | solution.py:1014
  26.9 11.0 %collective-permute-start.7 = (bf16[4,48,1280]{2,1,0:T(8,128)(2,1)S(1)}, bf16[4,48,1280]{2,1,0:T(8,128)(2,1)S(1)}, u32[]{:S(2)}, u32[]{:S(2)}) collective-permute-start(bf16[4,48,1280]{2,1,0:T(8,128)(2,1)S(1)} %pad_maximum_fusion.7.b_ref), channel_id=1, source_target_pairs={{0,1},{1,0},{2,3},{3,2},{4,5},{5,4},{6,7},{7,6},{8,9},{9,8},{10,11... | collective-permute-start | bytes 1474568 | tf_op jit(solution)/shard_map/ppermute | solution.py:1014
  48.6 21.6 %collective-permute-start.12 = (bf16[2,48,2048]{2,1,0:T(8,128)(2,1)S(1)}, bf16[2,48,2048]{2,1,0:T(8,128)(2,1)S(1)}, u32[]{:S(2)}, u32[]{:S(2)}) collective-permute-start(bf16[2,48,2048]{2,1,0:T(8,128)(2,1)S(1)} %pad_maximum_fusion.8), channel_id=1, source_target_pairs={{0,1},{1,0},{2,3},{3,2},{4,5},{5,4},{6,7},{7,6},{8,9},{9,8},{10,11... | collective-permute-start | bytes 1179656 | tf_op jit(solution)/shard_map/ppermute | solution.py:1014
  49.4 20.8 %collective-permute-start.13 = (bf16[2,48,2048]{2,1,0:T(8,128)(2,1)S(1)}, bf16[2,48,2048]{2,1,0:T(8,128)(2,1)S(1)}, u32[]{:S(2)}, u32[]{:S(2)}) collective-permute-start(bf16[2,48,2048]{2,1,0:T(8,128)(2,1)S(1)} %pad_maximum_fusion.9), channel_id=1, source_target_pairs={{0,16},{8,24},{16,0},{24,8},{1,17},{9,25},{17,1},{25,9},{2,18},{10... | collective-permute-start | bytes 1179656 | tf_op jit(solution)/shard_map/ppermute | solution.py:1014
  50.0 20.2 %collective-permute-start.16 = (bf16[2,48,768]{2,1,0:T(8,128)(2,1)S(1)}, bf16[2,48,768]{2,1,0:T(8,128)(2,1)S(1)}, u32[]{:S(2)}, u32[]{:S(2)}) collective-permute-start(bf16[2,48,768]{2,1,0:T(8,128)(2,1)S(1)} %bitcast.108), channel_id=1, source_target_pairs={{0,6},{1,7},{2,4},{3,5},{4,2},{5,3},{6,0},{7,1},{8,14},{9,15},{10,... | collective-permute-start | bytes 442376 | tf_op jit(solution)/shard_map/ppermute | solution.py:1014
  52.6 17.5 %collective-permute-start.15 = (bf16[2,48,768]{2,1,0:T(8,128)(2,1)S(1)}, bf16[2,48,768]{2,1,0:T(8,128)(2,1)S(1)}, u32[]{:S(2)}, u32[]{:S(2)}) collective-permute-start(bf16[2,48,768]{2,1,0:T(8,128)(2,1)S(1)} %bitcast.109), channel_id=1, source_target_pairs={{0,4},{1,5},{2,6},{3,7},{4,0},{5,1},{6,2},{7,3},{8,12},{9,13},{10,... | collective-permute-start | bytes 442376 | tf_op jit(solution)/shard_map/ppermute | solution.py:1014
  54.3 15.9 %collective-permute-start.14 = (bf16[2,48,768]{2,1,0:T(8,128)(2,1)S(1)}, bf16[2,48,768]{2,1,0:T(8,128)(2,1)S(1)}, u32[]{:S(2)}, u32[]{:S(2)}) collective-permute-start(bf16[2,48,768]{2,1,0:T(8,128)(2,1)S(1)} %bitcast.110), channel_id=1, source_target_pairs={{0,2},{1,3},{2,0},{3,1},{4,6},{5,7},{6,4},{7,5},{8,10},{9,11},{10,... | collective-permute-start | bytes 442376 | tf_op jit(solution)/shard_map/ppermute | solution.py:1014
  70.5 19.6 %collective-permute-start.21 = (bf16[4,48,2048]{2,1,0:T(8,128)(2,1)S(1)}, bf16[4,48,2048]{2,1,0:T(8,128)(2,1)S(1)}, u32[]{:S(2)}, u32[]{:S(2)}) collective-permute-start(bf16[4,48,2048]{2,1,0:T(8,128)(2,1)S(1)} %pad_maximum_fusion.2.refs_4_), channel_id=1, source_target_pairs={{0,8},{8,0},{16,24},{24,16},{1,9},{9,1},{17,25},{25,17},{2,10},{10... | collective-permute-start | bytes 2359304 | tf_op jit(solution)/shard_map/ppermute | solution.py:1014
  70.5 20.0 %collective-permute-start.19 = (bf16[4,48,2048]{2,1,0:T(8,128)(2,1)S(1)}, bf16[4,48,2048]{2,1,0:T(8,128)(2,1)S(1)}, u32[]{:S(2)}, u32[]{:S(2)}) collective-permute-start(bf16[4,48,2048]{2,1,0:T(8,128)(2,1)S(1)} %pad_maximum_fusion.2.refs_4_), channel_id=1, source_target_pairs={{0,16},{8,24},{16,0},{24,8},{1,17},{9,25},{17,1},{25,9},{2,18},{10... | collective-permute-start | bytes 2359304 | tf_op jit(solution)/shard_map/ppermute | solution.py:1014
  72.1 18.4 %collective-permute-start.22 = (bf16[4,48,2048]{2,1,0:T(8,128)(2,1)S(1)}, bf16[4,48,2048]{2,1,0:T(8,128)(2,1)S(1)}, u32[]{:S(2)}, u32[]{:S(2)}) collective-permute-start(bf16[4,48,2048]{2,1,0:T(8,128)(2,1)S(1)} %pad_maximum_fusion.3.refs_6_), channel_id=1, source_target_pairs={{0,8},{8,0},{16,24},{24,16},{1,9},{9,1},{17,25},{25,17},{2,10},{10... | collective-permute-start | bytes 2359304 | tf_op jit(solution)/shard_map/ppermute | solution.py:1014
  72.3 19.8 %collective-permute-start.20 = (bf16[4,48,2048]{2,1,0:T(8,128)(2,1)S(1)}, bf16[4,48,2048]{2,1,0:T(8,128)(2,1)S(1)}, u32[]{:S(2)}, u32[]{:S(2)}) collective-permute-start(bf16[4,48,2048]{2,1,0:T(8,128)(2,1)S(1)} %pad_maximum_fusion.3.refs_6_), channel_id=1, source_target_pairs={{0,1},{1,0},{2,3},{3,2},{4,5},{5,4},{6,7},{7,6},{8,9},{9,8},{10,11... | collective-permute-start | bytes 2359304 | tf_op jit(solution)/shard_map/ppermute | solution.py:1014
  102.7 27.4 %collective-permute-start.27 = (bf16[4,2,48,768]{3,2,1,0:T(8,128)(2,1)S(1)}, bf16[4,2,48,768]{3,2,1,0:T(8,128)(2,1)S(1)}, u32[]{:S(2)}, u32[]{:S(2)}) collective-permute-start(bf16[4,2,48,768]{3,2,1,0:T(8,128)(2,1)S(1)} %pad_maximum_fusion.4.refs_9_), channel_id=1, source_target_pairs={{0,8},{8,0},{16,24},{24,16},{1,9},{9,1},{17,25},{25,17},{2,10},{10... | collective-permute-start | bytes 1769480 | tf_op jit(solution)/shard_map/ppermute | solution.py:1014
  102.8 27.4 %collective-permute-start.25 = (bf16[4,2,48,768]{3,2,1,0:T(8,128)(2,1)S(1)}, bf16[4,2,48,768]{3,2,1,0:T(8,128)(2,1)S(1)}, u32[]{:S(2)}, u32[]{:S(2)}) collective-permute-start(bf16[4,2,48,768]{3,2,1,0:T(8,128)(2,1)S(1)} %pad_maximum_fusion.4.refs_9_), channel_id=1, source_target_pairs={{0,16},{8,24},{16,0},{24,8},{1,17},{9,25},{17,1},{25,9},{2,18},{10... | collective-permute-start | bytes 1769480 | tf_op jit(solution)/shard_map/ppermute | solution.py:1014
  103.5 26.7 %collective-permute-start.28 = (bf16[4,2,48,768]{3,2,1,0:T(8,128)(2,1)S(1)}, bf16[4,2,48,768]{3,2,1,0:T(8,128)(2,1)S(1)}, u32[]{:S(2)}, u32[]{:S(2)}) collective-permute-start(bf16[4,2,48,768]{3,2,1,0:T(8,128)(2,1)S(1)} %pad_maximum_fusion.5.refs_11_), channel_id=1, source_target_pairs={{0,8},{8,0},{16,24},{24,16},{1,9},{9,1},{17,25},{25,17},{2,10},{10... | collective-permute-start | bytes 1769480 | tf_op jit(solution)/shard_map/ppermute | solution.py:1014
  103.8 26.5 %collective-permute-start.26 = (bf16[4,2,48,768]{3,2,1,0:T(8,128)(2,1)S(1)}, bf16[4,2,48,768]{3,2,1,0:T(8,128)(2,1)S(1)}, u32[]{:S(2)}, u32[]{:S(2)}) collective-permute-start(bf16[4,2,48,768]{3,2,1,0:T(8,128)(2,1)S(1)} %pad_maximum_fusion.5.refs_11_), channel_id=1, source_target_pairs={{0,1},{1,0},{2,3},{3,2},{4,5},{5,4},{6,7},{7,6},{8,9},{9,8},{10,11... | collective-permute-start | bytes 1769480 | tf_op jit(solution)/shard_map/ppermute | solution.py:1014
  201.8 12.7 %collective-permute-start.34 = (bf16[16,2,48,768]{3,2,1,0:T(8,128)(2,1)}, bf16[16,2,48,768]{3,2,1,0:T(8,128)(2,1)S(1)}, u32[]{:S(2)}, u32[]{:S(2)}) collective-permute-start(bf16[16,2,48,768]{3,2,1,0:T(8,128)(2,1)} %up_grad.2), channel_id=1, source_target_pairs={{0,8},{8,0},{16,24},{24,16},{1,9},{9,1},{17,25},{25,17},{2,10},{10... | collective-permute-start | bytes 7077896 | tf_op jit(solution)/shard_map/ppermute | solution.py:1014
  202.2 22.8 %collective-permute-start.32 = (bf16[4,3,48,768]{3,2,1,0:T(8,128)(2,1)}, bf16[4,3,48,768]{3,2,1,0:T(8,128)(2,1)}, u32[]{:S(2)}, u32[]{:S(2)}) collective-permute-start(bf16[4,3,48,768]{3,2,1,0:T(8,128)(2,1)} %get-tuple-element.316), channel_id=1, source_target_pairs={{0,16},{8,24},{16,0},{24,8},{1,17},{9,25},{17,1},{25,9},{2,18},{10... | collective-permute-start | bytes 2654216 | tf_op jit(solution)/shard_map/ppermute | solution.py:1014
  203.5 22.9 %collective-permute-start.33 = (bf16[4,3,48,768]{3,2,1,0:T(8,128)(2,1)}, bf16[4,3,48,768]{3,2,1,0:T(8,128)(2,1)}, u32[]{:S(2)}, u32[]{:S(2)}) collective-permute-start(bf16[4,3,48,768]{3,2,1,0:T(8,128)(2,1)} %get-tuple-element.317), channel_id=1, source_target_pairs={{0,1},{1,0},{2,3},{3,2},{4,5},{5,4},{6,7},{7,6},{8,9},{9,8},{10,11... | collective-permute-start | bytes 2654216 | tf_op jit(solution)/shard_map/ppermute | solution.py:1014
  216.2 31.0 %collective-permute-start.37 = (bf16[4,2,48,768]{3,2,1,0:T(8,128)(2,1)S(1)}, bf16[4,2,48,768]{3,2,1,0:T(8,128)(2,1)S(1)}, u32[]{:S(2)}, u32[]{:S(2)}) collective-permute-start(bf16[4,2,48,768]{3,2,1,0:T(8,128)(2,1)S(1)} %get-tuple-element.338), channel_id=1, source_target_pairs={{0,16},{8,24},{16,0},{24,8},{1,17},{9,25},{17,1},{25,9},{2,18},{10... | collective-permute-start | bytes 1769480 | tf_op jit(solution)/shard_map/ppermute | solution.py:1014
  217.0 30.2 %collective-permute-start.38 = (bf16[4,2,48,768]{3,2,1,0:T(8,128)(2,1)S(1)}, bf16[4,2,48,768]{3,2,1,0:T(8,128)(2,1)S(1)}, u32[]{:S(2)}, u32[]{:S(2)}) collective-permute-start(bf16[4,2,48,768]{3,2,1,0:T(8,128)(2,1)S(1)} %get-tuple-element.339), channel_id=1, source_target_pairs={{0,1},{1,0},{2,3},{3,2},{4,5},{5,4},{6,7},{7,6},{8,9},{9,8},{10,11... | collective-permute-start | bytes 1769480 | tf_op jit(solution)/shard_map/ppermute | solution.py:1014
  229.0 18.2 %collective-permute-start.35 = (bf16[2,3,48,768]{3,2,1,0:T(8,128)(2,1)S(1)}, bf16[2,3,48,768]{3,2,1,0:T(8,128)(2,1)S(1)}, u32[]{:S(2)}, u32[]{:S(2)}) collective-permute-start(bf16[2,3,48,768]{3,2,1,0:T(8,128)(2,1)S(1)} %slice.241), channel_id=1, source_target_pairs={{0,1},{1,0},{2,3},{3,2},{4,5},{5,4},{6,7},{7,6},{8,9},{9,8},{10,11... | collective-permute-start | bytes 1327112 | tf_op jit(solution)/shard_map/ppermute | solution.py:1014
  230.5 16.8 %collective-permute-start.36 = (bf16[2,3,48,768]{3,2,1,0:T(8,128)(2,1)S(1)}, bf16[2,3,48,768]{3,2,1,0:T(8,128)(2,1)S(1)}, u32[]{:S(2)}, u32[]{:S(2)}) collective-permute-start(bf16[2,3,48,768]{3,2,1,0:T(8,128)(2,1)S(1)} %slice.242), channel_id=1, source_target_pairs={{0,16},{8,24},{16,0},{24,8},{1,17},{9,25},{17,1},{25,9},{2,18},{10... | collective-permute-start | bytes 1327112 | tf_op jit(solution)/shard_map/ppermute | solution.py:1014
  248.1 14.0 %collective-permute-start.39 = (bf16[2,2,48,768]{3,2,1,0:T(8,128)(2,1)S(1)}, bf16[2,2,48,768]{3,2,1,0:T(8,128)(2,1)S(1)}, u32[]{:S(2)}, u32[]{:S(2)}) collective-permute-start(bf16[2,2,48,768]{3,2,1,0:T(8,128)(2,1)S(1)} %slice.248), channel_id=1, source_target_pairs={{0,1},{1,0},{2,3},{3,2},{4,5},{5,4},{6,7},{7,6},{8,9},{9,8},{10,11... | collective-permute-start | bytes 884744 | tf_op jit(solution)/shard_map/ppermute | solution.py:1014
  249.5 12.5 %collective-permute-start.40 = (bf16[2,2,48,768]{3,2,1,0:T(8,128)(2,1)S(1)}, bf16[2,2,48,768]{3,2,1,0:T(8,128)(2,1)S(1)}, u32[]{:S(2)}, u32[]{:S(2)}) collective-permute-start(bf16[2,2,48,768]{3,2,1,0:T(8,128)(2,1)S(1)} %slice.249), channel_id=1, source_target_pairs={{0,16},{8,24},{16,0},{24,8},{1,17},{9,25},{17,1},{25,9},{2,18},{10... | collective-permute-start | bytes 884744 | tf_op jit(solution)/shard_map/ppermute | solution.py:1014
  250.2 11.8 %collective-permute-start.41 = (bf16[3,48,768]{2,1,0:T(8,128)(2,1)S(1)}, bf16[3,48,768]{2,1,0:T(8,128)(2,1)S(1)}, u32[]{:S(2)}, u32[]{:S(2)}) collective-permute-start(bf16[3,48,768]{2,1,0:T(8,128)(2,1)S(1)} %get-tuple-element.356), channel_id=1, source_target_pairs={{0,2},{1,3},{2,0},{3,1},{4,6},{5,7},{6,4},{7,5},{8,10},{9,11},{10,... | collective-permute-start | bytes 663560 | tf_op jit(solution)/shard_map/ppermute | solution.py:1014
  252.2 27.3 %collective-permute-start.42 = (bf16[3,48,768]{2,1,0:T(8,128)(2,1)S(1)}, bf16[3,48,768]{2,1,0:T(8,128)(2,1)S(1)}, u32[]{:S(2)}, u32[]{:S(2)}) collective-permute-start(bf16[3,48,768]{2,1,0:T(8,128)(2,1)S(1)} %get-tuple-element.364), channel_id=1, source_target_pairs={{0,4},{1,5},{2,6},{3,7},{4,0},{5,1},{6,2},{7,3},{8,12},{9,13},{10,... | collective-permute-start | bytes 663560 | tf_op jit(solution)/shard_map/ppermute | solution.py:1014
  253.2 26.3 %collective-permute-start.43 = (bf16[3,48,768]{2,1,0:T(8,128)(2,1)S(1)}, bf16[3,48,768]{2,1,0:T(8,128)(2,1)S(1)}, u32[]{:S(2)}, u32[]{:S(2)}) collective-permute-start(bf16[3,48,768]{2,1,0:T(8,128)(2,1)S(1)} %get-tuple-element.365), channel_id=1, source_target_pairs={{0,6},{1,7},{2,4},{3,5},{4,2},{5,3},{6,0},{7,1},{8,14},{9,15},{10,... | collective-permute-start | bytes 663560 | tf_op jit(solution)/shard_map/ppermute | solution.py:1014
  298.2 15.4 %collective-permute-start.46 = (bf16[4,48,1280]{2,1,0:T(8,128)(2,1)S(1)}, bf16[4,48,1280]{2,1,0:T(8,128)(2,1)S(1)}, u32[]{:S(2)}, u32[]{:S(2)}) collective-permute-start(bf16[4,48,1280]{2,1,0:T(8,128)(2,1)S(1)} %get-tuple-element.387), channel_id=1, source_target_pairs={{0,16},{8,24},{16,0},{24,8},{1,17},{9,25},{17,1},{25,9},{2,18},{10... | collective-permute-start | bytes 1474568 | tf_op jit(solution)/shard_map/ppermute | solution.py:1014
  299.6 14.0 %collective-permute-start.47 = (bf16[4,48,1280]{2,1,0:T(8,128)(2,1)S(1)}, bf16[4,48,1280]{2,1,0:T(8,128)(2,1)S(1)}, u32[]{:S(2)}, u32[]{:S(2)}) collective-permute-start(bf16[4,48,1280]{2,1,0:T(8,128)(2,1)S(1)} %get-tuple-element.388), channel_id=1, source_target_pairs={{0,1},{1,0},{2,3},{3,2},{4,5},{5,4},{6,7},{7,6},{8,9},{9,8},{10,11... | collective-permute-start | bytes 1474568 | tf_op jit(solution)/shard_map/ppermute | solution.py:1014
  300.2 13.4 %collective-permute-start.48 = (bf16[2,48,768]{2,1,0:T(8,128)(2,1)S(1)}, bf16[2,48,768]{2,1,0:T(8,128)(2,1)S(1)}, u32[]{:S(2)}, u32[]{:S(2)}) collective-permute-start(bf16[2,48,768]{2,1,0:T(8,128)(2,1)S(1)} %get-tuple-element.390), channel_id=1, source_target_pairs={{0,4},{1,5},{2,6},{3,7},{4,0},{5,1},{6,2},{7,3},{8,12},{9,13},{10,... | collective-permute-start | bytes 442376 | tf_op jit(solution)/shard_map/ppermute | solution.py:1014
  302.3 11.3 %collective-permute-start.49 = (bf16[2,48,768]{2,1,0:T(8,128)(2,1)S(1)}, bf16[2,48,768]{2,1,0:T(8,128)(2,1)S(1)}, u32[]{:S(2)}, u32[]{:S(2)}) collective-permute-start(bf16[2,48,768]{2,1,0:T(8,128)(2,1)S(1)} %get-tuple-element.391), channel_id=1, source_target_pairs={{0,6},{1,7},{2,4},{3,5},{4,2},{5,3},{6,0},{7,1},{8,14},{9,15},{10,... | collective-permute-start | bytes 442376 | tf_op jit(solution)/shard_map/ppermute | solution.py:1014
  322.5 15.1 %collective-permute-start.55 = (bf16[5,48,768]{2,1,0:T(8,128)(2,1)S(1)}, bf16[5,48,768]{2,1,0:T(8,128)(2,1)S(1)}, u32[]{:S(2)}, u32[]{:S(2)}) collective-permute-start(bf16[5,48,768]{2,1,0:T(8,128)(2,1)S(1)} %pad_maximum_fusion.10.refs_0_), channel_id=1, source_target_pairs={{0,16},{8,24},{16,0},{24,8},{1,17},{9,25},{17,1},{25,9},{2,18},{10... | collective-permute-start | bytes 1105928 | tf_op jit(solution)/shard_map/ppermute | solution.py:1014
  (71 other events, 607.4 us)

commit v6 on v5

--- a/solution.py
+++ b/solution.py
@@ -30,7 +30,7 @@
 NOTES = 128
 STEPS = (3, 4, 1)
 COST = 1e8
-BACK_STEPS = (2, 4, 2)
+BACK_STEPS = (2, 5, 1)
 
 
 def nn(left, right):
@@ -519,14 +519,17 @@
     def _():
         sums_ref[...] = refs[1][...] if earlier else jnp.zeros_like(sums_ref)
 
+    keep = jnp.concatenate(
+        [keep_column(base_ref, first + step * group + at) for at in range(group)], axis=0
+    )
+    rows = group * ROWS
+    grad_first = keep * nt(dqkv_ref[...].reshape(rows, 3 * D), w_ref[...])
+    scaled, inv_std = norm_parts(tok_ref[...].reshape(rows, D).astype(F32))
+    sums_ref[0:1, :] += jnp.sum(grad_first * scaled, axis=0, keepdims=True)
+    sums_ref[1:2, :] += jnp.sum(grad_first, axis=0, keepdims=True)
+    total = gh_ref[...].reshape(rows, D) + norm_grad(grad_first, scaled, inv_std, vec_ref[0:1, :])
     for at in range(group):
-        keep = keep_column(base_ref, first + step * group + at)
-        grad_first = keep * nt(dqkv_ref[at], w_ref[...])
-        scaled, inv_std = norm_parts(tok_ref[at].astype(F32))
-        sums_ref[0:1, :] += jnp.sum(grad_first * scaled, axis=0, keepdims=True)
-        sums_ref[1:2, :] += jnp.sum(grad_first, axis=0, keepdims=True)
-        total = gh_ref[at] + norm_grad(grad_first, scaled, inv_std, vec_ref[0:1, :])
-        out_ref[:, first + step * group + at, :] = total[0:SLOTS]
+        out_ref[:, first + step * group + at, :] = total[at * ROWS : at * ROWS + SLOTS]
 
 
 def weight_grad_kernel(*refs):

time: 354 us -> 350 us (0.989)
  transfers between devices with their start and end apart: 61 -> 61, of which waited for: 19 -> 19; matrix products, arithmetic and copies ran while one was open for 5% -> 5% of each run, Pallas kernels for 41% -> 42%
where the time goes in v6:
time: 350 us; the launch traced here: 346 us
  Pallas kernels  202 us (58%)
  starting transfers between devices  59.5 us (17%)
  waiting for transfers between devices  50.1 us (14%)
  local copies, waits for them, and re-layouts  16.3 us (5%)
  other arithmetic  13.9 us (4%)
  between operations  4.45 us (1%)
    ppermute x61, starting transfers between devices, swap(): return lax.ppermute(values, axis, [(at, at ^ mask) for at in range(size)])  59.5 us
    ppermute x61, waiting for transfers between devices, swap(): return lax.ppermute(values, axis, [(at, at ^ mask) for at in range(size)])  50.1 us
    pallas_call x3, Pallas kernels, attend(): pl.pallas_call(functools.partial(attend_kernel, first=first, pieces=piece...  38.3 us
    pallas_call x1, Pallas kernels, mlp_down(): pl.pallas_call(functools.partial(down_kernel, group=group, pieces=pieces,...  37.9 us
    pallas_call x3, Pallas kernels, attend_back(): pl.pallas_call(functools.partial(attend_back_kernel, earlier=len(earlier)...  27.1 us
    pallas_call x1, Pallas kernels, mlp_up(): pl.pallas_call(functools.partial(up_kernel, group=group, pieces=pieces),...  25.7 us
    pallas_call x2, Pallas kernels, up_grad(): pl.pallas_call(up_grad_kernel, grid_spec=pltpu.PrefetchScalarGridSpec(num...  19.5 us
    pallas_call x1, Pallas kernels, down_grad(): pl.pallas_call(down_grad_kernel, grid=(5,), in_specs=[SMEM, pl.BlockSpec(...  16.7 us
  transfers between devices with their start and end apart: 61, of which 19 were waited for; matrix products, arithmetic and copies ran while one was open for 5% of the time, Pallas kernels for 42%

profile of v6, /device:TPU:0, one launch (start us, length us, event | category | flops | bytes accessed | tf_op | source)
XLA Modules:
  0.0 346.2 jit_solution(12750978735948647629)
XLA Ops:
  2.4 5.1 %collective-permute-start.2 = (bf16[48,1280]{1,0:T(8,128)(2,1)S(1)}, bf16[48,1280]{1,0:T(8,128)(2,1)S(1)}, u32[]{:S(2)}, u32[]{:S(2)}) collective-permute-start(bf16[48,1280]{1,0:T(8,128)(2,1)S(1)} %pad_maximum_fusion.16), channel_id=1, source_target_pairs={{0,6},{1,7},{2,4},{3,5},{4,2},{5,3},{6,0},{7,1},{8,14},{9,15},{10,... | collective-permute-start | bytes 368648 | tf_op jit(solution)/shard_map/ppermute | solution.py:1017
  23.7 3.1 collective-permute-done.5
  32.2 5.7 %collective-permute-done.8 = bf16[48,2048]{1,0:T(8,128)(2,1)S(1)} collective-permute-done((bf16[48,2048]{1,0:T(8,128)(2,1)S(1)}, bf16[48,2048]{1,0:T(8,128)(2,1)S(1)}, u32[]{:S(2)}, u32[]{:S(2)}) %collective-permute-start.8) | collective-permute-done | bytes 196640 | tf_op jit(solution)/shard_map/ppermute | solution.py:1017
  39.7 2.5 collective-permute-start.11
  44.3 4.2 %collective-permute-done.11 = bf16[48,2048]{1,0:T(8,128)(2,1)S(1)} collective-permute-done((bf16[48,2048]{1,0:T(8,128)(2,1)S(1)}, bf16[48,2048]{1,0:T(8,128)(2,1)S(1)}, u32[]{:S(2)}, u32[]{:S(2)}) %collective-permute-start.11) | collective-permute-done | bytes 196640 | tf_op jit(solution)/shard_map/ppermute | solution.py:1017
  50.0 2.6 collective-permute-start.16
  54.4 15.8 %attend.3 = (bf16[8,208,2304]{2,1,0:T(8,128)(2,1)}, bf16[8,12,208,256]{3,2,1,0:T(8,128)(2,1)}, bf16[8,208,768]{2,1,0:T(8,128)(2,1)}, bf16[8,208,768]{2,1,0:T(8,128)(2,1)}, bf16[768,2304]{1,0:T(8,128)(2,1)}) custom-call(s32[3]{0:T(128)} %copy-done.11, bf16[8,208,768]{2,1,0:T(8,128)(2,1)} %pad.68.refs_1_.tok_ref, bf16[8,48,1280]{2,1,0:T(8,128)(2,1)} %copy-done.17, ...), custom_call_target="tpu_custom_call" | custom-call | flops 100000000 | bytes 100000 | tf_op jit(solution)/shard_map/attend/pallas_call | solution.py:703
  73.6 16.4 %attend.4 = (bf16[8,208,2304]{2,1,0:T(8,128)(2,1)}, bf16[8,12,208,256]{3,2,1,0:T(8,128)(2,1)}, bf16[8,208,768]{2,1,0:T(8,128)(2,1)}, bf16[8,208,768]{2,1,0:T(8,128)(2,1)}) custom-call(s32[3]{0:T(128)} %copy-done.11, bf16[8,208,768]{2,1,0:T(8,128)(2,1)} %pad.68.refs_1_.tok_ref, ...), custom_call_target="tpu_custom_call", output_to_operand_aliasing={{0}: (6, {}), {1}: (7, {}), {2}: (8, {}), {3}: (9, {})} | custom-call | flops 100000000 | bytes 100000 | tf_op jit(solution)/shard_map/attend/pallas_call | solution.py:703
  94.5 6.1 %attend.5 = (bf16[8,208,2304]{2,1,0:T(8,128)(2,1)}, bf16[8,12,208,256]{3,2,1,0:T(8,128)(2,1)}, bf16[8,208,768]{2,1,0:T(8,128)(2,1)}, bf16[8,208,768]{2,1,0:T(8,128)(2,1)}) custom-call(s32[3]{0:T(128)} %copy-done.11, bf16[8,208,768]{2,1,0:T(8,128)(2,1)} %pad.68.refs_1_.tok_ref, ...), custom_call_target="tpu_custom_call", output_to_operand_aliasing={{0}: (6, {}), {1}: (7, {}), {2}: (8, {}), {3}: (9, {})} | custom-call | flops 100000000 | bytes 100000 | tf_op jit(solution)/shard_map/attend/pallas_call | solution.py:703
  104.4 25.7 %mlp_up.1 = (f32[8,208,768]{2,1,0:T(8,128)}, bf16[8,208,768]{2,1,0:T(8,128)(2,1)}, bf16[8,208,3072]{2,1,0:T(8,128)(2,1)}, bf16[8,208,3072]{2,1,0:T(8,128)(2,1)},...) custom-call(s32[3]{0:T(128)} %copy-done.11, ...), custom_call_target="tpu_custom_call" | custom-call | flops 800000000 | bytes 100000 | tf_op jit(solution)/shard_map/mlp_up/pallas_call | solution.py:734
  134.0 37.9 %mlp_down.1 = (bf16[8,196,768]{2,1,0:T(8,128)(2,1)}, f32[8,208,768]{2,1,0:T(8,128)}, bf16[8,208,768]{2,1,0:T(8,128)(2,1)}, bf16[8,208,768]{2,1,0:T(8,128)(2,1)},...) custom-call(s32[3]{0:T(128)} %copy-done.11, f32[8,208,768]{2,1,0:T(8,128)} %get-tuple-element.293.refs_1_, ...), custom_call_target="tpu_custom_call" | custom-call | flops 800000000 | bytes 100000 | tf_op jit(solution)/shard_map/mlp_down/pallas_call | solution.py:758
  171.9 16.7 %down_grad.1 = (bf16[16,3,48,768]{3,2,1,0:T(8,128)(2,1)}, bf16[16,3,48,768]{3,2,1,0:T(8,128)(2,1)}) custom-call(s32[3]{0:T(128)} %copy-done.11, bf16[1664,3072]{1,0:T(8,128)(2,1)} %bitcast.90, bf16[1664,768]{1,0:T(8,128)(2,1)} %bitcast.94, bf16[1664,768]{1,0:T(8,128)(2,1)} %bitcast.91, bf16[1664,768]{1,0:T(8,128)(2,1)} %bitcast.83), custom_call_target="tpu_custom_call" | custom-call | flops 100000000 | bytes 100000 | tf_op jit(solution)/shard_map/down_grad/pallas_call | solution.py:995
  188.8 9.9 %up_grad.2 = bf16[16,2,48,768]{3,2,1,0:T(8,128)(2,1)} custom-call(s32[3]{0:T(128)} %copy-done.11, bf16[1664,768]{1,0:T(8,128)(2,1)} %bitcast.92, bf16[1664,3072]{1,0:T(8,128)(2,1)} %bitcast.88), custom_call_target="tpu_custom_call" | custom-call | flops 100000000 | bytes 100000 | tf_op jit(solution)/shard_map/up_grad/pallas_call | solution.py:974
  198.7 3.1 add_convert_fusion.3
  204.8 9.6 %up_grad.3 = bf16[16,2,48,768]{3,2,1,0:T(8,128)(2,1)} custom-call(s32[3]{0:T(128)} %copy-done.11, bf16[1664,768]{1,0:T(8,128)(2,1)} %bitcast.93, bf16[1664,3072]{1,0:T(8,128)(2,1)} %bitcast.89), custom_call_target="tpu_custom_call" | custom-call | flops 100000000 | bytes 100000 | tf_op jit(solution)/shard_map/up_grad/pallas_call | solution.py:974
  217.7 7.3 %attend_back.3 = (bf16[8,208,2304]{2,1,0:T(8,128)(2,1)}, f32[128,128]{1,0:T(8,128)S(1)}, f32[2,768]{1,0:T(2,128)S(1)}) custom-call(bf16[8,208,768]{2,1,0:T(8,128)(2,1)S(1)} %copy-done.3, bf16[768,768]{1,0:T(8,128)(2,1)S(1)} %copy-done.6, bf16[8,208,2304]{2,1,0:T(8,128)(2,1)} %get-tuple-element.325.refs_2_, ...), custom_call_target="tpu_custom_call" | custom-call | flops 100000000 | bytes 100000 | tf_op jit(solution)/shard_map/attend_back/pallas_call | solution.py:780
  226.3 2.6 add_convert_fusion
  231.2 14.7 %attend_back.4 = (bf16[8,208,2304]{2,1,0:T(8,128)(2,1)}, f32[128,128]{1,0:T(8,128)S(1)}, f32[2,768]{1,0:T(2,128)S(1)}) custom-call(bf16[8,208,768]{2,1,0:T(8,128)(2,1)S(1)} %copy-done.3, bf16[768,768]{1,0:T(8,128)(2,1)S(1)} %copy-done.6, bf16[8,208,2304]{2,1,0:T(8,128)(2,1)} %get-tuple-element.325.refs_2_, ...), custom_call_target="tpu_custom_call", output_to_operand_aliasing={{0}: (6, {})} | custom-call | flops 100000000 | bytes 100000 | tf_op jit(solution)/shard_map/attend_back/pallas_call | solution.py:780
  250.2 2.0 collective-permute-start.41
  254.6 5.1 %attend_back.5 = (bf16[8,208,2304]{2,1,0:T(8,128)(2,1)}, f32[128,128]{1,0:T(8,128)S(1)}, f32[2,768]{1,0:T(2,128)S(1)}) custom-call(bf16[8,208,768]{2,1,0:T(8,128)(2,1)S(1)} %copy-done.3, bf16[768,768]{1,0:T(8,128)(2,1)S(1)} %copy-done.6, bf16[8,208,2304]{2,1,0:T(8,128)(2,1)} %get-tuple-element.325.refs_2_, ...), custom_call_target="tpu_custom_call", output_to_operand_aliasing={{0}: (6, {})} | custom-call | flops 100000000 | bytes 100000 | tf_op jit(solution)/shard_map/attend_back/pallas_call | solution.py:780
  260.4 15.2 %input_back.1 = (f32[196,8,768]{2,1,0:T(8,128)}, f32[2,768]{1,0:T(2,128)S(1)}) custom-call(s32[3]{0:T(128)S(1)} %copy-done.12, bf16[8,208,2304]{2,1,0:T(8,128)(2,1)} %get-tuple-element.380.dqkv_ref, bf16[768,2304]{1,0:T(8,128)(2,1)S(1)} %copy-done.5, bf16[8,208,768]{2,1,0:T(8,128)(2,1)S(1)} %copy-done.2, f32[8,208,768]{2,1,0:T(8,128)} %get-tuple-element.367.gh_ref, ...), custom_call_target="tpu_custom_call" | custom-call | flops 100000000 | bytes 100000 | tf_op jit(solution)/shard_map/input_back/pallas_call | solution.py:808
  275.8 2.0 pack.1.notes_ref
  279.0 7.6 %qkv_grad.2 = bf16[16,48,1280]{2,1,0:T(8,128)(2,1)S(1)} custom-call(s32[3]{0:T(128)S(1)} %copy-done.12, bf16[1664,768]{1,0:T(8,128)(2,1)S(1)} %bitcast.84, bf16[1664,2304]{1,0:T(8,128)(2,1)} %bitcast.86, bf16[4,8,48,128]{3,2,1,0:T(8,128)(2,1)S(1)} %pack.1.notes_ref), custom_call_target="tpu_custom_call" | custom-call | flops 100000000 | bytes 100000 | tf_op jit(solution)/shard_map/qkv_grad/pallas_call | solution.py:952
  286.6 7.4 %qkv_grad.3 = bf16[16,48,1280]{2,1,0:T(8,128)(2,1)S(1)} custom-call(s32[3]{0:T(128)S(1)} %copy-done.12, bf16[1664,768]{1,0:T(8,128)(2,1)S(1)} %bitcast.85, bf16[1664,2304]{1,0:T(8,128)(2,1)} %bitcast.87, bf16[4,8,48,128]{3,2,1,0:T(8,128)(2,1)S(1)} %pack.1.notes_ref), custom_call_target="tpu_custom_call" | custom-call | flops 100000000 | bytes 100000 | tf_op jit(solution)/shard_map/qkv_grad/pallas_call | solution.py:952
  296.3 2.1 collective-permute-start.48
  299.6 10.1 %collective-permute-done.48 = bf16[2,48,768]{2,1,0:T(8,128)(2,1)S(1)} collective-permute-done((bf16[2,48,768]{2,1,0:T(8,128)(2,1)S(1)}, bf16[2,48,768]{2,1,0:T(8,128)(2,1)S(1)}, u32[]{:S(2)}, u32[]{:S(2)}) %collective-permute-start.48) | collective-permute-done | bytes 147488 | tf_op jit(solution)/shard_map/ppermute | solution.py:1017
  312.5 4.8 %collective-permute-done.50 = bf16[2,48,1280]{2,1,0:T(8,128)(2,1)S(1)} collective-permute-done((bf16[2,48,1280]{2,1,0:T(8,128)(2,1)S(1)}, bf16[2,48,1280]{2,1,0:T(8,128)(2,1)S(1)}, u32[]{:S(2)}, u32[]{:S(2)}) %collective-permute-start.50) | collective-permute-done | bytes 245792 | tf_op jit(solution)/shard_map/ppermute | solution.py:1017
  319.4 3.7 %collective-permute-start.52 = (bf16[48,1280]{1,0:T(8,128)(2,1)S(1)}, bf16[48,1280]{1,0:T(8,128)(2,1)S(1)}, u32[]{:S(2)}, u32[]{:S(2)}) collective-permute-start(bf16[48,1280]{1,0:T(8,128)(2,1)S(1)} %get-tuple-element.402), channel_id=1, source_target_pairs={{0,2},{1,3},{2,0},{3,1},{4,6},{5,7},{6,4},{7,5},{8,10},{9,11},{10,... | collective-permute-start | bytes 368648 | tf_op jit(solution)/shard_map/ppermute | solution.py:1017
  326.7 6.9 %collective-permute-done.53 = bf16[48,1280]{1,0:T(8,128)(2,1)S(1)} collective-permute-done((bf16[48,1280]{1,0:T(8,128)(2,1)S(1)}, bf16[48,1280]{1,0:T(8,128)(2,1)S(1)}, u32[]{:S(2)}, u32[]{:S(2)}) %collective-permute-start.53) | collective-permute-done | bytes 122912 | tf_op jit(solution)/shard_map/ppermute | solution.py:1017
  335.4 2.2 shard.1
  337.6 1.9 collective-permute-done.56.refs_1_
  339.5 1.9 copy.62
  (262 shorter events, 79.7 us)
Async XLA Ops:
  2.4 14.5 %collective-permute-start.2 = (bf16[48,1280]{1,0:T(8,128)(2,1)S(1)}, bf16[48,1280]{1,0:T(8,128)(2,1)S(1)}, u32[]{:S(2)}, u32[]{:S(2)}) collective-permute-start(bf16[48,1280]{1,0:T(8,128)(2,1)S(1)} %pad_maximum_fusion.16), channel_id=1, source_target_pairs={{0,6},{1,7},{2,4},{3,5},{4,2},{5,3},{6,0},{7,1},{8,14},{9,15},{10,... | collective-permute-start | bytes 368648 | tf_op jit(solution)/shard_map/ppermute | solution.py:1017
  26.9 11.0 %collective-permute-start.7 = (bf16[4,48,1280]{2,1,0:T(8,128)(2,1)S(1)}, bf16[4,48,1280]{2,1,0:T(8,128)(2,1)S(1)}, u32[]{:S(2)}, u32[]{:S(2)}) collective-permute-start(bf16[4,48,1280]{2,1,0:T(8,128)(2,1)S(1)} %pad_maximum_fusion.7.b_ref), channel_id=1, source_target_pairs={{0,1},{1,0},{2,3},{3,2},{4,5},{5,4},{6,7},{7,6},{8,9},{9,8},{10,11... | collective-permute-start | bytes 1474568 | tf_op jit(solution)/shard_map/ppermute | solution.py:1017
  28.0 10.8 %collective-permute-start.6 = (bf16[4,48,1280]{2,1,0:T(8,128)(2,1)S(1)}, bf16[4,48,1280]{2,1,0:T(8,128)(2,1)S(1)}, u32[]{:S(2)}, u32[]{:S(2)}) collective-permute-start(bf16[4,48,1280]{2,1,0:T(8,128)(2,1)S(1)} %pad_maximum_fusion.6.a_ref), channel_id=1, source_target_pairs={{0,16},{8,24},{16,0},{24,8},{1,17},{9,25},{17,1},{25,9},{2,18},{10... | collective-permute-start | bytes 1474568 | tf_op jit(solution)/shard_map/ppermute | solution.py:1017
  48.6 21.6 %collective-permute-start.12 = (bf16[2,48,2048]{2,1,0:T(8,128)(2,1)S(1)}, bf16[2,48,2048]{2,1,0:T(8,128)(2,1)S(1)}, u32[]{:S(2)}, u32[]{:S(2)}) collective-permute-start(bf16[2,48,2048]{2,1,0:T(8,128)(2,1)S(1)} %pad_maximum_fusion.8), channel_id=1, source_target_pairs={{0,1},{1,0},{2,3},{3,2},{4,5},{5,4},{6,7},{7,6},{8,9},{9,8},{10,11... | collective-permute-start | bytes 1179656 | tf_op jit(solution)/shard_map/ppermute | solution.py:1017
  49.4 20.8 %collective-permute-start.13 = (bf16[2,48,2048]{2,1,0:T(8,128)(2,1)S(1)}, bf16[2,48,2048]{2,1,0:T(8,128)(2,1)S(1)}, u32[]{:S(2)}, u32[]{:S(2)}) collective-permute-start(bf16[2,48,2048]{2,1,0:T(8,128)(2,1)S(1)} %pad_maximum_fusion.9), channel_id=1, source_target_pairs={{0,16},{8,24},{16,0},{24,8},{1,17},{9,25},{17,1},{25,9},{2,18},{10... | collective-permute-start | bytes 1179656 | tf_op jit(solution)/shard_map/ppermute | solution.py:1017
  50.0 20.2 %collective-permute-start.16 = (bf16[2,48,768]{2,1,0:T(8,128)(2,1)S(1)}, bf16[2,48,768]{2,1,0:T(8,128)(2,1)S(1)}, u32[]{:S(2)}, u32[]{:S(2)}) collective-permute-start(bf16[2,48,768]{2,1,0:T(8,128)(2,1)S(1)} %bitcast.108), channel_id=1, source_target_pairs={{0,6},{1,7},{2,4},{3,5},{4,2},{5,3},{6,0},{7,1},{8,14},{9,15},{10,... | collective-permute-start | bytes 442376 | tf_op jit(solution)/shard_map/ppermute | solution.py:1017
  52.6 17.5 %collective-permute-start.15 = (bf16[2,48,768]{2,1,0:T(8,128)(2,1)S(1)}, bf16[2,48,768]{2,1,0:T(8,128)(2,1)S(1)}, u32[]{:S(2)}, u32[]{:S(2)}) collective-permute-start(bf16[2,48,768]{2,1,0:T(8,128)(2,1)S(1)} %bitcast.109), channel_id=1, source_target_pairs={{0,4},{1,5},{2,6},{3,7},{4,0},{5,1},{6,2},{7,3},{8,12},{9,13},{10,... | collective-permute-start | bytes 442376 | tf_op jit(solution)/shard_map/ppermute | solution.py:1017
  54.3 15.9 %collective-permute-start.14 = (bf16[2,48,768]{2,1,0:T(8,128)(2,1)S(1)}, bf16[2,48,768]{2,1,0:T(8,128)(2,1)S(1)}, u32[]{:S(2)}, u32[]{:S(2)}) collective-permute-start(bf16[2,48,768]{2,1,0:T(8,128)(2,1)S(1)} %bitcast.110), channel_id=1, source_target_pairs={{0,2},{1,3},{2,0},{3,1},{4,6},{5,7},{6,4},{7,5},{8,10},{9,11},{10,... | collective-permute-start | bytes 442376 | tf_op jit(solution)/shard_map/ppermute | solution.py:1017
  70.5 19.6 %collective-permute-start.21 = (bf16[4,48,2048]{2,1,0:T(8,128)(2,1)S(1)}, bf16[4,48,2048]{2,1,0:T(8,128)(2,1)S(1)}, u32[]{:S(2)}, u32[]{:S(2)}) collective-permute-start(bf16[4,48,2048]{2,1,0:T(8,128)(2,1)S(1)} %pad_maximum_fusion.2.refs_4_), channel_id=1, source_target_pairs={{0,8},{8,0},{16,24},{24,16},{1,9},{9,1},{17,25},{25,17},{2,10},{10... | collective-permute-start | bytes 2359304 | tf_op jit(solution)/shard_map/ppermute | solution.py:1017
  70.5 20.0 %collective-permute-start.19 = (bf16[4,48,2048]{2,1,0:T(8,128)(2,1)S(1)}, bf16[4,48,2048]{2,1,0:T(8,128)(2,1)S(1)}, u32[]{:S(2)}, u32[]{:S(2)}) collective-permute-start(bf16[4,48,2048]{2,1,0:T(8,128)(2,1)S(1)} %pad_maximum_fusion.2.refs_4_), channel_id=1, source_target_pairs={{0,16},{8,24},{16,0},{24,8},{1,17},{9,25},{17,1},{25,9},{2,18},{10... | collective-permute-start | bytes 2359304 | tf_op jit(solution)/shard_map/ppermute | solution.py:1017
  72.1 18.4 %collective-permute-start.22 = (bf16[4,48,2048]{2,1,0:T(8,128)(2,1)S(1)}, bf16[4,48,2048]{2,1,0:T(8,128)(2,1)S(1)}, u32[]{:S(2)}, u32[]{:S(2)}) collective-permute-start(bf16[4,48,2048]{2,1,0:T(8,128)(2,1)S(1)} %pad_maximum_fusion.3.refs_6_), channel_id=1, source_target_pairs={{0,8},{8,0},{16,24},{24,16},{1,9},{9,1},{17,25},{25,17},{2,10},{10... | collective-permute-start | bytes 2359304 | tf_op jit(solution)/shard_map/ppermute | solution.py:1017
  72.3 19.8 %collective-permute-start.20 = (bf16[4,48,2048]{2,1,0:T(8,128)(2,1)S(1)}, bf16[4,48,2048]{2,1,0:T(8,128)(2,1)S(1)}, u32[]{:S(2)}, u32[]{:S(2)}) collective-permute-start(bf16[4,48,2048]{2,1,0:T(8,128)(2,1)S(1)} %pad_maximum_fusion.3.refs_6_), channel_id=1, source_target_pairs={{0,1},{1,0},{2,3},{3,2},{4,5},{5,4},{6,7},{7,6},{8,9},{9,8},{10,11... | collective-permute-start | bytes 2359304 | tf_op jit(solution)/shard_map/ppermute | solution.py:1017
  92.1 10.5 %collective-permute-start.24 = (bf16[4,48,2048]{2,1,0:T(8,128)(2,1)S(1)}, bf16[4,48,2048]{2,1,0:T(8,128)(2,1)S(1)}, u32[]{:S(2)}, u32[]{:S(2)}) collective-permute-start(bf16[4,48,2048]{2,1,0:T(8,128)(2,1)S(1)} %collective-permute-done.20.refs_7_), channel_id=1, source_target_pairs={{0,8},{8,0},{16,24},{24,16},{1,9},{9,1},{17,25},{25,17},{2,10},{10... | collective-permute-start | bytes 2359304 | tf_op jit(solution)/shard_map/ppermute | solution.py:1017
  102.7 27.4 %collective-permute-start.27 = (bf16[4,2,48,768]{3,2,1,0:T(8,128)(2,1)S(1)}, bf16[4,2,48,768]{3,2,1,0:T(8,128)(2,1)S(1)}, u32[]{:S(2)}, u32[]{:S(2)}) collective-permute-start(bf16[4,2,48,768]{3,2,1,0:T(8,128)(2,1)S(1)} %pad_maximum_fusion.4.refs_9_), channel_id=1, source_target_pairs={{0,8},{8,0},{16,24},{24,16},{1,9},{9,1},{17,25},{25,17},{2,10},{10... | collective-permute-start | bytes 1769480 | tf_op jit(solution)/shard_map/ppermute | solution.py:1017
  102.8 27.4 %collective-permute-start.25 = (bf16[4,2,48,768]{3,2,1,0:T(8,128)(2,1)S(1)}, bf16[4,2,48,768]{3,2,1,0:T(8,128)(2,1)S(1)}, u32[]{:S(2)}, u32[]{:S(2)}) collective-permute-start(bf16[4,2,48,768]{3,2,1,0:T(8,128)(2,1)S(1)} %pad_maximum_fusion.4.refs_9_), channel_id=1, source_target_pairs={{0,16},{8,24},{16,0},{24,8},{1,17},{9,25},{17,1},{25,9},{2,18},{10... | collective-permute-start | bytes 1769480 | tf_op jit(solution)/shard_map/ppermute | solution.py:1017
  103.5 26.7 %collective-permute-start.28 = (bf16[4,2,48,768]{3,2,1,0:T(8,128)(2,1)S(1)}, bf16[4,2,48,768]{3,2,1,0:T(8,128)(2,1)S(1)}, u32[]{:S(2)}, u32[]{:S(2)}) collective-permute-start(bf16[4,2,48,768]{3,2,1,0:T(8,128)(2,1)S(1)} %pad_maximum_fusion.5.refs_11_), channel_id=1, source_target_pairs={{0,8},{8,0},{16,24},{24,16},{1,9},{9,1},{17,25},{25,17},{2,10},{10... | collective-permute-start | bytes 1769480 | tf_op jit(solution)/shard_map/ppermute | solution.py:1017
  103.8 26.5 %collective-permute-start.26 = (bf16[4,2,48,768]{3,2,1,0:T(8,128)(2,1)S(1)}, bf16[4,2,48,768]{3,2,1,0:T(8,128)(2,1)S(1)}, u32[]{:S(2)}, u32[]{:S(2)}) collective-permute-start(bf16[4,2,48,768]{3,2,1,0:T(8,128)(2,1)S(1)} %pad_maximum_fusion.5.refs_11_), channel_id=1, source_target_pairs={{0,1},{1,0},{2,3},{3,2},{4,5},{5,4},{6,7},{7,6},{8,9},{9,8},{10,11... | collective-permute-start | bytes 1769480 | tf_op jit(solution)/shard_map/ppermute | solution.py:1017
  201.8 12.7 %collective-permute-start.34 = (bf16[16,2,48,768]{3,2,1,0:T(8,128)(2,1)}, bf16[16,2,48,768]{3,2,1,0:T(8,128)(2,1)S(1)}, u32[]{:S(2)}, u32[]{:S(2)}) collective-permute-start(bf16[16,2,48,768]{3,2,1,0:T(8,128)(2,1)} %up_grad.2), channel_id=1, source_target_pairs={{0,8},{8,0},{16,24},{24,16},{1,9},{9,1},{17,25},{25,17},{2,10},{10... | collective-permute-start | bytes 7077896 | tf_op jit(solution)/shard_map/ppermute | solution.py:1017
  202.2 22.8 %collective-permute-start.32 = (bf16[4,3,48,768]{3,2,1,0:T(8,128)(2,1)}, bf16[4,3,48,768]{3,2,1,0:T(8,128)(2,1)}, u32[]{:S(2)}, u32[]{:S(2)}) collective-permute-start(bf16[4,3,48,768]{3,2,1,0:T(8,128)(2,1)} %get-tuple-element.316), channel_id=1, source_target_pairs={{0,16},{8,24},{16,0},{24,8},{1,17},{9,25},{17,1},{25,9},{2,18},{10... | collective-permute-start | bytes 2654216 | tf_op jit(solution)/shard_map/ppermute | solution.py:1017
  203.5 22.9 %collective-permute-start.33 = (bf16[4,3,48,768]{3,2,1,0:T(8,128)(2,1)}, bf16[4,3,48,768]{3,2,1,0:T(8,128)(2,1)}, u32[]{:S(2)}, u32[]{:S(2)}) collective-permute-start(bf16[4,3,48,768]{3,2,1,0:T(8,128)(2,1)} %get-tuple-element.317), channel_id=1, source_target_pairs={{0,1},{1,0},{2,3},{3,2},{4,5},{5,4},{6,7},{7,6},{8,9},{9,8},{10,11... | collective-permute-start | bytes 2654216 | tf_op jit(solution)/shard_map/ppermute | solution.py:1017
  216.2 31.0 %collective-permute-start.37 = (bf16[4,2,48,768]{3,2,1,0:T(8,128)(2,1)S(1)}, bf16[4,2,48,768]{3,2,1,0:T(8,128)(2,1)S(1)}, u32[]{:S(2)}, u32[]{:S(2)}) collective-permute-start(bf16[4,2,48,768]{3,2,1,0:T(8,128)(2,1)S(1)} %get-tuple-element.338), channel_id=1, source_target_pairs={{0,16},{8,24},{16,0},{24,8},{1,17},{9,25},{17,1},{25,9},{2,18},{10... | collective-permute-start | bytes 1769480 | tf_op jit(solution)/shard_map/ppermute | solution.py:1017
  217.0 30.2 %collective-permute-start.38 = (bf16[4,2,48,768]{3,2,1,0:T(8,128)(2,1)S(1)}, bf16[4,2,48,768]{3,2,1,0:T(8,128)(2,1)S(1)}, u32[]{:S(2)}, u32[]{:S(2)}) collective-permute-start(bf16[4,2,48,768]{3,2,1,0:T(8,128)(2,1)S(1)} %get-tuple-element.339), channel_id=1, source_target_pairs={{0,1},{1,0},{2,3},{3,2},{4,5},{5,4},{6,7},{7,6},{8,9},{9,8},{10,11... | collective-permute-start | bytes 1769480 | tf_op jit(solution)/shard_map/ppermute | solution.py:1017
  229.0 18.2 %collective-permute-start.35 = (bf16[2,3,48,768]{3,2,1,0:T(8,128)(2,1)S(1)}, bf16[2,3,48,768]{3,2,1,0:T(8,128)(2,1)S(1)}, u32[]{:S(2)}, u32[]{:S(2)}) collective-permute-start(bf16[2,3,48,768]{3,2,1,0:T(8,128)(2,1)S(1)} %slice.241), channel_id=1, source_target_pairs={{0,1},{1,0},{2,3},{3,2},{4,5},{5,4},{6,7},{7,6},{8,9},{9,8},{10,11... | collective-permute-start | bytes 1327112 | tf_op jit(solution)/shard_map/ppermute | solution.py:1017
  230.5 16.8 %collective-permute-start.36 = (bf16[2,3,48,768]{3,2,1,0:T(8,128)(2,1)S(1)}, bf16[2,3,48,768]{3,2,1,0:T(8,128)(2,1)S(1)}, u32[]{:S(2)}, u32[]{:S(2)}) collective-permute-start(bf16[2,3,48,768]{3,2,1,0:T(8,128)(2,1)S(1)} %slice.242), channel_id=1, source_target_pairs={{0,16},{8,24},{16,0},{24,8},{1,17},{9,25},{17,1},{25,9},{2,18},{10... | collective-permute-start | bytes 1327112 | tf_op jit(solution)/shard_map/ppermute | solution.py:1017
  248.1 11.6 %collective-permute-start.39 = (bf16[2,2,48,768]{3,2,1,0:T(8,128)(2,1)S(1)}, bf16[2,2,48,768]{3,2,1,0:T(8,128)(2,1)S(1)}, u32[]{:S(2)}, u32[]{:S(2)}) collective-permute-start(bf16[2,2,48,768]{3,2,1,0:T(8,128)(2,1)S(1)} %slice.248), channel_id=1, source_target_pairs={{0,1},{1,0},{2,3},{3,2},{4,5},{5,4},{6,7},{7,6},{8,9},{9,8},{10,11... | collective-permute-start | bytes 884744 | tf_op jit(solution)/shard_map/ppermute | solution.py:1017
  252.2 23.4 %collective-permute-start.42 = (bf16[3,48,768]{2,1,0:T(8,128)(2,1)S(1)}, bf16[3,48,768]{2,1,0:T(8,128)(2,1)S(1)}, u32[]{:S(2)}, u32[]{:S(2)}) collective-permute-start(bf16[3,48,768]{2,1,0:T(8,128)(2,1)S(1)} %get-tuple-element.364), channel_id=1, source_target_pairs={{0,4},{1,5},{2,6},{3,7},{4,0},{5,1},{6,2},{7,3},{8,12},{9,13},{10,... | collective-permute-start | bytes 663560 | tf_op jit(solution)/shard_map/ppermute | solution.py:1017
  253.3 22.3 %collective-permute-start.43 = (bf16[3,48,768]{2,1,0:T(8,128)(2,1)S(1)}, bf16[3,48,768]{2,1,0:T(8,128)(2,1)S(1)}, u32[]{:S(2)}, u32[]{:S(2)}) collective-permute-start(bf16[3,48,768]{2,1,0:T(8,128)(2,1)S(1)} %get-tuple-element.365), channel_id=1, source_target_pairs={{0,6},{1,7},{2,4},{3,5},{4,2},{5,3},{6,0},{7,1},{8,14},{9,15},{10,... | collective-permute-start | bytes 663560 | tf_op jit(solution)/shard_map/ppermute | solution.py:1017
  294.3 15.5 %collective-permute-start.46 = (bf16[4,48,1280]{2,1,0:T(8,128)(2,1)S(1)}, bf16[4,48,1280]{2,1,0:T(8,128)(2,1)S(1)}, u32[]{:S(2)}, u32[]{:S(2)}) collective-permute-start(bf16[4,48,1280]{2,1,0:T(8,128)(2,1)S(1)} %get-tuple-element.387), channel_id=1, source_target_pairs={{0,16},{8,24},{16,0},{24,8},{1,17},{9,25},{17,1},{25,9},{2,18},{10... | collective-permute-start | bytes 1474568 | tf_op jit(solution)/shard_map/ppermute | solution.py:1017
  295.7 14.1 %collective-permute-start.47 = (bf16[4,48,1280]{2,1,0:T(8,128)(2,1)S(1)}, bf16[4,48,1280]{2,1,0:T(8,128)(2,1)S(1)}, u32[]{:S(2)}, u32[]{:S(2)}) collective-permute-start(bf16[4,48,1280]{2,1,0:T(8,128)(2,1)S(1)} %get-tuple-element.388), channel_id=1, source_target_pairs={{0,1},{1,0},{2,3},{3,2},{4,5},{5,4},{6,7},{7,6},{8,9},{9,8},{10,11... | collective-permute-start | bytes 1474568 | tf_op jit(solution)/shard_map/ppermute | solution.py:1017
  296.3 13.4 %collective-permute-start.48 = (bf16[2,48,768]{2,1,0:T(8,128)(2,1)S(1)}, bf16[2,48,768]{2,1,0:T(8,128)(2,1)S(1)}, u32[]{:S(2)}, u32[]{:S(2)}) collective-permute-start(bf16[2,48,768]{2,1,0:T(8,128)(2,1)S(1)} %get-tuple-element.390), channel_id=1, source_target_pairs={{0,4},{1,5},{2,6},{3,7},{4,0},{5,1},{6,2},{7,3},{8,12},{9,13},{10,... | collective-permute-start | bytes 442376 | tf_op jit(solution)/shard_map/ppermute | solution.py:1017
  298.4 11.3 %collective-permute-start.49 = (bf16[2,48,768]{2,1,0:T(8,128)(2,1)S(1)}, bf16[2,48,768]{2,1,0:T(8,128)(2,1)S(1)}, u32[]{:S(2)}, u32[]{:S(2)}) collective-permute-start(bf16[2,48,768]{2,1,0:T(8,128)(2,1)S(1)} %get-tuple-element.391), channel_id=1, source_target_pairs={{0,6},{1,7},{2,4},{3,5},{4,2},{5,3},{6,0},{7,1},{8,14},{9,15},{10,... | collective-permute-start | bytes 442376 | tf_op jit(solution)/shard_map/ppermute | solution.py:1017
  318.6 15.0 %collective-permute-start.55 = (bf16[5,48,768]{2,1,0:T(8,128)(2,1)S(1)}, bf16[5,48,768]{2,1,0:T(8,128)(2,1)S(1)}, u32[]{:S(2)}, u32[]{:S(2)}) collective-permute-start(bf16[5,48,768]{2,1,0:T(8,128)(2,1)S(1)} %pad_maximum_fusion.10.refs_0_), channel_id=1, source_target_pairs={{0,16},{8,24},{16,0},{24,8},{1,17},{9,25},{17,1},{25,9},{2,18},{10... | collective-permute-start | bytes 1105928 | tf_op jit(solution)/shard_map/ppermute | solution.py:1017
  (71 other events, 593.4 us)

commit v7 on v6

--- a/solution.py
+++ b/solution.py
@@ -386,8 +386,9 @@
     me_ref, hid_ref, act_ref, slope_ref, teach_ref, aux_ref, up_ref, vec_ref, total_ref = refs[0:9]
     at = 9 + (pieces or 1)
     out_ref, gh_ref, ga_ref, gd_ref, gu_ref, sums_ref, usum_ref = refs[at : at + 7]
+    final_ref = refs[at + 7]
     if pieces:
-        down3_ref, sem = refs[at + 7 :]
+        down3_ref, sem = refs[at + 8 :]
 
         @pl.when(step == 0)
         def _():
@@ -413,7 +414,12 @@
         down = down + nn(act_ref[:, :, cols].reshape(rows, D), down_rows(part))
     final = keep * (hidden + down)
     for at in range(group):
-        out_ref[at] = final[at * ROWS : at * ROWS + SLOTS].astype(BF16)
+        final_ref[:, step * group + at, :] = final[at * ROWS : at * ROWS + SLOTS]
+
+    @pl.when(step == pl.num_programs(0) - 1)
+    def _():
+        out_ref[...] = final_ref[...].astype(BF16)
+
     error = final - teach_ref[...].reshape(rows, D).astype(F32)
     weighted = valid * error
     grad_final = coef * weighted
@@ -749,10 +755,9 @@
     count = hidden.shape[0]
     group = math.gcd(count, 2)
     win = lambda width: windows_from(0, (group, ROWS, width))
-    plain = windows_from(0, (group, SLOTS, D))
     arr = lambda width, dtype: shape_of((count, ROWS, width), dtype)
     pieces = len(weights) if chunked else 0
-    scratch = []
+    scratch = [pltpu.VMEM((SLOTS, count, D), F32)]
     if pieces:
         scratch += [pltpu.VMEM((MLP // 48, 48, D), BF16), pltpu.SemaphoreType.DMA((1,))]
     return pl.pallas_call(
@@ -761,9 +766,9 @@
         in_specs=[SMEM, win(D), win(MLP), win(MLP), win(D), win(2), whole((D, MLP)), whole((8, D)),
                   whole((1, 128))]
         + ([ANY] * pieces if pieces else [whole(v.shape) for v in weights]),
-        out_specs=[plain, win(D), win(D), win(D), win(MLP), whole_out((5, D)), whole_out((1, MLP))],
+        out_specs=[whole_out((SLOTS, count, D)), win(D), win(D), win(D), win(MLP), whole_out((5, D)), whole_out((1, MLP))],
         out_shape=[
-            shape_of((count, SLOTS, D), BF16), arr(D, F32), arr(D, BF16), arr(D, BF16),
+            shape_of((SLOTS, count, D), BF16), arr(D, F32), arr(D, BF16), arr(D, BF16),
             arr(MLP, BF16), shape_of((5, D), F32), shape_of((1, MLP), F32),
         ],
         scratch_shapes=scratch,
@@ -872,7 +877,7 @@
 
 
 def qkv_shard_kernel(me_ref, total_ref, *refs):
-    quarters, out_ref, notes_ref = refs[0:4], refs[4], refs[5]
+    quarters, out_ref, notes_ref, turned_ref = refs[0:4], refs[4], refs[5], refs[6]
     core, far_x = me_ref[0] % 2, me_ref[0] // 2
     for at, ref in enumerate(quarters):
         this_core, this_x = core ^ (at // 2), far_x ^ (at % 2)
@@ -882,11 +887,12 @@
         here = pl.ds(pl.multiple_of((this_core * 2 + this_x) * 8, 8), 8)
         notes_ref[here, :] = ref[0:16, QKV_HALF : QKV_HALF + NOTES].astype(F32)[0:8]
     errors = jnp.sum(notes_ref[30:31, :], axis=1, keepdims=True)
+    turned_ref[...] = notes_ref[...].T[96:112]
     notes_ref[31:32, :] = errors / (total_ref[...] * D)
 
 
 def qkv_shard(me, total, quarters):
-    shapes = [(96, 3 * D), (32, 128)]
+    shapes = [(96, 3 * D), (32, 128), (16, 32)]
     return pl.pallas_call(
         qkv_shard_kernel,
         grid=(1,),
@@ -1267,11 +1273,11 @@
             me, (own, from_x, swap(own, "rep", 1), swap(from_x, "rep", 1))
         )
         from_xq, d_up = tied(from_xq, d_up)
-        d_qkv, mine = qkv_shard(
+        d_qkv, mine, turned = qkv_shard(
             me, total, (own_q, from_xq, swap(own_q, "rep", 1), swap(from_xq, "rep", 1))
         )
         vectors = [mine[at, 0:96] for at in range(8)]
-        tables = [mine[0:27, 96 + 8 * at : 104 + 8 * at] for at in range(2)]
+        tables = [turned[8 * at : 8 * at + 8, 0:27].T for at in range(2)]
         outs = vectors + [mine[27:30].reshape(-1)] + tables
         loss = mine[31, 0]
     else:
@@ -1308,7 +1314,7 @@
         loss = mine[at] / (valid_total * D)
     (g_gain1, g_shift1, g_qb, g_vb, g_pb, g_gain2, g_shift2, g_db, g_ub, g_rh, g_rw) = outs
     return (
-        out, loss, input_grad.transpose(1, 0, 2), g_gain1, g_shift1, d_qkv, g_qb, g_vb, g_rh, g_rw, d_proj, g_pb,
+        out.transpose(1, 0, 2), loss, input_grad.transpose(1, 0, 2), g_gain1, g_shift1, d_qkv, g_qb, g_vb, g_rh, g_rw, d_proj, g_pb,
         g_gain2, g_shift2, d_up, g_ub, d_down, g_db,
     )
 

time: 350 us -> 352 us (level)
    unnamed x89 -> x84, local copies, waits for them, and re-layouts: 7.1 us -> 3.9 us
  transfers between devices with their start and end apart: 61 -> 61, of which waited for: 19 -> 20; matrix products, arithmetic and copies ran while one was open for 5% -> 4% of each run, Pallas kernels for 42% -> 41%
where the time goes in v7:
time: 352 us; the launch traced here: 348 us
  Pallas kernels  205 us (58%)
  starting transfers between devices  59.4 us (17%)
  waiting for transfers between devices  51.9 us (15%)
  other arithmetic  13.9 us (4%)
  local copies, waits for them, and re-layouts  13.6 us (4%)
  between operations  4.48 us (1%)
    ppermute x61, starting transfers between devices, swap(): return lax.ppermute(values, axis, [(at, at ^ mask) for at in range(size)])  59.4 us
    ppermute x61, waiting for transfers between devices, swap(): return lax.ppermute(values, axis, [(at, at ^ mask) for at in range(size)])  51.9 us
    pallas_call x1, Pallas kernels, mlp_down(): pl.pallas_call(functools.partial(down_kernel, group=group, pieces=pieces,...  41.2 us
    pallas_call x3, Pallas kernels, attend(): pl.pallas_call(functools.partial(attend_kernel, first=first, pieces=piece...  38 us
    pallas_call x3, Pallas kernels, attend_back(): pl.pallas_call(functools.partial(attend_back_kernel, earlier=len(earlier)...  26.7 us
    pallas_call x1, Pallas kernels, mlp_up(): pl.pallas_call(functools.partial(up_kernel, group=group, pieces=pieces),...  25.9 us
    pallas_call x2, Pallas kernels, up_grad(): pl.pallas_call(up_grad_kernel, grid_spec=pltpu.PrefetchScalarGridSpec(num...  19.7 us
    pallas_call x1, Pallas kernels, down_grad(): pl.pallas_call(down_grad_kernel, grid=(5,), in_specs=[SMEM, pl.BlockSpec(...  16.5 us
  transfers between devices with their start and end apart: 61, of which 20 were waited for; matrix products, arithmetic and copies ran while one was open for 4% of the time, Pallas kernels for 41%

profile of v7, /device:TPU:0, one launch (start us, length us, event | category | flops | bytes accessed | tf_op | source)
XLA Modules:
  0.0 347.9 jit_solution(16706115442418242988)
XLA Ops:
  2.4 5.1 %collective-permute-start.2 = (bf16[48,1280]{1,0:T(8,128)(2,1)S(1)}, bf16[48,1280]{1,0:T(8,128)(2,1)S(1)}, u32[]{:S(2)}, u32[]{:S(2)}) collective-permute-start(bf16[48,1280]{1,0:T(8,128)(2,1)S(1)} %pad_maximum_fusion.16), channel_id=1, source_target_pairs={{0,6},{1,7},{2,4},{3,5},{4,2},{5,3},{6,0},{7,1},{8,14},{9,15},{10,... | collective-permute-start | bytes 368648 | tf_op jit(solution)/shard_map/ppermute | solution.py:1023
  23.7 3.1 collective-permute-done.5
  32.2 5.7 %collective-permute-done.8 = bf16[48,2048]{1,0:T(8,128)(2,1)S(1)} collective-permute-done((bf16[48,2048]{1,0:T(8,128)(2,1)S(1)}, bf16[48,2048]{1,0:T(8,128)(2,1)S(1)}, u32[]{:S(2)}, u32[]{:S(2)}) %collective-permute-start.8) | collective-permute-done | bytes 196640 | tf_op jit(solution)/shard_map/ppermute | solution.py:1023
  39.7 2.5 collective-permute-start.11
  44.3 4.2 %collective-permute-done.11 = bf16[48,2048]{1,0:T(8,128)(2,1)S(1)} collective-permute-done((bf16[48,2048]{1,0:T(8,128)(2,1)S(1)}, bf16[48,2048]{1,0:T(8,128)(2,1)S(1)}, u32[]{:S(2)}, u32[]{:S(2)}) %collective-permute-start.11) | collective-permute-done | bytes 196640 | tf_op jit(solution)/shard_map/ppermute | solution.py:1023
  50.0 2.6 collective-permute-start.16
  54.4 15.4 %attend.3 = (bf16[8,208,2304]{2,1,0:T(8,128)(2,1)}, bf16[8,12,208,256]{3,2,1,0:T(8,128)(2,1)}, bf16[8,208,768]{2,1,0:T(8,128)(2,1)}, bf16[8,208,768]{2,1,0:T(8,128)(2,1)}, bf16[768,2304]{1,0:T(8,128)(2,1)}) custom-call(s32[3]{0:T(128)} %copy-done.11, bf16[8,208,768]{2,1,0:T(8,128)(2,1)} %pad.68.refs_1_.tok_ref, bf16[8,48,1280]{2,1,0:T(8,128)(2,1)} %copy-done.17, ...), custom_call_target="tpu_custom_call" | custom-call | flops 100000000 | bytes 100000 | tf_op jit(solution)/shard_map/attend/pallas_call | solution.py:709
  73.3 16.4 %attend.4 = (bf16[8,208,2304]{2,1,0:T(8,128)(2,1)}, bf16[8,12,208,256]{3,2,1,0:T(8,128)(2,1)}, bf16[8,208,768]{2,1,0:T(8,128)(2,1)}, bf16[8,208,768]{2,1,0:T(8,128)(2,1)}) custom-call(s32[3]{0:T(128)} %copy-done.11, bf16[8,208,768]{2,1,0:T(8,128)(2,1)} %pad.68.refs_1_.tok_ref, ...), custom_call_target="tpu_custom_call", output_to_operand_aliasing={{0}: (6, {}), {1}: (7, {}), {2}: (8, {}), {3}: (9, {})} | custom-call | flops 100000000 | bytes 100000 | tf_op jit(solution)/shard_map/attend/pallas_call | solution.py:709
  94.1 6.1 %attend.5 = (bf16[8,208,2304]{2,1,0:T(8,128)(2,1)}, bf16[8,12,208,256]{3,2,1,0:T(8,128)(2,1)}, bf16[8,208,768]{2,1,0:T(8,128)(2,1)}, bf16[8,208,768]{2,1,0:T(8,128)(2,1)}) custom-call(s32[3]{0:T(128)} %copy-done.11, bf16[8,208,768]{2,1,0:T(8,128)(2,1)} %pad.68.refs_1_.tok_ref, ...), custom_call_target="tpu_custom_call", output_to_operand_aliasing={{0}: (6, {}), {1}: (7, {}), {2}: (8, {}), {3}: (9, {})} | custom-call | flops 100000000 | bytes 100000 | tf_op jit(solution)/shard_map/attend/pallas_call | solution.py:709
  104.1 25.9 %mlp_up.1 = (f32[8,208,768]{2,1,0:T(8,128)}, bf16[8,208,768]{2,1,0:T(8,128)(2,1)}, bf16[8,208,3072]{2,1,0:T(8,128)(2,1)}, bf16[8,208,3072]{2,1,0:T(8,128)(2,1)},...) custom-call(s32[3]{0:T(128)} %copy-done.11, ...), custom_call_target="tpu_custom_call" | custom-call | flops 800000000 | bytes 100000 | tf_op jit(solution)/shard_map/mlp_up/pallas_call | solution.py:740
  133.8 41.2 %mlp_down.1 = (bf16[196,8,768]{2,1,0:T(8,128)(2,1)}, f32[8,208,768]{2,1,0:T(8,128)}, bf16[8,208,768]{2,1,0:T(8,128)(2,1)}, bf16[8,208,768]{2,1,0:T(8,128)(2,1)},...) custom-call(s32[3]{0:T(128)} %copy-done.11, f32[8,208,768]{2,1,0:T(8,128)} %get-tuple-element.294.refs_1_, ...), custom_call_target="tpu_custom_call" | custom-call | flops 800000000 | bytes 100000 | tf_op jit(solution)/shard_map/mlp_down/pallas_call | solution.py:763
  175.1 16.5 %down_grad.1 = (bf16[16,3,48,768]{3,2,1,0:T(8,128)(2,1)}, bf16[16,3,48,768]{3,2,1,0:T(8,128)(2,1)}) custom-call(s32[3]{0:T(128)} %copy-done.11, bf16[1664,3072]{1,0:T(8,128)(2,1)} %bitcast.95, bf16[1664,768]{1,0:T(8,128)(2,1)} %bitcast.99, bf16[1664,768]{1,0:T(8,128)(2,1)} %bitcast.96, bf16[1664,768]{1,0:T(8,128)(2,1)} %bitcast.88), custom_call_target="tpu_custom_call" | custom-call | flops 100000000 | bytes 100000 | tf_op jit(solution)/shard_map/down_grad/pallas_call | solution.py:1001
  191.8 10.0 %up_grad.2 = bf16[16,2,48,768]{3,2,1,0:T(8,128)(2,1)} custom-call(s32[3]{0:T(128)} %copy-done.11, bf16[1664,768]{1,0:T(8,128)(2,1)} %bitcast.97, bf16[1664,3072]{1,0:T(8,128)(2,1)} %bitcast.93), custom_call_target="tpu_custom_call" | custom-call | flops 100000000 | bytes 100000 | tf_op jit(solution)/shard_map/up_grad/pallas_call | solution.py:980
  201.9 3.1 add_convert_fusion.3
  208.0 9.6 %up_grad.3 = bf16[16,2,48,768]{3,2,1,0:T(8,128)(2,1)} custom-call(s32[3]{0:T(128)} %copy-done.11, bf16[1664,768]{1,0:T(8,128)(2,1)} %bitcast.98, bf16[1664,3072]{1,0:T(8,128)(2,1)} %bitcast.94), custom_call_target="tpu_custom_call" | custom-call | flops 100000000 | bytes 100000 | tf_op jit(solution)/shard_map/up_grad/pallas_call | solution.py:980
  220.8 7.3 %attend_back.3 = (bf16[8,208,2304]{2,1,0:T(8,128)(2,1)}, f32[128,128]{1,0:T(8,128)S(1)}, f32[2,768]{1,0:T(2,128)S(1)}) custom-call(bf16[8,208,768]{2,1,0:T(8,128)(2,1)S(1)} %copy-done.3, bf16[768,768]{1,0:T(8,128)(2,1)S(1)} %copy-done.6, bf16[8,208,2304]{2,1,0:T(8,128)(2,1)} %get-tuple-element.326.refs_2_, ...), custom_call_target="tpu_custom_call" | custom-call | flops 100000000 | bytes 100000 | tf_op jit(solution)/shard_map/attend_back/pallas_call | solution.py:785
  229.5 2.6 add_convert_fusion
  234.3 14.3 %attend_back.4 = (bf16[8,208,2304]{2,1,0:T(8,128)(2,1)}, f32[128,128]{1,0:T(8,128)S(1)}, f32[2,768]{1,0:T(2,128)S(1)}) custom-call(bf16[8,208,768]{2,1,0:T(8,128)(2,1)S(1)} %copy-done.3, bf16[768,768]{1,0:T(8,128)(2,1)S(1)} %copy-done.6, bf16[8,208,2304]{2,1,0:T(8,128)(2,1)} %get-tuple-element.326.refs_2_, ...), custom_call_target="tpu_custom_call", output_to_operand_aliasing={{0}: (6, {})} | custom-call | flops 100000000 | bytes 100000 | tf_op jit(solution)/shard_map/attend_back/pallas_call | solution.py:785
  248.6 1.7 collective-permute-done.35
  253.4 2.0 collective-permute-start.41
  257.8 5.1 %attend_back.5 = (bf16[8,208,2304]{2,1,0:T(8,128)(2,1)}, f32[128,128]{1,0:T(8,128)S(1)}, f32[2,768]{1,0:T(2,128)S(1)}) custom-call(bf16[8,208,768]{2,1,0:T(8,128)(2,1)S(1)} %copy-done.3, bf16[768,768]{1,0:T(8,128)(2,1)S(1)} %copy-done.6, bf16[8,208,2304]{2,1,0:T(8,128)(2,1)} %get-tuple-element.326.refs_2_, ...), custom_call_target="tpu_custom_call", output_to_operand_aliasing={{0}: (6, {})} | custom-call | flops 100000000 | bytes 100000 | tf_op jit(solution)/shard_map/attend_back/pallas_call | solution.py:785
  263.6 15.4 %input_back.1 = (f32[196,8,768]{2,1,0:T(8,128)}, f32[2,768]{1,0:T(2,128)S(1)}) custom-call(s32[3]{0:T(128)S(1)} %copy-done.12, bf16[8,208,2304]{2,1,0:T(8,128)(2,1)} %get-tuple-element.381.dqkv_ref, bf16[768,2304]{1,0:T(8,128)(2,1)S(1)} %copy-done.5, bf16[8,208,768]{2,1,0:T(8,128)(2,1)S(1)} %copy-done.2, f32[8,208,768]{2,1,0:T(8,128)} %get-tuple-element.368.gh_ref, ...), custom_call_target="tpu_custom_call" | custom-call | flops 100000000 | bytes 100000 | tf_op jit(solution)/shard_map/input_back/pallas_call | solution.py:813
  279.2 2.0 pack.1.notes_ref
  282.3 7.4 %qkv_grad.2 = bf16[16,48,1280]{2,1,0:T(8,128)(2,1)S(1)} custom-call(s32[3]{0:T(128)S(1)} %copy-done.12, bf16[1664,768]{1,0:T(8,128)(2,1)S(1)} %bitcast.89, bf16[1664,2304]{1,0:T(8,128)(2,1)} %bitcast.91, bf16[4,8,48,128]{3,2,1,0:T(8,128)(2,1)S(1)} %pack.1.notes_ref), custom_call_target="tpu_custom_call" | custom-call | flops 100000000 | bytes 100000 | tf_op jit(solution)/shard_map/qkv_grad/pallas_call | solution.py:958
  289.7 7.4 %qkv_grad.3 = bf16[16,48,1280]{2,1,0:T(8,128)(2,1)S(1)} custom-call(s32[3]{0:T(128)S(1)} %copy-done.12, bf16[1664,768]{1,0:T(8,128)(2,1)S(1)} %bitcast.90, bf16[1664,2304]{1,0:T(8,128)(2,1)} %bitcast.92, bf16[4,8,48,128]{3,2,1,0:T(8,128)(2,1)S(1)} %pack.1.notes_ref), custom_call_target="tpu_custom_call" | custom-call | flops 100000000 | bytes 100000 | tf_op jit(solution)/shard_map/qkv_grad/pallas_call | solution.py:958
  299.4 2.1 collective-permute-start.48
  302.7 10.1 %collective-permute-done.48 = bf16[2,48,768]{2,1,0:T(8,128)(2,1)S(1)} collective-permute-done((bf16[2,48,768]{2,1,0:T(8,128)(2,1)S(1)}, bf16[2,48,768]{2,1,0:T(8,128)(2,1)S(1)}, u32[]{:S(2)}, u32[]{:S(2)}) %collective-permute-start.48) | collective-permute-done | bytes 147488 | tf_op jit(solution)/shard_map/ppermute | solution.py:1023
  315.5 4.8 %collective-permute-done.50 = bf16[2,48,1280]{2,1,0:T(8,128)(2,1)S(1)} collective-permute-done((bf16[2,48,1280]{2,1,0:T(8,128)(2,1)S(1)}, bf16[2,48,1280]{2,1,0:T(8,128)(2,1)S(1)}, u32[]{:S(2)}, u32[]{:S(2)}) %collective-permute-start.50) | collective-permute-done | bytes 245792 | tf_op jit(solution)/shard_map/ppermute | solution.py:1023
  322.4 3.7 %collective-permute-start.52 = (bf16[48,1280]{1,0:T(8,128)(2,1)S(1)}, bf16[48,1280]{1,0:T(8,128)(2,1)S(1)}, u32[]{:S(2)}, u32[]{:S(2)}) collective-permute-start(bf16[48,1280]{1,0:T(8,128)(2,1)S(1)} %get-tuple-element.403), channel_id=1, source_target_pairs={{0,2},{1,3},{2,0},{3,1},{4,6},{5,7},{6,4},{7,5},{8,10},{9,11},{10,... | collective-permute-start | bytes 368648 | tf_op jit(solution)/shard_map/ppermute | solution.py:1023
  329.9 6.8 %collective-permute-done.53 = bf16[48,1280]{1,0:T(8,128)(2,1)S(1)} collective-permute-done((bf16[48,1280]{1,0:T(8,128)(2,1)S(1)}, bf16[48,1280]{1,0:T(8,128)(2,1)S(1)}, u32[]{:S(2)}, u32[]{:S(2)}) %collective-permute-start.53) | collective-permute-done | bytes 122912 | tf_op jit(solution)/shard_map/ppermute | solution.py:1023
  338.4 2.2 shard.1
  340.6 2.0 collective-permute-done.56.refs_1_
  (257 shorter events, 79.0 us)
Async XLA Ops:
  2.4 14.5 %collective-permute-start.2 = (bf16[48,1280]{1,0:T(8,128)(2,1)S(1)}, bf16[48,1280]{1,0:T(8,128)(2,1)S(1)}, u32[]{:S(2)}, u32[]{:S(2)}) collective-permute-start(bf16[48,1280]{1,0:T(8,128)(2,1)S(1)} %pad_maximum_fusion.16), channel_id=1, source_target_pairs={{0,6},{1,7},{2,4},{3,5},{4,2},{5,3},{6,0},{7,1},{8,14},{9,15},{10,... | collective-permute-start | bytes 368648 | tf_op jit(solution)/shard_map/ppermute | solution.py:1023
  26.9 11.0 %collective-permute-start.7 = (bf16[4,48,1280]{2,1,0:T(8,128)(2,1)S(1)}, bf16[4,48,1280]{2,1,0:T(8,128)(2,1)S(1)}, u32[]{:S(2)}, u32[]{:S(2)}) collective-permute-start(bf16[4,48,1280]{2,1,0:T(8,128)(2,1)S(1)} %pad_maximum_fusion.7.b_ref), channel_id=1, source_target_pairs={{0,1},{1,0},{2,3},{3,2},{4,5},{5,4},{6,7},{7,6},{8,9},{9,8},{10,11... | collective-permute-start | bytes 1474568 | tf_op jit(solution)/shard_map/ppermute | solution.py:1023
  28.0 10.8 %collective-permute-start.6 = (bf16[4,48,1280]{2,1,0:T(8,128)(2,1)S(1)}, bf16[4,48,1280]{2,1,0:T(8,128)(2,1)S(1)}, u32[]{:S(2)}, u32[]{:S(2)}) collective-permute-start(bf16[4,48,1280]{2,1,0:T(8,128)(2,1)S(1)} %pad_maximum_fusion.6.a_ref), channel_id=1, source_target_pairs={{0,16},{8,24},{16,0},{24,8},{1,17},{9,25},{17,1},{25,9},{2,18},{10... | collective-permute-start | bytes 1474568 | tf_op jit(solution)/shard_map/ppermute | solution.py:1023
  48.6 21.2 %collective-permute-start.12 = (bf16[2,48,2048]{2,1,0:T(8,128)(2,1)S(1)}, bf16[2,48,2048]{2,1,0:T(8,128)(2,1)S(1)}, u32[]{:S(2)}, u32[]{:S(2)}) collective-permute-start(bf16[2,48,2048]{2,1,0:T(8,128)(2,1)S(1)} %pad_maximum_fusion.8), channel_id=1, source_target_pairs={{0,1},{1,0},{2,3},{3,2},{4,5},{5,4},{6,7},{7,6},{8,9},{9,8},{10,11... | collective-permute-start | bytes 1179656 | tf_op jit(solution)/shard_map/ppermute | solution.py:1023
  49.4 20.4 %collective-permute-start.13 = (bf16[2,48,2048]{2,1,0:T(8,128)(2,1)S(1)}, bf16[2,48,2048]{2,1,0:T(8,128)(2,1)S(1)}, u32[]{:S(2)}, u32[]{:S(2)}) collective-permute-start(bf16[2,48,2048]{2,1,0:T(8,128)(2,1)S(1)} %pad_maximum_fusion.9), channel_id=1, source_target_pairs={{0,16},{8,24},{16,0},{24,8},{1,17},{9,25},{17,1},{25,9},{2,18},{10... | collective-permute-start | bytes 1179656 | tf_op jit(solution)/shard_map/ppermute | solution.py:1023
  50.0 19.8 %collective-permute-start.16 = (bf16[2,48,768]{2,1,0:T(8,128)(2,1)S(1)}, bf16[2,48,768]{2,1,0:T(8,128)(2,1)S(1)}, u32[]{:S(2)}, u32[]{:S(2)}) collective-permute-start(bf16[2,48,768]{2,1,0:T(8,128)(2,1)S(1)} %bitcast.113), channel_id=1, source_target_pairs={{0,6},{1,7},{2,4},{3,5},{4,2},{5,3},{6,0},{7,1},{8,14},{9,15},{10,... | collective-permute-start | bytes 442376 | tf_op jit(solution)/shard_map/ppermute | solution.py:1023
  52.6 17.2 %collective-permute-start.15 = (bf16[2,48,768]{2,1,0:T(8,128)(2,1)S(1)}, bf16[2,48,768]{2,1,0:T(8,128)(2,1)S(1)}, u32[]{:S(2)}, u32[]{:S(2)}) collective-permute-start(bf16[2,48,768]{2,1,0:T(8,128)(2,1)S(1)} %bitcast.114), channel_id=1, source_target_pairs={{0,4},{1,5},{2,6},{3,7},{4,0},{5,1},{6,2},{7,3},{8,12},{9,13},{10,... | collective-permute-start | bytes 442376 | tf_op jit(solution)/shard_map/ppermute | solution.py:1023
  54.3 15.5 %collective-permute-start.14 = (bf16[2,48,768]{2,1,0:T(8,128)(2,1)S(1)}, bf16[2,48,768]{2,1,0:T(8,128)(2,1)S(1)}, u32[]{:S(2)}, u32[]{:S(2)}) collective-permute-start(bf16[2,48,768]{2,1,0:T(8,128)(2,1)S(1)} %bitcast.115), channel_id=1, source_target_pairs={{0,2},{1,3},{2,0},{3,1},{4,6},{5,7},{6,4},{7,5},{8,10},{9,11},{10,... | collective-permute-start | bytes 442376 | tf_op jit(solution)/shard_map/ppermute | solution.py:1023
  70.1 19.6 %collective-permute-start.21 = (bf16[4,48,2048]{2,1,0:T(8,128)(2,1)S(1)}, bf16[4,48,2048]{2,1,0:T(8,128)(2,1)S(1)}, u32[]{:S(2)}, u32[]{:S(2)}) collective-permute-start(bf16[4,48,2048]{2,1,0:T(8,128)(2,1)S(1)} %pad_maximum_fusion.2.refs_4_), channel_id=1, source_target_pairs={{0,8},{8,0},{16,24},{24,16},{1,9},{9,1},{17,25},{25,17},{2,10},{10... | collective-permute-start | bytes 2359304 | tf_op jit(solution)/shard_map/ppermute | solution.py:1023
  70.2 20.0 %collective-permute-start.19 = (bf16[4,48,2048]{2,1,0:T(8,128)(2,1)S(1)}, bf16[4,48,2048]{2,1,0:T(8,128)(2,1)S(1)}, u32[]{:S(2)}, u32[]{:S(2)}) collective-permute-start(bf16[4,48,2048]{2,1,0:T(8,128)(2,1)S(1)} %pad_maximum_fusion.2.refs_4_), channel_id=1, source_target_pairs={{0,16},{8,24},{16,0},{24,8},{1,17},{9,25},{17,1},{25,9},{2,18},{10... | collective-permute-start | bytes 2359304 | tf_op jit(solution)/shard_map/ppermute | solution.py:1023
  71.7 18.4 %collective-permute-start.22 = (bf16[4,48,2048]{2,1,0:T(8,128)(2,1)S(1)}, bf16[4,48,2048]{2,1,0:T(8,128)(2,1)S(1)}, u32[]{:S(2)}, u32[]{:S(2)}) collective-permute-start(bf16[4,48,2048]{2,1,0:T(8,128)(2,1)S(1)} %pad_maximum_fusion.3.refs_6_), channel_id=1, source_target_pairs={{0,8},{8,0},{16,24},{24,16},{1,9},{9,1},{17,25},{25,17},{2,10},{10... | collective-permute-start | bytes 2359304 | tf_op jit(solution)/shard_map/ppermute | solution.py:1023
  71.9 19.8 %collective-permute-start.20 = (bf16[4,48,2048]{2,1,0:T(8,128)(2,1)S(1)}, bf16[4,48,2048]{2,1,0:T(8,128)(2,1)S(1)}, u32[]{:S(2)}, u32[]{:S(2)}) collective-permute-start(bf16[4,48,2048]{2,1,0:T(8,128)(2,1)S(1)} %pad_maximum_fusion.3.refs_6_), channel_id=1, source_target_pairs={{0,1},{1,0},{2,3},{3,2},{4,5},{5,4},{6,7},{7,6},{8,9},{9,8},{10,11... | collective-permute-start | bytes 2359304 | tf_op jit(solution)/shard_map/ppermute | solution.py:1023
  102.4 27.6 %collective-permute-start.27 = (bf16[4,2,48,768]{3,2,1,0:T(8,128)(2,1)S(1)}, bf16[4,2,48,768]{3,2,1,0:T(8,128)(2,1)S(1)}, u32[]{:S(2)}, u32[]{:S(2)}) collective-permute-start(bf16[4,2,48,768]{3,2,1,0:T(8,128)(2,1)S(1)} %pad_maximum_fusion.4.refs_9_), channel_id=1, source_target_pairs={{0,8},{8,0},{16,24},{24,16},{1,9},{9,1},{17,25},{25,17},{2,10},{10... | collective-permute-start | bytes 1769480 | tf_op jit(solution)/shard_map/ppermute | solution.py:1023
  102.4 27.6 %collective-permute-start.25 = (bf16[4,2,48,768]{3,2,1,0:T(8,128)(2,1)S(1)}, bf16[4,2,48,768]{3,2,1,0:T(8,128)(2,1)S(1)}, u32[]{:S(2)}, u32[]{:S(2)}) collective-permute-start(bf16[4,2,48,768]{3,2,1,0:T(8,128)(2,1)S(1)} %pad_maximum_fusion.4.refs_9_), channel_id=1, source_target_pairs={{0,16},{8,24},{16,0},{24,8},{1,17},{9,25},{17,1},{25,9},{2,18},{10... | collective-permute-start | bytes 1769480 | tf_op jit(solution)/shard_map/ppermute | solution.py:1023
  103.1 26.9 %collective-permute-start.28 = (bf16[4,2,48,768]{3,2,1,0:T(8,128)(2,1)S(1)}, bf16[4,2,48,768]{3,2,1,0:T(8,128)(2,1)S(1)}, u32[]{:S(2)}, u32[]{:S(2)}) collective-permute-start(bf16[4,2,48,768]{3,2,1,0:T(8,128)(2,1)S(1)} %pad_maximum_fusion.5.refs_11_), channel_id=1, source_target_pairs={{0,8},{8,0},{16,24},{24,16},{1,9},{9,1},{17,25},{25,17},{2,10},{10... | collective-permute-start | bytes 1769480 | tf_op jit(solution)/shard_map/ppermute | solution.py:1023
  103.4 26.7 %collective-permute-start.26 = (bf16[4,2,48,768]{3,2,1,0:T(8,128)(2,1)S(1)}, bf16[4,2,48,768]{3,2,1,0:T(8,128)(2,1)S(1)}, u32[]{:S(2)}, u32[]{:S(2)}) collective-permute-start(bf16[4,2,48,768]{3,2,1,0:T(8,128)(2,1)S(1)} %pad_maximum_fusion.5.refs_11_), channel_id=1, source_target_pairs={{0,1},{1,0},{2,3},{3,2},{4,5},{5,4},{6,7},{7,6},{8,9},{9,8},{10,11... | collective-permute-start | bytes 1769480 | tf_op jit(solution)/shard_map/ppermute | solution.py:1023
  204.9 12.7 %collective-permute-start.34 = (bf16[16,2,48,768]{3,2,1,0:T(8,128)(2,1)}, bf16[16,2,48,768]{3,2,1,0:T(8,128)(2,1)S(1)}, u32[]{:S(2)}, u32[]{:S(2)}) collective-permute-start(bf16[16,2,48,768]{3,2,1,0:T(8,128)(2,1)} %up_grad.2), channel_id=1, source_target_pairs={{0,8},{8,0},{16,24},{24,16},{1,9},{9,1},{17,25},{25,17},{2,10},{10... | collective-permute-start | bytes 7077896 | tf_op jit(solution)/shard_map/ppermute | solution.py:1023
  205.3 22.8 %collective-permute-start.32 = (bf16[4,3,48,768]{3,2,1,0:T(8,128)(2,1)}, bf16[4,3,48,768]{3,2,1,0:T(8,128)(2,1)}, u32[]{:S(2)}, u32[]{:S(2)}) collective-permute-start(bf16[4,3,48,768]{3,2,1,0:T(8,128)(2,1)} %get-tuple-element.317), channel_id=1, source_target_pairs={{0,16},{8,24},{16,0},{24,8},{1,17},{9,25},{17,1},{25,9},{2,18},{10... | collective-permute-start | bytes 2654216 | tf_op jit(solution)/shard_map/ppermute | solution.py:1023
  206.6 22.9 %collective-permute-start.33 = (bf16[4,3,48,768]{3,2,1,0:T(8,128)(2,1)}, bf16[4,3,48,768]{3,2,1,0:T(8,128)(2,1)}, u32[]{:S(2)}, u32[]{:S(2)}) collective-permute-start(bf16[4,3,48,768]{3,2,1,0:T(8,128)(2,1)} %get-tuple-element.318), channel_id=1, source_target_pairs={{0,1},{1,0},{2,3},{3,2},{4,5},{5,4},{6,7},{7,6},{8,9},{9,8},{10,11... | collective-permute-start | bytes 2654216 | tf_op jit(solution)/shard_map/ppermute | solution.py:1023
  219.3 31.0 %collective-permute-start.37 = (bf16[4,2,48,768]{3,2,1,0:T(8,128)(2,1)S(1)}, bf16[4,2,48,768]{3,2,1,0:T(8,128)(2,1)S(1)}, u32[]{:S(2)}, u32[]{:S(2)}) collective-permute-start(bf16[4,2,48,768]{3,2,1,0:T(8,128)(2,1)S(1)} %get-tuple-element.339), channel_id=1, source_target_pairs={{0,16},{8,24},{16,0},{24,8},{1,17},{9,25},{17,1},{25,9},{2,18},{10... | collective-permute-start | bytes 1769480 | tf_op jit(solution)/shard_map/ppermute | solution.py:1023
  220.1 30.2 %collective-permute-start.38 = (bf16[4,2,48,768]{3,2,1,0:T(8,128)(2,1)S(1)}, bf16[4,2,48,768]{3,2,1,0:T(8,128)(2,1)S(1)}, u32[]{:S(2)}, u32[]{:S(2)}) collective-permute-start(bf16[4,2,48,768]{3,2,1,0:T(8,128)(2,1)S(1)} %get-tuple-element.340), channel_id=1, source_target_pairs={{0,1},{1,0},{2,3},{3,2},{4,5},{5,4},{6,7},{7,6},{8,9},{9,8},{10,11... | collective-permute-start | bytes 1769480 | tf_op jit(solution)/shard_map/ppermute | solution.py:1023
  232.2 18.2 %collective-permute-start.35 = (bf16[2,3,48,768]{3,2,1,0:T(8,128)(2,1)S(1)}, bf16[2,3,48,768]{3,2,1,0:T(8,128)(2,1)S(1)}, u32[]{:S(2)}, u32[]{:S(2)}) collective-permute-start(bf16[2,3,48,768]{3,2,1,0:T(8,128)(2,1)S(1)} %slice.241), channel_id=1, source_target_pairs={{0,1},{1,0},{2,3},{3,2},{4,5},{5,4},{6,7},{7,6},{8,9},{9,8},{10,11... | collective-permute-start | bytes 1327112 | tf_op jit(solution)/shard_map/ppermute | solution.py:1023
  233.6 16.8 %collective-permute-start.36 = (bf16[2,3,48,768]{3,2,1,0:T(8,128)(2,1)S(1)}, bf16[2,3,48,768]{3,2,1,0:T(8,128)(2,1)S(1)}, u32[]{:S(2)}, u32[]{:S(2)}) collective-permute-start(bf16[2,3,48,768]{3,2,1,0:T(8,128)(2,1)S(1)} %slice.242), channel_id=1, source_target_pairs={{0,16},{8,24},{16,0},{24,8},{1,17},{9,25},{17,1},{25,9},{2,18},{10... | collective-permute-start | bytes 1327112 | tf_op jit(solution)/shard_map/ppermute | solution.py:1023
  251.2 11.6 %collective-permute-start.39 = (bf16[2,2,48,768]{3,2,1,0:T(8,128)(2,1)S(1)}, bf16[2,2,48,768]{3,2,1,0:T(8,128)(2,1)S(1)}, u32[]{:S(2)}, u32[]{:S(2)}) collective-permute-start(bf16[2,2,48,768]{3,2,1,0:T(8,128)(2,1)S(1)} %slice.248), channel_id=1, source_target_pairs={{0,1},{1,0},{2,3},{3,2},{4,5},{5,4},{6,7},{7,6},{8,9},{9,8},{10,11... | collective-permute-start | bytes 884744 | tf_op jit(solution)/shard_map/ppermute | solution.py:1023
  255.4 23.6 %collective-permute-start.42 = (bf16[3,48,768]{2,1,0:T(8,128)(2,1)S(1)}, bf16[3,48,768]{2,1,0:T(8,128)(2,1)S(1)}, u32[]{:S(2)}, u32[]{:S(2)}) collective-permute-start(bf16[3,48,768]{2,1,0:T(8,128)(2,1)S(1)} %get-tuple-element.365), channel_id=1, source_target_pairs={{0,4},{1,5},{2,6},{3,7},{4,0},{5,1},{6,2},{7,3},{8,12},{9,13},{10,... | collective-permute-start | bytes 663560 | tf_op jit(solution)/shard_map/ppermute | solution.py:1023
  256.3 22.7 %collective-permute-start.43 = (bf16[3,48,768]{2,1,0:T(8,128)(2,1)S(1)}, bf16[3,48,768]{2,1,0:T(8,128)(2,1)S(1)}, u32[]{:S(2)}, u32[]{:S(2)}) collective-permute-start(bf16[3,48,768]{2,1,0:T(8,128)(2,1)S(1)} %get-tuple-element.366), channel_id=1, source_target_pairs={{0,6},{1,7},{2,4},{3,5},{4,2},{5,3},{6,0},{7,1},{8,14},{9,15},{10,... | collective-permute-start | bytes 663560 | tf_op jit(solution)/shard_map/ppermute | solution.py:1023
  297.4 15.4 %collective-permute-start.46 = (bf16[4,48,1280]{2,1,0:T(8,128)(2,1)S(1)}, bf16[4,48,1280]{2,1,0:T(8,128)(2,1)S(1)}, u32[]{:S(2)}, u32[]{:S(2)}) collective-permute-start(bf16[4,48,1280]{2,1,0:T(8,128)(2,1)S(1)} %get-tuple-element.388), channel_id=1, source_target_pairs={{0,16},{8,24},{16,0},{24,8},{1,17},{9,25},{17,1},{25,9},{2,18},{10... | collective-permute-start | bytes 1474568 | tf_op jit(solution)/shard_map/ppermute | solution.py:1023
  298.7 14.0 %collective-permute-start.47 = (bf16[4,48,1280]{2,1,0:T(8,128)(2,1)S(1)}, bf16[4,48,1280]{2,1,0:T(8,128)(2,1)S(1)}, u32[]{:S(2)}, u32[]{:S(2)}) collective-permute-start(bf16[4,48,1280]{2,1,0:T(8,128)(2,1)S(1)} %get-tuple-element.389), channel_id=1, source_target_pairs={{0,1},{1,0},{2,3},{3,2},{4,5},{5,4},{6,7},{7,6},{8,9},{9,8},{10,11... | collective-permute-start | bytes 1474568 | tf_op jit(solution)/shard_map/ppermute | solution.py:1023
  299.4 13.4 %collective-permute-start.48 = (bf16[2,48,768]{2,1,0:T(8,128)(2,1)S(1)}, bf16[2,48,768]{2,1,0:T(8,128)(2,1)S(1)}, u32[]{:S(2)}, u32[]{:S(2)}) collective-permute-start(bf16[2,48,768]{2,1,0:T(8,128)(2,1)S(1)} %get-tuple-element.391), channel_id=1, source_target_pairs={{0,4},{1,5},{2,6},{3,7},{4,0},{5,1},{6,2},{7,3},{8,12},{9,13},{10,... | collective-permute-start | bytes 442376 | tf_op jit(solution)/shard_map/ppermute | solution.py:1023
  301.5 11.3 %collective-permute-start.49 = (bf16[2,48,768]{2,1,0:T(8,128)(2,1)S(1)}, bf16[2,48,768]{2,1,0:T(8,128)(2,1)S(1)}, u32[]{:S(2)}, u32[]{:S(2)}) collective-permute-start(bf16[2,48,768]{2,1,0:T(8,128)(2,1)S(1)} %get-tuple-element.392), channel_id=1, source_target_pairs={{0,6},{1,7},{2,4},{3,5},{4,2},{5,3},{6,0},{7,1},{8,14},{9,15},{10,... | collective-permute-start | bytes 442376 | tf_op jit(solution)/shard_map/ppermute | solution.py:1023
  321.6 15.1 %collective-permute-start.55 = (bf16[5,48,768]{2,1,0:T(8,128)(2,1)S(1)}, bf16[5,48,768]{2,1,0:T(8,128)(2,1)S(1)}, u32[]{:S(2)}, u32[]{:S(2)}) collective-permute-start(bf16[5,48,768]{2,1,0:T(8,128)(2,1)S(1)} %pad_maximum_fusion.10.refs_0_), channel_id=1, source_target_pairs={{0,16},{8,24},{16,0},{24,8},{1,17},{9,25},{17,1},{25,9},{2,18},{10... | collective-permute-start | bytes 1105928 | tf_op jit(solution)/shard_map/ppermute | solution.py:1023
  326.1 10.6 %collective-permute-start.53 = (bf16[48,1280]{1,0:T(8,128)(2,1)S(1)}, bf16[48,1280]{1,0:T(8,128)(2,1)S(1)}, u32[]{:S(2)}, u32[]{:S(2)}) collective-permute-start(bf16[48,1280]{1,0:T(8,128)(2,1)S(1)} %get-tuple-element.404), channel_id=1, source_target_pairs={{0,4},{1,5},{2,6},{3,7},{4,0},{5,1},{6,2},{7,3},{8,12},{9,13},{10,... | collective-permute-start | bytes 368648 | tf_op jit(solution)/shard_map/ppermute | solution.py:1023
  (70 other events, 611.9 us)
